TPU v7x, 32 devices: a whole 2x2x4 slice. The times are simulated.
32 devices in a mesh: dp: 16 (over z, x, core), branch: 2 (over y).
Axes of the slice: x: 2, y: 2, z: 4, core: 2. Of those that a mesh axis runs over, the one named last changes fastest.
Arguments:
- tokens: bfloat16 [8192, 2048], P(('dp', 'branch')), may hold values from -6 to 6
- cotangent: bfloat16 [8192, 2048], P(('dp', 'branch')), may hold values from -6 to 6
- lengths: int32 [16, 2], P('dp'), may hold values from 64 to 256, as said below
- w_qkv: float32 [2048, 6144], P('dp', 'branch'), may hold values from -0.125 to 0.125
- w_out: float32 [2048, 2048], P('dp', 'branch'), may hold values from -0.5 to 0.5
- w_gate_up: float32 [2048, 11264], P('dp', 'branch'), may hold values from -0.125 to 0.125
- w_down: float32 [5632, 2048], P('dp', 'branch'), may hold values from -0.078125 to 0.078125
- vectors: float32 [5, 2048], P(None, ('dp', 'branch')), as said below
- first_qkv: float32 [2048, 6144], P('dp', 'branch'), may hold values from -27.1529 to 27.1529
- first_out: float32 [2048, 2048], P('dp', 'branch'), may hold values from -13.57645 to 13.57645
- first_gate_up: float32 [2048, 11264], P('dp', 'branch'), may hold values from -16.29174 to 16.29174
- first_down: float32 [5632, 2048], P('dp', 'branch'), may hold values from -27.1529 to 27.1529
- first_vectors: float32 [5, 2048], P(None, ('dp', 'branch')), may hold values from -54.3058 to 54.3058
- second_qkv: float32 [2048, 6144], P('dp', 'branch'), may hold values from 106.496 to 434.176
- second_out: float32 [2048, 2048], P('dp', 'branch'), may hold values from 27.0336 to 106.496
- second_gate_up: float32 [2048, 11264], P('dp', 'branch'), may hold values from 38.5024 to 155.648
- second_down: float32 [5632, 2048], P('dp', 'branch'), may hold values from 106.496 to 434.176
- second_vectors: float32 [5, 2048], P(None, ('dp', 'branch')), may hold values from 434.176 to 1720.32
Outputs:
- output: bfloat16 [8192, 2048], P(('dp', 'branch'))
- input_grad: bfloat16 [8192, 2048], P(('dp', 'branch'))
- new_qkv: float32 [2048, 6144], P('dp', 'branch')
- new_out: float32 [2048, 2048], P('dp', 'branch')
- new_gate_up: float32 [2048, 11264], P('dp', 'branch')
- new_down: float32 [5632, 2048], P('dp', 'branch')
- new_vectors: float32 [5, 2048], P(None, ('dp', 'branch'))
- moment_qkv: float32 [2048, 6144], P('dp', 'branch')
- moment_out: float32 [2048, 2048], P('dp', 'branch')
- moment_gate_up: float32 [2048, 11264], P('dp', 'branch')
- moment_down: float32 [5632, 2048], P('dp', 'branch')
- moment_vectors: float32 [5, 2048], P(None, ('dp', 'branch'))
- square_qkv: float32 [2048, 6144], P('dp', 'branch')
- square_out: float32 [2048, 2048], P('dp', 'branch')
- square_gate_up: float32 [2048, 11264], P('dp', 'branch')
- square_down: float32 [5632, 2048], P('dp', 'branch')
- square_vectors: float32 [5, 2048], P(None, ('dp', 'branch'))
Inputs may be any that keep to these rules, and one draw needn't show every extreme that they name: `lengths`: some slot has length exactly 256. `vectors`: row 0 is the norm's gain, row 1 its shift, rows 2 to 4 the query, key and value biases.
All inputs are finite; a program needn't handle non-finite values.
Results may differ from a plain program's by a relative error of at most 0.0091.
Values may be sent and summed in bfloat16 or wider, within the bound.
No kernel may reach another device: no remote copies, remote signals or barrier semaphores. Data moves between devices by JAX's collectives and lax.ppermute only.
A program may use at most 896 MiB of HBM per device.

v0:
```python
import jax
import jax.numpy as jnp
from jax import lax
from jax.sharding import PartitionSpec as P

HEADS = 32
HEAD = 64
ROT = 16
MB = 2
STEP = 10


theta_base = 10000.0
norm_eps = 1e-05
beta_one = 0.9
beta_two = 0.95
adam_eps = 1e-08
decay_rate = 0.1
rate_matrix = 0.05
rate_vector = 1.0


def rounded(value):
    return lax.optimization_barrier(value.astype(jnp.bfloat16)).astype(jnp.float32)


def rotary_tables(row_count):
    half_rot = ROT // 2
    freqs = theta_base ** (-2.0 * jnp.arange(half_rot, dtype=jnp.float32) / ROT)
    angles = jnp.arange(row_count, dtype=jnp.float32)[:, None] * freqs[None, :]
    return (jnp.cos(angles)[:, None, :], jnp.sin(angles)[:, None, :])


def rotate(values, cosine, sine):
    half_rot = cosine.shape[-1]
    rot_one = values[..., :half_rot]
    rot_two = values[..., half_rot : 2 * half_rot]
    return jnp.concatenate(
        [
            rot_one * cosine - rot_two * sine,
            rot_two * cosine + rot_one * sine,
            values[..., 2 * half_rot :],
        ],
        axis=-1,
    )


def unrotate(grads_in, cosine, sine):
    half_rot = cosine.shape[-1]
    rot_one = grads_in[..., :half_rot]
    rot_two = grads_in[..., half_rot : 2 * half_rot]
    return jnp.concatenate(
        [
            rot_one * cosine + rot_two * sine,
            rot_two * cosine - rot_one * sine,
            grads_in[..., 2 * half_rot :],
        ],
        axis=-1,
    )


def normalize(block_rows, gain_row, shift_row):
    row_mean = jnp.mean(block_rows, axis=-1, keepdims=True)
    centered = block_rows - row_mean
    inv_std = lax.rsqrt(jnp.mean(centered * centered, axis=-1, keepdims=True) + norm_eps)
    scaled = centered * inv_std
    return (scaled * gain_row + shift_row, scaled, inv_std)


def attention_pass(normed_rows, grad_rows, length, w_qkv_full, w_out_full, qkv_bias, cosine, sine):
    row_count = normed_rows.shape[0]
    width_model = w_out_full.shape[0]
    score_scale = HEAD ** (-0.5)
    qkv = jnp.dot(normed_rows, w_qkv_full, preferred_element_type=jnp.float32) + qkv_bias
    queries = rotate(qkv[:, :width_model].reshape(row_count, HEADS, HEAD), cosine, sine).astype(
        jnp.bfloat16
    )
    key_rot = rotate(
        qkv[:, width_model : 2 * width_model].reshape(row_count, HEADS, HEAD), cosine, sine
    ).astype(jnp.bfloat16)
    values = qkv[:, 2 * width_model :].reshape(row_count, HEADS, HEAD).astype(jnp.bfloat16)
    scores = (
        jnp.einsum("qhd,khd->hqk", queries, key_rot, preferred_element_type=jnp.float32)
        * score_scale
    )
    position = jnp.arange(row_count, dtype=jnp.int32)
    allowed = (position[None, :] <= position[:, None]) & (position[None, :] < length)
    masked = jnp.where(allowed[None], scores, -1e30)
    row_max = jnp.max(masked, axis=-1, keepdims=True)
    exp_scores = jnp.exp(masked - row_max)
    probs = exp_scores / jnp.sum(exp_scores, axis=-1, keepdims=True)
    probs_low = probs.astype(jnp.bfloat16)
    attended = jnp.einsum("hqk,khd->qhd", probs_low, values, preferred_element_type=jnp.float32)
    attended_low = attended.reshape(row_count, width_model).astype(jnp.bfloat16)
    branch_rows = rounded(jnp.dot(attended_low, w_out_full, preferred_element_type=jnp.float32))
    d_attn = jnp.einsum("re,de->rd", grad_rows, w_out_full, preferred_element_type=jnp.float32)
    d_attn = d_attn.astype(jnp.bfloat16).reshape(row_count, HEADS, HEAD)
    d_probs = jnp.einsum("qhd,khd->hqk", d_attn, values, preferred_element_type=jnp.float32)
    d_values = jnp.einsum("hqk,qhd->khd", probs_low, d_attn, preferred_element_type=jnp.float32)
    d_scores = probs * (d_probs - jnp.sum(probs * d_probs, axis=-1, keepdims=True))
    scores_low = d_scores.astype(jnp.bfloat16)
    d_query = (
        jnp.einsum("hqk,khd->qhd", scores_low, key_rot, preferred_element_type=jnp.float32)
        * score_scale
    )
    d_keys = (
        jnp.einsum("hqk,qhd->khd", scores_low, queries, preferred_element_type=jnp.float32)
        * score_scale
    )
    d_qkv = jnp.concatenate(
        [
            unrotate(d_query, cosine, sine).reshape(row_count, width_model),
            unrotate(d_keys, cosine, sine).reshape(row_count, width_model),
            d_values.reshape(row_count, width_model),
        ],
        axis=1,
    ).astype(jnp.bfloat16)
    g_bias = jnp.sum(d_qkv.astype(jnp.float32), axis=0)
    d_normed = jnp.einsum("rf,df->rd", d_qkv, w_qkv_full, preferred_element_type=jnp.float32)
    return (branch_rows, d_normed, attended_low, d_qkv, g_bias)


def mlp_pass(normed_rows, grad_rows, w_gu_full, w_down_full):
    hidden_width = w_down_full.shape[0]
    joined = jnp.dot(normed_rows, w_gu_full, preferred_element_type=jnp.float32)
    gate_part = joined[:, :hidden_width]
    up_part = joined[:, hidden_width:]
    sig_gate = jax.nn.sigmoid(gate_part)
    activated = gate_part * sig_gate
    hidden_low = (activated * up_part).astype(jnp.bfloat16)
    branch_rows = rounded(jnp.dot(hidden_low, w_down_full, preferred_element_type=jnp.float32))
    d_hidden = jnp.einsum("rd,fd->rf", grad_rows, w_down_full, preferred_element_type=jnp.float32)
    d_gate = d_hidden * up_part * sig_gate * (1.0 + gate_part * (1.0 - sig_gate))
    d_up = d_hidden * activated
    d_joined = jnp.concatenate([d_gate, d_up], axis=1).astype(jnp.bfloat16)
    d_normed = jnp.einsum("rf,df->rd", d_joined, w_gu_full, preferred_element_type=jnp.float32)
    return (branch_rows, d_normed, hidden_low, d_joined)


def attention_micro(operands):
    normed_rows, grad_rows, length, full_a, full_b, qkv_bias, cosine, sine, total_a, total_b = (
        operands
    )
    width_model = full_b.shape[1]
    w_qkv_full = full_a[:, : 3 * width_model]
    w_out_full = full_a[:, 3 * width_model : 4 * width_model]
    branch_rows, d_normed, attended_low, d_qkv, g_bias = attention_pass(
        normed_rows, grad_rows, length, w_qkv_full, w_out_full, qkv_bias, cosine, sine
    )
    g_qkv = jnp.einsum("rd,rf->df", normed_rows, d_qkv, preferred_element_type=jnp.float32)
    g_out = jnp.einsum("rd,re->de", attended_low, grad_rows, preferred_element_type=jnp.float32)
    total_a = total_a.at[:, : 3 * width_model].add(g_qkv)
    total_a = total_a.at[:, 3 * width_model : 4 * width_model].add(g_out)
    hidden_none = jnp.zeros((normed_rows.shape[0], full_b.shape[0]), jnp.bfloat16)
    return (branch_rows, d_normed, total_a, total_b, g_bias, hidden_none)


def mlp_micro(operands):
    normed_rows, grad_rows, length, full_a, full_b, qkv_bias, cosine, sine, total_a, total_b = (
        operands
    )
    branch_rows, d_normed, hidden_low, d_joined = mlp_pass(normed_rows, grad_rows, full_a, full_b)
    total_a = total_a + jnp.einsum(
        "rd,rf->df", normed_rows, d_joined, preferred_element_type=jnp.float32
    )
    total_b = total_b + jnp.einsum(
        "rf,rd->fd", hidden_low, grad_rows, preferred_element_type=jnp.float32
    )
    bias_none = jnp.zeros(qkv_bias.shape, jnp.float32)
    return (branch_rows, d_normed, total_a, total_b, bias_none, hidden_low)


def adam_update(weight, gradient, first_moment, second_moment, step_rate, decay):
    moment_new = beta_one * first_moment + (1.0 - beta_one) * gradient
    square_new = beta_two * second_moment + (1.0 - beta_two) * gradient * gradient
    moment_hat = moment_new / (1.0 - beta_one**STEP)
    square_hat = square_new / (1.0 - beta_two**STEP)
    weight_new = weight - step_rate * (
        moment_hat / (jnp.sqrt(square_hat) + adam_eps) + decay * weight
    )
    return (weight_new, moment_new, square_new)


def per_device(
    tokens,
    cotangent,
    lengths,
    w_qkv,
    w_out,
    w_gate_up,
    w_down,
    vectors,
    first_qkv,
    first_out,
    first_gate_up,
    first_down,
    first_vectors,
    second_qkv,
    second_out,
    second_gate_up,
    second_down,
    second_vectors,
):
    row_count = tokens.shape[0]
    pair_tokens, pair_grads = (
        lax.all_gather(tokens, "branch", axis=0, tiled=True),
        lax.all_gather(cotangent, "branch", axis=0, tiled=True),
    )
    pair_weights = (
        lax.all_gather(w_qkv.astype(jnp.bfloat16), "branch", axis=1, tiled=True),
        lax.all_gather(w_out.astype(jnp.bfloat16), "branch", axis=1, tiled=True),
        lax.all_gather(w_gate_up.astype(jnp.bfloat16), "branch", axis=1, tiled=True),
        lax.all_gather(w_down.astype(jnp.bfloat16), "branch", axis=1, tiled=True),
    )
    all_vectors = lax.all_gather(vectors, ("dp", "branch"), axis=1, tiled=True)
    gain_row = all_vectors[0]
    shift_row = all_vectors[1]
    qkv_bias = all_vectors[2:5].reshape(-1)
    normed_pair, scaled_pair, inv_pair = normalize(
        pair_tokens.astype(jnp.float32), gain_row, shift_row
    )
    normed_low = normed_pair.astype(jnp.bfloat16)
    cosine, sine = rotary_tables(row_count)
    side_index = lax.axis_index("branch")
    is_attention = side_index == 0
    width_qkv = pair_weights[0].shape[1]
    width_model = pair_weights[1].shape[1]
    width_joined = pair_weights[2].shape[1]
    attn_packed = jnp.concatenate([pair_weights[0], pair_weights[1]], axis=1)
    attn_packed = jnp.pad(attn_packed, ((0, 0), (0, width_joined - width_qkv - width_model)))
    held_a = jnp.where(is_attention, attn_packed, pair_weights[2])
    held_b = jnp.where(is_attention, jnp.zeros_like(pair_weights[3]), pair_weights[3])
    full_rows = pair_weights[0].shape[0] * lax.axis_size("dp")
    full_hidden = pair_weights[3].shape[0] * lax.axis_size("dp")
    total_a = jnp.zeros((full_rows, width_joined), jnp.float32)
    total_b = jnp.zeros((full_hidden, width_model), jnp.float32)
    branch_list = []
    normal_list = []
    hidden_list = []
    for micro_index in range(MB):
        full_a, full_b = (
            lax.all_gather(held_a, "dp", axis=0, tiled=True),
            lax.all_gather(held_b, "dp", axis=0, tiled=True),
        )
        lower = micro_index * row_count
        upper = lower + row_count
        start_a, start_b = (total_a, total_b)
        operands = (
            normed_low[lower:upper],
            pair_grads[lower:upper],
            lengths[0, micro_index],
            full_a,
            full_b,
            qkv_bias,
            cosine,
            sine,
            start_a,
            start_b,
        )
        branch_rows, d_normed, grad_a, grad_b, g_bias, hidden_low = lax.cond(
            is_attention, attention_micro, mlp_micro, operands
        )
        total_a, total_b = (grad_a, grad_b)
        if micro_index == 0:
            total_bias = g_bias
        else:
            total_bias = total_bias + g_bias
        branch_list.append(branch_rows)
        normal_list.append(d_normed)
        hidden_list.append(hidden_low)
    shard_a, shard_b = (
        lax.psum_scatter(total_a, "dp", scatter_dimension=0, tiled=True),
        lax.psum_scatter(total_b, "dp", scatter_dimension=0, tiled=True),
    )
    branch_pair = jnp.concatenate(branch_list, axis=0)
    normal_pair = jnp.concatenate(normal_list, axis=0)
    branch_own, normal_own = (
        lax.psum_scatter(branch_pair, "branch", scatter_dimension=0, tiled=True),
        lax.psum_scatter(normal_pair, "branch", scatter_dimension=0, tiled=True),
    )
    output = (tokens.astype(jnp.float32) + branch_own).astype(jnp.bfloat16)
    scaled_own = lax.dynamic_slice_in_dim(scaled_pair, side_index * row_count, row_count, 0)
    inv_own = lax.dynamic_slice_in_dim(inv_pair, side_index * row_count, row_count, 0)
    g_normed = rounded(normal_own)
    d_scaled = g_normed * gain_row
    input_grad = cotangent.astype(jnp.float32) + inv_own * (
        d_scaled
        - jnp.mean(d_scaled, axis=-1, keepdims=True)
        - scaled_own * jnp.mean(d_scaled * scaled_own, axis=-1, keepdims=True)
    )
    vector_part = jnp.concatenate(
        [
            jnp.sum(g_normed * scaled_own, axis=0)[None],
            jnp.sum(g_normed, axis=0)[None],
            total_bias.reshape(3, -1),
        ],
        axis=0,
    )
    vector_grad = lax.psum_scatter(vector_part, ("dp", "branch"), scatter_dimension=1, tiled=True)
    g_qkv = jnp.where(is_attention, shard_a[:, :width_qkv], 0.0)
    g_out = jnp.where(is_attention, shard_a[:, width_qkv : width_qkv + width_model], 0.0)
    g_gu = jnp.where(is_attention, 0.0, shard_a)
    own_qkv, own_out, own_gu, own_down = (
        lax.psum_scatter(g_qkv, "branch", scatter_dimension=1, tiled=True),
        lax.psum_scatter(g_out, "branch", scatter_dimension=1, tiled=True),
        lax.psum_scatter(g_gu, "branch", scatter_dimension=1, tiled=True),
        lax.psum_scatter(shard_b, "branch", scatter_dimension=1, tiled=True),
    )
    new_qkv, moment_qkv, square_qkv = adam_update(
        w_qkv, own_qkv, first_qkv, second_qkv, rate_matrix, decay_rate
    )
    new_out, moment_out, square_out = adam_update(
        w_out, own_out, first_out, second_out, rate_matrix, decay_rate
    )
    new_gu, moment_gu, square_gu = adam_update(
        w_gate_up, own_gu, first_gate_up, second_gate_up, rate_matrix, decay_rate
    )
    new_down, moment_down, square_down = adam_update(
        w_down, own_down, first_down, second_down, rate_matrix, decay_rate
    )
    new_vec, moment_vec, square_vec = adam_update(
        vectors, vector_grad, first_vectors, second_vectors, rate_vector, 0.0
    )
    return (
        output,
        input_grad.astype(jnp.bfloat16),
        new_qkv,
        new_out,
        new_gu,
        new_down,
        new_vec,
        moment_qkv,
        moment_out,
        moment_gu,
        moment_down,
        moment_vec,
        square_qkv,
        square_out,
        square_gu,
        square_down,
        square_vec,
    )


def solution(mesh):
    in_specs = (
        P(("dp", "branch"), None),
        P(("dp", "branch"), None),
        P("dp", None),
        P("dp", "branch"),
        P("dp", "branch"),
        P("dp", "branch"),
        P("dp", "branch"),
        P(None, ("dp", "branch")),
        P("dp", "branch"),
        P("dp", "branch"),
        P("dp", "branch"),
        P("dp", "branch"),
        P(None, ("dp", "branch")),
        P("dp", "branch"),
        P("dp", "branch"),
        P("dp", "branch"),
        P("dp", "branch"),
        P(None, ("dp", "branch")),
    )
    out_specs = (
        P(("dp", "branch"), None),
        P(("dp", "branch"), None),
        P("dp", "branch"),
        P("dp", "branch"),
        P("dp", "branch"),
        P("dp", "branch"),
        P(None, ("dp", "branch")),
        P("dp", "branch"),
        P("dp", "branch"),
        P("dp", "branch"),
        P("dp", "branch"),
        P(None, ("dp", "branch")),
        P("dp", "branch"),
        P("dp", "branch"),
        P("dp", "branch"),
        P("dp", "branch"),
        P(None, ("dp", "branch")),
    )
    return jax.shard_map(
        per_device, mesh=mesh, in_specs=in_specs, out_specs=out_specs, check_vma=False
    )
```

profile of v0, /device:TPU:0, one launch (start us, length us, event | category | flops | bytes accessed | tf_op | source)
XLA Modules:
  0.0 2785.7 jit_solution(2961871154834415139)
XLA Ops:
  14.8 23.8 all-gather.11.cloned.1.call-done
  39.9 8.8 all_gather.35
  48.7 19.2 all-gather.17.cloned.1.call-done
  68.0 44.1 %all-gather.19.cloned.1.call-done = bf16[128,11264]{1,0:T(8,128)(2,1)} async-done(((bf16[128,5632]{1,0:T(8,128)(2,1)}), bf16[128,11264]{1,0:T(8,128)(2,1)}) %all-gather.19.cloned.1.call-update) | async-done | bytes 2883600 | tf_op jit(solution)/shard_map/all_gather | solution.py:212
  115.2 69.5 %all-gather = f32[32,64,5]{1,2,0:T(8,128)S(1)} all-gather(f32[1,64,5]{1,2,0:T(8,128)S(1)} %bitcast.213), channel_id=1, replica_groups=mesh['dp'=16,'branch'=2] {'dp','branch'}, dimensions={0}, use_global_device_ids=true | all-gather | bytes 42240 | tf_op jit(solution)/shard_map/all_gather | solution.py:215
  192.0 3.3 fusion.116
  195.3 108.6 %all-gather.13.cloned.1.call-done = bf16[5632,2048]{1,0:T(8,128)(2,1)} async-done(((bf16[352,2048]{1,0:T(8,128)(2,1)}), bf16[5632,2048]{1,0:T(8,128)(2,1)}) %all-gather.13.cloned.1.call-update) | async-done | bytes 23068688 | tf_op jit(solution)/shard_map/all_gather | solution.py:243
  303.9 229.5 %all-gather.21.cloned.1.call-done = bf16[2048,11264]{1,0:T(8,128)(2,1)} async-done(((bf16[128,11264]{1,0:T(8,128)(2,1)}), bf16[2048,11264]{1,0:T(8,128)(2,1)}) %all-gather.21.cloned.1.call-update) | async-done | bytes 46137360 | tf_op jit(solution)/shard_map/all_gather | solution.py:242
  533.4 189.4 %conditional.6 = (f32[256,2048]{1,0:T(8,128)}, f32[2048,11264]{0,1:T(8,128)}, f32[5632,2048]{1,0:T(8,128)}, f32[6144]{0:T(1024)S(1)}, bf16[256,2048]{1,0:T(8,128)(2,1)}) conditional(s32[]{:T(128)} %convert_element_type.131, (bf16[256,2048]{1,0:T(8,128)(2,1)}, bf16[5632,2048]{1,0:T(8,128)(2,1)}, bf16[256,2048]{1,0:T(8,128)(2,1)S(1)}, ...), branch_computations={%region_2.3_spmd, %region_3.10_spmd} | conditional | flops 53195440128 | bytes 529827168
  540.6 7.0 fusion.20
  549.9 12.1 fusion.9
  572.8 3.3 copy.135
  580.5 8.1 fusion.112
  588.7 6.1 fusion.30
  597.3 6.8 fusion.23
  612.5 14.1 fusion.5
  629.5 21.8 select_bitcast_fusion
  651.4 46.2 %scatter-add.5 = f32[2048,11264]{0,1:T(8,128)} pad(f32[2048,6144]{0,1:T(8,128)} %select_bitcast_fusion, f32[]{:T(128)} %constant.193.clone), padding=0_0x0_5120 | pad | bytes 142606336 | tf_op jit(solution)/shard_map/cond/branch_1_fun/scatter-add | solution.py:152
  697.5 10.1 select_dynamic-update-slice_fusion
  707.6 15.0 broadcast_in_dim.37
  723.4 338.8 %conditional.7 = (f32[256,2048]{1,0:T(8,128)S(1)}, f32[5632,2048]{1,0:T(8,128)}, f32[6144]{0:T(1024)}, bf16[256,2048]{1,0:T(8,128)(2,1)}, f32[2048,11264]{1,0:T(8,128)}) conditional(s32[]{:T(128)} %convert_element_type.131, (bf16[256,2048]{1,0:T(8,128)(2,1)S(1)}, bf16[5632,2048]{1,0:T(8,128)(2,1)}, bf16[256,2048]{1,0:T(8,128)(2,1)S(1)}, ...), branch_computations={%region_10.11_spmd, %region_11.18_spmd} | conditional | flops 53230043136 | bytes 899220672
  739.6 5.8 fusion.62
  746.7 12.1 fusion.51
  773.9 5.0 fusion.114
  778.9 6.2 fusion.72
  787.4 6.8 fusion.65
  800.9 13.3 fusion.46
  816.8 33.2 %add_select_fusion = f32[2048,6144]{0,1:T(8,128)} fusion(f32[2048,11264]{0,1:T(8,128)} %get-tuple-element.210, bf16[256,2048]{1,0:T(8,128)(2,1)S(1)} %get-tuple-element.189, pred[]{:T(512)} %compare_reduce_fusion.3, bf16[256,2048]{0,1:T(8,128)(2,1)} %bitcast.158, bf16[256,2048]{0,1:T(8,128)(2,1)S(1)} %bitcast.144, bf16[256,2048]{0,1:T(8,128)(2,1)S(1)} %bitcast.138), kind=kOutput, calls=%fused_computation.82 | convolution fusion | flops 6477053952 | bytes 104857600 | tf_op jit(solution)/shard_map/cond/branch_1_fun/rd,rf->df/dot_general | solution.py:150
  850.1 83.7 %copy.150 = f32[2048,11264]{1,0:T(8,128)} copy(f32[2048,11264]{0,1:T(8,128)} %get-tuple-element.210) | data formatting | bytes 184549376 | tf_op jit(solution)/shard_map
  933.7 48.9 %copy.151 = f32[2048,6144]{1,0:T(8,128)} copy(f32[2048,6144]{0,1:T(8,128)} %add_select_fusion) | data formatting | bytes 100663296 | tf_op jit(solution)/shard_map/select.6
  982.6 34.9 %constant_dynamic-update-slice_fusion = f32[2048,11264]{1,0:T(8,128)} fusion(f32[2048,11264]{1,0:T(8,128)} %copy.150, f32[2048,6144]{1,0:T(8,128)} %copy.151), kind=kLoop, calls=%fused_computation.138 | loop fusion | bytes 100663296 | tf_op jit(solution)/shard_map/cond/branch_1_fun/scatter-add | solution.py:152
  1017.5 11.3 fusion.50
  1028.8 33.2 %copy.188 = f32[5632,2048]{1,0:T(8,128)} copy(f32[5632,2048]{1,0:T(8,128)} %get-tuple-element.360) | data formatting | bytes 92274688 | tf_op jit(solution)/shard_map/conditional.3
  1062.2 4.0 pad_maximum_fusion.40
  1072.6 47.1 %reduce-scatter.14.cloned.1.call-done = f32[256,2048]{1,0:T(8,128)} async-done(((f32[512,2048]{1,0:T(8,128)}), f32[256,2048]{1,0:T(8,128)}) %reduce-scatter.14.cloned.1.call-update) | async-done | bytes 2097168 | tf_op jit(solution)/shard_map/reduce_scatter | solution.py:279
  1125.3 432.3 %reduce-scatter.24.cloned.1.call-done = f32[352,2048]{1,0:T(8,128)} async-done(((f32[5632,2048]{1,0:T(8,128)}), f32[352,2048]{1,0:T(8,128)}) %reduce-scatter.24.cloned.1.call-update) | async-done | bytes 2883600 | tf_op jit(solution)/shard_map/reduce_scatter | solution.py:273
  1557.6 840.4 %reduce-scatter.16.cloned.1.call-done = f32[128,11264]{1,0:T(8,128)} async-done(((f32[2048,11264]{1,0:T(8,128)}), f32[128,11264]{1,0:T(8,128)}) %reduce-scatter.16.cloned.1.call-update) | async-done | bytes 5767184 | tf_op jit(solution)/shard_map/reduce_scatter | solution.py:272
  2400.4 3.9 slice_select_fusion
  2408.7 3.2 fusion.97
  2411.9 41.9 %reduce-scatter.12.cloned.1.call-done = f32[256,2048]{1,0:T(8,128)} async-done(((f32[512,2048]{1,0:T(8,128)}), f32[256,2048]{1,0:T(8,128)}) %reduce-scatter.12.cloned.1.call-update) | async-done | bytes 2097168 | tf_op jit(solution)/shard_map/reduce_scatter | solution.py:278
  2456.7 134.7 %reduce-scatter.28.cloned.1.call-done = f32[64,5]{1,0:T(8,128)} async-done(((f32[2048,5]{1,0:T(8,128)}), f32[64,5]{1,0:T(8,128)}) %reduce-scatter.28.cloned.1.call-update) | async-done | bytes 1296
  2592.8 37.3 %reduce-scatter.26.cloned.1.call-done = f32[352,1024]{1,0:T(8,128)} async-done(((f32[352,2048]{1,0:T(8,128)}), f32[352,1024]{1,0:T(8,128)}) %reduce-scatter.26.cloned.1.call-update) | async-done | bytes 1441808 | tf_op jit(solution)/shard_map/reduce_scatter | solution.py:307
  2630.2 5.2 multiply_subtract_fusion.2
  2635.4 17.9 reduce-scatter.20.cloned.1.call-done
  2655.7 43.0 %reduce-scatter.18.cloned.1.call-done = f32[128,3072]{1,0:T(8,128)} async-done(((f32[128,6144]{1,0:T(8,128)}), f32[128,3072]{1,0:T(8,128)}) %reduce-scatter.18.cloned.1.call-update) | async-done | bytes 1572880 | tf_op jit(solution)/shard_map/reduce_scatter | solution.py:304
  2698.7 5.9 multiply_subtract_fusion.1
  2704.6 67.8 %reduce-scatter.22.cloned.1.call-done = f32[128,5632]{1,0:T(8,128)} async-done(((f32[128,11264]{1,0:T(8,128)}), f32[128,5632]{1,0:T(8,128)}) %reduce-scatter.22.cloned.1.call-update) | async-done | bytes 2883600 | tf_op jit(solution)/shard_map/reduce_scatter | solution.py:306
  2772.4 6.3 multiply_subtract_fusion
  (209 shorter events, 110.4 us)
Async XLA Ops:
  7.2 5.1 copy-start.1
  7.2 31.4 %all-gather.11.cloned.1.call-start = ((), (), s32[]{:S(2)}) async-start(), calls=%async_computation.10 | async-start | bytes 2162688 | tf_op jit(solution)/shard_map/all_gather | solution.py:213
  9.8 58.2 %all-gather.17.cloned.1.call-start = ((), (), s32[]{:S(2)}) async-start(), calls=%async_computation.13 | async-start | bytes 2359296 | tf_op jit(solution)/shard_map/all_gather | solution.py:210
  12.2 99.9 %all-gather.19.cloned.1.call-start = ((), (), s32[]{:S(2)}) async-start(), calls=%async_computation.14 | async-start | bytes 4325376 | tf_op jit(solution)/shard_map/all_gather | solution.py:212
  13.5 26.4 copy-start.20
  13.6 171.5 %all-gather.15.cloned.1.call-start = ((), (), s32[]{:S(2)}) async-start(), calls=%async_computation.12 | async-start | bytes 3145728 | tf_op jit(solution)/shard_map/all_gather | solution.py:206
  14.1 177.8 %all-gather.9.cloned.1.call-start = ((), (), s32[]{:S(2)}) async-start(), calls=%async_computation.9 | async-start | bytes 3145728 | tf_op jit(solution)/shard_map/all_gather | solution.py:207
  14.7 289.1 %all-gather.13.cloned.1.call-start = ((), (), s32[]{:S(2)}) async-start(), calls=%async_computation.11 | async-start | bytes 24510464 | tf_op jit(solution)/shard_map/all_gather | solution.py:243
  39.8 493.5 %all-gather.21.cloned.1.call-start = ((), (), s32[]{:S(2)}) async-start(), calls=%async_computation.15 | async-start | bytes 49020928 | tf_op jit(solution)/shard_map/all_gather | solution.py:242
  48.7 66.5 %copy-start.40 = (f32[5,64]{1,0:T(8,128)S(1)}, f32[5,64]{1,0:T(8,128)}, u32[]{:S(2)}) copy-start(f32[5,64]{1,0:T(8,128)} %param.37) | copy-start | bytes 3844
  115.2 1004.6 %reduce-scatter.14.cloned.1.call-start = ((), (), s32[]{:S(2)}) async-start(), calls=%async_computation.17 | async-start | bytes 6291456 | tf_op jit(solution)/shard_map/reduce_scatter | solution.py:279
  184.8 348.6 %copy-start.33 = (f32[3,2048]{1,0:T(4,128)}, f32[3,2048]{1,0:T(4,128)S(1)}, u32[]{:S(2)}) copy-start(f32[3,2048]{1,0:T(4,128)S(1)} %slice.278) | copy-start | bytes 73732
  185.0 5.8 copy-start.34
  192.0 341.4 %copy-start.46 = (s32[1,2]{1,0:T(1,128)S(1)}, s32[1,2]{1,0:T(1,128)}, u32[]{:S(2)}) copy-start(s32[1,2]{1,0:T(1,128)} %param.32) | copy-start | bytes 28
  533.4 189.4 %copy-start.3 = (bf16[256,2048]{1,0:T(8,128)(2,1)S(1)}, bf16[256,2048]{1,0:T(8,128)(2,1)}, u32[]{:S(2)}) copy-start(bf16[256,2048]{1,0:T(8,128)(2,1)} %get-tuple-element.335) | copy-start | bytes 3145732
  533.4 189.4 %copy-start.4 = (bf16[256,2048]{1,0:T(8,128)(2,1)S(1)}, bf16[256,2048]{1,0:T(8,128)(2,1)}, u32[]{:S(2)}) copy-start(bf16[256,2048]{1,0:T(8,128)(2,1)} %get-tuple-element.337) | copy-start | bytes 3145732
  588.7 6.1 copy-start.9
  588.7 6.7 copy-start.26
  588.7 6.7 copy-start.39
  597.3 6.8 copy-start.24
  651.3 46.2 %copy-start.8 = (bf16[256,2048]{1,0:T(8,128)(2,1)S(1)}, bf16[256,2048]{1,0:T(8,128)(2,1)}, u32[]{:S(2)}) copy-start(bf16[256,2048]{1,0:T(8,128)(2,1)} %get-tuple-element.174) | copy-start | bytes 3145732 | tf_op jit(solution)/shard_map/conditional.2
  707.6 15.0 copy-start.36
  735.4 10.0 copy-start.5
  770.9 2.9 copy-start.16
  778.9 6.2 copy-start.10
  778.9 6.6 copy-start.27
  787.4 6.8 copy-start.25
  982.6 34.9 %copy-start.6 = (bf16[256,2048]{1,0:T(8,128)(2,1)S(1)}, bf16[256,2048]{1,0:T(8,128)(2,1)}, u32[]{:S(2)}) copy-start(bf16[256,2048]{1,0:T(8,128)(2,1)} %copy-done.5) | copy-start | bytes 3145732 | tf_op jit(solution)/shard_map/conditional.3
  982.6 34.9 %copy-start.19 = (bf16[32,64,256]{2,1,0:T(8,128)(2,1)S(1)}, bf16[32,64,256]{2,1,0:T(8,128)(2,1)}, u32[]{:S(2)}) copy-start(bf16[32,64,256]{2,1,0:T(8,128)(2,1)} %copy-done.18) | copy-start | bytes 3145732 | tf_op jit(solution)/shard_map/conditional.3
  1028.8 33.2 %copy-start.22 = (f32[256,2048]{1,0:T(8,128)S(1)}, f32[256,2048]{1,0:T(8,128)}, u32[]{:S(2)}) copy-start(f32[256,2048]{1,0:T(8,128)} %fusion.46) | copy-start | bytes 6291460 | tf_op jit(solution)/shard_map/conditional.3
  1066.2 491.4 %reduce-scatter.24.cloned.1.call-start = ((), (), s32[]{:S(2)}) async-start(), calls=%async_computation.22 | async-start | bytes 49020928 | tf_op jit(solution)/shard_map/reduce_scatter | solution.py:273
  1066.9 1331.1 %reduce-scatter.16.cloned.1.call-start = ((), (), s32[]{:S(2)}) async-start(), calls=%async_computation.18 | async-start | bytes 98041856 | tf_op jit(solution)/shard_map/reduce_scatter | solution.py:272
  1067.5 1386.3 %reduce-scatter.12.cloned.1.call-start = ((), (), s32[]{:S(2)}) async-start(), calls=%async_computation.16 | async-start | bytes 6291456 | tf_op jit(solution)/shard_map/reduce_scatter | solution.py:278
  1071.1 50.4 %copy-start.35 = (f32[1,2048]{1,0:T(1,128)S(1)}, f32[1,2048]{1,0:T(1,128)}, u32[]{:S(2)}) copy-start(f32[1,2048]{1,0:T(1,128)} %copy-done.34) | copy-start | bytes 24580
  1071.1 1520.2 %reduce-scatter.28.cloned.1.call-start = ((), (), s32[]{:S(2)}) async-start(), calls=%async_computation.24 | async-start | bytes 1081344
  1125.2 1504.9 %reduce-scatter.26.cloned.1.call-start = ((), (), s32[]{:S(2)}) async-start(), calls=%async_computation.23 | async-start | bytes 4325376 | tf_op jit(solution)/shard_map/reduce_scatter | solution.py:307
  1557.6 1095.7 %reduce-scatter.20.cloned.1.call-start = ((), (), s32[]{:S(2)}) async-start(), calls=%async_computation.20 | async-start | bytes 1572864 | tf_op jit(solution)/shard_map/reduce_scatter | solution.py:305
  2400.3 298.4 %reduce-scatter.18.cloned.1.call-start = ((), (), s32[]{:S(2)}) async-start(), calls=%async_computation.19 | async-start | bytes 4718592 | tf_op jit(solution)/shard_map/reduce_scatter | solution.py:304
  2404.3 368.1 %reduce-scatter.22.cloned.1.call-start = ((), (), s32[]{:S(2)}) async-start(), calls=%async_computation.21 | async-start | bytes 8650752 | tf_op jit(solution)/shard_map/reduce_scatter | solution.py:306
  2408.1 45.7 %copy-start.14 = (bf16[256,2048]{1,0:T(8,128)(2,1)S(1)}, bf16[256,2048]{1,0:T(8,128)(2,1)}, u32[]{:S(2)}) copy-start(bf16[256,2048]{1,0:T(8,128)(2,1)} %param.30) | copy-start | bytes 3145732
  2411.9 180.3 %copy-start.41 = (f32[5,64]{1,0:T(8,128)S(1)}, f32[5,64]{1,0:T(8,128)}, u32[]{:S(2)}) copy-start(f32[5,64]{1,0:T(8,128)} %param.37) | copy-start | bytes 3844
  2411.9 180.3 %copy-start.44 = (f32[5,64]{1,0:T(8,128)S(1)}, f32[5,64]{1,0:T(8,128)}, u32[]{:S(2)}) copy-start(f32[5,64]{1,0:T(8,128)} %param.42) | copy-start | bytes 3844
  2411.9 180.3 %copy-start.45 = (f32[5,64]{1,0:T(8,128)S(1)}, f32[5,64]{1,0:T(8,128)}, u32[]{:S(2)}) copy-start(f32[5,64]{1,0:T(8,128)} %param.47) | copy-start | bytes 3844
  2411.9 218.3 %copy-start.11 = (f32[352,1024]{1,0:T(8,128)S(1)}, f32[352,1024]{1,0:T(8,128)}, u32[]{:S(2)}) copy-start(f32[352,1024]{1,0:T(8,128)} %param.36) | copy-start | bytes 4325380
  2592.8 60.5 %copy-start.21 = (f32[128,1024]{1,0:T(8,128)S(1)}, f32[128,1024]{1,0:T(8,128)}, u32[]{:S(2)}) copy-start(f32[128,1024]{1,0:T(8,128)} %param.34) | copy-start | bytes 1572868
  2592.8 60.5 %copy-start.31 = (f32[128,1024]{1,0:T(8,128)S(1)}, f32[128,1024]{1,0:T(8,128)}, u32[]{:S(2)}) copy-start(f32[128,1024]{1,0:T(8,128)} %param.39) | copy-start | bytes 1572868
  2592.8 60.5 %copy-start.32 = (f32[128,1024]{1,0:T(8,128)S(1)}, f32[128,1024]{1,0:T(8,128)}, u32[]{:S(2)}) copy-start(f32[128,1024]{1,0:T(8,128)} %param.44) | copy-start | bytes 1572868
  2655.7 116.7 %copy-start.2 = (f32[128,5632]{1,0:T(8,128)S(1)}, f32[128,5632]{1,0:T(8,128)}, u32[]{:S(2)}) copy-start(f32[128,5632]{1,0:T(8,128)} %param.35) | copy-start | bytes 8650756
  (13 other events, 18.1 us)
Sparse Core Ops, SparseCore 0:
  10.2 28.4 all-gather.10
  40.7 27.2 all-gather.16
  70.1 41.9 all-gather.18
  113.5 34.1 all-gather.14
  149.1 34.0 all-gather.8
  185.3 118.5 all-gather.12
  306.0 227.3 all-gather.20
  1066.3 53.3 reduce-scatter.13
  1124.5 432.9 reduce-scatter.23
  1562.2 835.7 reduce-scatter.15
  2400.3 53.4 reduce-scatter.11
  2456.6 134.7 reduce-scatter.27
  2593.6 36.5 reduce-scatter.25
  2632.9 20.3 reduce-scatter.19
  2655.4 43.3 reduce-scatter.17
  2701.0 71.3 reduce-scatter.21
where the time goes:
time: 2790 us
  waiting for transfers between devices  2090 us (75%)
  local copies, waits for them, and re-layouts  311 us (11%)
  matrix products  190 us (7%)
  other arithmetic  82.9 us (3%)
  blocking collectives  78.3 us (3%)
    reduce_scatter x1, waiting for transfers between devices, per_device(): lax.psum_scatter(total_a, 'dp', scatter_dimension=0, tiled=True)  840 us
    reduce_scatter x1, waiting for transfers between devices, per_device(): lax.psum_scatter(total_b, 'dp', scatter_dimension=0, tiled=True)  432 us
    all_gather x1, waiting for transfers between devices, per_device(): lax.all_gather(held_a, 'dp', axis=0, tiled=True)  230 us
    another operation x42, local copies, waits for them, and re-layouts  169 us
    unnamed x17, waiting for transfers between devices  137 us
    all_gather x1, waiting for transfers between devices, per_device(): lax.all_gather(held_b, 'dp', axis=0, tiled=True)  109 us
    scatter-add x2, local copies, waits for them, and re-layouts, attention_micro(): total_a = total_a.at[:, :3 * width_model].add(g_qkv)  81.1 us
    all_gather x1, blocking collectives, per_device(): all_vectors = lax.all_gather(vectors, ('dp', 'branch'), axis=1, tiled=True)  69.5 us
  transfers between devices with their start and end apart: 16, of which 14 were waited for; matrix products, arithmetic and copies ran while one was open for 2% of the time, Pallas kernels for 0%

commit v1 on v0

v1 whole, which is shorter than its diff:
```python
import functools

import jax
import jax.numpy as jnp
from jax import lax
from jax.experimental import pallas as pl
from jax.experimental.pallas import tpu as pltpu
from jax.sharding import Mesh, PartitionSpec as P

HEADS = 32
HEAD = 64
ROT = 16
MB = 2
STEP = 10
SLICES = 8

theta_base = 10000.0
norm_eps = 1e-05
beta_one = 0.9
beta_two = 0.95
adam_eps = 1e-08
decay_rate = 0.1
rate_matrix = 0.05
rate_vector = 1.0

AXES = ("a", "t", "b", "y")
F32 = jnp.float32
BF16 = jnp.bfloat16


def dot(left, right):
    return jnp.dot(left, right, preferred_element_type=F32)


def dot_nt(left, right):
    return lax.dot_general(left, right, (((1,), (1,)), ((), ())), preferred_element_type=F32)


def dot_tn(left, right):
    return lax.dot_general(left, right, (((0,), (0,)), ((), ())), preferred_element_type=F32)


def rotary_lanes(row_count):
    half_rot = ROT // 2
    freqs = theta_base ** (-2.0 * jnp.arange(half_rot, dtype=F32) / ROT)
    angles = jnp.arange(row_count, dtype=F32)[:, None] * freqs[None, :]
    cosine, sine = jnp.cos(angles), jnp.sin(angles)
    rest = HEAD - ROT
    one, zero, gap = (
        jnp.ones((row_count, rest), F32),
        jnp.zeros((row_count, half_rot), F32),
        jnp.zeros((row_count, rest), F32),
    )
    cos_head = jnp.concatenate([cosine, cosine, one], axis=1)
    up_head = jnp.concatenate([sine, zero, gap], axis=1)
    down_head = jnp.concatenate([zero, sine, gap], axis=1)
    return tuple(jnp.concatenate([x, x], axis=1) for x in (cos_head, up_head, down_head))


def attention_kernel(lengths, qkv, dpo, cos_ref, up_ref, down_ref, o_ref, dqkv_ref, bias_ref):
    rows = qkv.shape[0]
    width = dpo.shape[1]
    length = lengths[pl.program_id(0)]
    cosine, sine_up, sine_down = cos_ref[...], up_ref[...], down_ref[...]
    query_at = lax.broadcasted_iota(jnp.int32, (rows, rows), 0)
    key_at = lax.broadcasted_iota(jnp.int32, (rows, rows), 1)
    allowed = (key_at <= query_at) & (key_at < length)
    lane = lax.broadcasted_iota(jnp.int32, (rows, 2 * HEAD), 1)
    lower = lane < HEAD
    half = ROT // 2
    scale = HEAD ** (-0.5)

    def turn(x, sign):
        ahead = pltpu.roll(x, 2 * HEAD - half, 1)
        behind = pltpu.roll(x, half, 1)
        return x * cosine + sign * (behind * sine_down - ahead * sine_up)

    for pair in range(width // (2 * HEAD)):
        at = pair * 2 * HEAD
        cols = slice(at, at + 2 * HEAD)
        k_cols = slice(width + at, width + at + 2 * HEAD)
        v_cols = slice(2 * width + at, 2 * width + at + 2 * HEAD)
        q_rot = turn(qkv[:, cols], 1.0).astype(BF16)
        k_rot = turn(qkv[:, k_cols], 1.0).astype(BF16)
        values = qkv[:, v_cols].astype(BF16)
        grad = dpo[:, cols]
        results = []
        for side in range(2):
            mine = lower if side == 0 else ~lower
            scores = dot_nt(jnp.where(mine, q_rot, 0.0).astype(BF16), k_rot) * scale
            masked = jnp.where(allowed, scores, -1e30)
            raised = jnp.exp(masked - jnp.max(masked, axis=1, keepdims=True))
            probs = raised * (1.0 / jnp.sum(raised, axis=1, keepdims=True))
            probs_low = probs.astype(BF16)
            out = dot(probs_low, values)
            d_probs = dot_nt(jnp.where(mine, grad, 0.0).astype(BF16), values)
            d_values = dot_tn(probs_low, grad)
            inner = jnp.sum(probs * d_probs, axis=1, keepdims=True)
            d_scores = (probs * (d_probs - inner)).astype(BF16)
            d_query = dot(d_scores, k_rot) * scale
            d_keys = dot_tn(d_scores, q_rot) * scale
            results.append((out, d_query, d_keys, d_values))
        out, d_query, d_keys, d_values = (
            jnp.where(lower, first, second) for first, second in zip(*results)
        )
        o_ref[:, cols] = out.astype(BF16)
        for spot, value in (
            (cols, turn(d_query, -1.0)),
            (k_cols, turn(d_keys, -1.0)),
            (v_cols, d_values),
        ):
            low = value.astype(BF16)
            dqkv_ref[:, spot] = low
            bias_ref[0, :, spot] = jnp.sum(low.astype(F32), axis=0, keepdims=True)


def attention(qkv, dpo, lengths, tables):
    slots = lengths.shape[0]
    rows = qkv.shape[0] // slots
    wide, width = qkv.shape[1], dpo.shape[1]
    table = pl.BlockSpec((rows, 2 * HEAD), lambda i, lens: (0, 0))
    return pl.pallas_call(
        attention_kernel,
        grid_spec=pltpu.PrefetchScalarGridSpec(
            num_scalar_prefetch=1,
            grid=(slots,),
            in_specs=[
                pl.BlockSpec((rows, wide), lambda i, lens: (i, 0)),
                pl.BlockSpec((rows, width), lambda i, lens: (i, 0)),
                table,
                table,
                table,
            ],
            out_specs=[
                pl.BlockSpec((rows, width), lambda i, lens: (i, 0)),
                pl.BlockSpec((rows, wide), lambda i, lens: (i, 0)),
                pl.BlockSpec((1, 1, wide), lambda i, lens: (i, 0, 0)),
            ],
        ),
        out_shape=[
            jax.ShapeDtypeStruct((qkv.shape[0], width), BF16),
            jax.ShapeDtypeStruct((qkv.shape[0], wide), BF16),
            jax.ShapeDtypeStruct((slots, 1, wide), F32),
        ],
        compiler_params=pltpu.CompilerParams(vmem_limit_bytes=40 * 2**20),
        name="attention",
    )(lengths, qkv, dpo, *tables)


def normalize(block_rows, gain_row, shift_row):
    row_mean = jnp.mean(block_rows, axis=-1, keepdims=True)
    centered = block_rows - row_mean
    inv_std = lax.rsqrt(jnp.mean(centered * centered, axis=-1, keepdims=True) + norm_eps)
    scaled = centered * inv_std
    return (scaled * gain_row + shift_row, scaled, inv_std)


def adam_update(weight, gradient, first_moment, second_moment, step_rate, decay):
    moment_new = beta_one * first_moment + (1.0 - beta_one) * gradient
    square_new = beta_two * second_moment + (1.0 - beta_two) * gradient * gradient
    moment_hat = moment_new / (1.0 - beta_one**STEP)
    square_hat = square_new / (1.0 - beta_two**STEP)
    weight_new = weight - step_rate * (
        moment_hat / (jnp.sqrt(square_hat) + adam_eps) + decay * weight
    )
    return (weight_new, moment_new, square_new)


def bits(count):
    found = []
    step = 1
    while step < count:
        found.append(step)
        step *= 2
    return found


def per_device(
    sizes,
    tokens,
    cotangent,
    lengths,
    w_qkv,
    w_out,
    w_gate_up,
    w_down,
    vectors,
    first_qkv,
    first_out,
    first_gate_up,
    first_down,
    first_vectors,
    second_qkv,
    second_out,
    second_gate_up,
    second_down,
    second_vectors,
):
    n_a, n_t, n_b, n_y = sizes
    total = n_a * n_t * n_b * n_y
    at_a, at_t, at_b, at_y = (lax.axis_index(name) for name in AXES)
    row_count, width = tokens.shape
    w_rows = w_qkv.shape[0]
    d_rows = w_down.shape[0]
    half = w_out.shape[1]

    def swap(value, name, step):
        mask = {"y": 1, "b": n_y, "t": n_y * n_b, "a": n_y * n_b * n_t}[name] * step
        return lax.ppermute(value, AXES, [(i, i ^ mask) for i in range(total)])

    n_blocks = w_qkv.shape[1] // (n_t * n_b * w_rows)
    head_cols = n_b * w_rows
    ff_cols = n_b * d_rows
    qkv_low = w_qkv.astype(BF16).reshape(w_rows, n_blocks, n_t, head_cols)
    gu_low = w_gate_up.astype(BF16).reshape(w_rows, n_a, n_t, ff_cols)
    qkv_part = qkv_low.transpose(2, 0, 1, 3).reshape(n_t, w_rows, n_blocks * head_cols)
    gu_part = gu_low.transpose(2, 0, 1, 3).reshape(n_t, w_rows, n_a * ff_cols)
    joined = jnp.concatenate([qkv_part, gu_part], axis=2)
    joined = lax.all_to_all(joined, "t", split_axis=0, concat_axis=0, tiled=True)
    qkv_own, gu_own = joined[:, :, : qkv_part.shape[2]], joined[:, :, qkv_part.shape[2] :]

    r_bits = [("a", s) for s in reversed(bits(n_a))] + [("b", s) for s in bits(n_b)]

    def gather_rows(part):
        part = part[None, :, None]
        for name, step in r_bits:
            other = swap(part, name, step)
            dim, at, size = (0, at_a, part.shape[0]) if name == "a" else (2, at_b, part.shape[2])
            upper = (at // step) % 2 == 1
            first, second = jnp.where(upper, other, part), jnp.where(upper, part, other)
            if name == "a":
                part = jnp.concatenate([first, second], axis=0)
            else:
                part = jnp.concatenate([first, second], axis=2)
        return part

    upper_y = at_y == 1

    def both(own):
        other = swap(own, "y", 1)
        return own, other

    def ordered(own, other):
        return jnp.where(upper_y, other, own), jnp.where(upper_y, own, other)

    def full_rows(part):
        return gather_rows(part).reshape(width, part.shape[-1])

    def pair_of(part):
        parts = [part[None, :, None]]
        masks = [{"a": 0, "b": 0}]
        for name, step in r_bits:
            parts = parts + [swap(p, name, step) for p in parts]
            masks = masks + [{**m, name: m[name] + step} for m in masks]
        others = [swap(p, "y", 1) for p in parts]
        return place(parts, masks), place(others, masks)

    def place(parts, masks):
        table = {(m["a"], m["b"]): p for m, p in zip(masks, parts)}
        for name, step in r_bits:
            at = at_a if name == "a" else at_b
            upper = (at // step) % 2 == 1
            fresh = {}
            for (ka, kb), value in table.items():
                mate = (ka ^ step, kb) if name == "a" else (ka, kb ^ step)
                fresh[(ka, kb)] = jnp.where(upper, table[mate], value)
            table = fresh
        return jnp.concatenate(
            [
                jnp.concatenate([table[(ka, kb)] for kb in range(n_b)], axis=2)
                for ka in range(n_a)
            ],
            axis=0,
        )

    def flat(value):
        return value.reshape(-1, value.shape[-1])

    gu_mine, gu_other = (flat(v) for v in pair_of(gu_own))
    down_mine, down_other = (flat(v) for v in pair_of(w_down.astype(BF16)[None]))
    qkv_mine, qkv_other = (flat(v) for v in pair_of(qkv_own))
    out_mine, out_other = (flat(v) for v in pair_of(w_out.astype(BF16)[None]))
    down_full = jnp.concatenate(ordered(down_mine, down_other), axis=1)
    qkv_full = jnp.concatenate(ordered(qkv_mine, qkv_other), axis=1)
    out_full = jnp.concatenate(ordered(out_mine, out_other), axis=1)

    grads = lax.all_gather(cotangent, "t", axis=0, tiled=True)
    all_vectors = lax.all_gather(vectors, AXES, axis=1, tiled=True)
    gain_row = all_vectors[0]
    shift_row = all_vectors[1]
    normed_own, scaled_own, inv_own = normalize(tokens.astype(F32), gain_row, shift_row)
    normed = lax.all_gather(normed_own.astype(BF16), "t", axis=0, tiled=True)
    group_lengths = lax.all_gather(lengths[0], "t", axis=0, tiled=False)
    slot_lengths = lax.dynamic_index_in_dim(group_lengths, at_y, 1, keepdims=False)
    bias = all_vectors[2:5].reshape(3 * n_a, n_t, head_cols)
    bias = lax.dynamic_index_in_dim(bias, at_t, 1, keepdims=False).reshape(1, -1)

    joined_mine, joined_other = dot(normed, gu_mine), dot(normed, gu_other)
    gate, up = ordered(joined_mine, joined_other)
    d_hidden = dot_nt(grads, down_full)
    sig = jax.nn.sigmoid(gate)
    act = gate * sig
    hidden = (act * up).astype(BF16)
    d_gate = (d_hidden * up * sig * (1.0 + gate * (1.0 - sig))).astype(BF16)
    d_up = (d_hidden * act).astype(BF16)
    d_mine, d_other = ordered(d_gate, d_up)

    qkv = dot(normed, qkv_full) + bias
    dpo = dot_nt(grads, out_full).astype(BF16)
    attended, d_qkv, bias_sums = attention(qkv, dpo, slot_lengths, rotary_lanes(row_count))

    def halves_y(value):
        kept, sent = ordered(value[:, : value.shape[1] // 2], value[:, value.shape[1] // 2 :])
        return kept, sent

    def reduce_rest(kept, sent, parts_shape):
        summed = kept + swap(sent.astype(BF16), "y", 1).astype(F32)
        summed = summed.reshape(parts_shape + (summed.shape[-1],))
        for name, step in r_bits:
            dim = 0 if name == "a" else 2
            at = at_a if name == "a" else at_b
            size = summed.shape[dim] // 2
            low_half = lax.slice_in_dim(summed, 0, size, axis=dim)
            high_half = lax.slice_in_dim(summed, size, 2 * size, axis=dim)
            upper = (at // step) % 2 == 1
            keep = jnp.where(upper, high_half, low_half)
            send = jnp.where(upper, low_half, high_half)
            summed = keep + swap(send.astype(BF16), name, step).astype(F32)
        return summed

    shape_w = (n_a, n_t, n_b, w_rows)
    g_gu = reduce_rest(dot_tn(normed, d_mine), dot_tn(normed, d_other), shape_w)
    g_down = reduce_rest(*halves_y(dot_tn(hidden, grads)), (n_a, 1, n_b, d_rows))
    g_qkv = reduce_rest(*halves_y(dot_tn(normed, d_qkv)), shape_w)
    g_out = reduce_rest(*halves_y(dot_tn(attended, grads)), (n_a, 1, n_b, w_rows))
    g_joined = jnp.concatenate([g_qkv[0, :, 0], g_gu[0, :, 0]], axis=2).astype(BF16)
    g_joined = lax.all_to_all(g_joined, "t", split_axis=0, concat_axis=0, tiled=True)
    g_qkv = g_joined[:, :, : n_blocks * head_cols].reshape(n_t, w_rows, n_blocks, head_cols)
    g_gu = g_joined[:, :, n_blocks * head_cols :].reshape(n_t, w_rows, n_a, ff_cols)
    own_qkv = g_qkv.transpose(1, 2, 0, 3).reshape(w_qkv.shape).astype(F32)
    own_gu = g_gu.transpose(1, 2, 0, 3).reshape(w_gate_up.shape).astype(F32)
    own_out = g_out.reshape(w_out.shape)
    own_down = g_down.reshape(w_down.shape)

    branch_part = dot(attended, out_full) + dot(hidden, down_full)
    normal_part = dot_nt(d_qkv, qkv_full) + dot_nt(d_mine, gu_mine) + dot_nt(d_other, gu_other)

    def scatter_rows(part, order):
        part = part.astype(BF16).reshape((2,) * len(order) + (row_count, width))
        steps = bits(n_t)
        for which in order:
            step = steps[len(order) - 1 - which]
            upper = (at_t // step) % 2 == 1
            low_half = lax.index_in_dim(part, 0, which, keepdims=True)
            high_half = lax.index_in_dim(part, 1, which, keepdims=True)
            keep = jnp.where(upper, high_half, low_half)
            send = jnp.where(upper, low_half, high_half)
            got = swap(send, "t", step)
            part = keep.astype(F32) + got.astype(F32)
            if which != order[-1]:
                part = part.astype(BF16)
        return part.reshape(row_count, width)

    n_bits = len(bits(n_t))
    order_one = [n_bits - 1] + list(range(n_bits - 1))
    order_two = [n_bits - 1] + list(reversed(range(n_bits - 1)))
    branch_own = scatter_rows(branch_part, order_one)
    normal_own = scatter_rows(normal_part, order_two)

    output = (tokens.astype(F32) + branch_own).astype(BF16)
    g_normed = normal_own
    d_scaled = g_normed * gain_row
    input_grad = cotangent.astype(F32) + inv_own * (
        d_scaled
        - jnp.mean(d_scaled, axis=-1, keepdims=True)
        - scaled_own * jnp.mean(d_scaled * scaled_own, axis=-1, keepdims=True)
    )
    g_bias = jnp.sum(bias_sums, axis=0).reshape(3 * n_a, 1, head_cols)
    here = (jnp.arange(n_t) == at_t)[None, :, None]
    g_bias = jnp.where(here, g_bias, 0.0).reshape(3, width)
    vector_part = jnp.concatenate(
        [
            jnp.sum(g_normed * scaled_own, axis=0)[None],
            jnp.sum(g_normed, axis=0)[None],
            g_bias,
        ],
        axis=0,
    )
    vector_grad = lax.psum_scatter(vector_part, AXES, scatter_dimension=1, tiled=True)

    new_qkv, moment_qkv, square_qkv = adam_update(
        w_qkv, own_qkv, first_qkv, second_qkv, rate_matrix, decay_rate
    )
    new_out, moment_out, square_out = adam_update(
        w_out, own_out, first_out, second_out, rate_matrix, decay_rate
    )
    new_gu, moment_gu, square_gu = adam_update(
        w_gate_up, own_gu, first_gate_up, second_gate_up, rate_matrix, decay_rate
    )
    new_down, moment_down, square_down = adam_update(
        w_down, own_down, first_down, second_down, rate_matrix, decay_rate
    )
    new_vec, moment_vec, square_vec = adam_update(
        vectors, vector_grad, first_vectors, second_vectors, rate_vector, 0.0
    )
    return (
        output,
        input_grad.astype(BF16),
        new_qkv,
        new_out,
        new_gu,
        new_down,
        new_vec,
        moment_qkv,
        moment_out,
        moment_gu,
        moment_down,
        moment_vec,
        square_qkv,
        square_out,
        square_gu,
        square_down,
        square_vec,
    )


def solution(mesh):
    n_dp, n_y = mesh.shape["dp"], mesh.shape["branch"]
    n_b = max(1, HEAD * n_dp // (HEADS * HEAD))
    n_t = min(SLICES, n_dp // n_b)
    sizes = (n_dp // (n_t * n_b), n_t, n_b, n_y)
    split = Mesh(mesh.devices.reshape(sizes), AXES)
    dp = ("a", "t", "b")
    rows = P(AXES, None)
    matrix = P(dp, "y")
    vector = P(None, AXES)
    weights = (matrix, matrix, matrix, matrix, vector)
    return jax.shard_map(
        functools.partial(per_device, sizes),
        mesh=split,
        in_specs=(rows, rows, P(dp, None)) + weights * 3,
        out_specs=(rows, rows) + weights * 3,
        check_vma=False,
    )
```

time: 2790 us -> 946 us (0.34)
  waiting for transfers between devices: 2090 us -> 419 us
  local copies, waits for them, and re-layouts: 311 us -> 62.5 us
  blocking collectives: 78.3 us -> 140 us
  matrix products: 190 us -> 149 us
  starting transfers between devices: 0.65 us -> 32.1 us
    reduce_scatter x8 -> x0, waiting for transfers between devices: 1530 us -> none  [the longest x1 840 us: per_device(): lax.psum_scatter(total_a, 'dp', scatter_dimension=0, tiled=True)]
    all_gather x7 -> x2, waiting for transfers between devices: 425 us -> 0.01 us  [the longest x1 0.01 us: per_device(): normed = lax.all_gather(normed_own.astype(BF16), 't', axis=0, tiled=True)]
    ppermute x0 -> x26, waiting for transfers between devices: none -> 290 us  [swap(): return lax.ppermute(value, AXES, [(i, i ^ mask) for i in range(total)])]
    another operation x42 -> x0, local copies, waits for them, and re-layouts: 169 us -> none
    scatter-add x2 -> x0, local copies, waits for them, and re-layouts: 81.1 us -> none  [attention_micro(): total_a = total_a.at[:, :3 * width_model].add(g_qkv)]
    all_gather x2, blocking collectives: 78.3 us -> 140 us  [the longest x1 70.6 us: per_device(): all_vectors = lax.all_gather(vectors, AXES, axis=1, tiled=True)]
    slice x22 -> x3, local copies, waits for them, and re-layouts: 36.3 us -> 3.27 us  [the longest x1 1.46 us: per_device(): g_joined[:, :, n_blocks * head_cols:].reshape(n_t, w_rows, n_a, ff_cols)]
    unnamed x55 -> x144, local copies, waits for them, and re-layouts: 5.8 us -> 34.5 us
  transfers between devices with their start and end apart: 16 -> 31, of which waited for: 14 -> 14; matrix products, arithmetic and copies ran while one was open for 2% -> 24% of each run, Pallas kernels for 0% -> 2%
where the time goes in v1:
time: 946 us; the launch traced here: 941 us
  waiting for transfers between devices  419 us (44%)
  matrix products  149 us (16%)
  blocking collectives  140 us (15%)
  other arithmetic  99.8 us (11%)
  local copies, waits for them, and re-layouts  62.5 us (7%)
  starting transfers between devices  32.1 us (3%)
  Pallas kernels  22.3 us (2%)
  between operations  15.3 us (2%)
    ppermute x26, waiting for transfers between devices, swap(): return lax.ppermute(value, AXES, [(i, i ^ mask) for i in range(total)])  290 us
    unnamed x4, waiting for transfers between devices  129 us
    all_gather x1, blocking collectives, per_device(): all_vectors = lax.all_gather(vectors, AXES, axis=1, tiled=True)  70.6 us
    all_gather x1, blocking collectives, per_device(): group_lengths = lax.all_gather(lengths[0], 't', axis=0, tiled=False)  69.5 us
    dot_general x5, matrix products, dot_nt(): lax.dot_general(left, right, (((1,), (1,)), ((), ())), preferred_element_...  61.5 us
    dot_general x5, matrix products, dot(): return jnp.dot(left, right, preferred_element_type=F32)  50.6 us
    dot_general x5, matrix products, dot_tn(): lax.dot_general(left, right, (((0,), (0,)), ((), ())), preferred_element_...  37.3 us
    unnamed x144, local copies, waits for them, and re-layouts  34.5 us
  transfers between devices with their start and end apart: 31, of which 14 were waited for; matrix products, arithmetic and copies ran while one was open for 24% of the time, Pallas kernels for 2%

profile of v1, /device:TPU:0, one launch (start us, length us, event | category | flops | bytes accessed | tf_op | source)
XLA Modules:
  0.0 940.9 jit_solution(17946441196103481909)
XLA Ops:
  10.6 70.6 %all-gather.1 = f32[32,64,5]{1,2,0:T(8,128)S(1)} all-gather(f32[1,64,5]{1,2,0:T(8,128)} %bitcast.224), channel_id=1, replica_groups=mesh['a'=2,'t'=8,'b'=1,'y'=2] {'a','t','b','y'}, dimensions={0}, use_global_device_ids=true | all-gather | bytes 42240 | tf_op jit(solution)/shard_map/all_gather | solution.py:288
  90.7 3.7 all-to-all-start
  99.6 3.0 collective-permute-start.9
  103.1 69.5 %all-gather = s32[8,1,2]{2,1,0:T(1,128)S(1)} all-gather(s32[1,1,2]{2,1,0:T(1,128)S(1)} %bitcast.227), channel_id=1, replica_groups=mesh['a'=2,'t'=8,'b'=1,'y'=2] {'t'}, dimensions={0}, use_global_device_ids=true | all-gather | bytes 72 | tf_op jit(solution)/shard_map/all_gather | solution.py:293
  174.6 3.6 copy.90
  178.2 3.7 copy.92
  188.2 4.1 collective-permute-done.4
  197.2 9.9 %collective-permute-done.10 = bf16[1,1,1,352,1024]{4,3,2,1,0:T(8,128)(2,1)S(1)} collective-permute-done((bf16[1,1,1,352,1024]{4,3,2,1,0:T(8,128)(2,1)}, bf16[1,1,1,352,1024]{4,3,2,1,0:T(8,128)(2,1)S(1)}, u32[]{:S(2)}, u32[]{:S(2)}) %collective-permute-start.10) | collective-permute-done | bytes 720928 | tf_op jit(solution)/shard_map/ppermute | solution.py:209
  210.3 58.7 %collective-permute-done.6 = bf16[1,8,1,128,704]{3,4,1,2,0:T(8,128)(2,1)} collective-permute-done((bf16[1,8,1,128,704]{3,4,1,2,0:T(8,128)(2,1)}, bf16[1,8,1,128,704]{3,4,1,2,0:T(8,128)(2,1)}, u32[]{:S(2)}, u32[]{:S(2)}) %collective-permute-start.6) | collective-permute-done | bytes 1441824 | tf_op jit(solution)/shard_map/ppermute | solution.py:209
  272.8 12.4 %collective-permute-done = bf16[1,8,1,128,384]{3,4,1,2,0:T(8,128)(2,1)} collective-permute-done((bf16[1,8,1,128,384]{3,4,1,2,0:T(8,128)(2,1)}, bf16[1,8,1,128,384]{3,4,1,2,0:T(8,128)(2,1)}, u32[]{:S(2)}, u32[]{:S(2)}) %collective-permute-start) | collective-permute-done | bytes 786464 | tf_op jit(solution)/shard_map/ppermute | solution.py:209
  294.3 26.3 %collective-permute-done.2 = bf16[1,8,1,128,384]{3,4,1,2,0:T(8,128)(2,1)} collective-permute-done((bf16[1,8,1,128,384]{3,4,1,2,0:T(8,128)(2,1)}, bf16[1,8,1,128,384]{3,4,1,2,0:T(8,128)(2,1)}, u32[]{:S(2)}, u32[]{:S(2)}) %collective-permute-start.2) | collective-permute-done | bytes 786464 | tf_op jit(solution)/shard_map/ppermute | solution.py:209
  320.6 14.8 %collective-permute-done.1 = bf16[1,8,1,128,384]{3,4,1,2,0:T(8,128)(2,1)} collective-permute-done((bf16[1,8,1,128,384]{3,4,1,2,0:T(8,128)(2,1)}, bf16[1,8,1,128,384]{3,4,1,2,0:T(8,128)(2,1)}, u32[]{:S(2)}, u32[]{:S(2)}) %collective-permute-start.1) | collective-permute-done | bytes 786464 | tf_op jit(solution)/shard_map/ppermute | solution.py:209
  347.2 11.2 %fusion.63 = f32[2048,704]{0,1:T(8,128)} fusion(bf16[2048,2048]{1,0:T(8,128)(2,1)} %all-gather.5.cloned.1.call-done, bf16[2048,704]{0,1:T(8,128)(2,1)} %reshape.266), kind=kOutput, calls=%fused_computation.167 | convolution fusion | flops 5905580032 | bytes 17039360 | tf_op jit(solution)/shard_map/dot_general | solution.py:32
  358.3 8.2 fusion.62
  366.5 16.2 %fusion = (bf16[2048,704]{0,1:T(8,128)(2,1)}, bf16[2048,704]{0,1:T(8,128)(2,1)}, bf16[2048,704]{0,1:T(8,128)(2,1)}) fusion(f32[2048,704]{0,1:T(8,128)} %fusion.62, f32[2048,704]{0,1:T(8,128)} %fusion.63, pred[]{:T(512)S(6)} %eq.61, bf16[2048,2048]{1,0:T(8,128)(2,1)} %all-gather.7.cloned.1.call-done, bf16[704,1024]{1,0:T(8,128)(2,1)} %bitcast.213, ...), kind=kOutput, calls=%fused_computation.6 | convolution fusion | flops 5935857664 | bytes 31457280 | tf_op jit(solution)/shard_map/dot_general | solution.py:36
  382.8 12.4 %fusion.37 = f32[2048,2048]{1,0:T(8,128)} fusion(bf16[2048,704]{0,1:T(8,128)(2,1)S(1)} %copy-done.27, bf16[2048,704]{0,1:T(8,128)(2,1)} %get-tuple-element.95, bf16[2048,704]{0,1:T(8,128)(2,1)} %get-tuple-element.94, pred[]{:T(512)S(6)} %eq.61), kind=kOutput, calls=%fused_computation.106 | convolution fusion | flops 5907021824 | bytes 25427968 | tf_op jit(solution)/shard_map/dot_general | solution.py:36
  395.3 10.8 %fusion.36 = f32[2048,2048]{1,0:T(8,128)} fusion(bf16[2048,704]{0,1:T(8,128)(2,1)S(1)} %copy-done.26, bf16[2048,704]{0,1:T(8,128)(2,1)S(1)} %copy-done.48, bf16[2048,704]{0,1:T(8,128)(2,1)S(1)} %copy-done.50, pred[]{:T(512)S(6)} %eq.61), kind=kOutput, calls=%fused_computation.105 | convolution fusion | flops 5907021824 | bytes 25427968 | tf_op jit(solution)/shard_map/dot_general | solution.py:36
  406.1 7.6 convolution_convert_fusion
  413.9 12.5 %fusion.26 = f32[2048,2048]{1,0:T(8,128)} fusion(bf16[2048,704]{0,1:T(8,128)(2,1)} %get-tuple-element.96, bf16[704,1024]{1,0:T(8,128)(2,1)S(1)} %bitcast.214, bf16[704,1024]{1,0:T(8,128)(2,1)S(1)} %bitcast.212), kind=kOutput, calls=%fused_computation.72 | convolution fusion | flops 5911347200 | bytes 22544384 | tf_op jit(solution)/shard_map/dot_general | solution.py:32
  426.5 6.2 fusion.66
  438.3 7.3 broadcast_add_fusion.qkv
  445.6 22.3 %attention.1 = (bf16[2048,256]{1,0:T(8,128)(2,1)S(1)}, bf16[2048,768]{1,0:T(8,128)(2,1)S(1)}, f32[8,1,768]{2,1,0:T(1,128)S(1)}) custom-call(s32[8]{0:T(128)S(1)} %dynamic-slice_reduce_fusion.lengths, f32[2048,768]{1,0:T(8,128)S(1)} %broadcast_add_fusion.qkv, bf16[2048,256]{1,0:T(8,128)(2,1)S(1)} %fusion.14.dpo, f32[256,128]{1,0:T(8,128)S(1)} %concatenate.65.cos_ref, ...), custom_call_target="tpu_custom_call" | custom-call | tf_op jit(solution)/shard_map/attention/pallas_call | solution.py:122
  468.0 6.9 fusion.65
  475.8 7.4 fusion.64
  488.5 11.5 %add_convert_fusion.1 = bf16[2048,2048]{1,0:T(8,128)(2,1)} fusion(f32[2048,2048]{1,0:T(8,128)} %fusion.26, bf16[2048,256]{1,0:T(8,128)(2,1)S(1)} %get-tuple-element.20, bf16[256,1024]{1,0:T(8,128)(2,1)S(1)} %bitcast.206, bf16[256,1024]{1,0:T(8,128)(2,1)S(1)} %bitcast.204), kind=kOutput, calls=%fused_computation.1 | convolution fusion | flops 2157969408 | bytes 27262976 | tf_op jit(solution)/shard_map/dot_general | solution.py:32
  500.0 5.2 broadcast_select_fusion.1
  505.2 19.5 %add_convert_fusion = bf16[2048,2048]{1,0:T(8,128)(2,1)} fusion(f32[2048,2048]{1,0:T(8,128)} %fusion.37, f32[2048,2048]{1,0:T(8,128)} %fusion.36, bf16[2048,768]{1,0:T(8,128)(2,1)} %copy-done, bf16[2048,384]{1,0:T(8,128)(2,1)} %bitcast.209, bf16[2048,384]{1,0:T(8,128)(2,1)} %bitcast.207), kind=kOutput, calls=%fused_computation | convolution fusion | flops 6461325312 | bytes 48234496 | tf_op jit(solution)/shard_map/dot_general | solution.py:36
  527.3 5.3 broadcast_select_fusion
  532.6 9.6 %collective-permute-done.23 = bf16[1,1,1,128,1024]{4,3,2,1,0:T(8,128)(2,1)S(1)} collective-permute-done((bf16[1,1,1,128,1024]{4,3,2,1,0:T(8,128)(2,1)S(1)}, bf16[1,1,1,128,1024]{4,3,2,1,0:T(8,128)(2,1)S(1)}, u32[]{:S(2)}, u32[]{:S(2)}) %collective-permute-start.23) | collective-permute-done | bytes 262176 | tf_op jit(solution)/shard_map/ppermute | solution.py:209
  543.8 4.3 convert_add_fusion.3
  558.9 3.2 copy.86
  562.1 37.9 %collective-permute-done.25 = bf16[1,1,1,352,1024]{4,3,2,1,0:T(8,128)(2,1)} collective-permute-done((bf16[1,1,1,352,1024]{4,3,2,1,0:T(8,128)(2,1)}, bf16[1,1,1,352,1024]{4,3,2,1,0:T(8,128)(2,1)}, u32[]{:S(2)}, u32[]{:S(2)}) %collective-permute-start.25) | collective-permute-done | bytes 720928 | tf_op jit(solution)/shard_map/ppermute | solution.py:209
  600.0 5.7 multiply_subtract_fusion.2
  605.6 11.1 %collective-permute-done.19 = bf16[1,8,1,128,384]{3,4,1,2,0:T(8,128)(2,1)} collective-permute-done((bf16[1,8,1,128,384]{3,4,1,2,0:T(8,128)(2,1)}, bf16[1,8,1,128,384]{3,4,1,2,0:T(8,128)(2,1)}, u32[]{:S(2)}, u32[]{:S(2)}) %collective-permute-start.19) | collective-permute-done | bytes 786464 | tf_op jit(solution)/shard_map/ppermute | solution.py:209
  618.3 9.2 convert_add_fusion
  628.6 4.6 add_convert_fusion.2
  635.2 4.2 add_convert_fusion.3
  646.1 47.7 %collective-permute-done.21 = bf16[1,8,1,128,704]{3,4,1,2,0:T(8,128)(2,1)S(1)} collective-permute-done((bf16[1,8,1,128,704]{3,4,1,2,0:T(8,128)(2,1)S(1)}, bf16[1,8,1,128,704]{3,4,1,2,0:T(8,128)(2,1)S(1)}, u32[]{:S(2)}, u32[]{:S(2)}) %collective-permute-start.21) | collective-permute-done | bytes 1441824 | tf_op jit(solution)/shard_map/ppermute | solution.py:209
  696.0 4.4 all-to-all-start.1
  700.4 4.3 add_convert_fusion.4
  706.7 15.6 %collective-permute-done.13 = bf16[1,2,1,256,2048]{4,3,2,1,0:T(8,128)(2,1)} collective-permute-done((bf16[1,2,1,256,2048]{4,3,2,1,0:T(8,128)(2,1)}, bf16[1,2,1,256,2048]{4,3,2,1,0:T(8,128)(2,1)}, u32[]{:S(2)}, u32[]{:S(2)}) %collective-permute-start.13) | collective-permute-done | bytes 2097184 | tf_op jit(solution)/shard_map/ppermute | solution.py:209
  728.4 39.4 %collective-permute-done.17 = bf16[1,1,1,256,2048]{4,3,2,1,0:T(8,128)(2,1)S(1)} collective-permute-done((bf16[1,1,1,256,2048]{4,3,2,1,0:T(8,128)(2,1)S(1)}, bf16[1,1,1,256,2048]{4,3,2,1,0:T(8,128)(2,1)S(1)}, u32[]{:S(2)}, u32[]{:S(2)}) %collective-permute-start.17) | collective-permute-done | bytes 1048608 | tf_op jit(solution)/shard_map/ppermute | solution.py:209
  770.9 5.0 fusion.21
  775.9 128.7 %reduce-scatter.4.cloned.1.call-done = f32[64,5]{1,0:T(8,128)} async-done(((f32[2048,5]{1,0:T(8,128)}), f32[64,5]{1,0:T(8,128)}) %reduce-scatter.4.cloned.1.call-update) | async-done | bytes 1296
  914.2 4.7 multiply_subtract_fusion
  918.8 3.6 copy.95
  922.4 3.4 copy.96
  928.0 6.0 multiply_subtract_fusion.1
  (279 shorter events, 122.5 us)
Async XLA Ops:
  7.2 74.1 %copy-start.4 = (bf16[256,2048]{1,0:T(8,128)(2,1)S(1)}, bf16[256,2048]{1,0:T(8,128)(2,1)}, u32[]{:S(2)}) copy-start(bf16[256,2048]{1,0:T(8,128)(2,1)} %param.18) | copy-start | bytes 3145732
  7.2 340.0 %all-gather.5.cloned.1.call-start = ((), (), s32[]{:S(2)}) async-start(), calls=%async_computation.3 | async-start | bytes 9437184 | tf_op jit(solution)/shard_map/all_gather | solution.py:292
  8.8 74.8 %copy-start.38 = (f32[256]{0:T(256)}, f32[256]{0:T(256)S(1)}, u32[]{:S(2)}) copy-start(f32[256]{0:T(256)S(1)} %broadcast_multiply_fusion.2) | copy-start | bytes 3076
  8.8 74.8 %copy-start.20 = (f32[128,3072]{1,0:T(8,128)S(1)}, f32[128,3072]{1,0:T(8,128)}, u32[]{:S(2)}) copy-start(f32[128,3072]{1,0:T(8,128)} %param.21) | copy-start | bytes 4718596
  10.6 73.4 %copy-start.40 = (f32[256]{0:T(256)}, f32[256]{0:T(256)S(1)}, u32[]{:S(2)}) copy-start(f32[256]{0:T(256)S(1)} %add_rsqrt_fusion) | copy-start | bytes 3076
  82.8 283.8 %all-gather.7.cloned.1.call-start = ((), (), s32[]{:S(2)}) async-start(), calls=%async_computation.4 | async-start | bytes 9437184 | tf_op jit(solution)/shard_map/all_gather | solution.py:287
  90.7 94.0 %all-to-all-start = ((bf16[8,128,1088]{1,2,0:T(8,128)(2,1)}), bf16[8,128,1088]{1,2,0:T(8,128)(2,1)S(1)}, u32[]{:S(2)}, u32[]{:S(2)}) async-start(bf16[8,128,1088]{1,2,0:T(8,128)(2,1)} %pad_maximum_fusion.4), calls=%async_computation | async-start | bytes 4456448 | tf_op jit(solution)/shard_map/all_to_all | solution.py:219
  95.2 93.0 %collective-permute-start.5 = (bf16[1,1,1,128,1024]{4,3,2,1,0:T(8,128)(2,1)}, bf16[1,1,1,128,1024]{4,3,2,1,0:T(8,128)(2,1)}, u32[]{:S(2)}, u32[]{:S(2)}) collective-permute-start(bf16[1,1,1,128,1024]{4,3,2,1,0:T(8,128)(2,1)} %convert_bitcast_fusion.3), channel_id=1, source_target_pairs={{0,1},{1,0},{2,3},{3,2},{4,5},{5,4},{6,7},{7,6},{8,9},{9,8},{10,11... | collective-permute-start | bytes 786440 | tf_op jit(solution)/shard_map/ppermute | solution.py:209
  95.2 87.8 %collective-permute-start.3 = (bf16[1,1,1,128,1024]{4,3,2,1,0:T(8,128)(2,1)}, bf16[1,1,1,128,1024]{4,3,2,1,0:T(8,128)(2,1)}, u32[]{:S(2)}, u32[]{:S(2)}) collective-permute-start(bf16[1,1,1,128,1024]{4,3,2,1,0:T(8,128)(2,1)} %convert_bitcast_fusion.3), channel_id=1, source_target_pairs={{0,16},{1,17},{2,18},{3,19},{4,20},{5,21},{6,22},{7,23},{8,24},{9,... | collective-permute-start | bytes 786440 | tf_op jit(solution)/shard_map/ppermute | solution.py:209
  97.5 99.7 %collective-permute-start.11 = (bf16[1,1,1,352,1024]{4,3,2,1,0:T(8,128)(2,1)}, bf16[1,1,1,352,1024]{4,3,2,1,0:T(8,128)(2,1)}, u32[]{:S(2)}, u32[]{:S(2)}) collective-permute-start(bf16[1,1,1,352,1024]{4,3,2,1,0:T(8,128)(2,1)} %convert_bitcast_fusion.2), channel_id=1, source_target_pairs={{0,1},{1,0},{2,3},{3,2},{4,5},{5,4},{6,7},{7,6},{8,9},{9,8},{10,11... | collective-permute-start | bytes 2162696 | tf_op jit(solution)/shard_map/ppermute | solution.py:209
  99.6 88.5 %collective-permute-start.9 = (bf16[1,1,1,352,1024]{4,3,2,1,0:T(8,128)(2,1)}, bf16[1,1,1,352,1024]{4,3,2,1,0:T(8,128)(2,1)}, u32[]{:S(2)}, u32[]{:S(2)}) collective-permute-start(bf16[1,1,1,352,1024]{4,3,2,1,0:T(8,128)(2,1)} %convert_bitcast_fusion.2), channel_id=1, source_target_pairs={{0,16},{1,17},{2,18},{3,19},{4,20},{5,21},{6,22},{7,23},{8,24},{9,... | collective-permute-start | bytes 2162696 | tf_op jit(solution)/shard_map/ppermute | solution.py:209
  183.0 9.3 collective-permute-start.4
  185.9 83.1 %collective-permute-start.6 = (bf16[1,8,1,128,704]{3,4,1,2,0:T(8,128)(2,1)}, bf16[1,8,1,128,704]{3,4,1,2,0:T(8,128)(2,1)}, u32[]{:S(2)}, u32[]{:S(2)}) collective-permute-start(bf16[1,8,1,128,704]{3,4,1,2,0:T(8,128)(2,1)} %slice_bitcast_fusion), channel_id=1, source_target_pairs={{0,16},{1,17},{2,18},{3,19},{4,20},{5,21},{6,22},{7,23},{8,24},{9,... | collective-permute-start | bytes 4325384 | tf_op jit(solution)/shard_map/ppermute | solution.py:209
  188.1 19.1 %collective-permute-start.10 = (bf16[1,1,1,352,1024]{4,3,2,1,0:T(8,128)(2,1)}, bf16[1,1,1,352,1024]{4,3,2,1,0:T(8,128)(2,1)S(1)}, u32[]{:S(2)}, u32[]{:S(2)}) collective-permute-start(bf16[1,1,1,352,1024]{4,3,2,1,0:T(8,128)(2,1)} %collective-permute-done.9), channel_id=1, source_target_pairs={{0,1},{1,0},{2,3},{3,2},{4,5},{5,4},{6,7},{7,6},{8,9},{9,8},{10,11... | collective-permute-start | bytes 2162696 | tf_op jit(solution)/shard_map/ppermute | solution.py:209
  195.3 89.9 %collective-permute-start = (bf16[1,8,1,128,384]{3,4,1,2,0:T(8,128)(2,1)}, bf16[1,8,1,128,384]{3,4,1,2,0:T(8,128)(2,1)}, u32[]{:S(2)}, u32[]{:S(2)}) collective-permute-start(bf16[1,8,1,128,384]{3,4,1,2,0:T(8,128)(2,1)} %slice_bitcast_fusion.1), channel_id=1, source_target_pairs={{0,16},{1,17},{2,18},{3,19},{4,20},{5,21},{6,22},{7,23},{8,24},{9,... | collective-permute-start | bytes 2359304 | tf_op jit(solution)/shard_map/ppermute | solution.py:209
  208.5 131.9 %collective-permute-start.8 = (bf16[1,8,1,128,704]{3,4,1,2,0:T(8,128)(2,1)}, bf16[1,8,1,128,704]{3,4,1,2,0:T(8,128)(2,1)}, u32[]{:S(2)}, u32[]{:S(2)}) collective-permute-start(bf16[1,8,1,128,704]{3,4,1,2,0:T(8,128)(2,1)} %slice_bitcast_fusion), channel_id=1, source_target_pairs={{0,1},{1,0},{2,3},{3,2},{4,5},{5,4},{6,7},{7,6},{8,9},{9,8},{10,11... | collective-permute-start | bytes 4325384 | tf_op jit(solution)/shard_map/ppermute | solution.py:209
  269.0 71.4 %collective-permute-start.7 = (bf16[1,8,1,128,704]{3,4,1,2,0:T(8,128)(2,1)}, bf16[1,8,1,128,704]{3,4,1,2,0:T(8,128)(2,1)}, u32[]{:S(2)}, u32[]{:S(2)}) collective-permute-start(bf16[1,8,1,128,704]{3,4,1,2,0:T(8,128)(2,1)} %collective-permute-done.6), channel_id=1, source_target_pairs={{0,1},{1,0},{2,3},{3,2},{4,5},{5,4},{6,7},{7,6},{8,9},{9,8},{10,11... | collective-permute-start | bytes 4325384 | tf_op jit(solution)/shard_map/ppermute | solution.py:209
  271.1 49.5 %collective-permute-start.2 = (bf16[1,8,1,128,384]{3,4,1,2,0:T(8,128)(2,1)}, bf16[1,8,1,128,384]{3,4,1,2,0:T(8,128)(2,1)}, u32[]{:S(2)}, u32[]{:S(2)}) collective-permute-start(bf16[1,8,1,128,384]{3,4,1,2,0:T(8,128)(2,1)} %slice_bitcast_fusion.1), channel_id=1, source_target_pairs={{0,1},{1,0},{2,3},{3,2},{4,5},{5,4},{6,7},{7,6},{8,9},{9,8},{10,11... | collective-permute-start | bytes 2359304 | tf_op jit(solution)/shard_map/ppermute | solution.py:209
  285.2 50.2 %collective-permute-start.1 = (bf16[1,8,1,128,384]{3,4,1,2,0:T(8,128)(2,1)}, bf16[1,8,1,128,384]{3,4,1,2,0:T(8,128)(2,1)}, u32[]{:S(2)}, u32[]{:S(2)}) collective-permute-start(bf16[1,8,1,128,384]{3,4,1,2,0:T(8,128)(2,1)} %collective-permute-done), channel_id=1, source_target_pairs={{0,1},{1,0},{2,3},{3,2},{4,5},{5,4},{6,7},{7,6},{8,9},{9,8},{10,11... | collective-permute-start | bytes 2359304 | tf_op jit(solution)/shard_map/ppermute | solution.py:209
  294.3 42.6 %copy-start.23 = (bf16[1,8,1,128,384]{3,4,1,2,0:T(8,128)(2,1)S(1)}, bf16[1,8,1,128,384]{3,4,1,2,0:T(8,128)(2,1)}, u32[]{:S(2)}) copy-start(bf16[1,8,1,128,384]{3,4,1,2,0:T(8,128)(2,1)} %get-tuple-element.101) | copy-start | bytes 2359300
  294.3 42.6 %copy-start.24 = (bf16[1,8,1,128,384]{3,4,1,2,0:T(8,128)(2,1)S(1)}, bf16[1,8,1,128,384]{3,4,1,2,0:T(8,128)(2,1)}, u32[]{:S(2)}) copy-start(bf16[1,8,1,128,384]{3,4,1,2,0:T(8,128)(2,1)} %get-tuple-element.102) | copy-start | bytes 2359300
  395.3 31.2 %slice-start.4 = ((s8[8388608]{0:T(1024)(128)(4,1)}), s8[4194304]{0:T(1024)(128)(4,1)S(1)}, s32[]{:S(2)}) async-start(s8[8388608]{0:T(1024)(128)(4,1)} %bitcast.187), calls=%async_computation.10 | async-start | bytes 8388608
  413.6 204.6 %collective-permute-start.20 = (bf16[2048,704]{0,1:T(8,128)(2,1)}, bf16[2048,704]{0,1:T(8,128)(2,1)}, u32[]{:S(2)}, u32[]{:S(2)}) collective-permute-start(bf16[2048,704]{0,1:T(8,128)(2,1)} %convolution_convert_fusion), channel_id=1, source_target_pairs={{0,1},{1,0},{2,3},{3,2},{4,5},{5,4},{6,7},{7,6},{8,9},{9,8},{10,11... | collective-permute-start | bytes 8650760 | tf_op jit(solution)/shard_map/ppermute | solution.py:209
  434.0 109.8 %collective-permute-start.24 = (bf16[704,1024]{1,0:T(8,128)(2,1)}, bf16[704,1024]{1,0:T(8,128)(2,1)}, u32[]{:S(2)}, u32[]{:S(2)}) collective-permute-start(bf16[704,1024]{1,0:T(8,128)(2,1)} %select_convert_fusion.1), channel_id=1, source_target_pairs={{0,1},{1,0},{2,3},{3,2},{4,5},{5,4},{6,7},{7,6},{8,9},{9,8},{10,11... | collective-permute-start | bytes 4325384 | tf_op jit(solution)/shard_map/ppermute | solution.py:209
  445.6 30.2 %slice-start.10 = ((s8[8388608]{0:T(1024)(128)(4,1)}), s8[4194304]{0:T(1024)(128)(4,1)S(1)}, s32[]{:S(2)}) async-start(s8[8388608]{0:T(1024)(128)(4,1)} %bitcast.230), calls=%async_computation.16 | async-start | bytes 8388608
  475.0 49.8 %collective-permute-start.22 = (bf16[256,1024]{1,0:T(8,128)(2,1)S(1)}, bf16[256,1024]{1,0:T(8,128)(2,1)}, u32[]{:S(2)}, u32[]{:S(2)}) collective-permute-start(bf16[256,1024]{1,0:T(8,128)(2,1)S(1)} %select_convert_fusion.5), channel_id=1, source_target_pairs={{0,1},{1,0},{2,3},{3,2},{4,5},{5,4},{6,7},{7,6},{8,9},{9,8},{10,11... | collective-permute-start | bytes 1572872 | tf_op jit(solution)/shard_map/ppermute | solution.py:209
  487.3 65.0 %collective-permute-start.18 = (bf16[2048,384]{1,0:T(8,128)(2,1)}, bf16[2048,384]{1,0:T(8,128)(2,1)}, u32[]{:S(2)}, u32[]{:S(2)}) collective-permute-start(bf16[2048,384]{1,0:T(8,128)(2,1)} %select_convert_fusion), channel_id=1, source_target_pairs={{0,1},{1,0},{2,3},{3,2},{4,5},{5,4},{6,7},{7,6},{8,9},{9,8},{10,11... | collective-permute-start | bytes 4718600 | tf_op jit(solution)/shard_map/ppermute | solution.py:209
  505.2 130.0 %collective-permute-start.12 = (bf16[2,2,1,256,2048]{4,3,2,1,0:T(8,128)(2,1)}, bf16[2,2,1,256,2048]{4,3,2,1,0:T(8,128)(2,1)}, u32[]{:S(2)}, u32[]{:S(2)}) collective-permute-start(bf16[2,2,1,256,2048]{4,3,2,1,0:T(8,128)(2,1)} %broadcast_select_fusion.1), channel_id=1, source_target_pairs={{0,2},{1,3},{2,0},{3,1},{4,6},{5,7},{6,4},{7,5},{8,10},{9,11},{10,... | collective-permute-start | bytes 12582920 | tf_op jit(solution)/shard_map/ppermute | solution.py:209
  527.1 15.1 %collective-permute-start.23 = (bf16[1,1,1,128,1024]{4,3,2,1,0:T(8,128)(2,1)S(1)}, bf16[1,1,1,128,1024]{4,3,2,1,0:T(8,128)(2,1)S(1)}, u32[]{:S(2)}, u32[]{:S(2)}) collective-permute-start(bf16[1,1,1,128,1024]{4,3,2,1,0:T(8,128)(2,1)S(1)} %fusion.42), channel_id=1, source_target_pairs={{0,16},{1,17},{2,18},{3,19},{4,20},{5,21},{6,22},{7,23},{8,24},{9,... | collective-permute-start | bytes 786440 | tf_op jit(solution)/shard_map/ppermute | solution.py:209
  542.2 86.3 %collective-permute-start.15 = (bf16[2,2,1,256,2048]{4,3,2,1,0:T(8,128)(2,1)}, bf16[2,2,1,256,2048]{4,3,2,1,0:T(8,128)(2,1)}, u32[]{:S(2)}, u32[]{:S(2)}) collective-permute-start(bf16[2,2,1,256,2048]{4,3,2,1,0:T(8,128)(2,1)} %broadcast_select_fusion), channel_id=1, source_target_pairs={{0,2},{1,3},{2,0},{3,1},{4,6},{5,7},{6,4},{7,5},{8,10},{9,11},{10,... | collective-permute-start | bytes 12582920 | tf_op jit(solution)/shard_map/ppermute | solution.py:209
  549.2 50.8 %collective-permute-start.25 = (bf16[1,1,1,352,1024]{4,3,2,1,0:T(8,128)(2,1)}, bf16[1,1,1,352,1024]{4,3,2,1,0:T(8,128)(2,1)}, u32[]{:S(2)}, u32[]{:S(2)}) collective-permute-start(bf16[1,1,1,352,1024]{4,3,2,1,0:T(8,128)(2,1)} %fusion.39), channel_id=1, source_target_pairs={{0,16},{1,17},{2,18},{3,19},{4,20},{5,21},{6,22},{7,23},{8,24},{9,... | collective-permute-start | bytes 2162696 | tf_op jit(solution)/shard_map/ppermute | solution.py:209
  557.6 59.2 %collective-permute-start.19 = (bf16[1,8,1,128,384]{3,4,1,2,0:T(8,128)(2,1)}, bf16[1,8,1,128,384]{3,4,1,2,0:T(8,128)(2,1)}, u32[]{:S(2)}, u32[]{:S(2)}) collective-permute-start(bf16[1,8,1,128,384]{3,4,1,2,0:T(8,128)(2,1)} %copy.85), channel_id=1, source_target_pairs={{0,16},{1,17},{2,18},{3,19},{4,20},{5,21},{6,22},{7,23},{8,24},{9,... | collective-permute-start | bytes 2359304 | tf_op jit(solution)/shard_map/ppermute | solution.py:209
  558.9 41.1 %copy-start.9 = (f32[704,1024]{1,0:T(8,128)S(1)}, f32[704,1024]{1,0:T(8,128)}, u32[]{:S(2)}) copy-start(f32[704,1024]{1,0:T(8,128)} %copy-done.8) | copy-start | bytes 8650756
  562.1 54.7 %copy-start.19 = (f32[1,8,1,128,384]{3,4,1,2,0:T(8,128)S(1)}, f32[1,8,1,128,384]{3,4,1,2,0:T(8,128)}, u32[]{:S(2)}) copy-start(f32[1,8,1,128,384]{3,4,1,2,0:T(8,128)} %copy.86) | copy-start | bytes 4718596
  628.4 65.4 %collective-permute-start.21 = (bf16[1,8,1,128,704]{3,4,1,2,0:T(8,128)(2,1)S(1)}, bf16[1,8,1,128,704]{3,4,1,2,0:T(8,128)(2,1)S(1)}, u32[]{:S(2)}, u32[]{:S(2)}) collective-permute-start(bf16[1,8,1,128,704]{3,4,1,2,0:T(8,128)(2,1)S(1)} %copy.87), channel_id=1, source_target_pairs={{0,16},{1,17},{2,18},{3,19},{4,20},{5,21},{6,22},{7,23},{8,24},{9,... | collective-permute-start | bytes 4325384 | tf_op jit(solution)/shard_map/ppermute | solution.py:209
  635.2 65.2 %collective-permute-start.16 = (bf16[2,1,1,256,2048]{4,3,2,1,0:T(8,128)(2,1)S(1)}, bf16[2,1,1,256,2048]{4,3,2,1,0:T(8,128)(2,1)}, u32[]{:S(2)}, u32[]{:S(2)}) collective-permute-start(bf16[2,1,1,256,2048]{4,3,2,1,0:T(8,128)(2,1)S(1)} %broadcast_select_fusion.6), channel_id=1, source_target_pairs={{0,4},{1,5},{2,6},{3,7},{4,0},{5,1},{6,2},{7,3},{8,12},{9,13},{10,... | collective-permute-start | bytes 6291464 | tf_op jit(solution)/shard_map/ppermute | solution.py:209
  642.0 80.3 %collective-permute-start.13 = (bf16[1,2,1,256,2048]{4,3,2,1,0:T(8,128)(2,1)}, bf16[1,2,1,256,2048]{4,3,2,1,0:T(8,128)(2,1)}, u32[]{:S(2)}, u32[]{:S(2)}) collective-permute-start(bf16[1,2,1,256,2048]{4,3,2,1,0:T(8,128)(2,1)} %broadcast_select_fusion.7), channel_id=1, source_target_pairs={{0,8},{1,9},{2,10},{3,11},{4,12},{5,13},{6,14},{7,15},{8,0},{9,1},... | collective-permute-start | bytes 6291464 | tf_op jit(solution)/shard_map/ppermute | solution.py:209
  696.0 210.1 %all-to-all-start.1 = ((bf16[8,128,1088]{1,2,0:T(8,128)(2,1)}), bf16[8,128,1088]{1,2,0:T(8,128)(2,1)}, u32[]{:S(2)}, u32[]{:S(2)}) async-start(bf16[8,128,1088]{1,2,0:T(8,128)(2,1)} %pad_maximum_fusion.5), calls=%async_computation.1 | async-start | bytes 4456448 | tf_op jit(solution)/shard_map/all_to_all | solution.py:337
  700.3 204.3 %reduce-scatter.4.cloned.1.call-start = ((), (), s32[]{:S(2)}) async-start(), calls=%async_computation.5 | async-start | bytes 1081344
  704.8 63.0 %collective-permute-start.17 = (bf16[1,1,1,256,2048]{4,3,2,1,0:T(8,128)(2,1)S(1)}, bf16[1,1,1,256,2048]{4,3,2,1,0:T(8,128)(2,1)S(1)}, u32[]{:S(2)}, u32[]{:S(2)}) collective-permute-start(bf16[1,1,1,256,2048]{4,3,2,1,0:T(8,128)(2,1)S(1)} %broadcast_select_fusion.22), channel_id=1, source_target_pairs={{0,8},{1,9},{2,10},{3,11},{4,12},{5,13},{6,14},{7,15},{8,0},{9,1},... | collective-permute-start | bytes 3145736 | tf_op jit(solution)/shard_map/ppermute | solution.py:209
  726.3 42.1 %copy-start.5 = (bf16[256,2048]{1,0:T(8,128)(2,1)S(1)}, bf16[256,2048]{1,0:T(8,128)(2,1)}, u32[]{:S(2)}) copy-start(bf16[256,2048]{1,0:T(8,128)(2,1)} %param.18) | copy-start | bytes 3145732
  726.3 42.1 %copy-start.37 = (f32[1,2048]{1,0:T(1,128)S(1)}, f32[1,2048]{1,0:T(1,128)}, u32[]{:S(2)}) copy-start(f32[1,2048]{1,0:T(1,128)} %copy-done.36) | copy-start | bytes 24580
  726.3 42.1 %copy-start.39 = (f32[256]{0:T(256)S(1)}, f32[256]{0:T(256)}, u32[]{:S(2)}) copy-start(f32[256]{0:T(256)} %copy-done.38) | copy-start | bytes 3076
  726.3 42.1 %copy-start.41 = (f32[256]{0:T(256)S(1)}, f32[256]{0:T(256)}, u32[]{:S(2)}) copy-start(f32[256]{0:T(256)} %copy-done.40) | copy-start | bytes 3076
  726.3 44.6 %collective-permute-start.14 = (bf16[1,1,1,256,2048]{4,3,2,1,0:T(8,128)(2,1)}, bf16[1,1,1,256,2048]{4,3,2,1,0:T(8,128)(2,1)}, u32[]{:S(2)}, u32[]{:S(2)}) collective-permute-start(bf16[1,1,1,256,2048]{4,3,2,1,0:T(8,128)(2,1)} %broadcast_select_fusion.24), channel_id=1, source_target_pairs={{0,4},{1,5},{2,6},{3,7},{4,0},{5,1},{6,2},{7,3},{8,12},{9,13},{10,... | collective-permute-start | bytes 3145736 | tf_op jit(solution)/shard_map/ppermute | solution.py:209
  770.9 134.6 %copy-start.42 = (f32[5,64]{1,0:T(8,128)S(1)}, f32[5,64]{1,0:T(8,128)}, u32[]{:S(2)}) copy-start(f32[5,64]{1,0:T(8,128)} %param.25) | copy-start | bytes 3844
  770.9 134.6 %copy-start.43 = (f32[5,64]{1,0:T(8,128)S(1)}, f32[5,64]{1,0:T(8,128)}, u32[]{:S(2)}) copy-start(f32[5,64]{1,0:T(8,128)} %param.30) | copy-start | bytes 3844
  770.9 134.6 %copy-start.44 = (f32[5,64]{1,0:T(8,128)S(1)}, f32[5,64]{1,0:T(8,128)}, u32[]{:S(2)}) copy-start(f32[5,64]{1,0:T(8,128)} %param.35) | copy-start | bytes 3844
  (49 other events, 411.2 us)
Sparse Core Ops, SparseCore 0:
  82.9 87.3 all-gather.4
  171.9 73.6 all-gather.6
  771.0 133.6 reduce-scatter.3

commit v2 on v1

v2 whole, which is shorter than its diff:
```python
import functools

import jax
import jax.numpy as jnp
from jax import lax
from jax.experimental import pallas as pl
from jax.experimental.pallas import tpu as pltpu
from jax.sharding import Mesh, PartitionSpec as P

HEADS = 32
HEAD = 64
ROT = 16
MB = 2
STEP = 10
SLICES = 8
LANES = 128

theta_base = 10000.0
norm_eps = 1e-05
beta_one = 0.9
beta_two = 0.95
adam_eps = 1e-08
decay_rate = 0.1
rate_matrix = 0.05
rate_vector = 1.0

AXES = ("a", "t", "b", "y")
F32 = jnp.float32
BF16 = jnp.bfloat16


def dot(left, right):
    return jnp.dot(left, right, preferred_element_type=F32)


def dot_nt(left, right):
    return lax.dot_general(left, right, (((1,), (1,)), ((), ())), preferred_element_type=F32)


def dot_tn(left, right):
    return lax.dot_general(left, right, (((0,), (0,)), ((), ())), preferred_element_type=F32)


def rotary_lanes(row_count):
    half_rot = ROT // 2
    freqs = theta_base ** (-2.0 * jnp.arange(half_rot, dtype=F32) / ROT)
    angles = jnp.arange(row_count, dtype=F32)[:, None] * freqs[None, :]
    cosine, sine = jnp.cos(angles), jnp.sin(angles)
    rest = HEAD - ROT
    one, zero, gap = (
        jnp.ones((row_count, rest), F32),
        jnp.zeros((row_count, half_rot), F32),
        jnp.zeros((row_count, rest), F32),
    )
    cos_head = jnp.concatenate([cosine, cosine, one], axis=1)
    up_head = jnp.concatenate([sine, zero, gap], axis=1)
    down_head = jnp.concatenate([zero, sine, gap], axis=1)
    return tuple(jnp.concatenate([x, x], axis=1) for x in (cos_head, up_head, down_head))


def normalize(block_rows, gain_row, shift_row):
    row_mean = jnp.mean(block_rows, axis=-1, keepdims=True)
    centered = block_rows - row_mean
    inv_std = lax.rsqrt(jnp.mean(centered * centered, axis=-1, keepdims=True) + norm_eps)
    scaled = centered * inv_std
    return (scaled * gain_row + shift_row, scaled, inv_std)


def adam_update(weight, gradient, first_moment, second_moment, step_rate, decay):
    moment_new = beta_one * first_moment + (1.0 - beta_one) * gradient
    square_new = beta_two * second_moment + (1.0 - beta_two) * gradient * gradient
    moment_hat = moment_new / (1.0 - beta_one**STEP)
    square_hat = square_new / (1.0 - beta_two**STEP)
    weight_new = weight - step_rate * (
        moment_hat / (jnp.sqrt(square_hat) + adam_eps) + decay * weight
    )
    return (weight_new, moment_new, square_new)


def bits(count):
    found = []
    step = 1
    while step < count:
        found.append(step)
        step *= 2
    return found


def params(count):
    return pltpu.CompilerParams(
        dimension_semantics=("arbitrary",) * count, vmem_limit_bytes=56 * 2**20
    )


def cost(flops, bytes_moved, transcendentals=0):
    return pl.CostEstimate(
        flops=int(flops), bytes_accessed=int(bytes_moved), transcendentals=int(transcendentals)
    )


def place(here, parts, masks, target, sems, first_sem):
    copies = []
    for n, (part, (ma, mb, my)) in enumerate(zip(parts, masks)):
        copy = pltpu.make_async_copy(
            part, target(here[0] ^ ma, here[2] ^ mb, here[3] ^ my), sems.at[first_sem + n]
        )
        copy.start()
        copies.append(copy)
    return copies


def by_rows(ref, first, count):
    return lambda a, b, y: ref.at[y, a, pl.ds(first, count), b]


def place_gu(here, parts, masks, ref, sems, first_sem):
    count = len(masks)
    copies = []
    for n in range(2):
        cut = parts[n * count].shape[0]
        target = by_rows(ref, n * (ref.shape[2] - cut), cut)
        copies += place(
            here, parts[n * count : (n + 1) * count], masks, target, sems, first_sem + n * count
        )
    return copies


def by_columns(ref, width):
    return lambda a, b, y: ref.at[a, :, b, :, pl.ds(pl.multiple_of(y * width, 128), width)]


def prep_kernel(sizes, n_blocks, head_cols, d_rows, unit, qkv, gu, qkv_out, gu_out):
    n_a, n_t, n_b, _ = sizes
    ff_cols = n_b * d_rows
    for t in range(n_t):
        for block in range(n_blocks):
            at = (block * n_t + t) * head_cols
            qkv_out[t, :, block * head_cols : (block + 1) * head_cols] = qkv[
                :, at : at + head_cols
            ].astype(BF16)
        pieces = []
        gap = jnp.zeros((gu.shape[0], unit - d_rows), F32)
        for a in range(n_a):
            for b in range(n_b):
                at = (a * n_t + t) * ff_cols + b * d_rows
                pieces += [gu[:, at : at + d_rows], gap]
        gu_out[t] = jnp.concatenate(pieces, axis=1).astype(BF16)


def prep(sizes, unit, w_qkv, w_gu, d_rows):
    n_a, n_t, n_b, _ = sizes
    rows = w_qkv.shape[0]
    head_cols = n_b * rows
    n_blocks = w_qkv.shape[1] // (n_t * head_cols)
    tile = 16
    wide_q, wide_g = n_blocks * head_cols, n_a * n_b * unit
    return pl.pallas_call(
        functools.partial(prep_kernel, sizes, n_blocks, head_cols, d_rows, unit),
        grid=(rows // tile,),
        in_specs=[
            pl.BlockSpec((tile, w_qkv.shape[1]), lambda i: (i, 0)),
            pl.BlockSpec((tile, w_gu.shape[1]), lambda i: (i, 0)),
        ],
        out_specs=[
            pl.BlockSpec((n_t, tile, wide_q), lambda i: (0, i, 0)),
            pl.BlockSpec((n_t, tile, wide_g), lambda i: (0, i, 0)),
        ],
        out_shape=[
            jax.ShapeDtypeStruct((n_t, rows, wide_q), BF16),
            jax.ShapeDtypeStruct((n_t, rows, wide_g), BF16),
        ],
        compiler_params=params(1),
        cost_estimate=cost(0, 20 * w_gu.size),
        name="prep",
    )(w_qkv, w_gu)


def adam(weight, gradient, first_moment, second_moment):
    return adam_update(weight, gradient, first_moment, second_moment, rate_matrix, decay_rate)


def finish_gu_kernel(sizes, d_rows, unit, g, w, m, v, w_out, m_out, v_out):
    n_a, n_t, n_b, _ = sizes
    pieces = []
    for a in range(n_a):
        for t in range(n_t):
            for b in range(n_b):
                at = (a * n_b + b) * unit
                pieces.append(g[t, :, at : at + d_rows].astype(F32))
    grad = jnp.concatenate(pieces, axis=1)
    w_out[...], m_out[...], v_out[...] = adam(w[...], grad, m[...], v[...])


def finish_qkv_kernel(sizes, head_cols, g, w, m, v, w_out, m_out, v_out):
    n_t = sizes[1]
    for block in range(w.shape[1] // (n_t * head_cols)):
        for t in range(n_t):
            at = (block * n_t + t) * head_cols
            cols = slice(at, at + head_cols)
            tile, lane = block * head_cols // LANES, block * head_cols % LANES
            grad = g[t, tile, :, lane : lane + head_cols].astype(F32)
            w_out[:, cols], m_out[:, cols], v_out[:, cols] = adam(
                w[:, cols], grad, m[:, cols], v[:, cols]
            )


def finish(kernel, name, gradient, weight, first, second):
    tile = 16
    rows, cols = weight.shape
    matrix = pl.BlockSpec((tile, cols), lambda i: (i, 0))
    lead, lanes = gradient.shape[:-2], gradient.shape[-1]
    gradient_block = pl.BlockSpec(
        lead + (tile, lanes), lambda i: (0,) * len(lead) + (i, 0)
    )
    return pl.pallas_call(
        kernel,
        grid=(rows // tile,),
        in_specs=[
            gradient_block,
            matrix,
            matrix,
            matrix,
        ],
        out_specs=[matrix] * 3,
        out_shape=[jax.ShapeDtypeStruct(weight.shape, F32)] * 3,
        compiler_params=params(1),
        cost_estimate=cost(20 * weight.size, 26 * weight.size),
        name=name,
    )(gradient, weight, first, second)


ANYWHERE = pl.BlockSpec(memory_space=pl.ANY)


def mlp_kernel(masks, steps, here, vec, x_even, x_odd, dy_even, dy_odd, *rest):
    count = len(masks)
    gu_parts, down_parts = rest[: 2 * count], rest[2 * count : 3 * count]
    normed, grads_out, hidden, d_joined, gu, down, rows, sems, row_sems = rest[-9:]
    step = pl.program_id(0)
    slot = normed.shape[0]

    def fetch(n):
        spot = pl.ds(n // 2 * slot, slot)
        sources = (x_odd, dy_odd) if n % 2 else (x_even, dy_even)
        return [
            pltpu.make_async_copy(
                source.at[spot], rows.at[n % 2, pl.ds(m * slot, slot)], row_sems.at[n % 2, m]
            )
            for m, source in enumerate(sources)
        ]

    @pl.when(step == 0)
    def _():
        for copy in fetch(0):
            copy.start()
        copies = place_gu(here, gu_parts, masks, gu, sems, 0)
        target = by_columns(down, down.shape[4] // 2)
        copies += place(here, down_parts, masks, target, sems, 2 * count)
        for copy in copies:
            copy.wait()

    for n in range(steps):

        @pl.when(step == n)
        def _(n=n):
            if n + 1 < steps:
                for copy in fetch(n + 1):
                    copy.start()
            for copy in fetch(n):
                copy.wait()

    now = step % 2
    low = normalize(rows[now, :slot].astype(F32), vec[0:1], vec[1:2])[0].astype(BF16)
    dy = rows[now, slot:]
    normed[...] = low
    grads_out[...] = dy
    wide = gu.shape[5]
    gate = dot(low, gu[0].reshape(-1, wide))
    up = dot(low, gu[1].reshape(-1, wide))
    d_hidden = dot_nt(dy, down[...].reshape(wide, -1))
    sig = jax.nn.sigmoid(gate)
    act = gate * sig
    hidden[...] = (act * up).astype(BF16)
    d_joined[0] = (d_hidden * up * sig * (1.0 + gate * (1.0 - sig))).astype(BF16)
    d_joined[1] = (d_hidden * act).astype(BF16)


def mlp(here, masks, held, vec, gu_parts, down_parts, sizes, unit):
    n_a, n_t, n_b, n_y = sizes
    width = held[0].shape[1]
    slot = held[0].shape[0] * 2 // n_t
    wide = n_a * n_b * unit
    rows = n_t * slot
    w_rows = gu_parts[0].shape[1]
    return pl.pallas_call(
        functools.partial(mlp_kernel, masks, n_t),
        grid_spec=pltpu.PrefetchScalarGridSpec(
            num_scalar_prefetch=1,
            grid=(n_t,),
            in_specs=[pl.BlockSpec(vec.shape, lambda i, h: (0, 0))]
            + [ANYWHERE] * (3 * len(masks) + 4),
            out_specs=[
                pl.BlockSpec((slot, width), lambda i, h: (i, 0)),
                pl.BlockSpec((slot, width), lambda i, h: (i, 0)),
                pl.BlockSpec((slot, wide), lambda i, h: (i, 0)),
                pl.BlockSpec((2, slot, wide), lambda i, h: (0, i, 0)),
            ],
            scratch_shapes=[
                pltpu.VMEM((n_y, n_a, n_t, n_b, w_rows, wide), BF16),
                pltpu.VMEM((n_a, 1, n_b, unit, width), BF16),
                pltpu.VMEM((2, 2 * slot, width), BF16),
                pltpu.SemaphoreType.DMA((3 * len(masks),)),
                pltpu.SemaphoreType.DMA((2, 2)),
            ],
        ),
        out_shape=[
            jax.ShapeDtypeStruct((rows, width), BF16),
            jax.ShapeDtypeStruct((rows, width), BF16),
            jax.ShapeDtypeStruct((rows, wide), BF16),
            jax.ShapeDtypeStruct((2, rows, wide), BF16),
        ],
        compiler_params=params(1),
        name="mlp",
    )(here, vec, *held, *gu_parts, *down_parts)


def attention_kernel(
    masks, here, lengths, normed, dy, bias, cos_ref, up_ref, down_ref, *rest
):
    count = len(masks)
    qkv_parts, out_parts = rest[:count], rest[count : 2 * count]
    o_ref, dqkv_ref, bias_ref, w_qkv, w_out, sems = rest[2 * count :]

    @pl.when(pl.program_id(0) == 0)
    def _():
        copies = place(here, qkv_parts, masks, by_columns(w_qkv, w_qkv.shape[4] // 2), sems, 0)
        copies += place(here, out_parts, masks, by_columns(w_out, w_out.shape[4] // 2), sems, count)
        for copy in copies:
            copy.wait()

    rows = normed.shape[0]
    wide = w_qkv.shape[4]
    width = wide // 3
    qkv = dot(normed[...], w_qkv[...].reshape(-1, wide)) + bias[...]
    dpo = dot_nt(dy[...], w_out[...].reshape(width, -1)).astype(BF16)
    length = lengths[pl.program_id(0)]
    cosine, sine_up, sine_down = cos_ref[...], up_ref[...], down_ref[...]
    query_at = lax.broadcasted_iota(jnp.int32, (rows, rows), 0)
    key_at = lax.broadcasted_iota(jnp.int32, (rows, rows), 1)
    allowed = (key_at <= query_at) & (key_at < length)
    lane = lax.broadcasted_iota(jnp.int32, (rows, 2 * HEAD), 1)
    lower = lane < HEAD
    half = ROT // 2
    scale = HEAD ** (-0.5)

    def turn(x, sign):
        ahead = pltpu.roll(x, 2 * HEAD - half, 1)
        behind = pltpu.roll(x, half, 1)
        return x * cosine + sign * (behind * sine_down - ahead * sine_up)

    for pair in range(width // (2 * HEAD)):
        at = pair * 2 * HEAD
        cols = slice(at, at + 2 * HEAD)
        k_cols = slice(width + at, width + at + 2 * HEAD)
        v_cols = slice(2 * width + at, 2 * width + at + 2 * HEAD)
        q_rot = turn(qkv[:, cols], 1.0).astype(BF16)
        k_rot = turn(qkv[:, k_cols], 1.0).astype(BF16)
        values = qkv[:, v_cols].astype(BF16)
        grad = dpo[:, cols]
        results = []
        for side in range(2):
            mine = lower if side == 0 else ~lower
            scores = dot_nt(jnp.where(mine, q_rot, 0.0).astype(BF16), k_rot) * scale
            masked = jnp.where(allowed, scores, -1e30)
            raised = jnp.exp(masked - jnp.max(masked, axis=1, keepdims=True))
            probs = raised * (1.0 / jnp.sum(raised, axis=1, keepdims=True))
            probs_low = probs.astype(BF16)
            out = dot(probs_low, values)
            d_probs = dot_nt(jnp.where(mine, grad, 0.0).astype(BF16), values)
            d_values = dot_tn(probs_low, grad)
            inner = jnp.sum(probs * d_probs, axis=1, keepdims=True)
            d_scores = (probs * (d_probs - inner)).astype(BF16)
            d_query = dot(d_scores, k_rot) * scale
            d_keys = dot_tn(d_scores, q_rot) * scale
            results.append((out, d_query, d_keys, d_values))
        out, d_query, d_keys, d_values = (
            jnp.where(lower, first, second) for first, second in zip(*results)
        )
        o_ref[:, cols] = out.astype(BF16)
        for spot, value in (
            (cols, turn(d_query, -1.0)),
            (k_cols, turn(d_keys, -1.0)),
            (v_cols, d_values),
        ):
            low = value.astype(BF16)
            dqkv_ref[:, spot] = low
            bias_ref[0, :, spot] = jnp.sum(low.astype(F32), axis=0, keepdims=True)


def attention(here, masks, lengths, normed, dy, bias, qkv_parts, out_parts, sizes):
    n_a, n_t, n_b, _ = sizes
    slots = lengths.shape[0]
    slot, width = dy.shape[0] // slots, dy.shape[1]
    tables = rotary_lanes(slot)
    wide = bias.shape[1]
    table = pl.BlockSpec((slot, 2 * HEAD), lambda i, h, lens: (0, 0))
    w_rows = qkv_parts[0].shape[1]
    return pl.pallas_call(
        functools.partial(attention_kernel, masks),
        grid_spec=pltpu.PrefetchScalarGridSpec(
            num_scalar_prefetch=2,
            grid=(n_t,),
            in_specs=[
                pl.BlockSpec((slot, width), lambda i, h, lens: (i, 0)),
                pl.BlockSpec((slot, width), lambda i, h, lens: (i, 0)),
                pl.BlockSpec((1, wide), lambda i, h, lens: (0, 0)),
                table,
                table,
                table,
            ]
            + [ANYWHERE] * (2 * len(masks)),
            out_specs=[
                pl.BlockSpec((slot, wide // 3), lambda i, h, lens: (i, 0)),
                pl.BlockSpec((slot, wide), lambda i, h, lens: (i, 0)),
                pl.BlockSpec((1, 1, wide), lambda i, h, lens: (i, 0, 0)),
            ],
            scratch_shapes=[
                pltpu.VMEM((n_a, n_t, n_b, w_rows, wide), BF16),
                pltpu.VMEM((n_a, 1, n_b, w_rows, width), BF16),
                pltpu.SemaphoreType.DMA((2 * len(masks),)),
            ],
        ),
        out_shape=[
            jax.ShapeDtypeStruct((n_t * slot, wide // 3), BF16),
            jax.ShapeDtypeStruct((n_t * slot, wide), BF16),
            jax.ShapeDtypeStruct((n_t, 1, wide), F32),
        ],
        compiler_params=params(1),
        cost_estimate=cost(
            4 * n_t * slot * width * wide, 5 * n_t * slot * width * 2, n_t * slot * slot * 8
        ),
        name="attention",
    )(here, lengths, normed, dy, bias, *tables, *qkv_parts, *out_parts)


def grads_cols_kernel(where, left, d_sent, d_kept, sent, kept):
    tall = left[...]
    shape = (tall.shape[0], -1)
    sent[...] = dot_tn(tall, d_sent[...].reshape(shape)).astype(BF16)
    kept[...] = dot_tn(tall, d_kept[...].reshape(shape))


def grads_cols(where, normed, d_cols, name):
    rows, width = normed.shape
    half_rows = width // 2
    steps = 4
    tile = half_rows // steps
    if d_cols.ndim == 3:
        d_half = d_cols.shape[2]
        d_specs = [
            pl.BlockSpec((1, rows, d_half), lambda i, w: (1 - w[1], 0, 0)),
            pl.BlockSpec((1, rows, d_half), lambda i, w: (w[1], 0, 0)),
        ]
    else:
        d_half = d_cols.shape[1] // 2
        d_specs = [
            pl.BlockSpec((rows, d_half), lambda i, w: (0, 1 - w[1])),
            pl.BlockSpec((rows, d_half), lambda i, w: (0, w[1])),
        ]
    return pl.pallas_call(
        grads_cols_kernel,
        grid_spec=pltpu.PrefetchScalarGridSpec(
            num_scalar_prefetch=1,
            grid=(steps,),
            in_specs=[pl.BlockSpec((rows, tile), lambda i, w: (0, w[0] * steps + i))] + d_specs,
            out_specs=[pl.BlockSpec((tile, d_half), lambda i, w: (i, 0))] * 2,
        ),
        out_shape=[
            jax.ShapeDtypeStruct((half_rows, d_half), BF16),
            jax.ShapeDtypeStruct((half_rows, d_half), F32),
        ],
        compiler_params=params(1),
        cost_estimate=cost(2 * rows * width * d_half, 2 * rows * width + 4 * rows * d_half),
        name=name,
    )(where, normed, d_cols, d_cols)


def grads_rows_kernel(where, far, near, dy_sent, dy_kept, *outs):
    sent, kept = dy_sent[...], dy_kept[...]
    outs[0][...] = dot_tn(far[...], sent).astype(BF16)
    outs[1][...] = dot_tn(far[...], kept)
    outs[2][...] = dot_tn(near[...], sent).astype(BF16)
    outs[3][...] = dot_tn(near[...], kept)


def grads_rows(where, left, dy, name):
    rows, wide = left.shape
    width = dy.shape[1]
    half, dy_half = wide // 2, width // 2
    steps = 4
    tile = dy_half // steps
    block = (rows, tile)
    return pl.pallas_call(
        grads_rows_kernel,
        grid_spec=pltpu.PrefetchScalarGridSpec(
            num_scalar_prefetch=1,
            grid=(steps,),
            in_specs=[
                pl.BlockSpec((rows, half), lambda i, w: (0, w[0])),
                pl.BlockSpec((rows, half), lambda i, w: (0, 1 - w[0])),
                pl.BlockSpec(block, lambda i, w: (0, (1 - w[1]) * steps + i)),
                pl.BlockSpec(block, lambda i, w: (0, w[1] * steps + i)),
            ],
            out_specs=[pl.BlockSpec((half, tile), lambda i, w: (0, i))] * 4,
        ),
        out_shape=[jax.ShapeDtypeStruct((half, dy_half), t) for t in (BF16, F32, BF16, F32)],
        compiler_params=params(1),
        cost_estimate=cost(2 * rows * width * wide, 2 * rows * (width + wide) + 3 * wide * width),
        name=name,
    )(where, left, left, dy, dy)


def grads_attention_kernel(where, tall, d_sent, d_kept, far, near, dy_sent, dy_kept, *outs):
    step, steps = pl.program_id(0), pl.num_programs(0)
    left = tall[...]
    tile, half = left.shape[1], far.shape[1]
    part, first = step // (steps // 2), step % (steps // 2) * tile
    for out, d_cols, dy in ((outs[0], d_sent, dy_sent), (outs[1], d_kept, dy_kept)):
        result = dot_tn(left, d_cols[...]).astype(out.dtype)
        tiles = out.shape[1] - 1
        for n in range(tiles):
            spot = pl.ds(pl.multiple_of(first, tile), tile)
            out[part, n, spot, :] = result[:, n * LANES : (n + 1) * LANES]
        spot = pl.ds(pl.multiple_of(step * half, half), half)
        columns = dy[...]
        out[0, tiles, spot, :] = dot_tn(far[...], columns).astype(out.dtype)
        out[1, tiles, spot, :] = dot_tn(near[...], columns).astype(out.dtype)


def grads_attention(where, normed, d_qkv, attended, dy):
    rows, width = normed.shape
    d_half, half, dy_half = d_qkv.shape[1] // 2, attended.shape[1] // 2, width // 2
    steps = dy_half // LANES
    tile = width // steps
    block = (rows, LANES)
    shape = (2, d_half // LANES + 1, steps * half, LANES)
    assert shape[2] == width // 2

    def tall(i, w):
        return (0, jnp.where(i < steps // 2, w[0], 1 - w[0]) * (steps // 2) + i % (steps // 2))

    return pl.pallas_call(
        grads_attention_kernel,
        grid_spec=pltpu.PrefetchScalarGridSpec(
            num_scalar_prefetch=1,
            grid=(steps,),
            in_specs=[
                pl.BlockSpec((rows, tile), tall),
                pl.BlockSpec((rows, d_half), lambda i, w: (0, 1 - w[1])),
                pl.BlockSpec((rows, d_half), lambda i, w: (0, w[1])),
                pl.BlockSpec((rows, half), lambda i, w: (0, w[0])),
                pl.BlockSpec((rows, half), lambda i, w: (0, 1 - w[0])),
                pl.BlockSpec(block, lambda i, w: (0, (1 - w[1]) * steps + i)),
                pl.BlockSpec(block, lambda i, w: (0, w[1] * steps + i)),
            ],
            out_specs=[pl.BlockSpec(shape, lambda i, w: (0, 0, 0, 0))] * 2,
        ),
        out_shape=[jax.ShapeDtypeStruct(shape, t) for t in (BF16, F32)],
        compiler_params=params(1),
        name="grads_attention",
    )(where, normed, d_qkv, d_qkv, attended, attended, dy, dy)


def row_blocks(kernel, name, here, kept, inputs, parts, scratch, slot, width, n_t):
    def slot_of(i, h):
        return i % 2 * 4 + i // 2 * 2 + (0 if kept else 1)

    in_specs = []
    for value in inputs:
        block = (slot, value.shape[-1])
        if value.ndim == 3:
            block = (value.shape[0],) + block
            in_specs.append(pl.BlockSpec(block, lambda i, h: (0, slot_of(i, h), 0)))
        else:
            in_specs.append(pl.BlockSpec(block, lambda i, h: (slot_of(i, h), 0)))
    return pl.pallas_call(
        kernel,
        grid_spec=pltpu.PrefetchScalarGridSpec(
            num_scalar_prefetch=1,
            grid=(n_t // 2,),
            in_specs=in_specs + [ANYWHERE] * len(parts),
            out_specs=pl.BlockSpec((slot, width), lambda i, h: (i, 0)),
            scratch_shapes=scratch + [pltpu.SemaphoreType.DMA((len(parts),))],
        ),
        out_shape=jax.ShapeDtypeStruct((n_t // 2 * slot, width), BF16),
        compiler_params=params(1),
        name=name + ("_kept" if kept else "_sent"),
    )(here, *inputs, *parts)


def branch_kernel(masks, here, o, hidden, *rest):
    count = len(masks)
    out_parts, down_parts = rest[:count], rest[count : 2 * count]
    out, w_out, down, sems = rest[2 * count :]

    @pl.when(pl.program_id(0) == 0)
    def _():
        copies = place(here, out_parts, masks, by_columns(w_out, w_out.shape[4] // 2), sems, 0)
        copies += place(here, down_parts, masks, by_columns(down, down.shape[4] // 2), sems, count)
        for copy in copies:
            copy.wait()

    width = w_out.shape[4]
    branch = dot(o[...], w_out[...].reshape(-1, width))
    branch += dot(hidden[...], down[...].reshape(-1, width))
    out[...] = branch.astype(BF16)


def normal_kernel(masks, here, d_qkv, d_joined, *rest):
    count = len(masks)
    qkv_parts, gu_parts = rest[:count], rest[count : 3 * count]
    out, w_qkv, gu, sems = rest[3 * count :]

    @pl.when(pl.program_id(0) == 0)
    def _():
        copies = place(here, qkv_parts, masks, by_columns(w_qkv, w_qkv.shape[4] // 2), sems, 0)
        copies += place_gu(here, gu_parts, masks, gu, sems, count)
        for copy in copies:
            copy.wait()

    wide = w_qkv.shape[4]
    width = w_qkv.size // wide
    normal = dot_nt(d_qkv[...], w_qkv[...].reshape(width, -1))
    normal += dot_nt(d_joined[0], gu[0].reshape(width, -1))
    normal += dot_nt(d_joined[1], gu[1].reshape(width, -1))
    out[...] = normal.astype(BF16)


def after(value, *others):
    return lax.optimization_barrier((value,) + others)[0]


def per_device(
    sizes,
    tokens,
    cotangent,
    lengths,
    w_qkv,
    w_out,
    w_gate_up,
    w_down,
    vectors,
    first_qkv,
    first_out,
    first_gate_up,
    first_down,
    first_vectors,
    second_qkv,
    second_out,
    second_gate_up,
    second_down,
    second_vectors,
):
    barrier = lax.optimization_barrier
    n_a, n_t, n_b, n_y = sizes
    total = n_a * n_t * n_b * n_y
    at_a, at_t, at_b, at_y = (lax.axis_index(name).astype(jnp.int32) for name in AXES)
    here = jnp.stack([at_a, at_t, at_b, at_y])
    row_count, width = tokens.shape
    w_rows = w_qkv.shape[0]
    d_rows = w_down.shape[0]
    head_cols = n_b * w_rows
    unit = d_rows
    while unit % 16 or n_a * n_b * unit % 128:
        unit += 1

    def swap(value, name, step):
        mask = {"y": 1, "b": n_y, "t": n_y * n_b, "a": n_y * n_b * n_t}[name] * step
        return lax.ppermute(value, AXES, [(i, i ^ mask) for i in range(total)])

    def exchange(value):
        return lax.all_to_all(value, "t", split_axis=0, concat_axis=0, tiled=True)

    r_bits = [("a", s) for s in reversed(bits(n_a))] + [("b", s) for s in bits(n_b)]
    masks = [(0, 0, 0)]
    for name, step in r_bits:
        masks = masks + [
            (m[0] + step * (name == "a"), m[1] + step * (name == "b"), 0) for m in masks
        ]
    masks = tuple(masks + [(m[0], m[1], 1) for m in masks])

    small = 5 * vectors.shape[1] + lengths.shape[1]
    padded = -(-small // 128) * 128
    packed = jnp.concatenate(
        [
            vectors.reshape(1, 1, -1),
            lengths.astype(F32).reshape(1, 1, -1),
            jnp.zeros((1, 1, padded - small), F32),
        ],
        axis=2,
    )
    packed = jnp.broadcast_to(packed, (total, 1, padded))
    packed = lax.all_to_all(packed, AXES, split_axis=0, concat_axis=0, tiled=True)
    packed = packed.reshape(total, padded)

    def spread_top(part):
        parts = [part]
        for name, step in r_bits:
            parts = parts + [swap(p, name, step) for p in parts]
        return parts

    def over_y(value):
        return swap(value, "y", 1)

    def over_y_rest(parts):
        return [over_y(part) for part in parts[1:]]

    def over_top(value):
        return swap(value.astype(BF16), "a", top)

    def summed(kept, *got):
        return functools.reduce(lambda one, two: one.astype(F32) + two.astype(F32), got, kept)

    top = n_a // 2
    down_own = jnp.pad(w_down.astype(BF16), ((0, unit - d_rows), (0, 0)))[None]
    out_own = w_out.astype(BF16)[None]
    qkv_own, gu_own = prep(sizes, unit, w_qkv, w_gate_up, d_rows)
    x_top, x_middle, qkv_own, gu_own, down_own, out_own, packed = barrier(
        (
            swap(tokens, "t", n_t // 2),
            swap(tokens, "t", n_t // 4),
            qkv_own,
            gu_own,
            down_own,
            out_own,
            packed,
        )
    )

    gu_own, down_parts, down_other, x_far, cotangent = barrier(
        (
            exchange(gu_own),
            spread_top(down_own),
            over_y(down_own),
            swap(x_top, "t", n_t // 4),
            cotangent,
        )
    )
    cut = n_t // 2
    gu_first, gu_second = barrier((gu_own[:cut], gu_own[cut:]))
    gu_parts, gu_other, down_far, dy_top, dy_middle, gu_second, qkv_own = barrier(
        (
            spread_top(gu_first),
            over_y(gu_first),
            over_y_rest(down_parts),
            swap(cotangent, "t", n_t // 2),
            swap(cotangent, "t", n_t // 4),
            gu_second,
            qkv_own,
        )
    )
    down_parts = down_parts + [down_other] + down_far
    x_even = jnp.concatenate([tokens, x_middle, x_top, x_far], axis=0)
    gu_two, gu_two_other, gu_far, dy_far, x_odd, qkv_own = barrier(
        (
            spread_top(gu_second),
            over_y(gu_second),
            over_y_rest(gu_parts),
            swap(dy_top, "t", n_t // 4),
            swap(x_even, "t", 1),
            qkv_own,
        )
    )
    dy_even = jnp.concatenate([cotangent, dy_middle, dy_top, dy_far], axis=0)
    gu_two_far, qkv_own, dy_odd = barrier(
        (over_y_rest(gu_two), exchange(qkv_own), swap(dy_even, "t", 1))
    )
    gu_parts = gu_parts + [gu_other] + gu_far + gu_two + [gu_two_other] + gu_two_far

    all_vectors = packed[:, : 5 * vectors.shape[1]].reshape(total, 5, -1)
    all_vectors = all_vectors.transpose(1, 0, 2).reshape(5, width)
    group = packed[:, 5 * vectors.shape[1] : small].reshape(n_a, n_t, n_b, n_y, -1)
    group = lax.dynamic_index_in_dim(group, at_a, 0, keepdims=False)
    group = lax.dynamic_index_in_dim(group, at_b, 1, keepdims=False)
    group = jnp.where(at_y == 1, group[:, 0, 1], group[:, 0, 0])
    group = group.reshape(2, 2, 2)
    for dim, step in enumerate((4, 2, 1)):
        group = jnp.where(at_t // step % 2 == 1, jnp.flip(group, dim), group)
    slot_lengths = jnp.round(group.reshape(-1)).astype(jnp.int32)
    gain_row = all_vectors[0]
    bias = all_vectors[2:5].reshape(3 * n_a, n_t, head_cols)
    bias = lax.dynamic_index_in_dim(bias, at_t, 1, keepdims=False).reshape(1, -1)

    top = n_a // 2
    upper = at_a // top % 2
    other_half = jnp.stack([1 - upper, at_y])
    own_half = jnp.stack([upper, at_y])
    lower_bits = r_bits[1:]

    def over_rest(value, parts_shape):
        summed = value.reshape(parts_shape + (value.shape[-1],))
        for name, step in lower_bits:
            dim = 0 if name == "a" else 2
            at = at_a if name == "a" else at_b
            size = summed.shape[dim] // 2
            low_half = lax.slice_in_dim(summed, 0, size, axis=dim)
            high_half = lax.slice_in_dim(summed, size, 2 * size, axis=dim)
            is_upper = (at // step) % 2 == 1
            keep = jnp.where(is_upper, high_half, low_half)
            send = jnp.where(is_upper, low_half, high_half)
            summed = keep + swap(send.astype(BF16), name, step).astype(F32)
        return summed.reshape(summed.shape[1], summed.shape[3], summed.shape[4])

    def first_sums(got, kept):
        shape = (2, 2, row_count, width)
        both = got.reshape(shape).astype(F32) + kept.reshape(shape).astype(F32)
        left, right = both[..., :half_width], both[..., half_width:]
        return [v.astype(BF16) for v in (left[0], left[1], right[:, 0], right[:, 1])]

    def second_sums(left_kept, left_got, right_kept, right_got):
        sums = []
        for kept, got in ((left_kept, left_got), (right_kept, right_got)):
            both = (kept.astype(F32) + got.astype(F32)).astype(BF16)
            sums += [both[0], both[1]]
        return sums

    def third_sums(left_kept, left_got, right_kept, right_got):
        left = left_kept.astype(F32) + left_got.astype(F32)
        return jnp.concatenate([left, right_kept.astype(F32) + right_got.astype(F32)], axis=1)

    half_width = width // 2
    shape_w = (top, n_t, n_b, w_rows)
    normed, dy, hidden, d_joined = mlp(
        after(here, qkv_own),
        masks,
        (x_even, x_odd, dy_even, dy_odd),
        all_vectors[:2],
        gu_parts,
        down_parts,
        sizes,
        unit,
    )
    qkv_parts, qkv_other, out_parts, out_other, normed, dy, hidden, d_joined = barrier(
        (
            spread_top(qkv_own),
            over_y(qkv_own),
            spread_top(out_own),
            over_y(out_own),
            normed,
            dy,
            hidden,
            d_joined,
        )
    )

    qkv_far, out_far = over_y_rest(qkv_parts), over_y_rest(out_parts)
    down_far_sent, down_far_kept, down_sent, down_kept = grads_rows(
        other_half, hidden, dy, "grads_down"
    )
    gu_far_sent, gu_far_kept = grads_cols(
        after(other_half, down_kept), normed, d_joined, "grads_gate_up_far"
    )
    down_far_got = over_y(down_far_sent)
    gu_sent, gu_kept = grads_cols(
        after(own_half, gu_far_kept), normed, d_joined, "grads_gate_up_near"
    )
    qkv_far, out_far, down_far_got, gu_far_sent, down_sent, gu_sent, gu_kept = barrier(
        (qkv_far, out_far, down_far_got, gu_far_sent, down_sent, gu_sent, gu_kept)
    )
    qkv_parts = qkv_parts + [qkv_other] + qkv_far
    out_parts = out_parts + [out_other] + out_far

    down_far = barrier(summed(down_far_kept, down_far_got).astype(BF16))
    attended, d_qkv, bias_sums = attention(
        after(here, down_far),
        masks,
        slot_lengths,
        normed,
        dy,
        bias,
        qkv_parts,
        out_parts,
        sizes,
    )
    gu_rows = gu_sent.shape[0] // 2
    down_far_got, gu_far_got, down_sent, gu_sent, attended, d_qkv = barrier(
        (
            over_top(down_far),
            over_y(gu_far_sent),
            down_sent,
            (gu_sent[:gu_rows], gu_sent[gu_rows:]),
            attended,
            d_qkv,
        )
    )

    def quarters(value):
        value = value.reshape(value.shape[0] // (n_b * w_rows), n_b * w_rows, -1)
        part = value.shape[1] // 4
        return [value[:, n * part : (n + 1) * part] for n in range(4)]

    gu_far = [summed(k, g).astype(BF16) for k, g in zip(quarters(gu_far_kept), quarters(gu_far_got))]
    gu_far = barrier(gu_far)
    qo_sent, qo_kept = grads_attention(after(other_half, *gu_far), normed, d_qkv, attended, dy)
    gu_far_one, gu_got, gu_far, qo_far_sent, qo_sent = barrier(
        (
            over_top(gu_far[0]),
            over_y(gu_sent[0]),
            gu_far,
            (qo_sent[0, :2], qo_sent[0, 2:]),
            qo_sent[1],
        )
    )

    branch_rows = functools.partial(
        row_blocks,
        functools.partial(branch_kernel, masks),
        "branch_rows",
        inputs=(attended, hidden),
        parts=out_parts + down_parts,
        scratch=[
            pltpu.VMEM((n_a, 1, n_b, w_rows, width), BF16),
            pltpu.VMEM((n_a, 1, n_b, unit, width), BF16),
        ],
        slot=row_count,
        width=width,
        n_t=n_t,
    )
    branch_sent = branch_rows(after(here, *qo_far_sent), False)
    gu_far_two, qo_far_got, branch_sent, gu_far, qo_far_sent = barrier(
        (over_top(gu_far[1]), over_y(qo_far_sent[0]), branch_sent, gu_far, qo_far_sent[1])
    )
    branch_kept = branch_rows(after(here, branch_sent), True)
    gu_far_three, branch_got, qo_far_more, branch_kept, gu_far = barrier(
        (
            over_top(gu_far[2]),
            swap(branch_sent, "t", 1),
            over_y(qo_far_sent),
            branch_kept,
            gu_far,
        )
    )

    branch = barrier(first_sums(branch_got, branch_kept))
    normal_rows = functools.partial(
        row_blocks,
        functools.partial(normal_kernel, masks),
        "normal_rows",
        inputs=(d_qkv, d_joined),
        parts=qkv_parts + gu_parts,
        scratch=[
            pltpu.VMEM((n_a, n_t, n_b, w_rows, d_qkv.shape[1]), BF16),
            pltpu.VMEM((n_y, n_a, n_t, n_b, w_rows, n_a * n_b * unit), BF16),
        ],
        slot=row_count,
        width=width,
        n_t=n_t,
    )
    normal_sent = normal_rows(after(here, *branch), False)
    branch_got = [swap(branch[1], "t", 2), swap(branch[3], "t", 4)]
    qo_far_got = jnp.concatenate([qo_far_got, qo_far_more], axis=0)
    qo_far = summed(qo_kept[0], qo_far_got).astype(BF16)
    qo_far = (qo_far[:2], qo_far[2:])
    gu_far_four, gu_got_more, branch_got, normal_sent, qo_far, qo_sent, down_sent = barrier(
        (
            over_top(gu_far[3]),
            over_y(gu_sent[1]),
            branch_got,
            normal_sent,
            qo_far,
            qo_sent,
            down_sent,
        )
    )
    gu_got = jnp.concatenate([gu_got, gu_got_more], axis=0)
    gu_far_got = jnp.concatenate([gu_far_one, gu_far_two, gu_far_three, gu_far_four], axis=1)
    g_gu = summed(gu_kept, gu_got, gu_far_got.reshape(gu_kept.shape))
    g_gu = over_rest(g_gu, shape_w).astype(BF16)
    g_gu, qo_far = barrier((g_gu, qo_far))
    normal_kept = normal_rows(after(here, normal_sent, g_gu), True)
    qo_far_got, down_sent, normal_got, g_gu, normal_kept, qo_far, qo_got = barrier(
        (
            over_top(qo_far[0]),
            down_sent,
            swap(normal_sent, "t", 1),
            exchange(g_gu),
            normal_kept,
            qo_far[1],
            over_y(qo_sent),
        )
    )

    qo_far_more, down_got = over_top(qo_far), over_y(down_sent)
    normal = barrier(first_sums(normal_got, normal_kept))
    normal_got = [swap(normal[1], "t", 2), swap(normal[3], "t", 4)]
    branch = second_sums(branch[0], branch_got[0], branch[2], branch_got[1])
    branch = [after(part, *normal) for part in branch]
    new_gu, moment_gu, square_gu = finish(
        functools.partial(finish_gu_kernel, sizes, d_rows, unit),
        "finish_gate_up",
        after(g_gu, *branch),
        w_gate_up,
        first_gate_up,
        second_gate_up,
    )
    normal_got, qo_far_more, down_got, branch, new_gu = barrier(
        (normal_got, qo_far_more, down_got, branch, new_gu)
    )

    normal = barrier(second_sums(normal[0], normal_got[0], normal[2], normal_got[1]))
    normal_got = [swap(normal[1], "t", 4), swap(normal[3], "t", 2)]
    branch = barrier([after(part, *normal) for part in branch])
    branch_got = [swap(branch[1], "t", 4), swap(branch[3], "t", 2)]
    qo_far_got = jnp.concatenate([qo_far_got, qo_far_more], axis=0)
    qo = after(summed(qo_kept[1], qo_got, qo_far_got), *normal)
    g_qkv = over_rest(qo[:-1].transpose(1, 0, 2).reshape(qo.shape[1], -1), shape_w)
    g_out = qo[-1].reshape(half_width // LANES, -1, LANES).transpose(1, 0, 2)
    g_out = over_rest(g_out.reshape(-1, half_width), (top, 1, n_b, w_rows))
    g_qkv = g_qkv.astype(BF16).reshape(n_t, w_rows, -1, LANES).transpose(0, 2, 1, 3)
    g_qkv = barrier(g_qkv)
    g_down = summed(down_kept, down_got, down_far_got)
    g_down = over_rest(after(g_down, g_qkv), (top, 1, n_b, unit))
    new_down, moment_down, square_down = adam(w_down, g_down[0, :d_rows], first_down, second_down)
    g_qkv, normal_got, g_out, branch_got, new_down = barrier(
        (exchange(g_qkv), normal_got, g_out, branch_got, new_down)
    )
    normal_own = third_sums(normal[0], normal_got[0], normal[2], normal_got[1])
    _, scaled_own, inv_own = normalize(tokens.astype(F32), gain_row, all_vectors[1])
    d_scaled = normal_own * gain_row
    input_grad = cotangent.astype(F32) + inv_own * (
        d_scaled
        - jnp.mean(d_scaled, axis=-1, keepdims=True)
        - scaled_own * jnp.mean(d_scaled * scaled_own, axis=-1, keepdims=True)
    )
    g_bias = jnp.sum(bias_sums, axis=0).reshape(3 * n_a, 1, head_cols)
    is_here = (jnp.arange(n_t) == at_t)[None, :, None]
    g_bias = jnp.where(is_here, g_bias, 0.0).reshape(3, width)
    vector_part = jnp.concatenate(
        [
            jnp.sum(normal_own * scaled_own, axis=0)[None],
            jnp.sum(normal_own, axis=0)[None],
            g_bias,
        ],
        axis=0,
    )
    vector_part = vector_part.reshape(5, total, -1).transpose(1, 0, 2).reshape(total, 1, -1)
    vector_part = jnp.pad(vector_part, ((0, 0), (0, 0), (0, -vector_part.shape[2] % 128)))
    vector_part = lax.all_to_all(vector_part, AXES, split_axis=0, concat_axis=0, tiled=True)
    vector_grad = jnp.sum(vector_part, axis=0)[0, : vectors.size].reshape(vectors.shape)
    branch_own = third_sums(branch[0], branch_got[0], branch[2], branch_got[1])
    output = (tokens.astype(F32) + after(branch_own, vector_part)).astype(BF16)
    new_out, moment_out, square_out = adam(w_out, g_out[0], first_out, second_out)
    new_qkv, moment_qkv, square_qkv = finish(
        functools.partial(finish_qkv_kernel, sizes, head_cols),
        "finish_qkv",
        g_qkv,
        w_qkv,
        first_qkv,
        second_qkv,
    )
    new_vec, moment_vec, square_vec = adam_update(
        vectors, vector_grad, first_vectors, second_vectors, rate_vector, 0.0
    )
    return (
        output,
        input_grad.astype(BF16),
        new_qkv,
        new_out,
        new_gu,
        new_down,
        new_vec,
        moment_qkv,
        moment_out,
        moment_gu,
        moment_down,
        moment_vec,
        square_qkv,
        square_out,
        square_gu,
        square_down,
        square_vec,
    )


def solution(mesh):
    n_dp, n_y = mesh.shape["dp"], mesh.shape["branch"]
    n_b = max(1, HEAD * n_dp // (HEADS * HEAD))
    n_t = min(SLICES, n_dp // n_b)
    sizes = (n_dp // (n_t * n_b), n_t, n_b, n_y)
    split = Mesh(mesh.devices.reshape(sizes), AXES)
    dp = ("a", "t", "b")
    rows = P(AXES, None)
    matrix = P(dp, "y")
    vector = P(None, AXES)
    weights = (matrix, matrix, matrix, matrix, vector)
    return jax.shard_map(
        functools.partial(per_device, sizes),
        mesh=split,
        in_specs=(rows, rows, P(dp, None)) + weights * 3,
        out_specs=(rows, rows) + weights * 3,
        check_vma=False,
    )
```

time: 946 us -> 588 us (0.62)
  waiting for transfers between devices: 419 us -> 197 us
  Pallas kernels: 22.3 us -> 205 us
  matrix products: 149 us -> 0 us
  blocking collectives: 140 us -> 0 us
  other arithmetic: 99.8 us -> 48.3 us
  starting transfers between devices: 32.1 us -> 74.1 us
  between operations: 15.3 us -> 1.74 us
    pallas_call x1 -> x13, Pallas kernels: 22.3 us -> 205 us  [the longest x4 55.9 us: row_blocks(): pl.pallas_call(kernel, grid_spec=pltpu.PrefetchScalarGridSpec(num_scalar_...]
    dot_general x15 -> x0, matrix products: 149 us -> none  [the longest x5 61.5 us: dot_nt(): lax.dot_general(left, right, (((1,), (1,)), ((), ())), preferred_element_...]
    all_gather x2 -> x0, blocking collectives: 140 us -> none  [the longest x1 70.6 us: per_device(): all_vectors = lax.all_gather(vectors, AXES, axis=1, tiled=True)]
    unnamed x4 -> x0, waiting for transfers between devices: 129 us -> none
    ppermute x26 -> x48, waiting for transfers between devices: 290 us -> 184 us  [swap(): return lax.ppermute(value, AXES, [(i, i ^ mask) for i in range(total)])]
    select_n x19 -> x4, other arithmetic: 30.1 us -> 0.11 us  [the longest x1 0.07 us: per_device(): g_bias = jnp.where(is_here, g_bias, 0.0).reshape(3, width)]
    ppermute x26 -> x48, starting transfers between devices: 23.9 us -> 49.4 us  [swap(): return lax.ppermute(value, AXES, [(i, i ^ mask) for i in range(total)])]
    unnamed x144 -> x135, local copies, waits for them, and re-layouts: 34.5 us -> 15.7 us
  transfers between devices with their start and end apart: 31 -> 54, of which waited for: 14 -> 20; matrix products, arithmetic and copies ran while one was open for 24% -> 11% of each run, Pallas kernels for 2% -> 35%
where the time goes in v2:
time: 588 us; the launch traced here: 583 us
  Pallas kernels  205 us (35%)
  waiting for transfers between devices  197 us (34%)
  starting transfers between devices  74.1 us (13%)
  local copies, waits for them, and re-layouts  56.6 us (10%)
  other arithmetic  48.3 us (8%)
    ppermute x48, waiting for transfers between devices, swap(): return lax.ppermute(value, AXES, [(i, i ^ mask) for i in range(total)])  184 us
    pallas_call x4, Pallas kernels, row_blocks(): pl.pallas_call(kernel, grid_spec=pltpu.PrefetchScalarGridSpec(num_scalar_...  55.9 us
    ppermute x48, starting transfers between devices, swap(): return lax.ppermute(value, AXES, [(i, i ^ mask) for i in range(total)])  49.4 us
    pallas_call x1, Pallas kernels, attention(): pl.pallas_call(functools.partial(attention_kernel, masks), grid_spec=pltp...  33.7 us
    pallas_call x1, Pallas kernels, mlp(): pl.pallas_call(functools.partial(mlp_kernel, masks, n_t), grid_spec=pltpu...  33.5 us
    pallas_call x2, Pallas kernels, grads_cols(): pl.pallas_call(grads_cols_kernel, grid_spec=pltpu.PrefetchScalarGridSpec(...  24.4 us
    pallas_call x1, Pallas kernels, grads_attention(): pl.pallas_call(grads_attention_kernel, grid_spec=pltpu.PrefetchScalarGrid...  21.5 us
    pallas_call x2, Pallas kernels, finish(): pl.pallas_call(kernel, grid=(rows // tile,), in_specs=[gradient_block, ma...  17.8 us
  transfers between devices with their start and end apart: 54, of which 20 were waited for; matrix products, arithmetic and copies ran while one was open for 11% of the time, Pallas kernels for 35%

profile of v2, /device:TPU:0, one launch (start us, length us, event | category | flops | bytes accessed | tf_op | source)
XLA Modules:
  0.0 582.7 jit_solution(11116126732795837998)
XLA Ops:
  0.7 3.1 collective-permute-start
  7.5 3.9 all-to-all-start
  12.9 6.7 %prep.1 = (bf16[8,128,384]{2,1,0:T(8,128)(2,1)}, bf16[8,128,768]{2,1,0:T(8,128)(2,1)}) custom-call(f32[128,3072]{1,0:T(8,128)} %w.3, f32[128,5632]{1,0:T(8,128)} %w.2), custom_call_target="tpu_custom_call" | custom-call | bytes 14417920 | tf_op jit(solution)/shard_map/prep/pallas_call | solution.py:157
  20.4 11.6 %all-to-all-done = f32[32,1,384]{2,1,0:T(1,128)S(1)} async-done(((f32[32,1,384]{2,1,0:T(1,128)}), f32[32,1,384]{2,1,0:T(1,128)S(1)}, u32[]{:S(2)}, u32[]{:S(2)}) %all-to-all-start) | async-done | bytes 49184 | tf_op jit(solution)/shard_map/all_to_all | solution.py:703
  32.6 4.3 all-to-all-start.1
  42.8 15.3 %collective-permute-done.3.rest_10_.rest_6_ = bf16[1,384,1024]{2,1,0:T(8,128)(2,1)S(1)} collective-permute-done((bf16[1,384,1024]{2,1,0:T(8,128)(2,1)S(1)}, bf16[1,384,1024]{2,1,0:T(8,128)(2,1)S(1)}, u32[]{:S(2)}, u32[]{:S(2)}) %collective-permute-start.3) | collective-permute-done | bytes 786464 | tf_op jit(solution)/shard_map/ppermute | solution.py:679
  58.1 17.9 %collective-permute-done.2.rest_9_.rest_5_ = bf16[1,384,1024]{2,1,0:T(8,128)(2,1)S(1)} collective-permute-done((bf16[1,384,1024]{2,1,0:T(8,128)(2,1)S(1)}, bf16[1,384,1024]{2,1,0:T(8,128)(2,1)S(1)}, u32[]{:S(2)}, u32[]{:S(2)}) %collective-permute-start.2) | collective-permute-done | bytes 786464 | tf_op jit(solution)/shard_map/ppermute | solution.py:679
  76.1 3.4 collective-permute-done.4
  79.4 2.3 constant_dynamic-update-slice_fusion.x_even
  86.8 16.5 %collective-permute-done.6.rest_2_.rest_6_ = bf16[4,128,768]{2,1,0:T(8,128)(2,1)S(1)} collective-permute-done((bf16[4,128,768]{2,1,0:T(8,128)(2,1)S(1)}, bf16[4,128,768]{2,1,0:T(8,128)(2,1)S(1)}, u32[]{:S(2)}, u32[]{:S(2)}) %collective-permute-start.6) | collective-permute-done | bytes 786464 | tf_op jit(solution)/shard_map/ppermute | solution.py:679
  103.7 21.5 %collective-permute-done.5.rest_1_.rest_5_ = bf16[4,128,768]{2,1,0:T(8,128)(2,1)S(1)} collective-permute-done((bf16[4,128,768]{2,1,0:T(8,128)(2,1)S(1)}, bf16[4,128,768]{2,1,0:T(8,128)(2,1)S(1)}, u32[]{:S(2)}, u32[]{:S(2)}) %collective-permute-start.5) | collective-permute-done | bytes 786464 | tf_op jit(solution)/shard_map/ppermute | solution.py:679
  129.3 2.5 collective-permute-start.10
  135.5 12.7 %collective-permute-done.11.rest_6_.rest_10_ = bf16[4,128,768]{2,1,0:T(8,128)(2,1)S(1)} collective-permute-done((bf16[4,128,768]{2,1,0:T(8,128)(2,1)S(1)}, bf16[4,128,768]{2,1,0:T(8,128)(2,1)S(1)}, u32[]{:S(2)}, u32[]{:S(2)}) %collective-permute-start.11) | collective-permute-done | bytes 786464 | tf_op jit(solution)/shard_map/ppermute | solution.py:679
  148.1 16.8 %collective-permute-done.10.rest_5_.rest_9_ = bf16[4,128,768]{2,1,0:T(8,128)(2,1)S(1)} collective-permute-done((bf16[4,128,768]{2,1,0:T(8,128)(2,1)S(1)}, bf16[4,128,768]{2,1,0:T(8,128)(2,1)S(1)}, u32[]{:S(2)}, u32[]{:S(2)}) %collective-permute-start.10) | collective-permute-done | bytes 786464 | tf_op jit(solution)/shard_map/ppermute | solution.py:679
  169.8 4.4 all-to-all-start.2
  177.2 2.1 concatenate.55.down_ref
  179.3 2.1 concatenate.54.up_ref
  188.2 6.4 %collective-permute-done.15.rest_7_.rest_11_ = bf16[4,128,768]{2,1,0:T(8,128)(2,1)S(1)} collective-permute-done((bf16[4,128,768]{2,1,0:T(8,128)(2,1)S(1)}, bf16[4,128,768]{2,1,0:T(8,128)(2,1)S(1)}, u32[]{:S(2)}, u32[]{:S(2)}) %collective-permute-start.15) | collective-permute-done | bytes 786464 | tf_op jit(solution)/shard_map/ppermute | solution.py:679
  203.6 33.5 %mlp.1 = (bf16[2048,2048]{1,0:T(8,128)(2,1)}, bf16[2048,2048]{1,0:T(8,128)(2,1)}, bf16[2048,768]{1,0:T(8,128)(2,1)}, bf16[2,2048,768]{2,1,0:T(8,128)(2,1)}) custom-call(s32[4]{0:T(128)} %pad_add_fusion.here, f32[2,2048]{1,0:T(2,128)} %slice.168.vec, bf16[1024,2048]{1,0:T(8,128)(2,1)} %constant_dynamic-update-slice_fusion.x_even, ...), custom_call_target="tpu_custom_call" | custom-call | tf_op jit(solution)/shard_map/mlp/pallas_call | solution.py:295
  239.2 11.5 %grads_down.1 = (bf16[384,1024]{1,0:T(8,128)(2,1)}, f32[384,1024]{1,0:T(8,128)}, bf16[384,1024]{1,0:T(8,128)(2,1)}, f32[384,1024]{1,0:T(8,128)}) custom-call(s32[2]{0:T(128)} %get-tuple-element.270.where, bf16[2048,768]{1,0:T(8,128)(2,1)} %get-tuple-element.236.far.near.hidden, bf16[2048,768]{1,0:T(8,128)(2,1)} %get-tuple-element.236.far.near.hidden, ...), custom_call_target="tpu_custom_call" | custom-call | flops 6442450944 | bytes 16252928 | tf_op jit(solution)/shard_map/grads_down/pallas_call | solution.py:503
  251.9 12.1 %grads_gate_up_far.1 = (bf16[1024,768]{1,0:T(8,128)(2,1)}, f32[1024,768]{1,0:T(8,128)}) custom-call(s32[2]{0:T(128)} %get-tuple-element.270.where, bf16[2048,2048]{1,0:T(8,128)(2,1)} %get-tuple-element.241.left.normed.tall, bf16[2,2048,768]{2,1,0:T(8,128)(2,1)} %get-tuple-element.242.d_sent.d_kept.d_joined, ...), custom_call_target="tpu_custom_call" | custom-call | flops 6442450944 | bytes 14680064 | tf_op jit(solution)/shard_map/grads_gate_up_far/pallas_call | solution.py:470
  264.0 12.3 %grads_gate_up_near.1 = (bf16[1024,768]{1,0:T(8,128)(2,1)}, f32[1024,768]{1,0:T(8,128)}) custom-call(s32[2]{0:T(128)} %get-tuple-element.246.where, bf16[2048,2048]{1,0:T(8,128)(2,1)} %get-tuple-element.241.left.normed.tall, bf16[2,2048,768]{2,1,0:T(8,128)(2,1)} %get-tuple-element.242.d_sent.d_kept.d_joined, ...), custom_call_target="tpu_custom_call" | custom-call | flops 6442450944 | bytes 14680064 | tf_op jit(solution)/shard_map/grads_gate_up_near/pallas_call | solution.py:470
  280.6 2.6 collective-permute-start.24
  284.5 33.7 %attention.1 = (bf16[2048,256]{1,0:T(8,128)(2,1)}, bf16[2048,768]{1,0:T(8,128)(2,1)}, f32[8,1,768]{2,1,0:T(1,128)}) custom-call(s32[4]{0:T(128)} %pad_add_fusion.here, s32[8]{0:T(128)} %convert_element_type.217.lengths, bf16[2048,2048]{1,0:T(8,128)(2,1)} %get-tuple-element.241.left.normed.tall, bf16[2048,2048]{1,0:T(8,128)(2,1)} %get-tuple-element.237.dy_sent.dy_kept.dy, ...), custom_call_target="tpu_custom_call" | custom-call | flops 12884901888 | bytes 41943040 | tf_op jit(solution)/shard_map/attention/pallas_call | solution.py:408
  320.5 21.5 %grads_attention.1 = (bf16[2,4,1024,128]{3,2,1,0:T(8,128)(2,1)}, f32[2,4,1024,128]{3,2,1,0:T(8,128)}) custom-call(s32[2]{0:T(128)} %get-tuple-element.270.where, bf16[2048,2048]{1,0:T(8,128)(2,1)} %get-tuple-element.241.left.normed.tall, bf16[2048,768]{1,0:T(8,128)(2,1)} %get-tuple-element.271.d_sent.d_kept.d_qkv, ...), custom_call_target="tpu_custom_call" | custom-call | tf_op jit(solution)/shard_map/grads_attention/pallas_call | solution.py:552
  346.4 2.6 collective-permute-start.28
  349.0 10.3 %branch_rows_sent.1 = bf16[1024,2048]{1,0:T(8,128)(2,1)} custom-call(s32[4]{0:T(128)} %pad_add_fusion.here, bf16[2048,256]{1,0:T(8,128)(2,1)} %get-tuple-element.272.far.near.o, bf16[2048,768]{1,0:T(8,128)(2,1)} %get-tuple-element.236.far.near.hidden, bf16[1,128,1024]{2,1,0:T(8,128)(2,1)} %convert_bitcast_fusion.rest_4_.rest_0_, ...), custom_call_target="tpu_custom_call" | custom-call | tf_op jit(solution)/shard_map/branch_rows_sent/pallas_call | solution.py:586
  359.3 4.2 collective-permute-done.28
  363.9 10.3 %branch_rows_kept.1 = bf16[1024,2048]{1,0:T(8,128)(2,1)} custom-call(s32[4]{0:T(128)} %pad_add_fusion.here, bf16[2048,256]{1,0:T(8,128)(2,1)} %get-tuple-element.272.far.near.o, bf16[2048,768]{1,0:T(8,128)(2,1)} %get-tuple-element.236.far.near.hidden, bf16[1,128,1024]{2,1,0:T(8,128)(2,1)} %convert_bitcast_fusion.rest_4_.rest_0_, ...), custom_call_target="tpu_custom_call" | custom-call | tf_op jit(solution)/shard_map/branch_rows_kept/pallas_call | solution.py:586
  374.2 10.0 %collective-permute-done.30 = bf16[8,32,768]{2,1,0:T(8,128)(2,1)S(1)} collective-permute-done((bf16[8,32,768]{2,1,0:T(8,128)(2,1)S(1)}, bf16[8,32,768]{2,1,0:T(8,128)(2,1)S(1)}, u32[]{:S(2)}, u32[]{:S(2)}) %collective-permute-start.30) | collective-permute-done | bytes 393248 | tf_op jit(solution)/shard_map/ppermute | solution.py:679
  384.3 4.4 add_convert_fusion.1
  396.4 17.9 %normal_rows_sent.1 = bf16[1024,2048]{1,0:T(8,128)(2,1)} custom-call(s32[4]{0:T(128)} %pad_add_fusion.here, bf16[2048,768]{1,0:T(8,128)(2,1)} %get-tuple-element.271.d_sent.d_kept.d_qkv, bf16[2,2048,768]{2,1,0:T(8,128)(2,1)} %get-tuple-element.242.d_sent.d_kept.d_joined, bf16[8,128,384]{2,1,0:T(8,128)(2,1)} %all-to-all-done.2.rest_0_, ...), custom_call_target="tpu_custom_call" | custom-call | tf_op jit(solution)/shard_map/normal_rows_sent/pallas_call | solution.py:586
  415.4 7.6 %collective-permute-done.33 = bf16[8,32,768]{2,1,0:T(8,128)(2,1)} collective-permute-done((bf16[8,32,768]{2,1,0:T(8,128)(2,1)}, bf16[8,32,768]{2,1,0:T(8,128)(2,1)}, u32[]{:S(2)}, u32[]{:S(2)}) %collective-permute-start.33) | collective-permute-done | bytes 393248 | tf_op jit(solution)/shard_map/ppermute | solution.py:679
  423.0 2.1 collective-permute-done.36
  428.4 3.7 all-to-all-start.3
  435.5 17.5 %normal_rows_kept.1 = bf16[1024,2048]{1,0:T(8,128)(2,1)} custom-call(s32[4]{0:T(128)} %pad_add_fusion.here, bf16[2048,768]{1,0:T(8,128)(2,1)} %get-tuple-element.271.d_sent.d_kept.d_qkv, bf16[2,2048,768]{2,1,0:T(8,128)(2,1)} %get-tuple-element.242.d_sent.d_kept.d_joined, bf16[8,128,384]{2,1,0:T(8,128)(2,1)} %all-to-all-done.2.rest_0_, ...), custom_call_target="tpu_custom_call" | custom-call | tf_op jit(solution)/shard_map/normal_rows_kept/pallas_call | solution.py:586
  452.9 8.3 %collective-permute-done.37 = bf16[2,1024,128]{2,1,0:T(8,128)(2,1)S(1)} collective-permute-done((bf16[2,1024,128]{2,1,0:T(8,128)(2,1)S(1)}, bf16[2,1024,128]{2,1,0:T(8,128)(2,1)S(1)}, u32[]{:S(2)}, u32[]{:S(2)}) %collective-permute-start.37) | collective-permute-done | bytes 524320 | tf_op jit(solution)/shard_map/ppermute | solution.py:679
  463.4 5.9 %add_convert_fusion = bf16[1024,2048]{1,0:T(8,128)(2,1)S(1)} fusion(bf16[1024,2048]{1,0:T(8,128)(2,1)} %normal_rows_kept.1, bf16[1024,2048]{1,0:T(8,128)(2,1)} %collective-permute-done.38), kind=kLoop, calls=%fused_computation | loop fusion | flops 8388608 | bytes 12582912 | tf_op jit(solution)/shard_map/convert.5
  471.4 2.2 collective-permute-start.41
  477.8 10.3 %finish_gate_up.1 = (f32[128,5632]{1,0:T(8,128)}, f32[128,5632]{1,0:T(8,128)}, f32[128,5632]{1,0:T(8,128)}) custom-call(bf16[8,128,768]{2,1,0:T(8,128)(2,1)} %copy-done.15, f32[128,5632]{1,0:T(8,128)} %w.2, f32[128,5632]{1,0:T(8,128)} %m.2, f32[128,5632]{1,0:T(8,128)} %v.2), custom_call_target="tpu_custom_call" | custom-call | flops 14417920 | bytes 18743296 | tf_op jit(solution)/shard_map/finish_gate_up/pallas_call | solution.py:215
  488.1 18.7 %collective-permute-done.42 = bf16[2,1024,128]{2,1,0:T(8,128)(2,1)} collective-permute-done((bf16[2,1024,128]{2,1,0:T(8,128)(2,1)}, bf16[2,1024,128]{2,1,0:T(8,128)(2,1)}, u32[]{:S(2)}, u32[]{:S(2)}) %collective-permute-start.42) | collective-permute-done | bytes 524320 | tf_op jit(solution)/shard_map/ppermute | solution.py:679
  515.4 3.7 all-to-all-start.4
  523.5 2.2 convert_add_fusion.2
  528.7 5.1 multiply_subtract_fusion
  533.8 19.5 %collective-permute-done.46 = bf16[256,1024]{1,0:T(8,128)(2,1)} collective-permute-done((bf16[256,1024]{1,0:T(8,128)(2,1)}, bf16[256,1024]{1,0:T(8,128)(2,1)}, u32[]{:S(2)}, u32[]{:S(2)}) %collective-permute-start.46) | collective-permute-done | bytes 524320 | tf_op jit(solution)/shard_map/ppermute | solution.py:679
  558.9 4.7 all-to-all-start.5
  569.9 7.5 %finish_qkv.1 = (f32[128,3072]{1,0:T(8,128)}, f32[128,3072]{1,0:T(8,128)}, f32[128,3072]{1,0:T(8,128)}) custom-call(bf16[8,3,128,128]{3,2,1,0:T(8,128)(2,1)} %copy-done.28, f32[128,3072]{1,0:T(8,128)} %w.3, f32[128,3072]{1,0:T(8,128)} %m.3, f32[128,3072]{1,0:T(8,128)} %v.3), custom_call_target="tpu_custom_call" | custom-call | flops 7864320 | bytes 10223616 | tf_op jit(solution)/shard_map/finish_qkv/pallas_call | solution.py:215
  578.3 4.2 fusion.11
  (312 shorter events, 117.4 us)
Async XLA Ops:
  0.7 31.9 %collective-permute-start = (bf16[256,2048]{1,0:T(8,128)(2,1)}, bf16[256,2048]{1,0:T(8,128)(2,1)}, u32[]{:S(2)}, u32[]{:S(2)}) collective-permute-start(bf16[256,2048]{1,0:T(8,128)(2,1)} %param.18), channel_id=1, source_target_pairs={{0,8},{1,9},{2,10},{3,11},{4,12},{5,13},{6,14},{7,15},{8,0},{9,1},... | collective-permute-start | bytes 3145736 | tf_op jit(solution)/shard_map/ppermute | solution.py:679
  3.7 28.8 %collective-permute-start.1 = (bf16[256,2048]{1,0:T(8,128)(2,1)}, bf16[256,2048]{1,0:T(8,128)(2,1)}, u32[]{:S(2)}, u32[]{:S(2)}) collective-permute-start(bf16[256,2048]{1,0:T(8,128)(2,1)} %param.18), channel_id=1, source_target_pairs={{0,4},{1,5},{2,6},{3,7},{4,0},{5,1},{6,2},{7,3},{8,12},{9,13},{10,... | collective-permute-start | bytes 3145736 | tf_op jit(solution)/shard_map/ppermute | solution.py:679
  7.5 24.5 %all-to-all-start = ((f32[32,1,384]{2,1,0:T(1,128)}), f32[32,1,384]{2,1,0:T(1,128)S(1)}, u32[]{:S(2)}, u32[]{:S(2)}) async-start(f32[32,1,384]{2,1,0:T(1,128)} %broadcast_in_dim.60), calls=%async_computation | async-start | bytes 98304 | tf_op jit(solution)/shard_map/all_to_all | solution.py:703
  32.6 46.8 %all-to-all-start.1 = ((bf16[8,128,768]{2,1,0:T(8,128)(2,1)}), bf16[8,128,768]{2,1,0:T(8,128)(2,1)}, u32[]{:S(2)}, u32[]{:S(2)}) async-start(bf16[8,128,768]{2,1,0:T(8,128)(2,1)} %get-tuple-element.196), calls=%async_computation.1 | async-start | bytes 3145728 | tf_op jit(solution)/shard_map/all_to_all | solution.py:682
  36.9 42.5 %collective-permute-start.4 = (bf16[256,2048]{1,0:T(8,128)(2,1)}, bf16[256,2048]{1,0:T(8,128)(2,1)}, u32[]{:S(2)}, u32[]{:S(2)}) collective-permute-start(bf16[256,2048]{1,0:T(8,128)(2,1)} %collective-permute-done), channel_id=1, source_target_pairs={{0,4},{1,5},{2,6},{3,7},{4,0},{5,1},{6,2},{7,3},{8,12},{9,13},{10,... | collective-permute-start | bytes 3145736 | tf_op jit(solution)/shard_map/ppermute | solution.py:679
  39.2 36.8 %collective-permute-start.2 = (bf16[1,384,1024]{2,1,0:T(8,128)(2,1)S(1)}, bf16[1,384,1024]{2,1,0:T(8,128)(2,1)S(1)}, u32[]{:S(2)}, u32[]{:S(2)}) collective-permute-start(bf16[1,384,1024]{2,1,0:T(8,128)(2,1)S(1)} %pad_bitcast_fusion.rest_8_.rest_4_), channel_id=1, source_target_pairs={{0,16},{1,17},{2,18},{3,19},{4,20},{5,21},{6,22},{7,23},{8,24},{9,... | collective-permute-start | bytes 2359304 | tf_op jit(solution)/shard_map/ppermute | solution.py:679
  81.8 85.0 %collective-permute-start.14 = (bf16[1024,2048]{1,0:T(8,128)(2,1)}, bf16[1024,2048]{1,0:T(8,128)(2,1)S(1)}, u32[]{:S(2)}, u32[]{:S(2)}) collective-permute-start(bf16[1024,2048]{1,0:T(8,128)(2,1)} %constant_dynamic-update-slice_fusion.x_even), channel_id=1, source_target_pairs={{0,2},{1,3},{2,0},{3,1},{4,6},{5,7},{6,4},{7,5},{8,10},{9,11},{10,... | collective-permute-start | bytes 12582920 | tf_op jit(solution)/shard_map/ppermute | solution.py:679
  83.8 41.4 %collective-permute-start.9 = (bf16[256,2048]{1,0:T(8,128)(2,1)S(1)}, bf16[256,2048]{1,0:T(8,128)(2,1)S(1)}, u32[]{:S(2)}, u32[]{:S(2)}) collective-permute-start(bf16[256,2048]{1,0:T(8,128)(2,1)S(1)} %copy-done.20), channel_id=1, source_target_pairs={{0,4},{1,5},{2,6},{3,7},{4,0},{5,1},{6,2},{7,3},{8,12},{9,13},{10,... | collective-permute-start | bytes 3145736 | tf_op jit(solution)/shard_map/ppermute | solution.py:679
  84.2 41.8 %collective-permute-start.8 = (bf16[256,2048]{1,0:T(8,128)(2,1)S(1)}, bf16[256,2048]{1,0:T(8,128)(2,1)S(1)}, u32[]{:S(2)}, u32[]{:S(2)}) collective-permute-start(bf16[256,2048]{1,0:T(8,128)(2,1)S(1)} %copy-done.20), channel_id=1, source_target_pairs={{0,8},{1,9},{2,10},{3,11},{4,12},{5,13},{6,14},{7,15},{8,0},{9,1},... | collective-permute-start | bytes 3145736 | tf_op jit(solution)/shard_map/ppermute | solution.py:679
  85.9 39.3 %collective-permute-start.5 = (bf16[4,128,768]{2,1,0:T(8,128)(2,1)S(1)}, bf16[4,128,768]{2,1,0:T(8,128)(2,1)S(1)}, u32[]{:S(2)}, u32[]{:S(2)}) collective-permute-start(bf16[4,128,768]{2,1,0:T(8,128)(2,1)S(1)} %get-tuple-element.221.rest_0_.rest_4_), channel_id=1, source_target_pairs={{0,16},{1,17},{2,18},{3,19},{4,20},{5,21},{6,22},{7,23},{8,24},{9,... | collective-permute-start | bytes 2359304 | tf_op jit(solution)/shard_map/ppermute | solution.py:679
  103.3 21.9 %collective-permute-start.7 = (bf16[1,384,1024]{2,1,0:T(8,128)(2,1)S(1)}, bf16[1,384,1024]{2,1,0:T(8,128)(2,1)S(1)}, u32[]{:S(2)}, u32[]{:S(2)}) collective-permute-start(bf16[1,384,1024]{2,1,0:T(8,128)(2,1)S(1)} %collective-permute-done.2.rest_9_.rest_5_), channel_id=1, source_target_pairs={{0,1},{1,0},{2,3},{3,2},{4,5},{5,4},{6,7},{7,6},{8,9},{9,8},{10,11... | collective-permute-start | bytes 2359304 | tf_op jit(solution)/shard_map/ppermute | solution.py:679
  126.0 39.8 %collective-permute-start.13 = (bf16[256,2048]{1,0:T(8,128)(2,1)S(1)}, bf16[256,2048]{1,0:T(8,128)(2,1)S(1)}, u32[]{:S(2)}, u32[]{:S(2)}) collective-permute-start(bf16[256,2048]{1,0:T(8,128)(2,1)S(1)} %collective-permute-done.8), channel_id=1, source_target_pairs={{0,4},{1,5},{2,6},{3,7},{4,0},{5,1},{6,2},{7,3},{8,12},{9,13},{10,... | collective-permute-start | bytes 3145736 | tf_op jit(solution)/shard_map/ppermute | solution.py:679
  127.7 20.5 %collective-permute-start.11 = (bf16[4,128,768]{2,1,0:T(8,128)(2,1)S(1)}, bf16[4,128,768]{2,1,0:T(8,128)(2,1)S(1)}, u32[]{:S(2)}, u32[]{:S(2)}) collective-permute-start(bf16[4,128,768]{2,1,0:T(8,128)(2,1)S(1)} %get-tuple-element.224.rest_4_.rest_8_), channel_id=1, source_target_pairs={{0,1},{1,0},{2,3},{3,2},{4,5},{5,4},{6,7},{7,6},{8,9},{9,8},{10,11... | collective-permute-start | bytes 2359304 | tf_op jit(solution)/shard_map/ppermute | solution.py:679
  129.3 35.6 %collective-permute-start.10 = (bf16[4,128,768]{2,1,0:T(8,128)(2,1)S(1)}, bf16[4,128,768]{2,1,0:T(8,128)(2,1)S(1)}, u32[]{:S(2)}, u32[]{:S(2)}) collective-permute-start(bf16[4,128,768]{2,1,0:T(8,128)(2,1)S(1)} %get-tuple-element.224.rest_4_.rest_8_), channel_id=1, source_target_pairs={{0,16},{1,17},{2,18},{3,19},{4,20},{5,21},{6,22},{7,23},{8,24},{9,... | collective-permute-start | bytes 2359304 | tf_op jit(solution)/shard_map/ppermute | solution.py:679
  131.7 33.2 %collective-permute-start.12 = (bf16[4,128,768]{2,1,0:T(8,128)(2,1)S(1)}, bf16[4,128,768]{2,1,0:T(8,128)(2,1)S(1)}, u32[]{:S(2)}, u32[]{:S(2)}) collective-permute-start(bf16[4,128,768]{2,1,0:T(8,128)(2,1)S(1)} %collective-permute-done.5.rest_1_.rest_5_), channel_id=1, source_target_pairs={{0,1},{1,0},{2,3},{3,2},{4,5},{5,4},{6,7},{7,6},{8,9},{9,8},{10,11... | collective-permute-start | bytes 2359304 | tf_op jit(solution)/shard_map/ppermute | solution.py:679
  169.8 24.8 %collective-permute-start.16 = (bf16[1024,2048]{1,0:T(8,128)(2,1)}, bf16[1024,2048]{1,0:T(8,128)(2,1)}, u32[]{:S(2)}, u32[]{:S(2)}) collective-permute-start(bf16[1024,2048]{1,0:T(8,128)(2,1)} %constant_dynamic-update-slice_fusion.4.dy_even), channel_id=1, source_target_pairs={{0,2},{1,3},{2,0},{3,1},{4,6},{5,7},{6,4},{7,5},{8,10},{9,11},{10,... | collective-permute-start | bytes 12582920 | tf_op jit(solution)/shard_map/ppermute | solution.py:679
  169.8 24.8 %all-to-all-start.2 = ((bf16[8,128,384]{2,1,0:T(8,128)(2,1)}), bf16[8,128,384]{2,1,0:T(8,128)(2,1)}, u32[]{:S(2)}, u32[]{:S(2)}) async-start(bf16[8,128,384]{2,1,0:T(8,128)(2,1)} %get-tuple-element.212), calls=%async_computation.2 | async-start | bytes 1572864 | tf_op jit(solution)/shard_map/all_to_all | solution.py:682
  174.2 20.4 %collective-permute-start.15 = (bf16[4,128,768]{2,1,0:T(8,128)(2,1)S(1)}, bf16[4,128,768]{2,1,0:T(8,128)(2,1)S(1)}, u32[]{:S(2)}, u32[]{:S(2)}) collective-permute-start(bf16[4,128,768]{2,1,0:T(8,128)(2,1)S(1)} %copy-done.8), channel_id=1, source_target_pairs={{0,1},{1,0},{2,3},{3,2},{4,5},{5,4},{6,7},{7,6},{8,9},{9,8},{10,11... | collective-permute-start | bytes 2359304 | tf_op jit(solution)/shard_map/ppermute | solution.py:679
  186.5 50.5 %collective-permute-start.20 = (bf16[1,128,1024]{2,1,0:T(8,128)(2,1)}, bf16[1,128,1024]{2,1,0:T(8,128)(2,1)}, u32[]{:S(2)}, u32[]{:S(2)}) collective-permute-start(bf16[1,128,1024]{2,1,0:T(8,128)(2,1)} %convert_bitcast_fusion.rest_4_.rest_0_), channel_id=1, source_target_pairs={{0,1},{1,0},{2,3},{3,2},{4,5},{5,4},{6,7},{7,6},{8,9},{9,8},{10,11... | collective-permute-start | bytes 786440 | tf_op jit(solution)/shard_map/ppermute | solution.py:679
  188.1 48.9 %collective-permute-start.19 = (bf16[1,128,1024]{2,1,0:T(8,128)(2,1)}, bf16[1,128,1024]{2,1,0:T(8,128)(2,1)}, u32[]{:S(2)}, u32[]{:S(2)}) collective-permute-start(bf16[1,128,1024]{2,1,0:T(8,128)(2,1)} %convert_bitcast_fusion.rest_4_.rest_0_), channel_id=1, source_target_pairs={{0,16},{1,17},{2,18},{3,19},{4,20},{5,21},{6,22},{7,23},{8,24},{9,... | collective-permute-start | bytes 786440 | tf_op jit(solution)/shard_map/ppermute | solution.py:679
  194.6 42.4 %collective-permute-start.18 = (bf16[8,128,384]{2,1,0:T(8,128)(2,1)}, bf16[8,128,384]{2,1,0:T(8,128)(2,1)S(1)}, u32[]{:S(2)}, u32[]{:S(2)}) collective-permute-start(bf16[8,128,384]{2,1,0:T(8,128)(2,1)} %all-to-all-done.2.rest_0_), channel_id=1, source_target_pairs={{0,1},{1,0},{2,3},{3,2},{4,5},{5,4},{6,7},{7,6},{8,9},{9,8},{10,11... | collective-permute-start | bytes 2359304 | tf_op jit(solution)/shard_map/ppermute | solution.py:679
  195.1 42.0 %collective-permute-start.17 = (bf16[8,128,384]{2,1,0:T(8,128)(2,1)}, bf16[8,128,384]{2,1,0:T(8,128)(2,1)S(1)}, u32[]{:S(2)}, u32[]{:S(2)}) collective-permute-start(bf16[8,128,384]{2,1,0:T(8,128)(2,1)} %all-to-all-done.2.rest_0_), channel_id=1, source_target_pairs={{0,16},{1,17},{2,18},{3,19},{4,20},{5,21},{6,22},{7,23},{8,24},{9,... | collective-permute-start | bytes 2359304 | tf_op jit(solution)/shard_map/ppermute | solution.py:679
  237.1 39.1 %collective-permute-start.22 = (bf16[1,128,1024]{2,1,0:T(8,128)(2,1)}, bf16[1,128,1024]{2,1,0:T(8,128)(2,1)S(1)}, u32[]{:S(2)}, u32[]{:S(2)}) collective-permute-start(bf16[1,128,1024]{2,1,0:T(8,128)(2,1)} %collective-permute-done.19.rest_5_.rest_1_), channel_id=1, source_target_pairs={{0,1},{1,0},{2,3},{3,2},{4,5},{5,4},{6,7},{7,6},{8,9},{9,8},{10,11... | collective-permute-start | bytes 786440 | tf_op jit(solution)/shard_map/ppermute | solution.py:679
  238.2 38.0 %collective-permute-start.21 = (bf16[8,128,384]{2,1,0:T(8,128)(2,1)S(1)}, bf16[8,128,384]{2,1,0:T(8,128)(2,1)S(1)}, u32[]{:S(2)}, u32[]{:S(2)}) collective-permute-start(bf16[8,128,384]{2,1,0:T(8,128)(2,1)S(1)} %collective-permute-done.17.rest_1_), channel_id=1, source_target_pairs={{0,1},{1,0},{2,3},{3,2},{4,5},{5,4},{6,7},{7,6},{8,9},{9,8},{10,11... | collective-permute-start | bytes 2359304 | tf_op jit(solution)/shard_map/ppermute | solution.py:679
  250.7 27.3 %collective-permute-start.23 = (bf16[384,1024]{1,0:T(8,128)(2,1)}, bf16[384,1024]{1,0:T(8,128)(2,1)S(1)}, u32[]{:S(2)}, u32[]{:S(2)}) collective-permute-start(bf16[384,1024]{1,0:T(8,128)(2,1)} %get-tuple-element.238), channel_id=1, source_target_pairs={{0,1},{1,0},{2,3},{3,2},{4,5},{5,4},{6,7},{7,6},{8,9},{9,8},{10,11... | collective-permute-start | bytes 2359304 | tf_op jit(solution)/shard_map/ppermute | solution.py:679
  278.1 40.1 %collective-permute-start.25 = (bf16[1024,768]{1,0:T(8,128)(2,1)}, bf16[1024,768]{1,0:T(8,128)(2,1)S(1)}, u32[]{:S(2)}, u32[]{:S(2)}) collective-permute-start(bf16[1024,768]{1,0:T(8,128)(2,1)} %get-tuple-element.252), channel_id=1, source_target_pairs={{0,1},{1,0},{2,3},{3,2},{4,5},{5,4},{6,7},{7,6},{8,9},{9,8},{10,11... | collective-permute-start | bytes 4718600 | tf_op jit(solution)/shard_map/ppermute | solution.py:679
  280.6 37.6 %collective-permute-start.24 = (bf16[384,1024]{1,0:T(8,128)(2,1)}, bf16[384,1024]{1,0:T(8,128)(2,1)S(1)}, u32[]{:S(2)}, u32[]{:S(2)}) collective-permute-start(bf16[384,1024]{1,0:T(8,128)(2,1)} %add_convert_fusion.6), channel_id=1, source_target_pairs={{0,16},{1,17},{2,18},{3,19},{4,20},{5,21},{6,22},{7,23},{8,24},{9,... | collective-permute-start | bytes 2359304 | tf_op jit(solution)/shard_map/ppermute | solution.py:679
  318.2 26.8 %collective-permute-start.27 = (bf16[512,768]{1,0:T(8,128)(2,1)}, bf16[512,768]{1,0:T(8,128)(2,1)S(1)}, u32[]{:S(2)}, u32[]{:S(2)}) collective-permute-start(bf16[512,768]{1,0:T(8,128)(2,1)} %get-tuple-element.266), channel_id=1, source_target_pairs={{0,1},{1,0},{2,3},{3,2},{4,5},{5,4},{6,7},{7,6},{8,9},{9,8},{10,11... | collective-permute-start | bytes 2359304 | tf_op jit(solution)/shard_map/ppermute | solution.py:679
  320.0 25.0 %collective-permute-start.26 = (bf16[8,32,768]{2,1,0:T(8,128)(2,1)}, bf16[8,32,768]{2,1,0:T(8,128)(2,1)S(1)}, u32[]{:S(2)}, u32[]{:S(2)}) collective-permute-start(bf16[8,32,768]{2,1,0:T(8,128)(2,1)} %get-tuple-element.265), channel_id=1, source_target_pairs={{0,16},{1,17},{2,18},{3,19},{4,20},{5,21},{6,22},{7,23},{8,24},{9,... | collective-permute-start | bytes 1179656 | tf_op jit(solution)/shard_map/ppermute | solution.py:679
  363.5 20.8 %collective-permute-start.31 = (bf16[1024,2048]{1,0:T(8,128)(2,1)}, bf16[1024,2048]{1,0:T(8,128)(2,1)S(1)}, u32[]{:S(2)}, u32[]{:S(2)}) collective-permute-start(bf16[1024,2048]{1,0:T(8,128)(2,1)} %branch_rows_sent.1), channel_id=1, source_target_pairs={{0,2},{1,3},{2,0},{3,1},{4,6},{5,7},{6,4},{7,5},{8,10},{9,11},{10,... | collective-permute-start | bytes 12582920 | tf_op jit(solution)/shard_map/ppermute | solution.py:679
  363.5 20.8 %collective-permute-start.32 = (bf16[2,1024,128]{2,1,0:T(8,128)(2,1)S(1)}, bf16[2,1024,128]{2,1,0:T(8,128)(2,1)S(1)}, u32[]{:S(2)}, u32[]{:S(2)}) collective-permute-start(bf16[2,1024,128]{2,1,0:T(8,128)(2,1)S(1)} %get-tuple-element.283), channel_id=1, source_target_pairs={{0,1},{1,0},{2,3},{3,2},{4,5},{5,4},{6,7},{7,6},{8,9},{9,8},{10,11... | collective-permute-start | bytes 1572872 | tf_op jit(solution)/shard_map/ppermute | solution.py:679
  391.2 31.8 %collective-permute-start.35 = (bf16[2,256,1024]{2,1,0:T(8,128)(2,1)S(1)}, bf16[2,256,1024]{2,1,0:T(8,128)(2,1)S(1)}, u32[]{:S(2)}, u32[]{:S(2)}) collective-permute-start(bf16[2,256,1024]{2,1,0:T(8,128)(2,1)S(1)} %get-tuple-element.290), channel_id=1, source_target_pairs={{0,4},{1,5},{2,6},{3,7},{4,0},{5,1},{6,2},{7,3},{8,12},{9,13},{10,... | collective-permute-start | bytes 3145736 | tf_op jit(solution)/shard_map/ppermute | solution.py:679
  392.2 32.9 %collective-permute-start.36 = (bf16[2,256,1024]{2,1,0:T(8,128)(2,1)S(1)}, bf16[2,256,1024]{2,1,0:T(8,128)(2,1)S(1)}, u32[]{:S(2)}, u32[]{:S(2)}) collective-permute-start(bf16[2,256,1024]{2,1,0:T(8,128)(2,1)S(1)} %get-tuple-element.291), channel_id=1, source_target_pairs={{0,8},{1,9},{2,10},{3,11},{4,12},{5,13},{6,14},{7,15},{8,0},{9,1},... | collective-permute-start | bytes 3145736 | tf_op jit(solution)/shard_map/ppermute | solution.py:679
  392.2 23.2 %collective-permute-start.34 = (bf16[512,768]{1,0:T(8,128)(2,1)S(1)}, bf16[512,768]{1,0:T(8,128)(2,1)S(1)}, u32[]{:S(2)}, u32[]{:S(2)}) collective-permute-start(bf16[512,768]{1,0:T(8,128)(2,1)S(1)} %copy-done.43), channel_id=1, source_target_pairs={{0,1},{1,0},{2,3},{3,2},{4,5},{5,4},{6,7},{7,6},{8,9},{9,8},{10,11... | collective-permute-start | bytes 2359304 | tf_op jit(solution)/shard_map/ppermute | solution.py:679
  393.4 29.6 %collective-permute-start.33 = (bf16[8,32,768]{2,1,0:T(8,128)(2,1)}, bf16[8,32,768]{2,1,0:T(8,128)(2,1)}, u32[]{:S(2)}, u32[]{:S(2)}) collective-permute-start(bf16[8,32,768]{2,1,0:T(8,128)(2,1)} %get-tuple-element.286), channel_id=1, source_target_pairs={{0,16},{1,17},{2,18},{3,19},{4,20},{5,21},{6,22},{7,23},{8,24},{9,... | collective-permute-start | bytes 1179656 | tf_op jit(solution)/shard_map/ppermute | solution.py:679
  425.1 38.3 %collective-permute-start.38 = (bf16[1024,2048]{1,0:T(8,128)(2,1)}, bf16[1024,2048]{1,0:T(8,128)(2,1)}, u32[]{:S(2)}, u32[]{:S(2)}) collective-permute-start(bf16[1024,2048]{1,0:T(8,128)(2,1)} %normal_rows_sent.1), channel_id=1, source_target_pairs={{0,2},{1,3},{2,0},{3,1},{4,6},{5,7},{6,4},{7,5},{8,10},{9,11},{10,... | collective-permute-start | bytes 12582920 | tf_op jit(solution)/shard_map/ppermute | solution.py:679
  428.4 35.0 %all-to-all-start.3 = ((bf16[8,128,768]{2,1,0:T(8,128)(2,1)}), bf16[8,128,768]{2,1,0:T(8,128)(2,1)S(1)}, u32[]{:S(2)}, u32[]{:S(2)}) async-start(bf16[8,128,768]{2,1,0:T(8,128)(2,1)} %bitcast.114), calls=%async_computation.3 | async-start | bytes 3145728 | tf_op jit(solution)/shard_map/all_to_all | solution.py:682
  432.1 30.0 %collective-permute-start.39 = (bf16[4,1024,128]{2,1,0:T(8,128)(2,1)}, bf16[4,1024,128]{2,1,0:T(8,128)(2,1)}, u32[]{:S(2)}, u32[]{:S(2)}) collective-permute-start(bf16[4,1024,128]{2,1,0:T(8,128)(2,1)} %slice_bitcast_fusion.9), channel_id=1, source_target_pairs={{0,1},{1,0},{2,3},{3,2},{4,5},{5,4},{6,7},{7,6},{8,9},{9,8},{10,11... | collective-permute-start | bytes 3145736 | tf_op jit(solution)/shard_map/ppermute | solution.py:679
  433.6 27.7 %collective-permute-start.37 = (bf16[2,1024,128]{2,1,0:T(8,128)(2,1)S(1)}, bf16[2,1024,128]{2,1,0:T(8,128)(2,1)S(1)}, u32[]{:S(2)}, u32[]{:S(2)}) collective-permute-start(bf16[2,1024,128]{2,1,0:T(8,128)(2,1)S(1)} %copy-done.50), channel_id=1, source_target_pairs={{0,16},{1,17},{2,18},{3,19},{4,20},{5,21},{6,22},{7,23},{8,24},{9,... | collective-permute-start | bytes 1572872 | tf_op jit(solution)/shard_map/ppermute | solution.py:679
  469.8 37.1 %collective-permute-start.40 = (bf16[2,256,1024]{2,1,0:T(8,128)(2,1)S(1)}, bf16[2,256,1024]{2,1,0:T(8,128)(2,1)S(1)}, u32[]{:S(2)}, u32[]{:S(2)}) collective-permute-start(bf16[2,256,1024]{2,1,0:T(8,128)(2,1)S(1)} %get-tuple-element.316), channel_id=1, source_target_pairs={{0,4},{1,5},{2,6},{3,7},{4,0},{5,1},{6,2},{7,3},{8,12},{9,13},{10,... | collective-permute-start | bytes 3145736 | tf_op jit(solution)/shard_map/ppermute | solution.py:679
  471.4 36.1 %collective-permute-start.41 = (bf16[2,256,1024]{2,1,0:T(8,128)(2,1)S(1)}, bf16[2,256,1024]{2,1,0:T(8,128)(2,1)S(1)}, u32[]{:S(2)}, u32[]{:S(2)}) collective-permute-start(bf16[2,256,1024]{2,1,0:T(8,128)(2,1)S(1)} %get-tuple-element.317), channel_id=1, source_target_pairs={{0,8},{1,9},{2,10},{3,11},{4,12},{5,13},{6,14},{7,15},{8,0},{9,1},... | collective-permute-start | bytes 3145736 | tf_op jit(solution)/shard_map/ppermute | solution.py:679
  474.0 32.9 %collective-permute-start.43 = (bf16[384,1024]{1,0:T(8,128)(2,1)}, bf16[384,1024]{1,0:T(8,128)(2,1)S(1)}, u32[]{:S(2)}, u32[]{:S(2)}) collective-permute-start(bf16[384,1024]{1,0:T(8,128)(2,1)} %get-tuple-element.319), channel_id=1, source_target_pairs={{0,1},{1,0},{2,3},{3,2},{4,5},{5,4},{6,7},{7,6},{8,9},{9,8},{10,11... | collective-permute-start | bytes 2359304 | tf_op jit(solution)/shard_map/ppermute | solution.py:679
  475.7 31.2 %collective-permute-start.42 = (bf16[2,1024,128]{2,1,0:T(8,128)(2,1)}, bf16[2,1024,128]{2,1,0:T(8,128)(2,1)}, u32[]{:S(2)}, u32[]{:S(2)}) collective-permute-start(bf16[2,1024,128]{2,1,0:T(8,128)(2,1)} %get-tuple-element.318), channel_id=1, source_target_pairs={{0,16},{1,17},{2,18},{3,19},{4,20},{5,21},{6,22},{7,23},{8,24},{9,... | collective-permute-start | bytes 1572872 | tf_op jit(solution)/shard_map/ppermute | solution.py:679
  515.4 37.9 %all-to-all-start.4 = ((bf16[8,3,128,128]{3,2,1,0:T(8,128)(2,1)}), bf16[8,3,128,128]{3,2,1,0:T(8,128)(2,1)S(1)}, u32[]{:S(2)}, u32[]{:S(2)}) async-start(bf16[8,3,128,128]{3,2,1,0:T(8,128)(2,1)} %bitcast.107), calls=%async_computation.4 | async-start | bytes 1572864 | tf_op jit(solution)/shard_map/all_to_all | solution.py:682
  519.4 33.8 %collective-permute-start.44 = (bf16[256,1024]{1,0:T(8,128)(2,1)}, bf16[256,1024]{1,0:T(8,128)(2,1)}, u32[]{:S(2)}, u32[]{:S(2)}) collective-permute-start(bf16[256,1024]{1,0:T(8,128)(2,1)} %get-tuple-element.335), channel_id=1, source_target_pairs={{0,8},{1,9},{2,10},{3,11},{4,12},{5,13},{6,14},{7,15},{8,0},{9,1},... | collective-permute-start | bytes 1572872 | tf_op jit(solution)/shard_map/ppermute | solution.py:679
  521.4 31.8 %collective-permute-start.45 = (bf16[256,1024]{1,0:T(8,128)(2,1)}, bf16[256,1024]{1,0:T(8,128)(2,1)}, u32[]{:S(2)}, u32[]{:S(2)}) collective-permute-start(bf16[256,1024]{1,0:T(8,128)(2,1)} %get-tuple-element.337), channel_id=1, source_target_pairs={{0,4},{1,5},{2,6},{3,7},{4,0},{5,1},{6,2},{7,3},{8,12},{9,13},{10,... | collective-permute-start | bytes 1572872 | tf_op jit(solution)/shard_map/ppermute | solution.py:679
  522.9 30.3 %collective-permute-start.46 = (bf16[256,1024]{1,0:T(8,128)(2,1)}, bf16[256,1024]{1,0:T(8,128)(2,1)}, u32[]{:S(2)}, u32[]{:S(2)}) collective-permute-start(bf16[256,1024]{1,0:T(8,128)(2,1)} %get-tuple-element.350), channel_id=1, source_target_pairs={{0,8},{1,9},{2,10},{3,11},{4,12},{5,13},{6,14},{7,15},{8,0},{9,1},... | collective-permute-start | bytes 1572872 | tf_op jit(solution)/shard_map/ppermute | solution.py:679
  523.4 29.8 %collective-permute-start.47 = (bf16[256,1024]{1,0:T(8,128)(2,1)}, bf16[256,1024]{1,0:T(8,128)(2,1)}, u32[]{:S(2)}, u32[]{:S(2)}) collective-permute-start(bf16[256,1024]{1,0:T(8,128)(2,1)} %get-tuple-element.351), channel_id=1, source_target_pairs={{0,4},{1,5},{2,6},{3,7},{4,0},{5,1},{6,2},{7,3},{8,12},{9,13},{10,... | collective-permute-start | bytes 1572872 | tf_op jit(solution)/shard_map/ppermute | solution.py:679
  (71 other events, 755.3 us)

commit v3 on v2

--- a/solution.py
+++ b/solution.py
@@ -397,11 +397,10 @@
             bias_ref[0, :, spot] = jnp.sum(low.astype(F32), axis=0, keepdims=True)
 
 
-def attention(here, masks, lengths, normed, dy, bias, qkv_parts, out_parts, sizes):
+def attention(here, masks, lengths, tables, normed, dy, bias, qkv_parts, out_parts, sizes):
     n_a, n_t, n_b, _ = sizes
     slots = lengths.shape[0]
     slot, width = dy.shape[0] // slots, dy.shape[1]
-    tables = rotary_lanes(slot)
     wide = bias.shape[1]
     table = pl.BlockSpec((slot, 2 * HEAD), lambda i, h, lens: (0, 0))
     w_rows = qkv_parts[0].shape[1]
@@ -443,44 +442,53 @@
     )(here, lengths, normed, dy, bias, *tables, *qkv_parts, *out_parts)
 
 
-def grads_cols_kernel(where, left, d_sent, d_kept, sent, kept):
+def grads_cols_kernel(where, left, d_sent, d_kept, *outs):
     tall = left[...]
-    shape = (tall.shape[0], -1)
-    sent[...] = dot_tn(tall, d_sent[...].reshape(shape)).astype(BF16)
-    kept[...] = dot_tn(tall, d_kept[...].reshape(shape))
+    sent = dot_tn(tall, d_sent[0]).astype(BF16)
+    kept = dot_tn(tall, d_kept[0])
+    far = pl.program_id(0) < pl.num_programs(0) // 2
+
+    @pl.when(far)
+    def _():
+        outs[0][...] = sent
+        outs[1][...] = kept
+
+    @pl.when(jnp.logical_not(far))
+    def _():
+        outs[2][...] = sent
+        outs[3][...] = kept
 
 
 def grads_cols(where, normed, d_cols, name):
     rows, width = normed.shape
+    wide = d_cols.shape[2]
     half_rows = width // 2
     steps = 4
     tile = half_rows // steps
-    if d_cols.ndim == 3:
-        d_half = d_cols.shape[2]
-        d_specs = [
-            pl.BlockSpec((1, rows, d_half), lambda i, w: (1 - w[1], 0, 0)),
-            pl.BlockSpec((1, rows, d_half), lambda i, w: (w[1], 0, 0)),
-        ]
-    else:
-        d_half = d_cols.shape[1] // 2
-        d_specs = [
-            pl.BlockSpec((rows, d_half), lambda i, w: (0, 1 - w[1])),
-            pl.BlockSpec((rows, d_half), lambda i, w: (0, w[1])),
-        ]
+
+    def tall(i, w):
+        return (0, jnp.where(i < steps, w[0], 1 - w[0]) * steps + i % steps)
+
+    def far(i, w):
+        return (jnp.minimum(i, steps - 1), 0)
+
+    def near(i, w):
+        return (jnp.maximum(i - steps, 0), 0)
+
     return pl.pallas_call(
         grads_cols_kernel,
         grid_spec=pltpu.PrefetchScalarGridSpec(
             num_scalar_prefetch=1,
-            grid=(steps,),
-            in_specs=[pl.BlockSpec((rows, tile), lambda i, w: (0, w[0] * steps + i))] + d_specs,
-            out_specs=[pl.BlockSpec((tile, d_half), lambda i, w: (i, 0))] * 2,
+            grid=(2 * steps,),
+            in_specs=[
+                pl.BlockSpec((rows, tile), tall),
+                pl.BlockSpec((1, rows, wide), lambda i, w: (1 - w[1], 0, 0)),
+                pl.BlockSpec((1, rows, wide), lambda i, w: (w[1], 0, 0)),
+            ],
+            out_specs=[pl.BlockSpec((tile, wide), at) for at in (far, far, near, near)],
         ),
-        out_shape=[
-            jax.ShapeDtypeStruct((half_rows, d_half), BF16),
-            jax.ShapeDtypeStruct((half_rows, d_half), F32),
-        ],
+        out_shape=[jax.ShapeDtypeStruct((half_rows, wide), t) for t in (BF16, F32, BF16, F32)],
         compiler_params=params(1),
-        cost_estimate=cost(2 * rows * width * d_half, 2 * rows * width + 4 * rows * d_half),
         name=name,
     )(where, normed, d_cols, d_cols)
 
@@ -520,21 +528,26 @@
     )(where, left, left, dy, dy)
 
 
-def grads_attention_kernel(where, tall, d_sent, d_kept, far, near, dy_sent, dy_kept, *outs):
+def grads_attention_kernel(where, tall, d_qkv, left, dy_sent, dy_kept, sent, kept):
     step, steps = pl.program_id(0), pl.num_programs(0)
-    left = tall[...]
-    tile, half = left.shape[1], far.shape[1]
+    tile, half = tall.shape[1], left.shape[1] // 2
+    tiles = sent.shape[1] - 1
     part, first = step // (steps // 2), step % (steps // 2) * tile
-    for out, d_cols, dy in ((outs[0], d_sent, dy_sent), (outs[1], d_kept, dy_kept)):
-        result = dot_tn(left, d_cols[...]).astype(out.dtype)
-        tiles = out.shape[1] - 1
+    result = dot_tn(tall[...], d_qkv[...])
+    low, high = result[:, : tiles * LANES], result[:, tiles * LANES :]
+    upper = where[1] == 1
+    for out, d_cols, dy in (
+        (sent, jnp.where(upper, low, high), dy_sent),
+        (kept, jnp.where(upper, high, low), dy_kept),
+    ):
+        d_cols = d_cols.astype(out.dtype)
+        spot = pl.ds(pl.multiple_of(first, tile), tile)
         for n in range(tiles):
-            spot = pl.ds(pl.multiple_of(first, tile), tile)
-            out[part, n, spot, :] = result[:, n * LANES : (n + 1) * LANES]
+            out[part, n, spot, :] = d_cols[:, n * LANES : (n + 1) * LANES]
+        columns = dot_tn(left[...], dy[...]).astype(out.dtype)
         spot = pl.ds(pl.multiple_of(step * half, half), half)
-        columns = dy[...]
-        out[0, tiles, spot, :] = dot_tn(far[...], columns).astype(out.dtype)
-        out[1, tiles, spot, :] = dot_tn(near[...], columns).astype(out.dtype)
+        out[where[0], tiles, spot, :] = columns[:half]
+        out[1 - where[0], tiles, spot, :] = columns[half:]
 
 
 def grads_attention(where, normed, d_qkv, attended, dy):
@@ -556,10 +569,8 @@
             grid=(steps,),
             in_specs=[
                 pl.BlockSpec((rows, tile), tall),
-                pl.BlockSpec((rows, d_half), lambda i, w: (0, 1 - w[1])),
-                pl.BlockSpec((rows, d_half), lambda i, w: (0, w[1])),
-                pl.BlockSpec((rows, half), lambda i, w: (0, w[0])),
-                pl.BlockSpec((rows, half), lambda i, w: (0, 1 - w[0])),
+                pl.BlockSpec((rows, 2 * d_half), lambda i, w: (0, 0)),
+                pl.BlockSpec((rows, 2 * half), lambda i, w: (0, 0)),
                 pl.BlockSpec(block, lambda i, w: (0, (1 - w[1]) * steps + i)),
                 pl.BlockSpec(block, lambda i, w: (0, w[1] * steps + i)),
             ],
@@ -568,12 +579,21 @@
         out_shape=[jax.ShapeDtypeStruct(shape, t) for t in (BF16, F32)],
         compiler_params=params(1),
         name="grads_attention",
-    )(where, normed, d_qkv, d_qkv, attended, attended, dy, dy)
+    )(where, normed, d_qkv, attended, dy, dy)
 
 
 def row_blocks(kernel, name, here, kept, inputs, parts, scratch, slot, width, n_t):
     def slot_of(i, h):
-        return i % 2 * 4 + i // 2 * 2 + (0 if kept else 1)
+        lowest = (i < n_t // 2).astype(jnp.int32) if kept is None else 1 - kept
+        return i % 2 * 4 + i // 2 % 2 * 2 + lowest
+
+    half = n_t // 2
+    blocks = [lambda i, h: (i, 0)]
+    if kept is None:
+        blocks = [
+            lambda i, h: (jnp.minimum(i, half - 1), 0),
+            lambda i, h: (jnp.maximum(i - half, 0), 0),
+        ]
 
     in_specs = []
     for value in inputs:
@@ -587,21 +607,21 @@
         kernel,
         grid_spec=pltpu.PrefetchScalarGridSpec(
             num_scalar_prefetch=1,
-            grid=(n_t // 2,),
+            grid=(half * len(blocks),),
             in_specs=in_specs + [ANYWHERE] * len(parts),
-            out_specs=pl.BlockSpec((slot, width), lambda i, h: (i, 0)),
+            out_specs=[pl.BlockSpec((slot, width), block) for block in blocks],
             scratch_shapes=scratch + [pltpu.SemaphoreType.DMA((len(parts),))],
         ),
-        out_shape=jax.ShapeDtypeStruct((n_t // 2 * slot, width), BF16),
+        out_shape=[jax.ShapeDtypeStruct((half * slot, width), BF16)] * len(blocks),
         compiler_params=params(1),
-        name=name + ("_kept" if kept else "_sent"),
+        name=name if kept is None else name + ("_kept" if kept else "_sent"),
     )(here, *inputs, *parts)
 
 
 def branch_kernel(masks, here, o, hidden, *rest):
     count = len(masks)
     out_parts, down_parts = rest[:count], rest[count : 2 * count]
-    out, w_out, down, sems = rest[2 * count :]
+    *outs, w_out, down, sems = rest[2 * count :]
 
     @pl.when(pl.program_id(0) == 0)
     def _():
@@ -613,7 +633,15 @@
     width = w_out.shape[4]
     branch = dot(o[...], w_out[...].reshape(-1, width))
     branch += dot(hidden[...], down[...].reshape(-1, width))
-    out[...] = branch.astype(BF16)
+    branch, step, half = branch.astype(BF16), pl.program_id(0), pl.num_programs(0) // 2
+
+    @pl.when(step < half)
+    def _():
+        outs[0][...] = branch
+
+    @pl.when(step >= half)
+    def _():
+        outs[1][...] = branch
 
 
 def normal_kernel(masks, here, d_qkv, d_joined, *rest):
@@ -725,58 +753,18 @@
     down_own = jnp.pad(w_down.astype(BF16), ((0, unit - d_rows), (0, 0)))[None]
     out_own = w_out.astype(BF16)[None]
     qkv_own, gu_own = prep(sizes, unit, w_qkv, w_gate_up, d_rows)
-    x_top, x_middle, qkv_own, gu_own, down_own, out_own, packed = barrier(
+    x_top, x_middle, down_parts, down_other, qkv_own, gu_own, out_own, packed = barrier(
         (
             swap(tokens, "t", n_t // 2),
             swap(tokens, "t", n_t // 4),
+            spread_top(down_own),
+            over_y(down_own),
             qkv_own,
             gu_own,
-            down_own,
             out_own,
             packed,
         )
     )
-
-    gu_own, down_parts, down_other, x_far, cotangent = barrier(
-        (
-            exchange(gu_own),
-            spread_top(down_own),
-            over_y(down_own),
-            swap(x_top, "t", n_t // 4),
-            cotangent,
-        )
-    )
-    cut = n_t // 2
-    gu_first, gu_second = barrier((gu_own[:cut], gu_own[cut:]))
-    gu_parts, gu_other, down_far, dy_top, dy_middle, gu_second, qkv_own = barrier(
-        (
-            spread_top(gu_first),
-            over_y(gu_first),
-            over_y_rest(down_parts),
-            swap(cotangent, "t", n_t // 2),
-            swap(cotangent, "t", n_t // 4),
-            gu_second,
-            qkv_own,
-        )
-    )
-    down_parts = down_parts + [down_other] + down_far
-    x_even = jnp.concatenate([tokens, x_middle, x_top, x_far], axis=0)
-    gu_two, gu_two_other, gu_far, dy_far, x_odd, qkv_own = barrier(
-        (
-            spread_top(gu_second),
-            over_y(gu_second),
-            over_y_rest(gu_parts),
-            swap(dy_top, "t", n_t // 4),
-            swap(x_even, "t", 1),
-            qkv_own,
-        )
-    )
-    dy_even = jnp.concatenate([cotangent, dy_middle, dy_top, dy_far], axis=0)
-    gu_two_far, qkv_own, dy_odd = barrier(
-        (over_y_rest(gu_two), exchange(qkv_own), swap(dy_even, "t", 1))
-    )
-    gu_parts = gu_parts + [gu_other] + gu_far + gu_two + [gu_two_other] + gu_two_far
-
     all_vectors = packed[:, : 5 * vectors.shape[1]].reshape(total, 5, -1)
     all_vectors = all_vectors.transpose(1, 0, 2).reshape(5, width)
     group = packed[:, 5 * vectors.shape[1] : small].reshape(n_a, n_t, n_b, n_y, -1)
@@ -787,14 +775,66 @@
     for dim, step in enumerate((4, 2, 1)):
         group = jnp.where(at_t // step % 2 == 1, jnp.flip(group, dim), group)
     slot_lengths = jnp.round(group.reshape(-1)).astype(jnp.int32)
-    gain_row = all_vectors[0]
     bias = all_vectors[2:5].reshape(3 * n_a, n_t, head_cols)
     bias = lax.dynamic_index_in_dim(bias, at_t, 1, keepdims=False).reshape(1, -1)
+    vec = all_vectors[:2]
+    tables = rotary_lanes(row_count)
+
+    gu_own, down_far, out_parts, out_other, cotangent, vec, bias, slot_lengths, tables = barrier(
+        (
+            exchange(gu_own),
+            over_y_rest(down_parts),
+            spread_top(out_own),
+            over_y(out_own),
+            cotangent,
+            vec,
+            bias,
+            slot_lengths,
+            tables,
+        )
+    )
+    down_parts = down_parts + [down_other] + down_far
+    cut = n_t // 2
+    gu_first, gu_second = barrier((gu_own[:cut], gu_own[cut:]))
+    gu_parts, gu_other, out_far, dy_top, dy_middle, gu_second, qkv_own, x_top = barrier(
+        (
+            spread_top(gu_first),
+            over_y(gu_first),
+            over_y_rest(out_parts),
+            swap(cotangent, "t", n_t // 2),
+            swap(cotangent, "t", n_t // 4),
+            gu_second,
+            qkv_own,
+            x_top,
+        )
+    )
+    out_parts = out_parts + [out_other] + out_far
+    gu_two, gu_two_other, gu_far, x_far, dy_far, qkv_own = barrier(
+        (
+            spread_top(gu_second),
+            over_y(gu_second),
+            over_y_rest(gu_parts),
+            swap(x_top, "t", n_t // 4),
+            swap(dy_top, "t", n_t // 4),
+            qkv_own,
+        )
+    )
+    x_even = jnp.concatenate([tokens, x_middle, x_top, x_far], axis=0)
+    dy_even = jnp.concatenate([cotangent, dy_middle, dy_top, dy_far], axis=0)
+    gu_two_far, qkv_own, x_odd, dy_odd = barrier(
+        (
+            over_y_rest(gu_two),
+            exchange(qkv_own),
+            swap(x_even, "t", 1),
+            swap(dy_even, "t", 1),
+        )
+    )
+    gu_parts = gu_parts + [gu_other] + gu_far + gu_two + [gu_two_other] + gu_two_far
+
 
     top = n_a // 2
     upper = at_a // top % 2
     other_half = jnp.stack([1 - upper, at_y])
-    own_half = jnp.stack([upper, at_y])
     lower_bits = r_bits[1:]
 
     def over_rest(value, parts_shape):
@@ -811,22 +851,32 @@
             summed = keep + swap(send.astype(BF16), name, step).astype(F32)
         return summed.reshape(summed.shape[1], summed.shape[3], summed.shape[4])
 
-    def first_sums(got, kept):
-        shape = (2, 2, row_count, width)
-        both = got.reshape(shape).astype(F32) + kept.reshape(shape).astype(F32)
-        left, right = both[..., :half_width], both[..., half_width:]
-        return [v.astype(BF16) for v in (left[0], left[1], right[:, 0], right[:, 1])]
-
-    def second_sums(left_kept, left_got, right_kept, right_got):
-        sums = []
-        for kept, got in ((left_kept, left_got), (right_kept, right_got)):
-            both = (kept.astype(F32) + got.astype(F32)).astype(BF16)
-            sums += [both[0], both[1]]
-        return sums
-
-    def third_sums(left_kept, left_got, right_kept, right_got):
-        left = left_kept.astype(F32) + left_got.astype(F32)
-        return jnp.concatenate([left, right_kept.astype(F32) + right_got.astype(F32)], axis=1)
+    def piece(raw, middle_bit, top_bit, left):
+        columns = slice(0, half_width) if left else slice(half_width, width)
+        got, kept = (part.reshape(2, 2, row_count, width) for part in raw)
+        spot = (middle_bit, top_bit, slice(None), columns)
+        return got[spot].astype(F32) + kept[spot].astype(F32)
+
+    every = slice(None)
+
+    def first_sends(raw):
+        return piece(raw, 1, every, True).astype(BF16), piece(raw, every, 1, False).astype(BF16)
+
+    def first_swaps(sends):
+        return swap(sends[0], "t", n_t // 4), swap(sends[1], "t", n_t // 2)
+
+    def second_sends(raw, got):
+        left = piece(raw, 0, 1, True) + got[0][1].astype(F32)
+        right = piece(raw, 1, 0, False) + got[1][1].astype(F32)
+        return left.astype(BF16), right.astype(BF16)
+
+    def second_swaps(sends):
+        return swap(sends[0], "t", n_t // 2), swap(sends[1], "t", n_t // 4)
+
+    def whole_rows(raw, got, last):
+        left = piece(raw, 0, 0, True) + got[0][0].astype(F32) + last[0].astype(F32)
+        right = piece(raw, 0, 0, False) + got[1][0].astype(F32) + last[1].astype(F32)
+        return jnp.concatenate([left, right], axis=1)
 
     half_width = width // 2
     shape_w = (top, n_t, n_b, w_rows)
@@ -834,18 +884,16 @@
         after(here, qkv_own),
         masks,
         (x_even, x_odd, dy_even, dy_odd),
-        all_vectors[:2],
+        vec,
         gu_parts,
         down_parts,
         sizes,
         unit,
     )
-    qkv_parts, qkv_other, out_parts, out_other, normed, dy, hidden, d_joined = barrier(
+    qkv_parts, qkv_other, normed, dy, hidden, d_joined = barrier(
         (
             spread_top(qkv_own),
             over_y(qkv_own),
-            spread_top(out_own),
-            over_y(out_own),
             normed,
             dy,
             hidden,
@@ -853,28 +901,28 @@
         )
     )
 
-    qkv_far, out_far = over_y_rest(qkv_parts), over_y_rest(out_parts)
+    qkv_far = over_y_rest(qkv_parts)
     down_far_sent, down_far_kept, down_sent, down_kept = grads_rows(
         other_half, hidden, dy, "grads_down"
     )
-    gu_far_sent, gu_far_kept = grads_cols(
-        after(other_half, down_kept), normed, d_joined, "grads_gate_up_far"
+    qkv_far, down_far_sent, down_sent, down_kept = barrier(
+        (qkv_far, down_far_sent, down_sent, down_kept)
     )
     down_far_got = over_y(down_far_sent)
-    gu_sent, gu_kept = grads_cols(
-        after(own_half, gu_far_kept), normed, d_joined, "grads_gate_up_near"
-    )
-    qkv_far, out_far, down_far_got, gu_far_sent, down_sent, gu_sent, gu_kept = barrier(
-        (qkv_far, out_far, down_far_got, gu_far_sent, down_sent, gu_sent, gu_kept)
+    gu_far_sent, gu_far_kept, gu_sent, gu_kept = grads_cols(
+        after(other_half, down_kept), normed, d_joined, "grads_gate_up"
+    )
+    down_far_got, gu_far_sent, down_sent, gu_sent, gu_kept = barrier(
+        (down_far_got, gu_far_sent, down_sent, gu_sent, gu_kept)
     )
     qkv_parts = qkv_parts + [qkv_other] + qkv_far
-    out_parts = out_parts + [out_other] + out_far
 
     down_far = barrier(summed(down_far_kept, down_far_got).astype(BF16))
     attended, d_qkv, bias_sums = attention(
         after(here, down_far),
         masks,
         slot_lengths,
+        tables,
         normed,
         dy,
         bias,
@@ -894,28 +942,18 @@
         )
     )
 
-    def quarters(value):
+    def thirds(value):
         value = value.reshape(value.shape[0] // (n_b * w_rows), n_b * w_rows, -1)
-        part = value.shape[1] // 4
-        return [value[:, n * part : (n + 1) * part] for n in range(4)]
-
-    gu_far = [summed(k, g).astype(BF16) for k, g in zip(quarters(gu_far_kept), quarters(gu_far_got))]
+        cuts = [n * value.shape[1] // 8 for n in (0, 3, 6, 8)]
+        return [value[:, low:high] for low, high in zip(cuts, cuts[1:])]
+
+    gu_far = [summed(k, g).astype(BF16) for k, g in zip(thirds(gu_far_kept), thirds(gu_far_got))]
     gu_far = barrier(gu_far)
-    qo_sent, qo_kept = grads_attention(after(other_half, *gu_far), normed, d_qkv, attended, dy)
-    gu_far_one, gu_got, gu_far, qo_far_sent, qo_sent = barrier(
-        (
-            over_top(gu_far[0]),
-            over_y(gu_sent[0]),
-            gu_far,
-            (qo_sent[0, :2], qo_sent[0, 2:]),
-            qo_sent[1],
-        )
-    )
-
-    branch_rows = functools.partial(
-        row_blocks,
+    branch_sent, branch_kept = row_blocks(
         functools.partial(branch_kernel, masks),
         "branch_rows",
+        after(here, *gu_far),
+        None,
         inputs=(attended, hidden),
         parts=out_parts + down_parts,
         scratch=[
@@ -926,22 +964,31 @@
         width=width,
         n_t=n_t,
     )
-    branch_sent = branch_rows(after(here, *qo_far_sent), False)
-    gu_far_two, qo_far_got, branch_sent, gu_far, qo_far_sent = barrier(
-        (over_top(gu_far[1]), over_y(qo_far_sent[0]), branch_sent, gu_far, qo_far_sent[1])
-    )
-    branch_kept = branch_rows(after(here, branch_sent), True)
-    gu_far_three, branch_got, qo_far_more, branch_kept, gu_far = barrier(
+    gu_far_one, gu_got, gu_far, branch_sent, branch_kept, gu_sent = barrier(
         (
-            over_top(gu_far[2]),
+            over_top(gu_far[0]),
+            over_y(gu_sent[0]),
+            gu_far,
+            branch_sent,
+            branch_kept,
+            gu_sent[1],
+        )
+    )
+
+    qo_sent, qo_kept = grads_attention(
+        after(other_half, branch_sent), normed, d_qkv, attended, dy
+    )
+    gu_far_two, branch_got, gu_got_more, gu_far, qo_far_sent, qo_sent = barrier(
+        (
+            over_top(gu_far[1]),
             swap(branch_sent, "t", 1),
-            over_y(qo_far_sent),
-            branch_kept,
+            over_y(gu_sent),
             gu_far,
-        )
-    )
-
-    branch = barrier(first_sums(branch_got, branch_kept))
+            qo_sent[0],
+            qo_sent[1],
+        )
+    )
+
     normal_rows = functools.partial(
         row_blocks,
         functools.partial(normal_kernel, masks),
@@ -956,63 +1003,58 @@
         width=width,
         n_t=n_t,
     )
-    normal_sent = normal_rows(after(here, *branch), False)
-    branch_got = [swap(branch[1], "t", 2), swap(branch[3], "t", 4)]
-    qo_far_got = jnp.concatenate([qo_far_got, qo_far_more], axis=0)
-    qo_far = summed(qo_kept[0], qo_far_got).astype(BF16)
-    qo_far = (qo_far[:2], qo_far[2:])
-    gu_far_four, gu_got_more, branch_got, normal_sent, qo_far, qo_sent, down_sent = barrier(
+    branch = (branch_got, branch_kept)
+    branch_sends = barrier(first_sends(branch))
+    (normal_sent,) = normal_rows(after(here, qo_far_sent, *branch_sends), 0)
+    gu_far_three, qo_far_got, branch_got, normal_sent, qo_sent, down_sent = barrier(
         (
-            over_top(gu_far[3]),
-            over_y(gu_sent[1]),
-            branch_got,
+            over_top(gu_far[2]),
+            over_y(qo_far_sent),
+            first_swaps(branch_sends),
             normal_sent,
-            qo_far,
             qo_sent,
             down_sent,
         )
     )
+    qo_far = summed(qo_kept[0], qo_far_got).astype(BF16)
     gu_got = jnp.concatenate([gu_got, gu_got_more], axis=0)
-    gu_far_got = jnp.concatenate([gu_far_one, gu_far_two, gu_far_three, gu_far_four], axis=1)
+    gu_far_got = jnp.concatenate([gu_far_one, gu_far_two, gu_far_three], axis=1)
     g_gu = summed(gu_kept, gu_got, gu_far_got.reshape(gu_kept.shape))
     g_gu = over_rest(g_gu, shape_w).astype(BF16)
-    g_gu, qo_far = barrier((g_gu, qo_far))
-    normal_kept = normal_rows(after(here, normal_sent, g_gu), True)
-    qo_far_got, down_sent, normal_got, g_gu, normal_kept, qo_far, qo_got = barrier(
+    qo_far_one, qo_far_two, g_gu = barrier((qo_far[:1], qo_far[1:], g_gu))
+    (normal_kept,) = normal_rows(after(here, normal_sent, g_gu), 1)
+    qo_far_one, normal_got, qo_got, g_gu, normal_kept, qo_far_two, down_sent, branch_got = barrier(
         (
-            over_top(qo_far[0]),
-            down_sent,
+            over_top(qo_far_one),
             swap(normal_sent, "t", 1),
+            over_y(qo_sent),
             exchange(g_gu),
             normal_kept,
-            qo_far[1],
-            over_y(qo_sent),
-        )
-    )
-
-    qo_far_more, down_got = over_top(qo_far), over_y(down_sent)
-    normal = barrier(first_sums(normal_got, normal_kept))
-    normal_got = [swap(normal[1], "t", 2), swap(normal[3], "t", 4)]
-    branch = second_sums(branch[0], branch_got[0], branch[2], branch_got[1])
-    branch = [after(part, *normal) for part in branch]
+            qo_far_two,
+            down_sent,
+            branch_got,
+        )
+    )
+
+    qo_far_two, down_got = over_top(qo_far_two), over_y(down_sent)
+    normal = (normal_got, normal_kept)
+    normal_sends = barrier(first_sends(normal))
     new_gu, moment_gu, square_gu = finish(
         functools.partial(finish_gu_kernel, sizes, d_rows, unit),
         "finish_gate_up",
-        after(g_gu, *branch),
+        after(g_gu, *normal_sends),
         w_gate_up,
         first_gate_up,
         second_gate_up,
     )
-    normal_got, qo_far_more, down_got, branch, new_gu = barrier(
-        (normal_got, qo_far_more, down_got, branch, new_gu)
-    )
-
-    normal = barrier(second_sums(normal[0], normal_got[0], normal[2], normal_got[1]))
-    normal_got = [swap(normal[1], "t", 4), swap(normal[3], "t", 2)]
-    branch = barrier([after(part, *normal) for part in branch])
-    branch_got = [swap(branch[1], "t", 4), swap(branch[3], "t", 2)]
-    qo_far_got = jnp.concatenate([qo_far_got, qo_far_more], axis=0)
-    qo = after(summed(qo_kept[1], qo_got, qo_far_got), *normal)
+    branch_sends = second_sends(branch, [after(got, *normal_sends) for got in branch_got])
+    normal_got, qo_far_two, down_got, branch_sends, new_gu = barrier(
+        (first_swaps(normal_sends), qo_far_two, down_got, branch_sends, new_gu)
+    )
+
+    normal_sends = barrier(second_sends(normal, normal_got))
+    qo_far_got = jnp.concatenate([qo_far_one, qo_far_two], axis=0)
+    qo = after(summed(qo_kept[1], qo_got, qo_far_got), *normal_sends)
     g_qkv = over_rest(qo[:-1].transpose(1, 0, 2).reshape(qo.shape[1], -1), shape_w)
     g_out = qo[-1].reshape(half_width // LANES, -1, LANES).transpose(1, 0, 2)
     g_out = over_rest(g_out.reshape(-1, half_width), (top, 1, n_b, w_rows))
@@ -1021,12 +1063,13 @@
     g_down = summed(down_kept, down_got, down_far_got)
     g_down = over_rest(after(g_down, g_qkv), (top, 1, n_b, unit))
     new_down, moment_down, square_down = adam(w_down, g_down[0, :d_rows], first_down, second_down)
-    g_qkv, normal_got, g_out, branch_got, new_down = barrier(
-        (exchange(g_qkv), normal_got, g_out, branch_got, new_down)
-    )
-    normal_own = third_sums(normal[0], normal_got[0], normal[2], normal_got[1])
-    _, scaled_own, inv_own = normalize(tokens.astype(F32), gain_row, all_vectors[1])
-    d_scaled = normal_own * gain_row
+    g_qkv, normal_last, g_out, branch_sends, new_down = barrier(
+        (exchange(g_qkv), second_swaps(normal_sends), g_out, branch_sends, new_down)
+    )
+    branch_last = second_swaps(branch_sends)
+    normal_own = whole_rows(normal, normal_got, normal_last)
+    _, scaled_own, inv_own = normalize(tokens.astype(F32), vec[0], vec[1])
+    d_scaled = normal_own * vec[0]
     input_grad = cotangent.astype(F32) + inv_own * (
         d_scaled
         - jnp.mean(d_scaled, axis=-1, keepdims=True)
@@ -1047,7 +1090,7 @@
     vector_part = jnp.pad(vector_part, ((0, 0), (0, 0), (0, -vector_part.shape[2] % 128)))
     vector_part = lax.all_to_all(vector_part, AXES, split_axis=0, concat_axis=0, tiled=True)
     vector_grad = jnp.sum(vector_part, axis=0)[0, : vectors.size].reshape(vectors.shape)
-    branch_own = third_sums(branch[0], branch_got[0], branch[2], branch_got[1])
+    branch_own = whole_rows(branch, branch_got, branch_last)
     output = (tokens.astype(F32) + after(branch_own, vector_part)).astype(BF16)
     new_out, moment_out, square_out = adam(w_out, g_out[0], first_out, second_out)
     new_qkv, moment_qkv, square_qkv = finish(

time: 588 us -> 570 us (0.969)
  local copies, waits for them, and re-layouts: 56.6 us -> 39.3 us
  Pallas kernels: 205 us -> 195 us
  starting transfers between devices: 74.1 us -> 80.3 us
    all_to_all x1, waiting for transfers between devices: 11.6 us -> 27 us  [per_device(): lax.all_to_all(packed, AXES, split_axis=0, concat_axis=0, tiled=True)]
    ppermute x48 -> x46, waiting for transfers between devices: 184 us -> 173 us  [swap(): return lax.ppermute(value, AXES, [(i, i ^ mask) for i in range(total)])]
    convert_element_type x4 -> x6, other arithmetic: 1.61 us -> 12.3 us  [the longest x2 7.02 us: second_sends(): return (left.astype(BF16), right.astype(BF16))]
    another operation x2 -> x0, other arithmetic: 10.4 us -> none
    ppermute x48 -> x46, starting transfers between devices: 49.4 us -> 55.5 us  [swap(): return lax.ppermute(value, AXES, [(i, i ^ mask) for i in range(total)])]
    pallas_call x4 -> x3, Pallas kernels: 55.9 us -> 51.8 us  [row_blocks(): pl.pallas_call(kernel, grid_spec=pltpu.PrefetchScalarGridSpec(num_scalar_...]
    pallas_call x2 -> x1, Pallas kernels: 24.4 us -> 21 us  [grads_cols(): pl.pallas_call(grads_cols_kernel, grid_spec=pltpu.PrefetchScalarGridSpec(...]
    unnamed x135 -> x111, local copies, waits for them, and re-layouts: 15.7 us -> 18.3 us
  transfers between devices with their start and end apart: 54 -> 52, of which waited for: 20 -> 24; matrix products, arithmetic and copies ran while one was open for 11% -> 10% of each run, Pallas kernels for 35% -> 35%
where the time goes in v3:
time: 570 us; the launch traced here: 564 us
  waiting for transfers between devices  200 us (35%)
  Pallas kernels  195 us (34%)
  starting transfers between devices  80.3 us (14%)
  other arithmetic  48 us (8%)
  local copies, waits for them, and re-layouts  39.3 us (7%)
    ppermute x46, waiting for transfers between devices, swap(): return lax.ppermute(value, AXES, [(i, i ^ mask) for i in range(total)])  173 us
    ppermute x46, starting transfers between devices, swap(): return lax.ppermute(value, AXES, [(i, i ^ mask) for i in range(total)])  55.5 us
    pallas_call x3, Pallas kernels, row_blocks(): pl.pallas_call(kernel, grid_spec=pltpu.PrefetchScalarGridSpec(num_scalar_...  51.8 us
    pallas_call x1, Pallas kernels, attention(): pl.pallas_call(functools.partial(attention_kernel, masks), grid_spec=pltp...  33.6 us
    pallas_call x1, Pallas kernels, mlp(): pl.pallas_call(functools.partial(mlp_kernel, masks, n_t), grid_spec=pltpu...  33.4 us
    all_to_all x1, waiting for transfers between devices, per_device(): lax.all_to_all(packed, AXES, split_axis=0, concat_axis=0, tiled=True)  27 us
    pallas_call x1, Pallas kernels, grads_cols(): pl.pallas_call(grads_cols_kernel, grid_spec=pltpu.PrefetchScalarGridSpec(...  21 us
    pallas_call x1, Pallas kernels, grads_attention(): pl.pallas_call(grads_attention_kernel, grid_spec=pltpu.PrefetchScalarGrid...  18.9 us
  transfers between devices with their start and end apart: 52, of which 24 were waited for; matrix products, arithmetic and copies ran while one was open for 10% of the time, Pallas kernels for 35%

profile of v3, /device:TPU:0, one launch (start us, length us, event | category | flops | bytes accessed | tf_op | source)
XLA Modules:
  0.0 564.3 jit_solution(10027333535539352798)
XLA Ops:
  0.7 3.1 collective-permute-start
  6.8 2.7 collective-permute-start.2
  11.9 2.6 all-to-all-start
  15.2 6.7 %prep.1 = (bf16[8,128,384]{2,1,0:T(8,128)(2,1)}, bf16[8,128,768]{2,1,0:T(8,128)(2,1)}) custom-call(f32[128,3072]{1,0:T(8,128)} %w.3, f32[128,5632]{1,0:T(8,128)} %w.2), custom_call_target="tpu_custom_call" | custom-call | bytes 14417920 | tf_op jit(solution)/shard_map/prep/pallas_call | solution.py:157
  21.9 27.0 %all-to-all-done = f32[32,1,384]{2,1,0:T(1,128)S(1)} async-done(((f32[32,1,384]{2,1,0:T(1,128)}), f32[32,1,384]{2,1,0:T(1,128)S(1)}, u32[]{:S(2)}, u32[]{:S(2)}) %all-to-all-start) | async-done | bytes 49184 | tf_op jit(solution)/shard_map/all_to_all | solution.py:731
  49.9 3.6 all-to-all-start.1
  65.1 11.9 %collective-permute-done.5.rest_5_.rest_1_ = bf16[1,128,1024]{2,1,0:T(8,128)(2,1)} collective-permute-done((bf16[1,128,1024]{2,1,0:T(8,128)(2,1)}, bf16[1,128,1024]{2,1,0:T(8,128)(2,1)}, u32[]{:S(2)}, u32[]{:S(2)}) %collective-permute-start.5) | collective-permute-done | bytes 262176 | tf_op jit(solution)/shard_map/ppermute | solution.py:707
  77.1 5.4 collective-permute-done.4.rest_11_.rest_7_
  85.8 2.7 collective-permute-start.7
  91.6 20.1 %collective-permute-done.9.rest_7_.rest_3_ = bf16[1,128,1024]{2,1,0:T(8,128)(2,1)S(1)} collective-permute-done((bf16[1,128,1024]{2,1,0:T(8,128)(2,1)}, bf16[1,128,1024]{2,1,0:T(8,128)(2,1)S(1)}, u32[]{:S(2)}, u32[]{:S(2)}) %collective-permute-start.9) | collective-permute-done | bytes 262176 | tf_op jit(solution)/shard_map/ppermute | solution.py:707
  111.7 11.1 %collective-permute-done.7.rest_1_.rest_5_ = bf16[4,128,768]{2,1,0:T(8,128)(2,1)S(1)} collective-permute-done((bf16[4,128,768]{2,1,0:T(8,128)(2,1)S(1)}, bf16[4,128,768]{2,1,0:T(8,128)(2,1)S(1)}, u32[]{:S(2)}, u32[]{:S(2)}) %collective-permute-start.7) | collective-permute-done | bytes 786464 | tf_op jit(solution)/shard_map/ppermute | solution.py:707
  125.9 2.3 constant_dynamic-update-slice_fusion.2
  128.2 2.4 collective-permute-start.12
  138.3 24.9 %collective-permute-done.12.rest_5_.rest_9_ = bf16[4,128,768]{2,1,0:T(8,128)(2,1)S(1)} collective-permute-done((bf16[4,128,768]{2,1,0:T(8,128)(2,1)S(1)}, bf16[4,128,768]{2,1,0:T(8,128)(2,1)S(1)}, u32[]{:S(2)}, u32[]{:S(2)}) %collective-permute-start.12) | collective-permute-done | bytes 786464 | tf_op jit(solution)/shard_map/ppermute | solution.py:707
  164.2 5.7 %collective-permute-done.16 = bf16[256,2048]{1,0:T(8,128)(2,1)S(1)} collective-permute-done((bf16[256,2048]{1,0:T(8,128)(2,1)S(1)}, bf16[256,2048]{1,0:T(8,128)(2,1)S(1)}, u32[]{:S(2)}, u32[]{:S(2)}) %collective-permute-start.16) | collective-permute-done | bytes 1048608 | tf_op jit(solution)/shard_map/ppermute | solution.py:707
  172.6 5.1 all-to-all-start.2
  178.2 19.5 %collective-permute-done.17.rest_7_.rest_11_ = bf16[4,128,768]{2,1,0:T(8,128)(2,1)S(1)} collective-permute-done((bf16[4,128,768]{2,1,0:T(8,128)(2,1)S(1)}, bf16[4,128,768]{2,1,0:T(8,128)(2,1)S(1)}, u32[]{:S(2)}, u32[]{:S(2)}) %collective-permute-start.17) | collective-permute-done | bytes 786464 | tf_op jit(solution)/shard_map/ppermute | solution.py:707
  200.8 33.4 %mlp.1 = (bf16[2048,2048]{1,0:T(8,128)(2,1)}, bf16[2048,2048]{1,0:T(8,128)(2,1)}, bf16[2048,768]{1,0:T(8,128)(2,1)}, bf16[2,2048,768]{2,1,0:T(8,128)(2,1)}) custom-call(s32[4]{0:T(128)} %pad_add_fusion.1.here, f32[2,2048]{1,0:T(2,128)} %slice.184.vec, bf16[1024,2048]{1,0:T(8,128)(2,1)} %constant_dynamic-update-slice_fusion.x_even, ...), custom_call_target="tpu_custom_call" | custom-call | tf_op jit(solution)/shard_map/mlp/pallas_call | solution.py:295
  237.4 11.5 %grads_down.1 = (bf16[384,1024]{1,0:T(8,128)(2,1)}, f32[384,1024]{1,0:T(8,128)}, bf16[384,1024]{1,0:T(8,128)(2,1)}, f32[384,1024]{1,0:T(8,128)}) custom-call(s32[2]{0:T(128)} %pad_add_fusion.where, bf16[2048,768]{1,0:T(8,128)(2,1)} %get-tuple-element.221.far.near.hidden, bf16[2048,768]{1,0:T(8,128)(2,1)} %get-tuple-element.221.far.near.hidden, ...), custom_call_target="tpu_custom_call" | custom-call | flops 6442450944 | bytes 16252928 | tf_op jit(solution)/shard_map/grads_down/pallas_call | solution.py:511
  248.9 5.5 collective-permute-done.22.rest_3_
  255.4 21.0 %grads_gate_up.1 = (bf16[1024,768]{1,0:T(8,128)(2,1)}, f32[1024,768]{1,0:T(8,128)}, bf16[1024,768]{1,0:T(8,128)(2,1)}, f32[1024,768]{1,0:T(8,128)}) custom-call(s32[2]{0:T(128)} %pad_add_fusion.where, bf16[2048,2048]{1,0:T(8,128)(2,1)} %get-tuple-element.228.left.normed.tall, bf16[2,2048,768]{2,1,0:T(8,128)(2,1)} %get-tuple-element.229.d_sent.d_kept.d_joined, ...), custom_call_target="tpu_custom_call" | custom-call | tf_op jit(solution)/shard_map/grads_gate_up/pallas_call | solution.py:478
  279.4 33.6 %attention.1 = (bf16[2048,256]{1,0:T(8,128)(2,1)}, bf16[2048,768]{1,0:T(8,128)(2,1)}, f32[8,1,768]{2,1,0:T(1,128)}) custom-call(s32[4]{0:T(128)} %pad_add_fusion.1.here, s32[8]{0:T(128)} %convert_element_type.294.lengths, bf16[2048,2048]{1,0:T(8,128)(2,1)} %get-tuple-element.228.left.normed.tall, bf16[2048,2048]{1,0:T(8,128)(2,1)} %get-tuple-element.222.dy_sent.dy_kept.dy, ...), custom_call_target="tpu_custom_call" | custom-call | flops 12884901888 | bytes 41943040 | tf_op jit(solution)/shard_map/attention/pallas_call | solution.py:407
  318.6 16.8 %branch_rows.1 = (bf16[1024,2048]{1,0:T(8,128)(2,1)}, bf16[1024,2048]{1,0:T(8,128)(2,1)}) custom-call(s32[4]{0:T(128)} %pad_add_fusion.1.here, bf16[2048,256]{1,0:T(8,128)(2,1)} %get-tuple-element.261.o.left, bf16[2048,768]{1,0:T(8,128)(2,1)} %get-tuple-element.221.far.near.hidden, bf16[1,128,1024]{2,1,0:T(8,128)(2,1)} %convert_bitcast_fusion.rest_4_.rest_0_, ...), custom_call_target="tpu_custom_call" | custom-call | tf_op jit(solution)/shard_map/branch_rows/pallas_call | solution.py:606
  335.4 9.6 %collective-permute-done.26 = bf16[8,48,768]{2,1,0:T(8,128)(2,1)S(1)} collective-permute-done((bf16[8,48,768]{2,1,0:T(8,128)(2,1)}, bf16[8,48,768]{2,1,0:T(8,128)(2,1)S(1)}, u32[]{:S(2)}, u32[]{:S(2)}) %collective-permute-start.26) | collective-permute-done | bytes 589856 | tf_op jit(solution)/shard_map/ppermute | solution.py:707
  346.7 18.9 %grads_attention.1 = (bf16[2,4,1024,128]{3,2,1,0:T(8,128)(2,1)}, f32[2,4,1024,128]{3,2,1,0:T(8,128)}) custom-call(s32[2]{0:T(128)} %pad_add_fusion.where, bf16[2048,2048]{1,0:T(8,128)(2,1)} %get-tuple-element.228.left.normed.tall, bf16[2048,768]{1,0:T(8,128)(2,1)} %get-tuple-element.270.d_qkv, bf16[2048,256]{1,0:T(8,128)(2,1)} %get-tuple-element.261.o.left, ...), custom_call_target="tpu_custom_call" | custom-call | tf_op jit(solution)/shard_map/grads_attention/pallas_call | solution.py:565
  365.5 3.2 slice_bitcast_fusion.1
  368.7 5.7 %collective-permute-done.28 = bf16[8,48,768]{2,1,0:T(8,128)(2,1)S(1)} collective-permute-done((bf16[8,48,768]{2,1,0:T(8,128)(2,1)}, bf16[8,48,768]{2,1,0:T(8,128)(2,1)S(1)}, u32[]{:S(2)}, u32[]{:S(2)}) %collective-permute-start.28) | collective-permute-done | bytes 589856 | tf_op jit(solution)/shard_map/ppermute | solution.py:707
  378.8 2.9 collective-permute-start.31
  381.7 17.5 %normal_rows_sent.1 = bf16[1024,2048]{1,0:T(8,128)(2,1)} custom-call(s32[4]{0:T(128)} %pad_add_fusion.1.here, bf16[2048,768]{1,0:T(8,128)(2,1)} %get-tuple-element.270.d_qkv, bf16[2,2048,768]{2,1,0:T(8,128)(2,1)} %get-tuple-element.229.d_sent.d_kept.d_joined, bf16[8,128,384]{2,1,0:T(8,128)(2,1)} %copy-done.9, bf16[8,128,384]{2,1,0:T(8,128)(2,1)} %copy-done.19, ...), custom_call_target="tpu_custom_call" | custom-call | tf_op jit(solution)/shard_map/normal_rows_sent/pallas_call | solution.py:606
  399.2 9.7 %collective-permute-done.31 = bf16[8,32,768]{2,1,0:T(8,128)(2,1)S(1)} collective-permute-done((bf16[8,32,768]{2,1,0:T(8,128)(2,1)}, bf16[8,32,768]{2,1,0:T(8,128)(2,1)S(1)}, u32[]{:S(2)}, u32[]{:S(2)}) %collective-permute-start.31) | collective-permute-done | bytes 393248 | tf_op jit(solution)/shard_map/ppermute | solution.py:707
  415.3 2.9 fusion
  418.2 4.5 all-to-all-start.3
  425.2 17.5 %normal_rows_kept.1 = bf16[1024,2048]{1,0:T(8,128)(2,1)} custom-call(s32[4]{0:T(128)} %pad_add_fusion.1.here, bf16[2048,768]{1,0:T(8,128)(2,1)} %get-tuple-element.270.d_qkv, bf16[2,2048,768]{2,1,0:T(8,128)(2,1)} %get-tuple-element.229.d_sent.d_kept.d_joined, bf16[8,128,384]{2,1,0:T(8,128)(2,1)} %copy-done.9, bf16[8,128,384]{2,1,0:T(8,128)(2,1)} %copy-done.19, ...), custom_call_target="tpu_custom_call" | custom-call | tf_op jit(solution)/shard_map/normal_rows_kept/pallas_call | solution.py:606
  442.7 3.7 collective-permute-done.35
  448.6 2.5 fusion.22
  459.4 10.3 %finish_gate_up.1 = (f32[128,5632]{1,0:T(8,128)}, f32[128,5632]{1,0:T(8,128)}, f32[128,5632]{1,0:T(8,128)}) custom-call(bf16[8,128,768]{2,1,0:T(8,128)(2,1)} %copy-done.11, f32[128,5632]{1,0:T(8,128)} %w.2, f32[128,5632]{1,0:T(8,128)} %m.2, f32[128,5632]{1,0:T(8,128)} %v.2), custom_call_target="tpu_custom_call" | custom-call | flops 14417920 | bytes 18743296 | tf_op jit(solution)/shard_map/finish_gate_up/pallas_call | solution.py:215
  469.8 3.5 fusion.28
  473.2 21.9 %collective-permute-done.40 = bf16[3,1024,128]{2,1,0:T(8,128)(2,1)S(1)} collective-permute-done((bf16[3,1024,128]{2,1,0:T(8,128)(2,1)S(1)}, bf16[3,1024,128]{2,1,0:T(8,128)(2,1)S(1)}, u32[]{:S(2)}, u32[]{:S(2)}) %collective-permute-start.40) | collective-permute-done | bytes 786464 | tf_op jit(solution)/shard_map/ppermute | solution.py:707
  495.8 3.6 fusion.26
  503.4 4.1 all-to-all-start.4
  516.4 5.1 multiply_subtract_fusion
  521.4 9.0 %collective-permute-done.42 = bf16[256,1024]{1,0:T(8,128)(2,1)} collective-permute-done((bf16[256,1024]{1,0:T(8,128)(2,1)}, bf16[256,1024]{1,0:T(8,128)(2,1)}, u32[]{:S(2)}, u32[]{:S(2)}) %collective-permute-start.42) | collective-permute-done | bytes 524320 | tf_op jit(solution)/shard_map/ppermute | solution.py:707
  531.3 3.0 fusion.24
  536.3 4.9 all-to-all-start.5
  544.6 2.9 multiply_subtract_fusion.1
  547.6 7.5 %finish_qkv.1 = (f32[128,3072]{1,0:T(8,128)}, f32[128,3072]{1,0:T(8,128)}, f32[128,3072]{1,0:T(8,128)}) custom-call(bf16[8,3,128,128]{3,2,1,0:T(8,128)(2,1)} %copy-done.26, f32[128,3072]{1,0:T(8,128)} %w.3, f32[128,3072]{1,0:T(8,128)} %m.3, f32[128,3072]{1,0:T(8,128)} %v.3), custom_call_target="tpu_custom_call" | custom-call | flops 7864320 | bytes 10223616 | tf_op jit(solution)/shard_map/finish_qkv/pallas_call | solution.py:215
  557.5 3.0 fusion.30
  561.7 2.4 fusion.11
  (271 shorter events, 104.4 us)
Async XLA Ops:
  0.7 48.2 %collective-permute-start = (bf16[256,2048]{1,0:T(8,128)(2,1)}, bf16[256,2048]{1,0:T(8,128)(2,1)}, u32[]{:S(2)}, u32[]{:S(2)}) collective-permute-start(bf16[256,2048]{1,0:T(8,128)(2,1)} %param.18), channel_id=1, source_target_pairs={{0,8},{1,9},{2,10},{3,11},{4,12},{5,13},{6,14},{7,15},{8,0},{9,1},... | collective-permute-start | bytes 3145736 | tf_op jit(solution)/shard_map/ppermute | solution.py:707
  3.8 45.1 %collective-permute-start.1 = (bf16[256,2048]{1,0:T(8,128)(2,1)}, bf16[256,2048]{1,0:T(8,128)(2,1)}, u32[]{:S(2)}, u32[]{:S(2)}) collective-permute-start(bf16[256,2048]{1,0:T(8,128)(2,1)} %param.18), channel_id=1, source_target_pairs={{0,4},{1,5},{2,6},{3,7},{4,0},{5,1},{6,2},{7,3},{8,12},{9,13},{10,... | collective-permute-start | bytes 3145736 | tf_op jit(solution)/shard_map/ppermute | solution.py:707
  6.8 42.0 %collective-permute-start.2 = (bf16[1,384,1024]{2,1,0:T(8,128)(2,1)S(1)}, bf16[1,384,1024]{2,1,0:T(8,128)(2,1)S(1)}, u32[]{:S(2)}, u32[]{:S(2)}) collective-permute-start(bf16[1,384,1024]{2,1,0:T(8,128)(2,1)S(1)} %pad_bitcast_fusion.rest_8_.rest_4_), channel_id=1, source_target_pairs={{0,16},{1,17},{2,18},{3,19},{4,20},{5,21},{6,22},{7,23},{8,24},{9,... | collective-permute-start | bytes 2359304 | tf_op jit(solution)/shard_map/ppermute | solution.py:707
  9.5 39.4 %collective-permute-start.3 = (bf16[1,384,1024]{2,1,0:T(8,128)(2,1)S(1)}, bf16[1,384,1024]{2,1,0:T(8,128)(2,1)S(1)}, u32[]{:S(2)}, u32[]{:S(2)}) collective-permute-start(bf16[1,384,1024]{2,1,0:T(8,128)(2,1)S(1)} %pad_bitcast_fusion.rest_8_.rest_4_), channel_id=1, source_target_pairs={{0,1},{1,0},{2,3},{3,2},{4,5},{5,4},{6,7},{7,6},{8,9},{9,8},{10,11... | collective-permute-start | bytes 2359304 | tf_op jit(solution)/shard_map/ppermute | solution.py:707
  11.9 36.9 %all-to-all-start = ((f32[32,1,384]{2,1,0:T(1,128)}), f32[32,1,384]{2,1,0:T(1,128)S(1)}, u32[]{:S(2)}, u32[]{:S(2)}) async-start(f32[32,1,384]{2,1,0:T(1,128)} %broadcast_in_dim.60), calls=%async_computation | async-start | bytes 98304 | tf_op jit(solution)/shard_map/all_to_all | solution.py:731
  49.9 32.6 %all-to-all-start.1 = ((bf16[8,128,768]{2,1,0:T(8,128)(2,1)}), bf16[8,128,768]{2,1,0:T(8,128)(2,1)S(1)}, u32[]{:S(2)}, u32[]{:S(2)}) async-start(bf16[8,128,768]{2,1,0:T(8,128)(2,1)} %get-tuple-element.180), calls=%async_computation.1 | async-start | bytes 3145728 | tf_op jit(solution)/shard_map/all_to_all | solution.py:710
  56.7 20.3 %collective-permute-start.5 = (bf16[1,128,1024]{2,1,0:T(8,128)(2,1)}, bf16[1,128,1024]{2,1,0:T(8,128)(2,1)}, u32[]{:S(2)}, u32[]{:S(2)}) collective-permute-start(bf16[1,128,1024]{2,1,0:T(8,128)(2,1)} %convert_bitcast_fusion.rest_4_.rest_0_), channel_id=1, source_target_pairs={{0,16},{1,17},{2,18},{3,19},{4,20},{5,21},{6,22},{7,23},{8,24},{9,... | collective-permute-start | bytes 786440 | tf_op jit(solution)/shard_map/ppermute | solution.py:707
  57.0 20.1 %collective-permute-start.6 = (bf16[1,128,1024]{2,1,0:T(8,128)(2,1)}, bf16[1,128,1024]{2,1,0:T(8,128)(2,1)}, u32[]{:S(2)}, u32[]{:S(2)}) collective-permute-start(bf16[1,128,1024]{2,1,0:T(8,128)(2,1)} %convert_bitcast_fusion.rest_4_.rest_0_), channel_id=1, source_target_pairs={{0,1},{1,0},{2,3},{3,2},{4,5},{5,4},{6,7},{7,6},{8,9},{9,8},{10,11... | collective-permute-start | bytes 786440 | tf_op jit(solution)/shard_map/ppermute | solution.py:707
  58.0 24.5 %collective-permute-start.4 = (bf16[1,384,1024]{2,1,0:T(8,128)(2,1)S(1)}, bf16[1,384,1024]{2,1,0:T(8,128)(2,1)}, u32[]{:S(2)}, u32[]{:S(2)}) collective-permute-start(bf16[1,384,1024]{2,1,0:T(8,128)(2,1)S(1)} %collective-permute-done.2.rest_9_.rest_5_), channel_id=1, source_target_pairs={{0,1},{1,0},{2,3},{3,2},{4,5},{5,4},{6,7},{7,6},{8,9},{9,8},{10,11... | collective-permute-start | bytes 2359304 | tf_op jit(solution)/shard_map/ppermute | solution.py:707
  82.5 41.4 %collective-permute-start.10 = (bf16[256,2048]{1,0:T(8,128)(2,1)}, bf16[256,2048]{1,0:T(8,128)(2,1)S(1)}, u32[]{:S(2)}, u32[]{:S(2)}) collective-permute-start(bf16[256,2048]{1,0:T(8,128)(2,1)} %param.19), channel_id=1, source_target_pairs={{0,8},{1,9},{2,10},{3,11},{4,12},{5,13},{6,14},{7,15},{8,0},{9,1},... | collective-permute-start | bytes 3145736 | tf_op jit(solution)/shard_map/ppermute | solution.py:707
  84.1 39.7 %collective-permute-start.11 = (bf16[256,2048]{1,0:T(8,128)(2,1)}, bf16[256,2048]{1,0:T(8,128)(2,1)S(1)}, u32[]{:S(2)}, u32[]{:S(2)}) collective-permute-start(bf16[256,2048]{1,0:T(8,128)(2,1)} %param.19), channel_id=1, source_target_pairs={{0,4},{1,5},{2,6},{3,7},{4,0},{5,1},{6,2},{7,3},{8,12},{9,13},{10,... | collective-permute-start | bytes 3145736 | tf_op jit(solution)/shard_map/ppermute | solution.py:707
  85.8 37.1 %collective-permute-start.7 = (bf16[4,128,768]{2,1,0:T(8,128)(2,1)S(1)}, bf16[4,128,768]{2,1,0:T(8,128)(2,1)S(1)}, u32[]{:S(2)}, u32[]{:S(2)}) collective-permute-start(bf16[4,128,768]{2,1,0:T(8,128)(2,1)S(1)} %get-tuple-element.207.rest_0_.rest_4_), channel_id=1, source_target_pairs={{0,16},{1,17},{2,18},{3,19},{4,20},{5,21},{6,22},{7,23},{8,24},{9,... | collective-permute-start | bytes 2359304 | tf_op jit(solution)/shard_map/ppermute | solution.py:707
  88.5 34.3 %collective-permute-start.8 = (bf16[4,128,768]{2,1,0:T(8,128)(2,1)S(1)}, bf16[4,128,768]{2,1,0:T(8,128)(2,1)S(1)}, u32[]{:S(2)}, u32[]{:S(2)}) collective-permute-start(bf16[4,128,768]{2,1,0:T(8,128)(2,1)S(1)} %get-tuple-element.207.rest_0_.rest_4_), channel_id=1, source_target_pairs={{0,1},{1,0},{2,3},{3,2},{4,5},{5,4},{6,7},{7,6},{8,9},{9,8},{10,11... | collective-permute-start | bytes 2359304 | tf_op jit(solution)/shard_map/ppermute | solution.py:707
  88.9 22.8 %collective-permute-start.9 = (bf16[1,128,1024]{2,1,0:T(8,128)(2,1)}, bf16[1,128,1024]{2,1,0:T(8,128)(2,1)S(1)}, u32[]{:S(2)}, u32[]{:S(2)}) collective-permute-start(bf16[1,128,1024]{2,1,0:T(8,128)(2,1)} %collective-permute-done.5.rest_5_.rest_1_), channel_id=1, source_target_pairs={{0,1},{1,0},{2,3},{3,2},{4,5},{5,4},{6,7},{7,6},{8,9},{9,8},{10,11... | collective-permute-start | bytes 786440 | tf_op jit(solution)/shard_map/ppermute | solution.py:707
  123.9 40.4 %collective-permute-start.15 = (bf16[256,2048]{1,0:T(8,128)(2,1)}, bf16[256,2048]{1,0:T(8,128)(2,1)S(1)}, u32[]{:S(2)}, u32[]{:S(2)}) collective-permute-start(bf16[256,2048]{1,0:T(8,128)(2,1)} %collective-permute-done), channel_id=1, source_target_pairs={{0,4},{1,5},{2,6},{3,7},{4,0},{5,1},{6,2},{7,3},{8,12},{9,13},{10,... | collective-permute-start | bytes 3145736 | tf_op jit(solution)/shard_map/ppermute | solution.py:707
  125.3 44.6 %collective-permute-start.16 = (bf16[256,2048]{1,0:T(8,128)(2,1)S(1)}, bf16[256,2048]{1,0:T(8,128)(2,1)S(1)}, u32[]{:S(2)}, u32[]{:S(2)}) collective-permute-start(bf16[256,2048]{1,0:T(8,128)(2,1)S(1)} %collective-permute-done.10), channel_id=1, source_target_pairs={{0,4},{1,5},{2,6},{3,7},{4,0},{5,1},{6,2},{7,3},{8,12},{9,13},{10,... | collective-permute-start | bytes 3145736 | tf_op jit(solution)/shard_map/ppermute | solution.py:707
  128.2 35.0 %collective-permute-start.12 = (bf16[4,128,768]{2,1,0:T(8,128)(2,1)S(1)}, bf16[4,128,768]{2,1,0:T(8,128)(2,1)S(1)}, u32[]{:S(2)}, u32[]{:S(2)}) collective-permute-start(bf16[4,128,768]{2,1,0:T(8,128)(2,1)S(1)} %get-tuple-element.210.rest_4_.rest_8_), channel_id=1, source_target_pairs={{0,16},{1,17},{2,18},{3,19},{4,20},{5,21},{6,22},{7,23},{8,24},{9,... | collective-permute-start | bytes 2359304 | tf_op jit(solution)/shard_map/ppermute | solution.py:707
  130.6 32.5 %collective-permute-start.13 = (bf16[4,128,768]{2,1,0:T(8,128)(2,1)S(1)}, bf16[4,128,768]{2,1,0:T(8,128)(2,1)S(1)}, u32[]{:S(2)}, u32[]{:S(2)}) collective-permute-start(bf16[4,128,768]{2,1,0:T(8,128)(2,1)S(1)} %get-tuple-element.210.rest_4_.rest_8_), channel_id=1, source_target_pairs={{0,1},{1,0},{2,3},{3,2},{4,5},{5,4},{6,7},{7,6},{8,9},{9,8},{10,11... | collective-permute-start | bytes 2359304 | tf_op jit(solution)/shard_map/ppermute | solution.py:707
  131.4 32.8 %collective-permute-start.14 = (bf16[4,128,768]{2,1,0:T(8,128)(2,1)S(1)}, bf16[4,128,768]{2,1,0:T(8,128)(2,1)S(1)}, u32[]{:S(2)}, u32[]{:S(2)}) collective-permute-start(bf16[4,128,768]{2,1,0:T(8,128)(2,1)S(1)} %collective-permute-done.7.rest_1_.rest_5_), channel_id=1, source_target_pairs={{0,1},{1,0},{2,3},{3,2},{4,5},{5,4},{6,7},{7,6},{8,9},{9,8},{10,11... | collective-permute-start | bytes 2359304 | tf_op jit(solution)/shard_map/ppermute | solution.py:707
  171.0 26.8 %collective-permute-start.19 = (bf16[1024,2048]{1,0:T(8,128)(2,1)}, bf16[1024,2048]{1,0:T(8,128)(2,1)}, u32[]{:S(2)}, u32[]{:S(2)}) collective-permute-start(bf16[1024,2048]{1,0:T(8,128)(2,1)} %constant_dynamic-update-slice_fusion.4.dy_even), channel_id=1, source_target_pairs={{0,2},{1,3},{2,0},{3,1},{4,6},{5,7},{6,4},{7,5},{8,10},{9,11},{10,... | collective-permute-start | bytes 12582920 | tf_op jit(solution)/shard_map/ppermute | solution.py:707
  172.1 25.7 %collective-permute-start.18 = (bf16[1024,2048]{1,0:T(8,128)(2,1)}, bf16[1024,2048]{1,0:T(8,128)(2,1)}, u32[]{:S(2)}, u32[]{:S(2)}) collective-permute-start(bf16[1024,2048]{1,0:T(8,128)(2,1)} %constant_dynamic-update-slice_fusion.x_even), channel_id=1, source_target_pairs={{0,2},{1,3},{2,0},{3,1},{4,6},{5,7},{6,4},{7,5},{8,10},{9,11},{10,... | collective-permute-start | bytes 12582920 | tf_op jit(solution)/shard_map/ppermute | solution.py:707
  172.6 25.2 %all-to-all-start.2 = ((bf16[8,128,384]{2,1,0:T(8,128)(2,1)}), bf16[8,128,384]{2,1,0:T(8,128)(2,1)S(1)}, u32[]{:S(2)}, u32[]{:S(2)}) async-start(bf16[8,128,384]{2,1,0:T(8,128)(2,1)} %get-tuple-element.197), calls=%async_computation.2 | async-start | bytes 1572864 | tf_op jit(solution)/shard_map/all_to_all | solution.py:710
  177.8 20.0 %collective-permute-start.17 = (bf16[4,128,768]{2,1,0:T(8,128)(2,1)S(1)}, bf16[4,128,768]{2,1,0:T(8,128)(2,1)S(1)}, u32[]{:S(2)}, u32[]{:S(2)}) collective-permute-start(bf16[4,128,768]{2,1,0:T(8,128)(2,1)S(1)} %collective-permute-done.12.rest_5_.rest_9_), channel_id=1, source_target_pairs={{0,1},{1,0},{2,3},{3,2},{4,5},{5,4},{6,7},{7,6},{8,9},{9,8},{10,11... | collective-permute-start | bytes 2359304 | tf_op jit(solution)/shard_map/ppermute | solution.py:707
  197.8 37.0 %collective-permute-start.20 = (bf16[8,128,384]{2,1,0:T(8,128)(2,1)S(1)}, bf16[8,128,384]{2,1,0:T(8,128)(2,1)S(1)}, u32[]{:S(2)}, u32[]{:S(2)}) collective-permute-start(bf16[8,128,384]{2,1,0:T(8,128)(2,1)S(1)} %all-to-all-done.2.rest_0_), channel_id=1, source_target_pairs={{0,16},{1,17},{2,18},{3,19},{4,20},{5,21},{6,22},{7,23},{8,24},{9,... | collective-permute-start | bytes 2359304 | tf_op jit(solution)/shard_map/ppermute | solution.py:707
  199.7 35.1 %collective-permute-start.21 = (bf16[8,128,384]{2,1,0:T(8,128)(2,1)S(1)}, bf16[8,128,384]{2,1,0:T(8,128)(2,1)S(1)}, u32[]{:S(2)}, u32[]{:S(2)}) collective-permute-start(bf16[8,128,384]{2,1,0:T(8,128)(2,1)S(1)} %all-to-all-done.2.rest_0_), channel_id=1, source_target_pairs={{0,1},{1,0},{2,3},{3,2},{4,5},{5,4},{6,7},{7,6},{8,9},{9,8},{10,11... | collective-permute-start | bytes 2359304 | tf_op jit(solution)/shard_map/ppermute | solution.py:707
  254.5 22.0 %collective-permute-start.23 = (bf16[384,1024]{1,0:T(8,128)(2,1)}, bf16[384,1024]{1,0:T(8,128)(2,1)S(1)}, u32[]{:S(2)}, u32[]{:S(2)}) collective-permute-start(bf16[384,1024]{1,0:T(8,128)(2,1)} %get-tuple-element.232), channel_id=1, source_target_pairs={{0,1},{1,0},{2,3},{3,2},{4,5},{5,4},{6,7},{7,6},{8,9},{9,8},{10,11... | collective-permute-start | bytes 2359304 | tf_op jit(solution)/shard_map/ppermute | solution.py:707
  276.4 37.5 %collective-permute-start.25 = (bf16[1024,768]{1,0:T(8,128)(2,1)}, bf16[1024,768]{1,0:T(8,128)(2,1)S(1)}, u32[]{:S(2)}, u32[]{:S(2)}) collective-permute-start(bf16[1024,768]{1,0:T(8,128)(2,1)} %get-tuple-element.238), channel_id=1, source_target_pairs={{0,1},{1,0},{2,3},{3,2},{4,5},{5,4},{6,7},{7,6},{8,9},{9,8},{10,11... | collective-permute-start | bytes 4718600 | tf_op jit(solution)/shard_map/ppermute | solution.py:707
  278.7 35.2 %collective-permute-start.24 = (bf16[384,1024]{1,0:T(8,128)(2,1)}, bf16[384,1024]{1,0:T(8,128)(2,1)S(1)}, u32[]{:S(2)}, u32[]{:S(2)}) collective-permute-start(bf16[384,1024]{1,0:T(8,128)(2,1)} %add_convert_fusion.4), channel_id=1, source_target_pairs={{0,16},{1,17},{2,18},{3,19},{4,20},{5,21},{6,22},{7,23},{8,24},{9,... | collective-permute-start | bytes 2359304 | tf_op jit(solution)/shard_map/ppermute | solution.py:707
  313.9 31.1 %collective-permute-start.27 = (bf16[512,768]{1,0:T(8,128)(2,1)S(1)}, bf16[512,768]{1,0:T(8,128)(2,1)}, u32[]{:S(2)}, u32[]{:S(2)}) collective-permute-start(bf16[512,768]{1,0:T(8,128)(2,1)S(1)} %get-tuple-element.257), channel_id=1, source_target_pairs={{0,1},{1,0},{2,3},{3,2},{4,5},{5,4},{6,7},{7,6},{8,9},{9,8},{10,11... | collective-permute-start | bytes 2359304 | tf_op jit(solution)/shard_map/ppermute | solution.py:707
  317.0 28.0 %collective-permute-start.26 = (bf16[8,48,768]{2,1,0:T(8,128)(2,1)}, bf16[8,48,768]{2,1,0:T(8,128)(2,1)S(1)}, u32[]{:S(2)}, u32[]{:S(2)}) collective-permute-start(bf16[8,48,768]{2,1,0:T(8,128)(2,1)} %get-tuple-element.256), channel_id=1, source_target_pairs={{0,16},{1,17},{2,18},{3,19},{4,20},{5,21},{6,22},{7,23},{8,24},{9,... | collective-permute-start | bytes 1769480 | tf_op jit(solution)/shard_map/ppermute | solution.py:707
  345.9 28.5 %collective-permute-start.29 = (bf16[1024,2048]{1,0:T(8,128)(2,1)}, bf16[1024,2048]{1,0:T(8,128)(2,1)S(1)}, u32[]{:S(2)}, u32[]{:S(2)}) collective-permute-start(bf16[1024,2048]{1,0:T(8,128)(2,1)} %get-tuple-element.266), channel_id=1, source_target_pairs={{0,2},{1,3},{2,0},{3,1},{4,6},{5,7},{6,4},{7,5},{8,10},{9,11},{10,... | collective-permute-start | bytes 12582920 | tf_op jit(solution)/shard_map/ppermute | solution.py:707
  345.9 28.5 %collective-permute-start.30 = (bf16[512,768]{1,0:T(8,128)(2,1)S(1)}, bf16[512,768]{1,0:T(8,128)(2,1)S(1)}, u32[]{:S(2)}, u32[]{:S(2)}) collective-permute-start(bf16[512,768]{1,0:T(8,128)(2,1)S(1)} %get-tuple-element.267), channel_id=1, source_target_pairs={{0,1},{1,0},{2,3},{3,2},{4,5},{5,4},{6,7},{7,6},{8,9},{9,8},{10,11... | collective-permute-start | bytes 2359304 | tf_op jit(solution)/shard_map/ppermute | solution.py:707
  346.6 27.7 %collective-permute-start.28 = (bf16[8,48,768]{2,1,0:T(8,128)(2,1)}, bf16[8,48,768]{2,1,0:T(8,128)(2,1)S(1)}, u32[]{:S(2)}, u32[]{:S(2)}) collective-permute-start(bf16[8,48,768]{2,1,0:T(8,128)(2,1)} %get-tuple-element.265), channel_id=1, source_target_pairs={{0,16},{1,17},{2,18},{3,19},{4,20},{5,21},{6,22},{7,23},{8,24},{9,... | collective-permute-start | bytes 1769480 | tf_op jit(solution)/shard_map/ppermute | solution.py:707
  377.1 31.8 %collective-permute-start.33 = (bf16[2,256,1024]{2,1,0:T(8,128)(2,1)S(1)}, bf16[2,256,1024]{2,1,0:T(8,128)(2,1)}, u32[]{:S(2)}, u32[]{:S(2)}) collective-permute-start(bf16[2,256,1024]{2,1,0:T(8,128)(2,1)S(1)} %fusion.19), channel_id=1, source_target_pairs={{0,4},{1,5},{2,6},{3,7},{4,0},{5,1},{6,2},{7,3},{8,12},{9,13},{10,... | collective-permute-start | bytes 3145736 | tf_op jit(solution)/shard_map/ppermute | solution.py:707
  377.7 33.4 %collective-permute-start.34 = (bf16[2,256,1024]{2,1,0:T(8,128)(2,1)S(1)}, bf16[2,256,1024]{2,1,0:T(8,128)(2,1)}, u32[]{:S(2)}, u32[]{:S(2)}) collective-permute-start(bf16[2,256,1024]{2,1,0:T(8,128)(2,1)S(1)} %fusion.20), channel_id=1, source_target_pairs={{0,8},{1,9},{2,10},{3,11},{4,12},{5,13},{6,14},{7,15},{8,0},{9,1},... | collective-permute-start | bytes 3145736 | tf_op jit(solution)/shard_map/ppermute | solution.py:707
  377.7 33.4 %collective-permute-start.32 = (bf16[4,1024,128]{2,1,0:T(8,128)(2,1)}, bf16[4,1024,128]{2,1,0:T(8,128)(2,1)}, u32[]{:S(2)}, u32[]{:S(2)}) collective-permute-start(bf16[4,1024,128]{2,1,0:T(8,128)(2,1)} %get-tuple-element.276), channel_id=1, source_target_pairs={{0,1},{1,0},{2,3},{3,2},{4,5},{5,4},{6,7},{7,6},{8,9},{9,8},{10,11... | collective-permute-start | bytes 3145736 | tf_op jit(solution)/shard_map/ppermute | solution.py:707
  378.8 30.1 %collective-permute-start.31 = (bf16[8,32,768]{2,1,0:T(8,128)(2,1)}, bf16[8,32,768]{2,1,0:T(8,128)(2,1)S(1)}, u32[]{:S(2)}, u32[]{:S(2)}) collective-permute-start(bf16[8,32,768]{2,1,0:T(8,128)(2,1)} %fusion.31), channel_id=1, source_target_pairs={{0,16},{1,17},{2,18},{3,19},{4,20},{5,21},{6,22},{7,23},{8,24},{9,... | collective-permute-start | bytes 1179656 | tf_op jit(solution)/shard_map/ppermute | solution.py:707
  411.1 37.5 %collective-permute-start.36 = (bf16[1024,2048]{1,0:T(8,128)(2,1)}, bf16[1024,2048]{1,0:T(8,128)(2,1)}, u32[]{:S(2)}, u32[]{:S(2)}) collective-permute-start(bf16[1024,2048]{1,0:T(8,128)(2,1)} %normal_rows_sent.1), channel_id=1, source_target_pairs={{0,2},{1,3},{2,0},{3,1},{4,6},{5,7},{6,4},{7,5},{8,10},{9,11},{10,... | collective-permute-start | bytes 12582920 | tf_op jit(solution)/shard_map/ppermute | solution.py:707
  418.2 30.5 %all-to-all-start.3 = ((bf16[8,128,768]{2,1,0:T(8,128)(2,1)}), bf16[8,128,768]{2,1,0:T(8,128)(2,1)S(1)}, u32[]{:S(2)}, u32[]{:S(2)}) async-start(bf16[8,128,768]{2,1,0:T(8,128)(2,1)} %bitcast.122), calls=%async_computation.3 | async-start | bytes 3145728 | tf_op jit(solution)/shard_map/all_to_all | solution.py:710
  422.7 26.0 %collective-permute-start.37 = (bf16[4,1024,128]{2,1,0:T(8,128)(2,1)}, bf16[4,1024,128]{2,1,0:T(8,128)(2,1)}, u32[]{:S(2)}, u32[]{:S(2)}) collective-permute-start(bf16[4,1024,128]{2,1,0:T(8,128)(2,1)} %get-tuple-element.291), channel_id=1, source_target_pairs={{0,1},{1,0},{2,3},{3,2},{4,5},{5,4},{6,7},{7,6},{8,9},{9,8},{10,11... | collective-permute-start | bytes 3145736 | tf_op jit(solution)/shard_map/ppermute | solution.py:707
  424.0 22.4 %collective-permute-start.35 = (bf16[1,1024,128]{2,1,0:T(8,128)(2,1)}, bf16[1,1024,128]{2,1,0:T(8,128)(2,1)S(1)}, u32[]{:S(2)}, u32[]{:S(2)}) collective-permute-start(bf16[1,1024,128]{2,1,0:T(8,128)(2,1)} %slice.258), channel_id=1, source_target_pairs={{0,16},{1,17},{2,18},{3,19},{4,20},{5,21},{6,22},{7,23},{8,24},{9,... | collective-permute-start | bytes 786440 | tf_op jit(solution)/shard_map/ppermute | solution.py:707
  453.1 42.0 %collective-permute-start.38 = (bf16[2,256,1024]{2,1,0:T(8,128)(2,1)S(1)}, bf16[2,256,1024]{2,1,0:T(8,128)(2,1)S(1)}, u32[]{:S(2)}, u32[]{:S(2)}) collective-permute-start(bf16[2,256,1024]{2,1,0:T(8,128)(2,1)S(1)} %fusion.21), channel_id=1, source_target_pairs={{0,4},{1,5},{2,6},{3,7},{4,0},{5,1},{6,2},{7,3},{8,12},{9,13},{10,... | collective-permute-start | bytes 3145736 | tf_op jit(solution)/shard_map/ppermute | solution.py:707
  454.9 41.0 %collective-permute-start.39 = (bf16[2,256,1024]{2,1,0:T(8,128)(2,1)S(1)}, bf16[2,256,1024]{2,1,0:T(8,128)(2,1)S(1)}, u32[]{:S(2)}, u32[]{:S(2)}) collective-permute-start(bf16[2,256,1024]{2,1,0:T(8,128)(2,1)S(1)} %fusion.22), channel_id=1, source_target_pairs={{0,8},{1,9},{2,10},{3,11},{4,12},{5,13},{6,14},{7,15},{8,0},{9,1},... | collective-permute-start | bytes 3145736 | tf_op jit(solution)/shard_map/ppermute | solution.py:707
  456.3 38.8 %collective-permute-start.40 = (bf16[3,1024,128]{2,1,0:T(8,128)(2,1)S(1)}, bf16[3,1024,128]{2,1,0:T(8,128)(2,1)S(1)}, u32[]{:S(2)}, u32[]{:S(2)}) collective-permute-start(bf16[3,1024,128]{2,1,0:T(8,128)(2,1)S(1)} %slice.259), channel_id=1, source_target_pairs={{0,16},{1,17},{2,18},{3,19},{4,20},{5,21},{6,22},{7,23},{8,24},{9,... | collective-permute-start | bytes 2359304 | tf_op jit(solution)/shard_map/ppermute | solution.py:707
  457.6 37.5 %collective-permute-start.41 = (bf16[384,1024]{1,0:T(8,128)(2,1)}, bf16[384,1024]{1,0:T(8,128)(2,1)S(1)}, u32[]{:S(2)}, u32[]{:S(2)}) collective-permute-start(bf16[384,1024]{1,0:T(8,128)(2,1)} %get-tuple-element.306), channel_id=1, source_target_pairs={{0,1},{1,0},{2,3},{3,2},{4,5},{5,4},{6,7},{7,6},{8,9},{9,8},{10,11... | collective-permute-start | bytes 2359304 | tf_op jit(solution)/shard_map/ppermute | solution.py:707
  503.4 27.1 %all-to-all-start.4 = ((bf16[8,3,128,128]{3,2,1,0:T(8,128)(2,1)}), bf16[8,3,128,128]{3,2,1,0:T(8,128)(2,1)S(1)}, u32[]{:S(2)}, u32[]{:S(2)}) async-start(bf16[8,3,128,128]{3,2,1,0:T(8,128)(2,1)} %bitcast.115), calls=%async_computation.4 | async-start | bytes 1572864 | tf_op jit(solution)/shard_map/all_to_all | solution.py:710
  507.7 22.8 %collective-permute-start.42 = (bf16[256,1024]{1,0:T(8,128)(2,1)}, bf16[256,1024]{1,0:T(8,128)(2,1)}, u32[]{:S(2)}, u32[]{:S(2)}) collective-permute-start(bf16[256,1024]{1,0:T(8,128)(2,1)} %get-tuple-element.316), channel_id=1, source_target_pairs={{0,8},{1,9},{2,10},{3,11},{4,12},{5,13},{6,14},{7,15},{8,0},{9,1},... | collective-permute-start | bytes 1572872 | tf_op jit(solution)/shard_map/ppermute | solution.py:707
  509.8 20.6 %collective-permute-start.43 = (bf16[256,1024]{1,0:T(8,128)(2,1)}, bf16[256,1024]{1,0:T(8,128)(2,1)}, u32[]{:S(2)}, u32[]{:S(2)}) collective-permute-start(bf16[256,1024]{1,0:T(8,128)(2,1)} %get-tuple-element.317), channel_id=1, source_target_pairs={{0,4},{1,5},{2,6},{3,7},{4,0},{5,1},{6,2},{7,3},{8,12},{9,13},{10,... | collective-permute-start | bytes 1572872 | tf_op jit(solution)/shard_map/ppermute | solution.py:707
  (57 other events, 693.4 us)

commit v4 on v3

--- a/solution.py
+++ b/solution.py
@@ -780,10 +780,9 @@
     vec = all_vectors[:2]
     tables = rotary_lanes(row_count)
 
-    gu_own, down_far, out_parts, out_other, cotangent, vec, bias, slot_lengths, tables = barrier(
+    gu_own, out_parts, out_other, cotangent, vec, bias, slot_lengths, tables = barrier(
         (
             exchange(gu_own),
-            over_y_rest(down_parts),
             spread_top(out_own),
             over_y(out_own),
             cotangent,
@@ -793,14 +792,13 @@
             tables,
         )
     )
-    down_parts = down_parts + [down_other] + down_far
-    cut = n_t // 2
+    cut = n_t * 5 // 8
     gu_first, gu_second = barrier((gu_own[:cut], gu_own[cut:]))
-    gu_parts, gu_other, out_far, dy_top, dy_middle, gu_second, qkv_own, x_top = barrier(
+    gu_parts, gu_other, down_far, dy_top, dy_middle, gu_second, qkv_own, x_top = barrier(
         (
             spread_top(gu_first),
             over_y(gu_first),
-            over_y_rest(out_parts),
+            over_y_rest(down_parts),
             swap(cotangent, "t", n_t // 2),
             swap(cotangent, "t", n_t // 4),
             gu_second,
@@ -808,7 +806,7 @@
             x_top,
         )
     )
-    out_parts = out_parts + [out_other] + out_far
+    down_parts = down_parts + [down_other] + down_far
     gu_two, gu_two_other, gu_far, x_far, dy_far, qkv_own = barrier(
         (
             spread_top(gu_second),
@@ -852,11 +850,12 @@
         return summed.reshape(summed.shape[1], summed.shape[3], summed.shape[4])
 
     def piece(raw, middle_bit, top_bit, left):
-        columns = slice(0, half_width) if left else slice(half_width, width)
+        columns = slice(0, split) if left else slice(split, width)
         got, kept = (part.reshape(2, 2, row_count, width) for part in raw)
         spot = (middle_bit, top_bit, slice(None), columns)
         return got[spot].astype(F32) + kept[spot].astype(F32)
 
+    split = width * 5 // 8
     every = slice(None)
 
     def first_sends(raw):
@@ -890,10 +889,11 @@
         sizes,
         unit,
     )
-    qkv_parts, qkv_other, normed, dy, hidden, d_joined = barrier(
+    qkv_parts, qkv_other, out_far, normed, dy, hidden, d_joined = barrier(
         (
             spread_top(qkv_own),
             over_y(qkv_own),
+            over_y_rest(out_parts),
             normed,
             dy,
             hidden,
@@ -901,6 +901,7 @@
         )
     )
 
+    out_parts = out_parts + [out_other] + out_far
     qkv_far = over_y_rest(qkv_parts)
     down_far_sent, down_far_kept, down_sent, down_kept = grads_rows(
         other_half, hidden, dy, "grads_down"
@@ -944,7 +945,7 @@
 
     def thirds(value):
         value = value.reshape(value.shape[0] // (n_b * w_rows), n_b * w_rows, -1)
-        cuts = [n * value.shape[1] // 8 for n in (0, 3, 6, 8)]
+        cuts = [n * value.shape[1] // 8 for n in (0, 2, 5, 8)]
         return [value[:, low:high] for low, high in zip(cuts, cuts[1:])]
 
     gu_far = [summed(k, g).astype(BF16) for k, g in zip(thirds(gu_far_kept), thirds(gu_far_got))]
@@ -1064,8 +1065,9 @@
     g_down = over_rest(after(g_down, g_qkv), (top, 1, n_b, unit))
     new_down, moment_down, square_down = adam(w_down, g_down[0, :d_rows], first_down, second_down)
     g_qkv, normal_last, g_out, branch_sends, new_down = barrier(
-        (exchange(g_qkv), second_swaps(normal_sends), g_out, branch_sends, new_down)
-    )
+        (g_qkv, second_swaps(normal_sends), g_out, branch_sends, new_down)
+    )
+    g_qkv = exchange(g_qkv)
     branch_last = second_swaps(branch_sends)
     normal_own = whole_rows(normal, normal_got, normal_last)
     _, scaled_own, inv_own = normalize(tokens.astype(F32), vec[0], vec[1])

time: 570 us -> 552 us (0.968)
  waiting for transfers between devices: 200 us -> 185 us
  starting transfers between devices: 80.3 us -> 72.2 us
  other arithmetic: 48 us -> 55.9 us
    ppermute x46, waiting for transfers between devices: 173 us -> 154 us  [swap(): return lax.ppermute(value, AXES, [(i, i ^ mask) for i in range(total)])]
    unnamed x111 -> x127, local copies, waits for them, and re-layouts: 18.3 us -> 14.9 us
  transfers between devices with their start and end apart: 52 -> 52, of which waited for: 24 -> 23; matrix products, arithmetic and copies ran while one was open for 10% -> 12% of each run, Pallas kernels for 35% -> 34%
where the time goes in v4:
time: 552 us; the launch traced here: 546 us
  Pallas kernels  195 us (35%)
  waiting for transfers between devices  185 us (34%)
  starting transfers between devices  72.2 us (13%)
  other arithmetic  55.9 us (10%)
  local copies, waits for them, and re-layouts  36.1 us (7%)
    ppermute x46, waiting for transfers between devices, swap(): return lax.ppermute(value, AXES, [(i, i ^ mask) for i in range(total)])  154 us
    pallas_call x3, Pallas kernels, row_blocks(): pl.pallas_call(kernel, grid_spec=pltpu.PrefetchScalarGridSpec(num_scalar_...  51.8 us
    ppermute x46, starting transfers between devices, swap(): return lax.ppermute(value, AXES, [(i, i ^ mask) for i in range(total)])  50.5 us
    pallas_call x1, Pallas kernels, attention(): pl.pallas_call(functools.partial(attention_kernel, masks), grid_spec=pltp...  33.6 us
    pallas_call x1, Pallas kernels, mlp(): pl.pallas_call(functools.partial(mlp_kernel, masks, n_t), grid_spec=pltpu...  33.5 us
    all_to_all x1, waiting for transfers between devices, per_device(): lax.all_to_all(packed, AXES, split_axis=0, concat_axis=0, tiled=True)  27 us
    pallas_call x1, Pallas kernels, grads_cols(): pl.pallas_call(grads_cols_kernel, grid_spec=pltpu.PrefetchScalarGridSpec(...  21.2 us
    pallas_call x1, Pallas kernels, grads_attention(): pl.pallas_call(grads_attention_kernel, grid_spec=pltpu.PrefetchScalarGrid...  18.9 us
  transfers between devices with their start and end apart: 52, of which 23 were waited for; matrix products, arithmetic and copies ran while one was open for 12% of the time, Pallas kernels for 34%

profile of v4, /device:TPU:0, one launch (start us, length us, event | category | flops | bytes accessed | tf_op | source)
XLA Modules:
  0.0 546.4 jit_solution(501781424372714165)
XLA Ops:
  0.7 3.1 collective-permute-start
  6.8 2.7 collective-permute-start.2
  11.9 2.6 all-to-all-start
  15.2 6.7 %prep.1 = (bf16[8,128,384]{2,1,0:T(8,128)(2,1)}, bf16[8,128,768]{2,1,0:T(8,128)(2,1)}) custom-call(f32[128,3072]{1,0:T(8,128)} %w.3, f32[128,5632]{1,0:T(8,128)} %w.2), custom_call_target="tpu_custom_call" | custom-call | bytes 14417920 | tf_op jit(solution)/shard_map/prep/pallas_call | solution.py:157
  21.9 27.0 %all-to-all-done = f32[32,1,384]{2,1,0:T(1,128)S(1)} async-done(((f32[32,1,384]{2,1,0:T(1,128)}), f32[32,1,384]{2,1,0:T(1,128)S(1)}, u32[]{:S(2)}, u32[]{:S(2)}) %all-to-all-start) | async-done | bytes 49184 | tf_op jit(solution)/shard_map/all_to_all | solution.py:731
  49.9 3.6 all-to-all-start.1
  64.0 13.0 %collective-permute-done.4.rest_5_.rest_1_ = bf16[1,128,1024]{2,1,0:T(8,128)(2,1)} collective-permute-done((bf16[1,128,1024]{2,1,0:T(8,128)(2,1)}, bf16[1,128,1024]{2,1,0:T(8,128)(2,1)}, u32[]{:S(2)}, u32[]{:S(2)}) %collective-permute-start.4) | collective-permute-done | bytes 262176 | tf_op jit(solution)/shard_map/ppermute | solution.py:707
  85.5 36.4 %collective-permute-done.8.rest_11_.rest_7_ = bf16[1,384,1024]{2,1,0:T(8,128)(2,1)S(1)} collective-permute-done((bf16[1,384,1024]{2,1,0:T(8,128)(2,1)S(1)}, bf16[1,384,1024]{2,1,0:T(8,128)(2,1)S(1)}, u32[]{:S(2)}, u32[]{:S(2)}) %collective-permute-start.8) | collective-permute-done | bytes 786464 | tf_op jit(solution)/shard_map/ppermute | solution.py:707
  121.9 2.3 collective-permute-done.6.rest_1_.rest_5_
  128.3 2.3 constant_dynamic-update-slice_fusion.2
  137.2 2.3 constant_dynamic-update-slice_fusion.1
  139.6 19.3 %collective-permute-done.11.rest_5_.rest_9_ = bf16[3,128,768]{2,1,0:T(8,128)(2,1)S(1)} collective-permute-done((bf16[3,128,768]{2,1,0:T(8,128)(2,1)S(1)}, bf16[3,128,768]{2,1,0:T(8,128)(2,1)S(1)}, u32[]{:S(2)}, u32[]{:S(2)}) %collective-permute-start.11) | collective-permute-done | bytes 589856 | tf_op jit(solution)/shard_map/ppermute | solution.py:707
  158.8 6.4 %collective-permute-done.12.rest_6_.rest_10_ = bf16[3,128,768]{2,1,0:T(8,128)(2,1)S(1)} collective-permute-done((bf16[3,128,768]{2,1,0:T(8,128)(2,1)S(1)}, bf16[3,128,768]{2,1,0:T(8,128)(2,1)S(1)}, u32[]{:S(2)}, u32[]{:S(2)}) %collective-permute-start.12) | collective-permute-done | bytes 589856 | tf_op jit(solution)/shard_map/ppermute | solution.py:707
  165.3 7.6 %collective-permute-done.15 = bf16[256,2048]{1,0:T(8,128)(2,1)S(1)} collective-permute-done((bf16[256,2048]{1,0:T(8,128)(2,1)S(1)}, bf16[256,2048]{1,0:T(8,128)(2,1)S(1)}, u32[]{:S(2)}, u32[]{:S(2)}) %collective-permute-start.15) | collective-permute-done | bytes 1048608 | tf_op jit(solution)/shard_map/ppermute | solution.py:707
  175.5 3.7 all-to-all-start.2
  179.3 15.6 %collective-permute-done.16.rest_7_.rest_11_ = bf16[3,128,768]{2,1,0:T(8,128)(2,1)S(1)} collective-permute-done((bf16[3,128,768]{2,1,0:T(8,128)(2,1)S(1)}, bf16[3,128,768]{2,1,0:T(8,128)(2,1)S(1)}, u32[]{:S(2)}, u32[]{:S(2)}) %collective-permute-start.16) | collective-permute-done | bytes 589856 | tf_op jit(solution)/shard_map/ppermute | solution.py:707
  198.6 33.5 %mlp.1 = (bf16[2048,2048]{1,0:T(8,128)(2,1)}, bf16[2048,2048]{1,0:T(8,128)(2,1)}, bf16[2048,768]{1,0:T(8,128)(2,1)}, bf16[2,2048,768]{2,1,0:T(8,128)(2,1)}) custom-call(s32[4]{0:T(128)} %pad_add_fusion.1.here, f32[2,2048]{1,0:T(2,128)} %slice.184.vec, bf16[1024,2048]{1,0:T(8,128)(2,1)} %constant_dynamic-update-slice_fusion.x_even, ...), custom_call_target="tpu_custom_call" | custom-call | tf_op jit(solution)/shard_map/mlp/pallas_call | solution.py:295
  234.5 11.5 %grads_down.1 = (bf16[384,1024]{1,0:T(8,128)(2,1)}, f32[384,1024]{1,0:T(8,128)}, bf16[384,1024]{1,0:T(8,128)(2,1)}, f32[384,1024]{1,0:T(8,128)}) custom-call(s32[2]{0:T(128)} %pad_add_fusion.where, bf16[2048,768]{1,0:T(8,128)(2,1)} %get-tuple-element.221.far.near.hidden, bf16[2048,768]{1,0:T(8,128)(2,1)} %get-tuple-element.221.far.near.hidden, ...), custom_call_target="tpu_custom_call" | custom-call | flops 6442450944 | bytes 16252928 | tf_op jit(solution)/shard_map/grads_down/pallas_call | solution.py:511
  246.0 5.4 collective-permute-done.22.rest_3_
  252.1 21.2 %grads_gate_up.1 = (bf16[1024,768]{1,0:T(8,128)(2,1)}, f32[1024,768]{1,0:T(8,128)}, bf16[1024,768]{1,0:T(8,128)(2,1)}, f32[1024,768]{1,0:T(8,128)}) custom-call(s32[2]{0:T(128)} %pad_add_fusion.where, bf16[2048,2048]{1,0:T(8,128)(2,1)} %get-tuple-element.228.left.normed.tall, bf16[2,2048,768]{2,1,0:T(8,128)(2,1)} %get-tuple-element.229.d_sent.d_kept.d_joined, ...), custom_call_target="tpu_custom_call" | custom-call | tf_op jit(solution)/shard_map/grads_gate_up/pallas_call | solution.py:478
  277.8 33.6 %attention.1 = (bf16[2048,256]{1,0:T(8,128)(2,1)}, bf16[2048,768]{1,0:T(8,128)(2,1)}, f32[8,1,768]{2,1,0:T(1,128)}) custom-call(s32[4]{0:T(128)} %pad_add_fusion.1.here, s32[8]{0:T(128)} %convert_element_type.294.lengths, bf16[2048,2048]{1,0:T(8,128)(2,1)} %get-tuple-element.228.left.normed.tall, bf16[2048,2048]{1,0:T(8,128)(2,1)} %get-tuple-element.222.dy_sent.dy_kept.dy, ...), custom_call_target="tpu_custom_call" | custom-call | flops 12884901888 | bytes 41943040 | tf_op jit(solution)/shard_map/attention/pallas_call | solution.py:407
  315.4 16.9 %branch_rows.1 = (bf16[1024,2048]{1,0:T(8,128)(2,1)}, bf16[1024,2048]{1,0:T(8,128)(2,1)}) custom-call(s32[4]{0:T(128)} %pad_add_fusion.1.here, bf16[2048,256]{1,0:T(8,128)(2,1)} %get-tuple-element.261.o.left, bf16[2048,768]{1,0:T(8,128)(2,1)} %get-tuple-element.221.far.near.hidden, bf16[1,128,1024]{2,1,0:T(8,128)(2,1)} %convert_bitcast_fusion.rest_4_.rest_0_, ...), custom_call_target="tpu_custom_call" | custom-call | tf_op jit(solution)/shard_map/branch_rows/pallas_call | solution.py:606
  336.2 18.9 %grads_attention.1 = (bf16[2,4,1024,128]{3,2,1,0:T(8,128)(2,1)}, f32[2,4,1024,128]{3,2,1,0:T(8,128)}) custom-call(s32[2]{0:T(128)} %pad_add_fusion.where, bf16[2048,2048]{1,0:T(8,128)(2,1)} %get-tuple-element.228.left.normed.tall, bf16[2048,768]{1,0:T(8,128)(2,1)} %get-tuple-element.270.d_qkv, bf16[2048,256]{1,0:T(8,128)(2,1)} %get-tuple-element.261.o.left, ...), custom_call_target="tpu_custom_call" | custom-call | tf_op jit(solution)/shard_map/grads_attention/pallas_call | solution.py:565
  355.1 3.2 slice_bitcast_fusion.1
  358.3 5.9 %collective-permute-done.28 = bf16[8,48,768]{2,1,0:T(8,128)(2,1)S(1)} collective-permute-done((bf16[8,48,768]{2,1,0:T(8,128)(2,1)}, bf16[8,48,768]{2,1,0:T(8,128)(2,1)S(1)}, u32[]{:S(2)}, u32[]{:S(2)}) %collective-permute-start.28) | collective-permute-done | bytes 589856 | tf_op jit(solution)/shard_map/ppermute | solution.py:707
  369.0 3.3 collective-permute-start.31
  372.2 17.5 %normal_rows_sent.1 = bf16[1024,2048]{1,0:T(8,128)(2,1)} custom-call(s32[4]{0:T(128)} %pad_add_fusion.1.here, bf16[2048,768]{1,0:T(8,128)(2,1)} %get-tuple-element.270.d_qkv, bf16[2,2048,768]{2,1,0:T(8,128)(2,1)} %get-tuple-element.229.d_sent.d_kept.d_joined, bf16[8,128,384]{2,1,0:T(8,128)(2,1)} %copy-done.6, bf16[8,128,384]{2,1,0:T(8,128)(2,1)} %copy-done.18, ...), custom_call_target="tpu_custom_call" | custom-call | tf_op jit(solution)/shard_map/normal_rows_sent/pallas_call | solution.py:606
  389.7 8.7 %collective-permute-done.31 = bf16[8,48,768]{2,1,0:T(8,128)(2,1)} collective-permute-done((bf16[8,48,768]{2,1,0:T(8,128)(2,1)}, bf16[8,48,768]{2,1,0:T(8,128)(2,1)}, u32[]{:S(2)}, u32[]{:S(2)}) %collective-permute-start.31) | collective-permute-done | bytes 589856 | tf_op jit(solution)/shard_map/ppermute | solution.py:707
  405.1 2.9 fusion
  408.0 3.8 all-to-all-start.3
  415.3 17.5 %normal_rows_kept.1 = bf16[1024,2048]{1,0:T(8,128)(2,1)} custom-call(s32[4]{0:T(128)} %pad_add_fusion.1.here, bf16[2048,768]{1,0:T(8,128)(2,1)} %get-tuple-element.270.d_qkv, bf16[2,2048,768]{2,1,0:T(8,128)(2,1)} %get-tuple-element.229.d_sent.d_kept.d_joined, bf16[8,128,384]{2,1,0:T(8,128)(2,1)} %copy-done.6, bf16[8,128,384]{2,1,0:T(8,128)(2,1)} %copy-done.18, ...), custom_call_target="tpu_custom_call" | custom-call | tf_op jit(solution)/shard_map/normal_rows_kept/pallas_call | solution.py:606
  432.8 2.7 collective-permute-done.35
  437.8 3.0 fusion.26
  440.8 3.1 fusion.18
  450.6 10.3 %finish_gate_up.1 = (f32[128,5632]{1,0:T(8,128)}, f32[128,5632]{1,0:T(8,128)}, f32[128,5632]{1,0:T(8,128)}) custom-call(bf16[8,128,768]{2,1,0:T(8,128)(2,1)} %copy-done.8, f32[128,5632]{1,0:T(8,128)} %w.2, f32[128,5632]{1,0:T(8,128)} %m.2, f32[128,5632]{1,0:T(8,128)} %v.2), custom_call_target="tpu_custom_call" | custom-call | flops 14417920 | bytes 18743296 | tf_op jit(solution)/shard_map/finish_gate_up/pallas_call | solution.py:215
  460.9 2.2 fusion.31
  463.1 2.4 fusion.21
  465.5 15.8 %collective-permute-done.39 = bf16[2,256,768]{2,1,0:T(8,128)(2,1)S(1)} collective-permute-done((bf16[2,256,768]{2,1,0:T(8,128)(2,1)}, bf16[2,256,768]{2,1,0:T(8,128)(2,1)S(1)}, u32[]{:S(2)}, u32[]{:S(2)}) %collective-permute-start.39) | collective-permute-done | bytes 786464 | tf_op jit(solution)/shard_map/ppermute | solution.py:707
  481.3 3.1 collective-permute-done.40
  486.6 2.6 fusion.20
  494.2 5.1 multiply_subtract_fusion
  499.2 3.2 collective-permute-done.42
  508.3 3.8 all-to-all-start.4
  515.4 2.9 multiply_subtract_fusion.1
  520.0 4.2 all-to-all-start.5
  533.6 2.4 fusion.11
  536.0 2.5 all-to-all-done.5.g
  538.4 7.5 %finish_qkv.1 = (f32[128,3072]{1,0:T(8,128)}, f32[128,3072]{1,0:T(8,128)}, f32[128,3072]{1,0:T(8,128)}) custom-call(bf16[8,3,128,128]{3,2,1,0:T(8,128)(2,1)} %all-to-all-done.5.g, f32[128,3072]{1,0:T(8,128)} %w.3, f32[128,3072]{1,0:T(8,128)} %m.3, f32[128,3072]{1,0:T(8,128)} %v.3), custom_call_target="tpu_custom_call" | custom-call | flops 7864320 | bytes 10223616 | tf_op jit(solution)/shard_map/finish_qkv/pallas_call | solution.py:215
  (291 shorter events, 109.5 us)
Async XLA Ops:
  0.7 48.2 %collective-permute-start = (bf16[256,2048]{1,0:T(8,128)(2,1)}, bf16[256,2048]{1,0:T(8,128)(2,1)}, u32[]{:S(2)}, u32[]{:S(2)}) collective-permute-start(bf16[256,2048]{1,0:T(8,128)(2,1)} %param.18), channel_id=1, source_target_pairs={{0,8},{1,9},{2,10},{3,11},{4,12},{5,13},{6,14},{7,15},{8,0},{9,1},... | collective-permute-start | bytes 3145736 | tf_op jit(solution)/shard_map/ppermute | solution.py:707
  3.8 45.1 %collective-permute-start.1 = (bf16[256,2048]{1,0:T(8,128)(2,1)}, bf16[256,2048]{1,0:T(8,128)(2,1)}, u32[]{:S(2)}, u32[]{:S(2)}) collective-permute-start(bf16[256,2048]{1,0:T(8,128)(2,1)} %param.18), channel_id=1, source_target_pairs={{0,4},{1,5},{2,6},{3,7},{4,0},{5,1},{6,2},{7,3},{8,12},{9,13},{10,... | collective-permute-start | bytes 3145736 | tf_op jit(solution)/shard_map/ppermute | solution.py:707
  6.8 42.0 %collective-permute-start.2 = (bf16[1,384,1024]{2,1,0:T(8,128)(2,1)S(1)}, bf16[1,384,1024]{2,1,0:T(8,128)(2,1)S(1)}, u32[]{:S(2)}, u32[]{:S(2)}) collective-permute-start(bf16[1,384,1024]{2,1,0:T(8,128)(2,1)S(1)} %pad_bitcast_fusion.rest_8_.rest_4_), channel_id=1, source_target_pairs={{0,16},{1,17},{2,18},{3,19},{4,20},{5,21},{6,22},{7,23},{8,24},{9,... | collective-permute-start | bytes 2359304 | tf_op jit(solution)/shard_map/ppermute | solution.py:707
  9.5 39.4 %collective-permute-start.3 = (bf16[1,384,1024]{2,1,0:T(8,128)(2,1)S(1)}, bf16[1,384,1024]{2,1,0:T(8,128)(2,1)S(1)}, u32[]{:S(2)}, u32[]{:S(2)}) collective-permute-start(bf16[1,384,1024]{2,1,0:T(8,128)(2,1)S(1)} %pad_bitcast_fusion.rest_8_.rest_4_), channel_id=1, source_target_pairs={{0,1},{1,0},{2,3},{3,2},{4,5},{5,4},{6,7},{7,6},{8,9},{9,8},{10,11... | collective-permute-start | bytes 2359304 | tf_op jit(solution)/shard_map/ppermute | solution.py:707
  11.9 36.9 %all-to-all-start = ((f32[32,1,384]{2,1,0:T(1,128)}), f32[32,1,384]{2,1,0:T(1,128)S(1)}, u32[]{:S(2)}, u32[]{:S(2)}) async-start(f32[32,1,384]{2,1,0:T(1,128)} %broadcast_in_dim.60), calls=%async_computation | async-start | bytes 98304 | tf_op jit(solution)/shard_map/all_to_all | solution.py:731
  49.9 29.2 %all-to-all-start.1 = ((bf16[8,128,768]{2,1,0:T(8,128)(2,1)}), bf16[8,128,768]{2,1,0:T(8,128)(2,1)S(1)}, u32[]{:S(2)}, u32[]{:S(2)}) async-start(bf16[8,128,768]{2,1,0:T(8,128)(2,1)} %get-tuple-element.180), calls=%async_computation.1 | async-start | bytes 3145728 | tf_op jit(solution)/shard_map/all_to_all | solution.py:710
  56.8 20.3 %collective-permute-start.4 = (bf16[1,128,1024]{2,1,0:T(8,128)(2,1)}, bf16[1,128,1024]{2,1,0:T(8,128)(2,1)}, u32[]{:S(2)}, u32[]{:S(2)}) collective-permute-start(bf16[1,128,1024]{2,1,0:T(8,128)(2,1)} %convert_bitcast_fusion.rest_4_.rest_0_), channel_id=1, source_target_pairs={{0,16},{1,17},{2,18},{3,19},{4,20},{5,21},{6,22},{7,23},{8,24},{9,... | collective-permute-start | bytes 786440 | tf_op jit(solution)/shard_map/ppermute | solution.py:707
  57.0 20.1 %collective-permute-start.5 = (bf16[1,128,1024]{2,1,0:T(8,128)(2,1)}, bf16[1,128,1024]{2,1,0:T(8,128)(2,1)}, u32[]{:S(2)}, u32[]{:S(2)}) collective-permute-start(bf16[1,128,1024]{2,1,0:T(8,128)(2,1)} %convert_bitcast_fusion.rest_4_.rest_0_), channel_id=1, source_target_pairs={{0,1},{1,0},{2,3},{3,2},{4,5},{5,4},{6,7},{7,6},{8,9},{9,8},{10,11... | collective-permute-start | bytes 786440 | tf_op jit(solution)/shard_map/ppermute | solution.py:707
  79.1 45.1 %collective-permute-start.10 = (bf16[256,2048]{1,0:T(8,128)(2,1)}, bf16[256,2048]{1,0:T(8,128)(2,1)S(1)}, u32[]{:S(2)}, u32[]{:S(2)}) collective-permute-start(bf16[256,2048]{1,0:T(8,128)(2,1)} %param.19), channel_id=1, source_target_pairs={{0,4},{1,5},{2,6},{3,7},{4,0},{5,1},{6,2},{7,3},{8,12},{9,13},{10,... | collective-permute-start | bytes 3145736 | tf_op jit(solution)/shard_map/ppermute | solution.py:707
  80.5 45.7 %collective-permute-start.9 = (bf16[256,2048]{1,0:T(8,128)(2,1)}, bf16[256,2048]{1,0:T(8,128)(2,1)S(1)}, u32[]{:S(2)}, u32[]{:S(2)}) collective-permute-start(bf16[256,2048]{1,0:T(8,128)(2,1)} %param.19), channel_id=1, source_target_pairs={{0,8},{1,9},{2,10},{3,11},{4,12},{5,13},{6,14},{7,15},{8,0},{9,1},... | collective-permute-start | bytes 3145736 | tf_op jit(solution)/shard_map/ppermute | solution.py:707
  81.1 43.1 %collective-permute-start.6 = (bf16[5,128,768]{2,1,0:T(8,128)(2,1)S(1)}, bf16[5,128,768]{2,1,0:T(8,128)(2,1)S(1)}, u32[]{:S(2)}, u32[]{:S(2)}) collective-permute-start(bf16[5,128,768]{2,1,0:T(8,128)(2,1)S(1)} %slice.189.rest_0_.rest_4_), channel_id=1, source_target_pairs={{0,16},{1,17},{2,18},{3,19},{4,20},{5,21},{6,22},{7,23},{8,24},{9,... | collective-permute-start | bytes 2949128 | tf_op jit(solution)/shard_map/ppermute | solution.py:707
  82.3 41.9 %collective-permute-start.7 = (bf16[5,128,768]{2,1,0:T(8,128)(2,1)S(1)}, bf16[5,128,768]{2,1,0:T(8,128)(2,1)S(1)}, u32[]{:S(2)}, u32[]{:S(2)}) collective-permute-start(bf16[5,128,768]{2,1,0:T(8,128)(2,1)S(1)} %slice.189.rest_0_.rest_4_), channel_id=1, source_target_pairs={{0,1},{1,0},{2,3},{3,2},{4,5},{5,4},{6,7},{7,6},{8,9},{9,8},{10,11... | collective-permute-start | bytes 2949128 | tf_op jit(solution)/shard_map/ppermute | solution.py:707
  82.7 39.2 %collective-permute-start.8 = (bf16[1,384,1024]{2,1,0:T(8,128)(2,1)S(1)}, bf16[1,384,1024]{2,1,0:T(8,128)(2,1)S(1)}, u32[]{:S(2)}, u32[]{:S(2)}) collective-permute-start(bf16[1,384,1024]{2,1,0:T(8,128)(2,1)S(1)} %collective-permute-done.2.rest_9_.rest_5_), channel_id=1, source_target_pairs={{0,1},{1,0},{2,3},{3,2},{4,5},{5,4},{6,7},{7,6},{8,9},{9,8},{10,11... | collective-permute-start | bytes 2359304 | tf_op jit(solution)/shard_map/ppermute | solution.py:707
  126.2 39.1 %collective-permute-start.14 = (bf16[256,2048]{1,0:T(8,128)(2,1)}, bf16[256,2048]{1,0:T(8,128)(2,1)S(1)}, u32[]{:S(2)}, u32[]{:S(2)}) collective-permute-start(bf16[256,2048]{1,0:T(8,128)(2,1)} %collective-permute-done), channel_id=1, source_target_pairs={{0,4},{1,5},{2,6},{3,7},{4,0},{5,1},{6,2},{7,3},{8,12},{9,13},{10,... | collective-permute-start | bytes 3145736 | tf_op jit(solution)/shard_map/ppermute | solution.py:707
  126.8 46.2 %collective-permute-start.15 = (bf16[256,2048]{1,0:T(8,128)(2,1)S(1)}, bf16[256,2048]{1,0:T(8,128)(2,1)S(1)}, u32[]{:S(2)}, u32[]{:S(2)}) collective-permute-start(bf16[256,2048]{1,0:T(8,128)(2,1)S(1)} %collective-permute-done.9), channel_id=1, source_target_pairs={{0,4},{1,5},{2,6},{3,7},{4,0},{5,1},{6,2},{7,3},{8,12},{9,13},{10,... | collective-permute-start | bytes 3145736 | tf_op jit(solution)/shard_map/ppermute | solution.py:707
  130.6 34.7 %collective-permute-start.13 = (bf16[5,128,768]{2,1,0:T(8,128)(2,1)S(1)}, bf16[5,128,768]{2,1,0:T(8,128)(2,1)S(1)}, u32[]{:S(2)}, u32[]{:S(2)}) collective-permute-start(bf16[5,128,768]{2,1,0:T(8,128)(2,1)S(1)} %collective-permute-done.6.rest_1_.rest_5_), channel_id=1, source_target_pairs={{0,1},{1,0},{2,3},{3,2},{4,5},{5,4},{6,7},{7,6},{8,9},{9,8},{10,11... | collective-permute-start | bytes 2949128 | tf_op jit(solution)/shard_map/ppermute | solution.py:707
  132.1 26.8 %collective-permute-start.11 = (bf16[3,128,768]{2,1,0:T(8,128)(2,1)S(1)}, bf16[3,128,768]{2,1,0:T(8,128)(2,1)S(1)}, u32[]{:S(2)}, u32[]{:S(2)}) collective-permute-start(bf16[3,128,768]{2,1,0:T(8,128)(2,1)S(1)} %slice.190.rest_4_.rest_8_), channel_id=1, source_target_pairs={{0,16},{1,17},{2,18},{3,19},{4,20},{5,21},{6,22},{7,23},{8,24},{9,... | collective-permute-start | bytes 1769480 | tf_op jit(solution)/shard_map/ppermute | solution.py:707
  133.8 31.4 %collective-permute-start.12 = (bf16[3,128,768]{2,1,0:T(8,128)(2,1)S(1)}, bf16[3,128,768]{2,1,0:T(8,128)(2,1)S(1)}, u32[]{:S(2)}, u32[]{:S(2)}) collective-permute-start(bf16[3,128,768]{2,1,0:T(8,128)(2,1)S(1)} %slice.190.rest_4_.rest_8_), channel_id=1, source_target_pairs={{0,1},{1,0},{2,3},{3,2},{4,5},{5,4},{6,7},{7,6},{8,9},{9,8},{10,11... | collective-permute-start | bytes 1769480 | tf_op jit(solution)/shard_map/ppermute | solution.py:707
  174.0 21.0 %collective-permute-start.18 = (bf16[1024,2048]{1,0:T(8,128)(2,1)}, bf16[1024,2048]{1,0:T(8,128)(2,1)}, u32[]{:S(2)}, u32[]{:S(2)}) collective-permute-start(bf16[1024,2048]{1,0:T(8,128)(2,1)} %constant_dynamic-update-slice_fusion.4.dy_even), channel_id=1, source_target_pairs={{0,2},{1,3},{2,0},{3,1},{4,6},{5,7},{6,4},{7,5},{8,10},{9,11},{10,... | collective-permute-start | bytes 12582920 | tf_op jit(solution)/shard_map/ppermute | solution.py:707
  175.0 20.0 %collective-permute-start.17 = (bf16[1024,2048]{1,0:T(8,128)(2,1)}, bf16[1024,2048]{1,0:T(8,128)(2,1)}, u32[]{:S(2)}, u32[]{:S(2)}) collective-permute-start(bf16[1024,2048]{1,0:T(8,128)(2,1)} %constant_dynamic-update-slice_fusion.x_even), channel_id=1, source_target_pairs={{0,2},{1,3},{2,0},{3,1},{4,6},{5,7},{6,4},{7,5},{8,10},{9,11},{10,... | collective-permute-start | bytes 12582920 | tf_op jit(solution)/shard_map/ppermute | solution.py:707
  175.5 19.5 %all-to-all-start.2 = ((bf16[8,128,384]{2,1,0:T(8,128)(2,1)}), bf16[8,128,384]{2,1,0:T(8,128)(2,1)S(1)}, u32[]{:S(2)}, u32[]{:S(2)}) async-start(bf16[8,128,384]{2,1,0:T(8,128)(2,1)} %get-tuple-element.196), calls=%async_computation.2 | async-start | bytes 1572864 | tf_op jit(solution)/shard_map/all_to_all | solution.py:710
  179.2 15.7 %collective-permute-start.16 = (bf16[3,128,768]{2,1,0:T(8,128)(2,1)S(1)}, bf16[3,128,768]{2,1,0:T(8,128)(2,1)S(1)}, u32[]{:S(2)}, u32[]{:S(2)}) collective-permute-start(bf16[3,128,768]{2,1,0:T(8,128)(2,1)S(1)} %collective-permute-done.11.rest_5_.rest_9_), channel_id=1, source_target_pairs={{0,1},{1,0},{2,3},{3,2},{4,5},{5,4},{6,7},{7,6},{8,9},{9,8},{10,11... | collective-permute-start | bytes 1769480 | tf_op jit(solution)/shard_map/ppermute | solution.py:707
  195.0 37.1 %collective-permute-start.19 = (bf16[8,128,384]{2,1,0:T(8,128)(2,1)S(1)}, bf16[8,128,384]{2,1,0:T(8,128)(2,1)S(1)}, u32[]{:S(2)}, u32[]{:S(2)}) collective-permute-start(bf16[8,128,384]{2,1,0:T(8,128)(2,1)S(1)} %all-to-all-done.2.rest_0_), channel_id=1, source_target_pairs={{0,16},{1,17},{2,18},{3,19},{4,20},{5,21},{6,22},{7,23},{8,24},{9,... | collective-permute-start | bytes 2359304 | tf_op jit(solution)/shard_map/ppermute | solution.py:707
  196.0 36.2 %collective-permute-start.20 = (bf16[8,128,384]{2,1,0:T(8,128)(2,1)S(1)}, bf16[8,128,384]{2,1,0:T(8,128)(2,1)S(1)}, u32[]{:S(2)}, u32[]{:S(2)}) collective-permute-start(bf16[8,128,384]{2,1,0:T(8,128)(2,1)S(1)} %all-to-all-done.2.rest_0_), channel_id=1, source_target_pairs={{0,1},{1,0},{2,3},{3,2},{4,5},{5,4},{6,7},{7,6},{8,9},{9,8},{10,11... | collective-permute-start | bytes 2359304 | tf_op jit(solution)/shard_map/ppermute | solution.py:707
  196.7 35.4 %collective-permute-start.21 = (bf16[1,128,1024]{2,1,0:T(8,128)(2,1)}, bf16[1,128,1024]{2,1,0:T(8,128)(2,1)S(1)}, u32[]{:S(2)}, u32[]{:S(2)}) collective-permute-start(bf16[1,128,1024]{2,1,0:T(8,128)(2,1)} %collective-permute-done.4.rest_5_.rest_1_), channel_id=1, source_target_pairs={{0,1},{1,0},{2,3},{3,2},{4,5},{5,4},{6,7},{7,6},{8,9},{9,8},{10,11... | collective-permute-start | bytes 786440 | tf_op jit(solution)/shard_map/ppermute | solution.py:707
  233.1 18.4 %collective-permute-start.22 = (bf16[8,128,384]{2,1,0:T(8,128)(2,1)S(1)}, bf16[8,128,384]{2,1,0:T(8,128)(2,1)S(1)}, u32[]{:S(2)}, u32[]{:S(2)}) collective-permute-start(bf16[8,128,384]{2,1,0:T(8,128)(2,1)S(1)} %collective-permute-done.19.rest_1_), channel_id=1, source_target_pairs={{0,1},{1,0},{2,3},{3,2},{4,5},{5,4},{6,7},{7,6},{8,9},{9,8},{10,11... | collective-permute-start | bytes 2359304 | tf_op jit(solution)/shard_map/ppermute | solution.py:707
  251.5 21.8 %collective-permute-start.23 = (bf16[384,1024]{1,0:T(8,128)(2,1)}, bf16[384,1024]{1,0:T(8,128)(2,1)S(1)}, u32[]{:S(2)}, u32[]{:S(2)}) collective-permute-start(bf16[384,1024]{1,0:T(8,128)(2,1)} %get-tuple-element.232), channel_id=1, source_target_pairs={{0,1},{1,0},{2,3},{3,2},{4,5},{5,4},{6,7},{7,6},{8,9},{9,8},{10,11... | collective-permute-start | bytes 2359304 | tf_op jit(solution)/shard_map/ppermute | solution.py:707
  273.3 38.1 %collective-permute-start.25 = (bf16[1024,768]{1,0:T(8,128)(2,1)}, bf16[1024,768]{1,0:T(8,128)(2,1)S(1)}, u32[]{:S(2)}, u32[]{:S(2)}) collective-permute-start(bf16[1024,768]{1,0:T(8,128)(2,1)} %get-tuple-element.238), channel_id=1, source_target_pairs={{0,1},{1,0},{2,3},{3,2},{4,5},{5,4},{6,7},{7,6},{8,9},{9,8},{10,11... | collective-permute-start | bytes 4718600 | tf_op jit(solution)/shard_map/ppermute | solution.py:707
  275.8 35.6 %collective-permute-start.24 = (bf16[384,1024]{1,0:T(8,128)(2,1)}, bf16[384,1024]{1,0:T(8,128)(2,1)S(1)}, u32[]{:S(2)}, u32[]{:S(2)}) collective-permute-start(bf16[384,1024]{1,0:T(8,128)(2,1)} %add_convert_fusion.4), channel_id=1, source_target_pairs={{0,16},{1,17},{2,18},{3,19},{4,20},{5,21},{6,22},{7,23},{8,24},{9,... | collective-permute-start | bytes 2359304 | tf_op jit(solution)/shard_map/ppermute | solution.py:707
  311.4 21.8 %collective-permute-start.27 = (bf16[512,768]{1,0:T(8,128)(2,1)S(1)}, bf16[512,768]{1,0:T(8,128)(2,1)}, u32[]{:S(2)}, u32[]{:S(2)}) collective-permute-start(bf16[512,768]{1,0:T(8,128)(2,1)S(1)} %get-tuple-element.257), channel_id=1, source_target_pairs={{0,1},{1,0},{2,3},{3,2},{4,5},{5,4},{6,7},{7,6},{8,9},{9,8},{10,11... | collective-permute-start | bytes 2359304 | tf_op jit(solution)/shard_map/ppermute | solution.py:707
  314.2 19.0 %collective-permute-start.26 = (bf16[8,32,768]{2,1,0:T(8,128)(2,1)}, bf16[8,32,768]{2,1,0:T(8,128)(2,1)S(1)}, u32[]{:S(2)}, u32[]{:S(2)}) collective-permute-start(bf16[8,32,768]{2,1,0:T(8,128)(2,1)} %fusion.27), channel_id=1, source_target_pairs={{0,16},{1,17},{2,18},{3,19},{4,20},{5,21},{6,22},{7,23},{8,24},{9,... | collective-permute-start | bytes 1179656 | tf_op jit(solution)/shard_map/ppermute | solution.py:707
  334.0 30.2 %collective-permute-start.29 = (bf16[1024,2048]{1,0:T(8,128)(2,1)}, bf16[1024,2048]{1,0:T(8,128)(2,1)S(1)}, u32[]{:S(2)}, u32[]{:S(2)}) collective-permute-start(bf16[1024,2048]{1,0:T(8,128)(2,1)} %get-tuple-element.266), channel_id=1, source_target_pairs={{0,2},{1,3},{2,0},{3,1},{4,6},{5,7},{6,4},{7,5},{8,10},{9,11},{10,... | collective-permute-start | bytes 12582920 | tf_op jit(solution)/shard_map/ppermute | solution.py:707
  334.0 30.2 %collective-permute-start.30 = (bf16[512,768]{1,0:T(8,128)(2,1)S(1)}, bf16[512,768]{1,0:T(8,128)(2,1)S(1)}, u32[]{:S(2)}, u32[]{:S(2)}) collective-permute-start(bf16[512,768]{1,0:T(8,128)(2,1)S(1)} %get-tuple-element.267), channel_id=1, source_target_pairs={{0,1},{1,0},{2,3},{3,2},{4,5},{5,4},{6,7},{7,6},{8,9},{9,8},{10,11... | collective-permute-start | bytes 2359304 | tf_op jit(solution)/shard_map/ppermute | solution.py:707
  334.9 29.2 %collective-permute-start.28 = (bf16[8,48,768]{2,1,0:T(8,128)(2,1)}, bf16[8,48,768]{2,1,0:T(8,128)(2,1)S(1)}, u32[]{:S(2)}, u32[]{:S(2)}) collective-permute-start(bf16[8,48,768]{2,1,0:T(8,128)(2,1)} %get-tuple-element.265), channel_id=1, source_target_pairs={{0,16},{1,17},{2,18},{3,19},{4,20},{5,21},{6,22},{7,23},{8,24},{9,... | collective-permute-start | bytes 1769480 | tf_op jit(solution)/shard_map/ppermute | solution.py:707
  367.3 33.1 %collective-permute-start.33 = (bf16[2,256,1280]{2,1,0:T(8,128)(2,1)S(1)}, bf16[2,256,1280]{2,1,0:T(8,128)(2,1)S(1)}, u32[]{:S(2)}, u32[]{:S(2)}) collective-permute-start(bf16[2,256,1280]{2,1,0:T(8,128)(2,1)S(1)} %fusion.17), channel_id=1, source_target_pairs={{0,4},{1,5},{2,6},{3,7},{4,0},{5,1},{6,2},{7,3},{8,12},{9,13},{10,... | collective-permute-start | bytes 3932168 | tf_op jit(solution)/shard_map/ppermute | solution.py:707
  368.0 32.4 %collective-permute-start.32 = (bf16[4,1024,128]{2,1,0:T(8,128)(2,1)}, bf16[4,1024,128]{2,1,0:T(8,128)(2,1)}, u32[]{:S(2)}, u32[]{:S(2)}) collective-permute-start(bf16[4,1024,128]{2,1,0:T(8,128)(2,1)} %get-tuple-element.276), channel_id=1, source_target_pairs={{0,1},{1,0},{2,3},{3,2},{4,5},{5,4},{6,7},{7,6},{8,9},{9,8},{10,11... | collective-permute-start | bytes 3145736 | tf_op jit(solution)/shard_map/ppermute | solution.py:707
  368.9 31.5 %collective-permute-start.34 = (bf16[2,256,768]{2,1,0:T(8,128)(2,1)}, bf16[2,256,768]{2,1,0:T(8,128)(2,1)}, u32[]{:S(2)}, u32[]{:S(2)}) collective-permute-start(bf16[2,256,768]{2,1,0:T(8,128)(2,1)} %fusion.25), channel_id=1, source_target_pairs={{0,8},{1,9},{2,10},{3,11},{4,12},{5,13},{6,14},{7,15},{8,0},{9,1},... | collective-permute-start | bytes 2359304 | tf_op jit(solution)/shard_map/ppermute | solution.py:707
  369.0 29.4 %collective-permute-start.31 = (bf16[8,48,768]{2,1,0:T(8,128)(2,1)}, bf16[8,48,768]{2,1,0:T(8,128)(2,1)}, u32[]{:S(2)}, u32[]{:S(2)}) collective-permute-start(bf16[8,48,768]{2,1,0:T(8,128)(2,1)} %get-tuple-element.275), channel_id=1, source_target_pairs={{0,16},{1,17},{2,18},{3,19},{4,20},{5,21},{6,22},{7,23},{8,24},{9,... | collective-permute-start | bytes 1769480 | tf_op jit(solution)/shard_map/ppermute | solution.py:707
  400.5 37.3 %collective-permute-start.36 = (bf16[1024,2048]{1,0:T(8,128)(2,1)}, bf16[1024,2048]{1,0:T(8,128)(2,1)}, u32[]{:S(2)}, u32[]{:S(2)}) collective-permute-start(bf16[1024,2048]{1,0:T(8,128)(2,1)} %normal_rows_sent.1), channel_id=1, source_target_pairs={{0,2},{1,3},{2,0},{3,1},{4,6},{5,7},{6,4},{7,5},{8,10},{9,11},{10,... | collective-permute-start | bytes 12582920 | tf_op jit(solution)/shard_map/ppermute | solution.py:707
  408.0 29.7 %all-to-all-start.3 = ((bf16[8,128,768]{2,1,0:T(8,128)(2,1)}), bf16[8,128,768]{2,1,0:T(8,128)(2,1)S(1)}, u32[]{:S(2)}, u32[]{:S(2)}) async-start(bf16[8,128,768]{2,1,0:T(8,128)(2,1)} %bitcast.124), calls=%async_computation.3 | async-start | bytes 3145728 | tf_op jit(solution)/shard_map/all_to_all | solution.py:710
  411.9 25.9 %collective-permute-start.37 = (bf16[4,1024,128]{2,1,0:T(8,128)(2,1)}, bf16[4,1024,128]{2,1,0:T(8,128)(2,1)}, u32[]{:S(2)}, u32[]{:S(2)}) collective-permute-start(bf16[4,1024,128]{2,1,0:T(8,128)(2,1)} %get-tuple-element.291), channel_id=1, source_target_pairs={{0,1},{1,0},{2,3},{3,2},{4,5},{5,4},{6,7},{7,6},{8,9},{9,8},{10,11... | collective-permute-start | bytes 3145736 | tf_op jit(solution)/shard_map/ppermute | solution.py:707
  413.3 22.2 %collective-permute-start.35 = (bf16[1,1024,128]{2,1,0:T(8,128)(2,1)}, bf16[1,1024,128]{2,1,0:T(8,128)(2,1)S(1)}, u32[]{:S(2)}, u32[]{:S(2)}) collective-permute-start(bf16[1,1024,128]{2,1,0:T(8,128)(2,1)} %slice.258), channel_id=1, source_target_pairs={{0,16},{1,17},{2,18},{3,19},{4,20},{5,21},{6,22},{7,23},{8,24},{9,... | collective-permute-start | bytes 786440 | tf_op jit(solution)/shard_map/ppermute | solution.py:707
  443.9 40.5 %collective-permute-start.38 = (bf16[2,256,1280]{2,1,0:T(8,128)(2,1)}, bf16[2,256,1280]{2,1,0:T(8,128)(2,1)}, u32[]{:S(2)}, u32[]{:S(2)}) collective-permute-start(bf16[2,256,1280]{2,1,0:T(8,128)(2,1)} %fusion.18), channel_id=1, source_target_pairs={{0,4},{1,5},{2,6},{3,7},{4,0},{5,1},{6,2},{7,3},{8,12},{9,13},{10,... | collective-permute-start | bytes 3932168 | tf_op jit(solution)/shard_map/ppermute | solution.py:707
  446.4 34.9 %collective-permute-start.39 = (bf16[2,256,768]{2,1,0:T(8,128)(2,1)}, bf16[2,256,768]{2,1,0:T(8,128)(2,1)S(1)}, u32[]{:S(2)}, u32[]{:S(2)}) collective-permute-start(bf16[2,256,768]{2,1,0:T(8,128)(2,1)} %fusion.26), channel_id=1, source_target_pairs={{0,8},{1,9},{2,10},{3,11},{4,12},{5,13},{6,14},{7,15},{8,0},{9,1},... | collective-permute-start | bytes 2359304 | tf_op jit(solution)/shard_map/ppermute | solution.py:707
  448.1 36.3 %collective-permute-start.40 = (bf16[3,1024,128]{2,1,0:T(8,128)(2,1)S(1)}, bf16[3,1024,128]{2,1,0:T(8,128)(2,1)S(1)}, u32[]{:S(2)}, u32[]{:S(2)}) collective-permute-start(bf16[3,1024,128]{2,1,0:T(8,128)(2,1)S(1)} %slice.259), channel_id=1, source_target_pairs={{0,16},{1,17},{2,18},{3,19},{4,20},{5,21},{6,22},{7,23},{8,24},{9,... | collective-permute-start | bytes 2359304 | tf_op jit(solution)/shard_map/ppermute | solution.py:707
  449.3 35.1 %collective-permute-start.41 = (bf16[384,1024]{1,0:T(8,128)(2,1)}, bf16[384,1024]{1,0:T(8,128)(2,1)S(1)}, u32[]{:S(2)}, u32[]{:S(2)}) collective-permute-start(bf16[384,1024]{1,0:T(8,128)(2,1)} %get-tuple-element.306), channel_id=1, source_target_pairs={{0,1},{1,0},{2,3},{3,2},{4,5},{5,4},{6,7},{7,6},{8,9},{9,8},{10,11... | collective-permute-start | bytes 2359304 | tf_op jit(solution)/shard_map/ppermute | solution.py:707
  512.2 18.4 %collective-permute-start.44 = (bf16[256,1280]{1,0:T(8,128)(2,1)}, bf16[256,1280]{1,0:T(8,128)(2,1)}, u32[]{:S(2)}, u32[]{:S(2)}) collective-permute-start(bf16[256,1280]{1,0:T(8,128)(2,1)} %fusion.21), channel_id=1, source_target_pairs={{0,8},{1,9},{2,10},{3,11},{4,12},{5,13},{6,14},{7,15},{8,0},{9,1},... | collective-permute-start | bytes 1966088 | tf_op jit(solution)/shard_map/ppermute | solution.py:707
  520.0 18.4 %all-to-all-start.5 = ((bf16[8,3,128,128]{3,2,1,0:T(8,128)(2,1)}), bf16[8,3,128,128]{3,2,1,0:T(8,128)(2,1)}, u32[]{:S(2)}, u32[]{:S(2)}) async-start(bf16[8,3,128,128]{3,2,1,0:T(8,128)(2,1)} %bitcast.140), calls=%async_computation.5 | async-start | bytes 1572864 | tf_op jit(solution)/shard_map/all_to_all | solution.py:710
  (64 other events, 858.5 us)

commit v5 on v4

--- a/solution.py
+++ b/solution.py
@@ -1068,7 +1068,7 @@
         (g_qkv, second_swaps(normal_sends), g_out, branch_sends, new_down)
     )
     g_qkv = exchange(g_qkv)
-    branch_last = second_swaps(branch_sends)
+    branch_last = second_swaps([after(part, g_qkv) for part in branch_sends])
     normal_own = whole_rows(normal, normal_got, normal_last)
     _, scaled_own, inv_own = normalize(tokens.astype(F32), vec[0], vec[1])
     d_scaled = normal_own * vec[0]

time: 552 us -> 555 us (level)
    unnamed x127 -> x123, local copies, waits for them, and re-layouts: 14.9 us -> 15 us
  transfers between devices with their start and end apart: 52 -> 52, of which waited for: 23 -> 22; matrix products, arithmetic and copies ran while one was open for 12% -> 12% of each run, Pallas kernels for 34% -> 35%
where the time goes in v5:
time: 555 us; the launch traced here: 549 us
  Pallas kernels  195 us (35%)
  waiting for transfers between devices  188 us (34%)
  starting transfers between devices  73 us (13%)
  other arithmetic  56 us (10%)
  local copies, waits for them, and re-layouts  35.5 us (6%)
    ppermute x46, waiting for transfers between devices, swap(): return lax.ppermute(value, AXES, [(i, i ^ mask) for i in range(total)])  152 us
    pallas_call x3, Pallas kernels, row_blocks(): pl.pallas_call(kernel, grid_spec=pltpu.PrefetchScalarGridSpec(num_scalar_...  51.8 us
    ppermute x46, starting transfers between devices, swap(): return lax.ppermute(value, AXES, [(i, i ^ mask) for i in range(total)])  50.4 us
    pallas_call x1, Pallas kernels, attention(): pl.pallas_call(functools.partial(attention_kernel, masks), grid_spec=pltp...  33.6 us
    pallas_call x1, Pallas kernels, mlp(): pl.pallas_call(functools.partial(mlp_kernel, masks, n_t), grid_spec=pltpu...  33.4 us
    all_to_all x1, waiting for transfers between devices, per_device(): lax.all_to_all(packed, AXES, split_axis=0, concat_axis=0, tiled=True)  27 us
    pallas_call x1, Pallas kernels, grads_cols(): pl.pallas_call(grads_cols_kernel, grid_spec=pltpu.PrefetchScalarGridSpec(...  21.1 us
    pallas_call x1, Pallas kernels, grads_attention(): pl.pallas_call(grads_attention_kernel, grid_spec=pltpu.PrefetchScalarGrid...  18.9 us
  transfers between devices with their start and end apart: 52, of which 22 were waited for; matrix products, arithmetic and copies ran while one was open for 12% of the time, Pallas kernels for 35%

profile of v5, /device:TPU:0, one launch (start us, length us, event | category | flops | bytes accessed | tf_op | source)
XLA Modules:
  0.0 548.8 jit_solution(12227152477972461187)
XLA Ops:
  0.7 3.1 collective-permute-start
  6.8 2.7 collective-permute-start.2
  11.9 2.6 all-to-all-start
  15.2 6.7 %prep.1 = (bf16[8,128,384]{2,1,0:T(8,128)(2,1)}, bf16[8,128,768]{2,1,0:T(8,128)(2,1)}) custom-call(f32[128,3072]{1,0:T(8,128)} %w.3, f32[128,5632]{1,0:T(8,128)} %w.2), custom_call_target="tpu_custom_call" | custom-call | bytes 14417920 | tf_op jit(solution)/shard_map/prep/pallas_call | solution.py:157
  21.9 27.0 %all-to-all-done = f32[32,1,384]{2,1,0:T(1,128)S(1)} async-done(((f32[32,1,384]{2,1,0:T(1,128)}), f32[32,1,384]{2,1,0:T(1,128)S(1)}, u32[]{:S(2)}, u32[]{:S(2)}) %all-to-all-start) | async-done | bytes 49184 | tf_op jit(solution)/shard_map/all_to_all | solution.py:731
  49.9 3.6 all-to-all-start.1
  63.9 13.1 %collective-permute-done.4.rest_5_.rest_1_ = bf16[1,128,1024]{2,1,0:T(8,128)(2,1)} collective-permute-done((bf16[1,128,1024]{2,1,0:T(8,128)(2,1)}, bf16[1,128,1024]{2,1,0:T(8,128)(2,1)}, u32[]{:S(2)}, u32[]{:S(2)}) %collective-permute-start.4) | collective-permute-done | bytes 262176 | tf_op jit(solution)/shard_map/ppermute | solution.py:707
  85.5 36.4 %collective-permute-done.8.rest_11_.rest_7_ = bf16[1,384,1024]{2,1,0:T(8,128)(2,1)S(1)} collective-permute-done((bf16[1,384,1024]{2,1,0:T(8,128)(2,1)S(1)}, bf16[1,384,1024]{2,1,0:T(8,128)(2,1)S(1)}, u32[]{:S(2)}, u32[]{:S(2)}) %collective-permute-start.8) | collective-permute-done | bytes 786464 | tf_op jit(solution)/shard_map/ppermute | solution.py:707
  121.9 2.3 collective-permute-done.6.rest_1_.rest_5_
  128.3 2.3 constant_dynamic-update-slice_fusion.2
  137.3 2.3 constant_dynamic-update-slice_fusion.1
  139.6 19.3 %collective-permute-done.11.rest_5_.rest_9_ = bf16[3,128,768]{2,1,0:T(8,128)(2,1)S(1)} collective-permute-done((bf16[3,128,768]{2,1,0:T(8,128)(2,1)S(1)}, bf16[3,128,768]{2,1,0:T(8,128)(2,1)S(1)}, u32[]{:S(2)}, u32[]{:S(2)}) %collective-permute-start.11) | collective-permute-done | bytes 589856 | tf_op jit(solution)/shard_map/ppermute | solution.py:707
  158.8 6.5 %collective-permute-done.12.rest_6_.rest_10_ = bf16[3,128,768]{2,1,0:T(8,128)(2,1)S(1)} collective-permute-done((bf16[3,128,768]{2,1,0:T(8,128)(2,1)S(1)}, bf16[3,128,768]{2,1,0:T(8,128)(2,1)S(1)}, u32[]{:S(2)}, u32[]{:S(2)}) %collective-permute-start.12) | collective-permute-done | bytes 589856 | tf_op jit(solution)/shard_map/ppermute | solution.py:707
  165.3 7.6 %collective-permute-done.15 = bf16[256,2048]{1,0:T(8,128)(2,1)S(1)} collective-permute-done((bf16[256,2048]{1,0:T(8,128)(2,1)S(1)}, bf16[256,2048]{1,0:T(8,128)(2,1)S(1)}, u32[]{:S(2)}, u32[]{:S(2)}) %collective-permute-start.15) | collective-permute-done | bytes 1048608 | tf_op jit(solution)/shard_map/ppermute | solution.py:707
  175.5 3.7 all-to-all-start.2
  179.4 15.6 %collective-permute-done.16.rest_7_.rest_11_ = bf16[3,128,768]{2,1,0:T(8,128)(2,1)S(1)} collective-permute-done((bf16[3,128,768]{2,1,0:T(8,128)(2,1)S(1)}, bf16[3,128,768]{2,1,0:T(8,128)(2,1)S(1)}, u32[]{:S(2)}, u32[]{:S(2)}) %collective-permute-start.16) | collective-permute-done | bytes 589856 | tf_op jit(solution)/shard_map/ppermute | solution.py:707
  198.7 33.4 %mlp.1 = (bf16[2048,2048]{1,0:T(8,128)(2,1)}, bf16[2048,2048]{1,0:T(8,128)(2,1)}, bf16[2048,768]{1,0:T(8,128)(2,1)}, bf16[2,2048,768]{2,1,0:T(8,128)(2,1)}) custom-call(s32[4]{0:T(128)} %pad_add_fusion.1.here, f32[2,2048]{1,0:T(2,128)} %slice.184.vec, bf16[1024,2048]{1,0:T(8,128)(2,1)} %constant_dynamic-update-slice_fusion.x_even, ...), custom_call_target="tpu_custom_call" | custom-call | tf_op jit(solution)/shard_map/mlp/pallas_call | solution.py:295
  234.4 11.5 %grads_down.1 = (bf16[384,1024]{1,0:T(8,128)(2,1)}, f32[384,1024]{1,0:T(8,128)}, bf16[384,1024]{1,0:T(8,128)(2,1)}, f32[384,1024]{1,0:T(8,128)}) custom-call(s32[2]{0:T(128)} %pad_add_fusion.where, bf16[2048,768]{1,0:T(8,128)(2,1)} %get-tuple-element.223.far.near.hidden, bf16[2048,768]{1,0:T(8,128)(2,1)} %get-tuple-element.223.far.near.hidden, ...), custom_call_target="tpu_custom_call" | custom-call | flops 6442450944 | bytes 16252928 | tf_op jit(solution)/shard_map/grads_down/pallas_call | solution.py:511
  246.0 5.5 %collective-permute-done.22.rest_3_ = bf16[8,128,384]{2,1,0:T(8,128)(2,1)S(1)} collective-permute-done((bf16[8,128,384]{2,1,0:T(8,128)(2,1)S(1)}, bf16[8,128,384]{2,1,0:T(8,128)(2,1)S(1)}, u32[]{:S(2)}, u32[]{:S(2)}) %collective-permute-start.22) | collective-permute-done | bytes 786464 | tf_op jit(solution)/shard_map/ppermute | solution.py:707
  252.1 21.1 %grads_gate_up.1 = (bf16[1024,768]{1,0:T(8,128)(2,1)}, f32[1024,768]{1,0:T(8,128)}, bf16[1024,768]{1,0:T(8,128)(2,1)}, f32[1024,768]{1,0:T(8,128)}) custom-call(s32[2]{0:T(128)} %pad_add_fusion.where, bf16[2048,2048]{1,0:T(8,128)(2,1)} %get-tuple-element.230.left.normed.tall, bf16[2,2048,768]{2,1,0:T(8,128)(2,1)} %get-tuple-element.231.d_sent.d_kept.d_joined, ...), custom_call_target="tpu_custom_call" | custom-call | tf_op jit(solution)/shard_map/grads_gate_up/pallas_call | solution.py:478
  277.8 33.6 %attention.1 = (bf16[2048,256]{1,0:T(8,128)(2,1)}, bf16[2048,768]{1,0:T(8,128)(2,1)}, f32[8,1,768]{2,1,0:T(1,128)}) custom-call(s32[4]{0:T(128)} %pad_add_fusion.1.here, s32[8]{0:T(128)} %convert_element_type.294.lengths, bf16[2048,2048]{1,0:T(8,128)(2,1)} %get-tuple-element.230.left.normed.tall, bf16[2048,2048]{1,0:T(8,128)(2,1)} %get-tuple-element.224.dy_sent.dy_kept.dy, ...), custom_call_target="tpu_custom_call" | custom-call | flops 12884901888 | bytes 41943040 | tf_op jit(solution)/shard_map/attention/pallas_call | solution.py:407
  315.4 16.9 %branch_rows.1 = (bf16[1024,2048]{1,0:T(8,128)(2,1)}, bf16[1024,2048]{1,0:T(8,128)(2,1)}) custom-call(s32[4]{0:T(128)} %pad_add_fusion.1.here, bf16[2048,256]{1,0:T(8,128)(2,1)} %get-tuple-element.263.o.left, bf16[2048,768]{1,0:T(8,128)(2,1)} %get-tuple-element.223.far.near.hidden, bf16[1,128,1024]{2,1,0:T(8,128)(2,1)} %convert_bitcast_fusion.rest_4_.rest_0_, ...), custom_call_target="tpu_custom_call" | custom-call | tf_op jit(solution)/shard_map/branch_rows/pallas_call | solution.py:606
  336.2 18.9 %grads_attention.1 = (bf16[2,4,1024,128]{3,2,1,0:T(8,128)(2,1)}, f32[2,4,1024,128]{3,2,1,0:T(8,128)}) custom-call(s32[2]{0:T(128)} %pad_add_fusion.where, bf16[2048,2048]{1,0:T(8,128)(2,1)} %get-tuple-element.230.left.normed.tall, bf16[2048,768]{1,0:T(8,128)(2,1)} %get-tuple-element.272.d_qkv, bf16[2048,256]{1,0:T(8,128)(2,1)} %get-tuple-element.263.o.left, ...), custom_call_target="tpu_custom_call" | custom-call | tf_op jit(solution)/shard_map/grads_attention/pallas_call | solution.py:565
  355.1 3.2 slice_bitcast_fusion.1
  358.3 5.9 %collective-permute-done.28 = bf16[8,48,768]{2,1,0:T(8,128)(2,1)S(1)} collective-permute-done((bf16[8,48,768]{2,1,0:T(8,128)(2,1)}, bf16[8,48,768]{2,1,0:T(8,128)(2,1)S(1)}, u32[]{:S(2)}, u32[]{:S(2)}) %collective-permute-start.28) | collective-permute-done | bytes 589856 | tf_op jit(solution)/shard_map/ppermute | solution.py:707
  368.9 3.3 collective-permute-start.31
  372.2 17.4 %normal_rows_sent.1 = bf16[1024,2048]{1,0:T(8,128)(2,1)} custom-call(s32[4]{0:T(128)} %pad_add_fusion.1.here, bf16[2048,768]{1,0:T(8,128)(2,1)} %get-tuple-element.272.d_qkv, bf16[2,2048,768]{2,1,0:T(8,128)(2,1)} %get-tuple-element.231.d_sent.d_kept.d_joined, bf16[8,128,384]{2,1,0:T(8,128)(2,1)} %copy-done.6, bf16[8,128,384]{2,1,0:T(8,128)(2,1)} %copy-done.18, ...), custom_call_target="tpu_custom_call" | custom-call | tf_op jit(solution)/shard_map/normal_rows_sent/pallas_call | solution.py:606
  389.6 8.7 %collective-permute-done.31 = bf16[8,48,768]{2,1,0:T(8,128)(2,1)} collective-permute-done((bf16[8,48,768]{2,1,0:T(8,128)(2,1)}, bf16[8,48,768]{2,1,0:T(8,128)(2,1)}, u32[]{:S(2)}, u32[]{:S(2)}) %collective-permute-start.31) | collective-permute-done | bytes 589856 | tf_op jit(solution)/shard_map/ppermute | solution.py:707
  405.1 2.9 fusion
  408.0 3.8 all-to-all-start.3
  415.3 17.5 %normal_rows_kept.1 = bf16[1024,2048]{1,0:T(8,128)(2,1)} custom-call(s32[4]{0:T(128)} %pad_add_fusion.1.here, bf16[2048,768]{1,0:T(8,128)(2,1)} %get-tuple-element.272.d_qkv, bf16[2,2048,768]{2,1,0:T(8,128)(2,1)} %get-tuple-element.231.d_sent.d_kept.d_joined, bf16[8,128,384]{2,1,0:T(8,128)(2,1)} %copy-done.6, bf16[8,128,384]{2,1,0:T(8,128)(2,1)} %copy-done.18, ...), custom_call_target="tpu_custom_call" | custom-call | tf_op jit(solution)/shard_map/normal_rows_kept/pallas_call | solution.py:606
  432.8 2.7 collective-permute-done.35
  437.8 3.0 fusion.26
  440.8 3.1 fusion.18
  450.0 10.3 %finish_gate_up.1 = (f32[128,5632]{1,0:T(8,128)}, f32[128,5632]{1,0:T(8,128)}, f32[128,5632]{1,0:T(8,128)}) custom-call(bf16[8,128,768]{2,1,0:T(8,128)(2,1)} %copy-done.8, f32[128,5632]{1,0:T(8,128)} %w.2, f32[128,5632]{1,0:T(8,128)} %m.2, f32[128,5632]{1,0:T(8,128)} %v.2), custom_call_target="tpu_custom_call" | custom-call | flops 14417920 | bytes 18743296 | tf_op jit(solution)/shard_map/finish_gate_up/pallas_call | solution.py:215
  462.4 2.4 fusion.21
  464.8 15.9 %collective-permute-done.39 = bf16[2,256,768]{2,1,0:T(8,128)(2,1)S(1)} collective-permute-done((bf16[2,256,768]{2,1,0:T(8,128)(2,1)}, bf16[2,256,768]{2,1,0:T(8,128)(2,1)S(1)}, u32[]{:S(2)}, u32[]{:S(2)}) %collective-permute-start.39) | collective-permute-done | bytes 786464 | tf_op jit(solution)/shard_map/ppermute | solution.py:707
  480.7 3.1 collective-permute-done.40
  485.9 2.6 fusion.20
  493.5 5.1 multiply_subtract_fusion
  498.7 3.2 collective-permute-done.42
  501.8 4.2 all-to-all-start.4
  512.0 2.9 multiply_subtract_fusion.1
  515.0 2.7 all-to-all-done.4.g
  517.7 4.7 all-to-all-start.5
  526.9 3.4 all-to-all-done.5
  533.8 7.5 %finish_qkv.1 = (f32[128,3072]{1,0:T(8,128)}, f32[128,3072]{1,0:T(8,128)}, f32[128,3072]{1,0:T(8,128)}) custom-call(bf16[8,3,128,128]{3,2,1,0:T(8,128)(2,1)} %all-to-all-done.4.g, f32[128,3072]{1,0:T(8,128)} %w.3, f32[128,3072]{1,0:T(8,128)} %m.3, f32[128,3072]{1,0:T(8,128)} %v.3), custom_call_target="tpu_custom_call" | custom-call | flops 7864320 | bytes 10223616 | tf_op jit(solution)/shard_map/finish_qkv/pallas_call | solution.py:215
  546.0 2.4 fusion.11
  (287 shorter events, 109.5 us)
Async XLA Ops:
  0.7 48.2 %collective-permute-start = (bf16[256,2048]{1,0:T(8,128)(2,1)}, bf16[256,2048]{1,0:T(8,128)(2,1)}, u32[]{:S(2)}, u32[]{:S(2)}) collective-permute-start(bf16[256,2048]{1,0:T(8,128)(2,1)} %param.18), channel_id=1, source_target_pairs={{0,8},{1,9},{2,10},{3,11},{4,12},{5,13},{6,14},{7,15},{8,0},{9,1},... | collective-permute-start | bytes 3145736 | tf_op jit(solution)/shard_map/ppermute | solution.py:707
  3.8 45.1 %collective-permute-start.1 = (bf16[256,2048]{1,0:T(8,128)(2,1)}, bf16[256,2048]{1,0:T(8,128)(2,1)}, u32[]{:S(2)}, u32[]{:S(2)}) collective-permute-start(bf16[256,2048]{1,0:T(8,128)(2,1)} %param.18), channel_id=1, source_target_pairs={{0,4},{1,5},{2,6},{3,7},{4,0},{5,1},{6,2},{7,3},{8,12},{9,13},{10,... | collective-permute-start | bytes 3145736 | tf_op jit(solution)/shard_map/ppermute | solution.py:707
  6.8 42.0 %collective-permute-start.2 = (bf16[1,384,1024]{2,1,0:T(8,128)(2,1)S(1)}, bf16[1,384,1024]{2,1,0:T(8,128)(2,1)S(1)}, u32[]{:S(2)}, u32[]{:S(2)}) collective-permute-start(bf16[1,384,1024]{2,1,0:T(8,128)(2,1)S(1)} %pad_bitcast_fusion.rest_8_.rest_4_), channel_id=1, source_target_pairs={{0,16},{1,17},{2,18},{3,19},{4,20},{5,21},{6,22},{7,23},{8,24},{9,... | collective-permute-start | bytes 2359304 | tf_op jit(solution)/shard_map/ppermute | solution.py:707
  9.5 39.4 %collective-permute-start.3 = (bf16[1,384,1024]{2,1,0:T(8,128)(2,1)S(1)}, bf16[1,384,1024]{2,1,0:T(8,128)(2,1)S(1)}, u32[]{:S(2)}, u32[]{:S(2)}) collective-permute-start(bf16[1,384,1024]{2,1,0:T(8,128)(2,1)S(1)} %pad_bitcast_fusion.rest_8_.rest_4_), channel_id=1, source_target_pairs={{0,1},{1,0},{2,3},{3,2},{4,5},{5,4},{6,7},{7,6},{8,9},{9,8},{10,11... | collective-permute-start | bytes 2359304 | tf_op jit(solution)/shard_map/ppermute | solution.py:707
  11.9 36.9 %all-to-all-start = ((f32[32,1,384]{2,1,0:T(1,128)}), f32[32,1,384]{2,1,0:T(1,128)S(1)}, u32[]{:S(2)}, u32[]{:S(2)}) async-start(f32[32,1,384]{2,1,0:T(1,128)} %broadcast_in_dim.60), calls=%async_computation | async-start | bytes 98304 | tf_op jit(solution)/shard_map/all_to_all | solution.py:731
  49.9 29.2 %all-to-all-start.1 = ((bf16[8,128,768]{2,1,0:T(8,128)(2,1)}), bf16[8,128,768]{2,1,0:T(8,128)(2,1)S(1)}, u32[]{:S(2)}, u32[]{:S(2)}) async-start(bf16[8,128,768]{2,1,0:T(8,128)(2,1)} %get-tuple-element.182), calls=%async_computation.1 | async-start | bytes 3145728 | tf_op jit(solution)/shard_map/all_to_all | solution.py:710
  56.7 20.4 %collective-permute-start.4 = (bf16[1,128,1024]{2,1,0:T(8,128)(2,1)}, bf16[1,128,1024]{2,1,0:T(8,128)(2,1)}, u32[]{:S(2)}, u32[]{:S(2)}) collective-permute-start(bf16[1,128,1024]{2,1,0:T(8,128)(2,1)} %convert_bitcast_fusion.rest_4_.rest_0_), channel_id=1, source_target_pairs={{0,16},{1,17},{2,18},{3,19},{4,20},{5,21},{6,22},{7,23},{8,24},{9,... | collective-permute-start | bytes 786440 | tf_op jit(solution)/shard_map/ppermute | solution.py:707
  57.0 20.1 %collective-permute-start.5 = (bf16[1,128,1024]{2,1,0:T(8,128)(2,1)}, bf16[1,128,1024]{2,1,0:T(8,128)(2,1)}, u32[]{:S(2)}, u32[]{:S(2)}) collective-permute-start(bf16[1,128,1024]{2,1,0:T(8,128)(2,1)} %convert_bitcast_fusion.rest_4_.rest_0_), channel_id=1, source_target_pairs={{0,1},{1,0},{2,3},{3,2},{4,5},{5,4},{6,7},{7,6},{8,9},{9,8},{10,11... | collective-permute-start | bytes 786440 | tf_op jit(solution)/shard_map/ppermute | solution.py:707
  79.1 45.1 %collective-permute-start.10 = (bf16[256,2048]{1,0:T(8,128)(2,1)}, bf16[256,2048]{1,0:T(8,128)(2,1)S(1)}, u32[]{:S(2)}, u32[]{:S(2)}) collective-permute-start(bf16[256,2048]{1,0:T(8,128)(2,1)} %param.19), channel_id=1, source_target_pairs={{0,4},{1,5},{2,6},{3,7},{4,0},{5,1},{6,2},{7,3},{8,12},{9,13},{10,... | collective-permute-start | bytes 3145736 | tf_op jit(solution)/shard_map/ppermute | solution.py:707
  80.5 45.7 %collective-permute-start.9 = (bf16[256,2048]{1,0:T(8,128)(2,1)}, bf16[256,2048]{1,0:T(8,128)(2,1)S(1)}, u32[]{:S(2)}, u32[]{:S(2)}) collective-permute-start(bf16[256,2048]{1,0:T(8,128)(2,1)} %param.19), channel_id=1, source_target_pairs={{0,8},{1,9},{2,10},{3,11},{4,12},{5,13},{6,14},{7,15},{8,0},{9,1},... | collective-permute-start | bytes 3145736 | tf_op jit(solution)/shard_map/ppermute | solution.py:707
  81.1 43.1 %collective-permute-start.6 = (bf16[5,128,768]{2,1,0:T(8,128)(2,1)S(1)}, bf16[5,128,768]{2,1,0:T(8,128)(2,1)S(1)}, u32[]{:S(2)}, u32[]{:S(2)}) collective-permute-start(bf16[5,128,768]{2,1,0:T(8,128)(2,1)S(1)} %slice.189.rest_0_.rest_4_), channel_id=1, source_target_pairs={{0,16},{1,17},{2,18},{3,19},{4,20},{5,21},{6,22},{7,23},{8,24},{9,... | collective-permute-start | bytes 2949128 | tf_op jit(solution)/shard_map/ppermute | solution.py:707
  82.3 41.9 %collective-permute-start.7 = (bf16[5,128,768]{2,1,0:T(8,128)(2,1)S(1)}, bf16[5,128,768]{2,1,0:T(8,128)(2,1)S(1)}, u32[]{:S(2)}, u32[]{:S(2)}) collective-permute-start(bf16[5,128,768]{2,1,0:T(8,128)(2,1)S(1)} %slice.189.rest_0_.rest_4_), channel_id=1, source_target_pairs={{0,1},{1,0},{2,3},{3,2},{4,5},{5,4},{6,7},{7,6},{8,9},{9,8},{10,11... | collective-permute-start | bytes 2949128 | tf_op jit(solution)/shard_map/ppermute | solution.py:707
  82.7 39.2 %collective-permute-start.8 = (bf16[1,384,1024]{2,1,0:T(8,128)(2,1)S(1)}, bf16[1,384,1024]{2,1,0:T(8,128)(2,1)S(1)}, u32[]{:S(2)}, u32[]{:S(2)}) collective-permute-start(bf16[1,384,1024]{2,1,0:T(8,128)(2,1)S(1)} %collective-permute-done.2.rest_9_.rest_5_), channel_id=1, source_target_pairs={{0,1},{1,0},{2,3},{3,2},{4,5},{5,4},{6,7},{7,6},{8,9},{9,8},{10,11... | collective-permute-start | bytes 2359304 | tf_op jit(solution)/shard_map/ppermute | solution.py:707
  126.2 39.1 %collective-permute-start.14 = (bf16[256,2048]{1,0:T(8,128)(2,1)}, bf16[256,2048]{1,0:T(8,128)(2,1)S(1)}, u32[]{:S(2)}, u32[]{:S(2)}) collective-permute-start(bf16[256,2048]{1,0:T(8,128)(2,1)} %collective-permute-done), channel_id=1, source_target_pairs={{0,4},{1,5},{2,6},{3,7},{4,0},{5,1},{6,2},{7,3},{8,12},{9,13},{10,... | collective-permute-start | bytes 3145736 | tf_op jit(solution)/shard_map/ppermute | solution.py:707
  126.8 46.2 %collective-permute-start.15 = (bf16[256,2048]{1,0:T(8,128)(2,1)S(1)}, bf16[256,2048]{1,0:T(8,128)(2,1)S(1)}, u32[]{:S(2)}, u32[]{:S(2)}) collective-permute-start(bf16[256,2048]{1,0:T(8,128)(2,1)S(1)} %collective-permute-done.9), channel_id=1, source_target_pairs={{0,4},{1,5},{2,6},{3,7},{4,0},{5,1},{6,2},{7,3},{8,12},{9,13},{10,... | collective-permute-start | bytes 3145736 | tf_op jit(solution)/shard_map/ppermute | solution.py:707
  130.6 34.7 %collective-permute-start.13 = (bf16[5,128,768]{2,1,0:T(8,128)(2,1)S(1)}, bf16[5,128,768]{2,1,0:T(8,128)(2,1)S(1)}, u32[]{:S(2)}, u32[]{:S(2)}) collective-permute-start(bf16[5,128,768]{2,1,0:T(8,128)(2,1)S(1)} %collective-permute-done.6.rest_1_.rest_5_), channel_id=1, source_target_pairs={{0,1},{1,0},{2,3},{3,2},{4,5},{5,4},{6,7},{7,6},{8,9},{9,8},{10,11... | collective-permute-start | bytes 2949128 | tf_op jit(solution)/shard_map/ppermute | solution.py:707
  132.1 26.8 %collective-permute-start.11 = (bf16[3,128,768]{2,1,0:T(8,128)(2,1)S(1)}, bf16[3,128,768]{2,1,0:T(8,128)(2,1)S(1)}, u32[]{:S(2)}, u32[]{:S(2)}) collective-permute-start(bf16[3,128,768]{2,1,0:T(8,128)(2,1)S(1)} %slice.190.rest_4_.rest_8_), channel_id=1, source_target_pairs={{0,16},{1,17},{2,18},{3,19},{4,20},{5,21},{6,22},{7,23},{8,24},{9,... | collective-permute-start | bytes 1769480 | tf_op jit(solution)/shard_map/ppermute | solution.py:707
  133.8 31.5 %collective-permute-start.12 = (bf16[3,128,768]{2,1,0:T(8,128)(2,1)S(1)}, bf16[3,128,768]{2,1,0:T(8,128)(2,1)S(1)}, u32[]{:S(2)}, u32[]{:S(2)}) collective-permute-start(bf16[3,128,768]{2,1,0:T(8,128)(2,1)S(1)} %slice.190.rest_4_.rest_8_), channel_id=1, source_target_pairs={{0,1},{1,0},{2,3},{3,2},{4,5},{5,4},{6,7},{7,6},{8,9},{9,8},{10,11... | collective-permute-start | bytes 1769480 | tf_op jit(solution)/shard_map/ppermute | solution.py:707
  174.0 21.0 %collective-permute-start.18 = (bf16[1024,2048]{1,0:T(8,128)(2,1)}, bf16[1024,2048]{1,0:T(8,128)(2,1)}, u32[]{:S(2)}, u32[]{:S(2)}) collective-permute-start(bf16[1024,2048]{1,0:T(8,128)(2,1)} %constant_dynamic-update-slice_fusion.4.dy_even), channel_id=1, source_target_pairs={{0,2},{1,3},{2,0},{3,1},{4,6},{5,7},{6,4},{7,5},{8,10},{9,11},{10,... | collective-permute-start | bytes 12582920 | tf_op jit(solution)/shard_map/ppermute | solution.py:707
  175.0 20.0 %collective-permute-start.17 = (bf16[1024,2048]{1,0:T(8,128)(2,1)}, bf16[1024,2048]{1,0:T(8,128)(2,1)}, u32[]{:S(2)}, u32[]{:S(2)}) collective-permute-start(bf16[1024,2048]{1,0:T(8,128)(2,1)} %constant_dynamic-update-slice_fusion.x_even), channel_id=1, source_target_pairs={{0,2},{1,3},{2,0},{3,1},{4,6},{5,7},{6,4},{7,5},{8,10},{9,11},{10,... | collective-permute-start | bytes 12582920 | tf_op jit(solution)/shard_map/ppermute | solution.py:707
  175.5 19.5 %all-to-all-start.2 = ((bf16[8,128,384]{2,1,0:T(8,128)(2,1)}), bf16[8,128,384]{2,1,0:T(8,128)(2,1)S(1)}, u32[]{:S(2)}, u32[]{:S(2)}) async-start(bf16[8,128,384]{2,1,0:T(8,128)(2,1)} %get-tuple-element.198), calls=%async_computation.2 | async-start | bytes 1572864 | tf_op jit(solution)/shard_map/all_to_all | solution.py:710
  195.0 37.1 %collective-permute-start.19 = (bf16[8,128,384]{2,1,0:T(8,128)(2,1)S(1)}, bf16[8,128,384]{2,1,0:T(8,128)(2,1)S(1)}, u32[]{:S(2)}, u32[]{:S(2)}) collective-permute-start(bf16[8,128,384]{2,1,0:T(8,128)(2,1)S(1)} %all-to-all-done.2.rest_0_), channel_id=1, source_target_pairs={{0,16},{1,17},{2,18},{3,19},{4,20},{5,21},{6,22},{7,23},{8,24},{9,... | collective-permute-start | bytes 2359304 | tf_op jit(solution)/shard_map/ppermute | solution.py:707
  196.0 36.2 %collective-permute-start.20 = (bf16[8,128,384]{2,1,0:T(8,128)(2,1)S(1)}, bf16[8,128,384]{2,1,0:T(8,128)(2,1)S(1)}, u32[]{:S(2)}, u32[]{:S(2)}) collective-permute-start(bf16[8,128,384]{2,1,0:T(8,128)(2,1)S(1)} %all-to-all-done.2.rest_0_), channel_id=1, source_target_pairs={{0,1},{1,0},{2,3},{3,2},{4,5},{5,4},{6,7},{7,6},{8,9},{9,8},{10,11... | collective-permute-start | bytes 2359304 | tf_op jit(solution)/shard_map/ppermute | solution.py:707
  196.7 35.3 %collective-permute-start.21 = (bf16[1,128,1024]{2,1,0:T(8,128)(2,1)}, bf16[1,128,1024]{2,1,0:T(8,128)(2,1)S(1)}, u32[]{:S(2)}, u32[]{:S(2)}) collective-permute-start(bf16[1,128,1024]{2,1,0:T(8,128)(2,1)} %collective-permute-done.4.rest_5_.rest_1_), channel_id=1, source_target_pairs={{0,1},{1,0},{2,3},{3,2},{4,5},{5,4},{6,7},{7,6},{8,9},{9,8},{10,11... | collective-permute-start | bytes 786440 | tf_op jit(solution)/shard_map/ppermute | solution.py:707
  233.1 18.4 %collective-permute-start.22 = (bf16[8,128,384]{2,1,0:T(8,128)(2,1)S(1)}, bf16[8,128,384]{2,1,0:T(8,128)(2,1)S(1)}, u32[]{:S(2)}, u32[]{:S(2)}) collective-permute-start(bf16[8,128,384]{2,1,0:T(8,128)(2,1)S(1)} %collective-permute-done.19.rest_1_), channel_id=1, source_target_pairs={{0,1},{1,0},{2,3},{3,2},{4,5},{5,4},{6,7},{7,6},{8,9},{9,8},{10,11... | collective-permute-start | bytes 2359304 | tf_op jit(solution)/shard_map/ppermute | solution.py:707
  251.5 21.8 %collective-permute-start.23 = (bf16[384,1024]{1,0:T(8,128)(2,1)}, bf16[384,1024]{1,0:T(8,128)(2,1)S(1)}, u32[]{:S(2)}, u32[]{:S(2)}) collective-permute-start(bf16[384,1024]{1,0:T(8,128)(2,1)} %get-tuple-element.234), channel_id=1, source_target_pairs={{0,1},{1,0},{2,3},{3,2},{4,5},{5,4},{6,7},{7,6},{8,9},{9,8},{10,11... | collective-permute-start | bytes 2359304 | tf_op jit(solution)/shard_map/ppermute | solution.py:707
  273.3 38.1 %collective-permute-start.25 = (bf16[1024,768]{1,0:T(8,128)(2,1)}, bf16[1024,768]{1,0:T(8,128)(2,1)S(1)}, u32[]{:S(2)}, u32[]{:S(2)}) collective-permute-start(bf16[1024,768]{1,0:T(8,128)(2,1)} %get-tuple-element.240), channel_id=1, source_target_pairs={{0,1},{1,0},{2,3},{3,2},{4,5},{5,4},{6,7},{7,6},{8,9},{9,8},{10,11... | collective-permute-start | bytes 4718600 | tf_op jit(solution)/shard_map/ppermute | solution.py:707
  275.7 35.6 %collective-permute-start.24 = (bf16[384,1024]{1,0:T(8,128)(2,1)}, bf16[384,1024]{1,0:T(8,128)(2,1)S(1)}, u32[]{:S(2)}, u32[]{:S(2)}) collective-permute-start(bf16[384,1024]{1,0:T(8,128)(2,1)} %add_convert_fusion.4), channel_id=1, source_target_pairs={{0,16},{1,17},{2,18},{3,19},{4,20},{5,21},{6,22},{7,23},{8,24},{9,... | collective-permute-start | bytes 2359304 | tf_op jit(solution)/shard_map/ppermute | solution.py:707
  311.4 21.9 %collective-permute-start.27 = (bf16[512,768]{1,0:T(8,128)(2,1)S(1)}, bf16[512,768]{1,0:T(8,128)(2,1)}, u32[]{:S(2)}, u32[]{:S(2)}) collective-permute-start(bf16[512,768]{1,0:T(8,128)(2,1)S(1)} %get-tuple-element.259), channel_id=1, source_target_pairs={{0,1},{1,0},{2,3},{3,2},{4,5},{5,4},{6,7},{7,6},{8,9},{9,8},{10,11... | collective-permute-start | bytes 2359304 | tf_op jit(solution)/shard_map/ppermute | solution.py:707
  314.2 19.1 %collective-permute-start.26 = (bf16[8,32,768]{2,1,0:T(8,128)(2,1)}, bf16[8,32,768]{2,1,0:T(8,128)(2,1)S(1)}, u32[]{:S(2)}, u32[]{:S(2)}) collective-permute-start(bf16[8,32,768]{2,1,0:T(8,128)(2,1)} %fusion.27), channel_id=1, source_target_pairs={{0,16},{1,17},{2,18},{3,19},{4,20},{5,21},{6,22},{7,23},{8,24},{9,... | collective-permute-start | bytes 1179656 | tf_op jit(solution)/shard_map/ppermute | solution.py:707
  334.0 30.1 %collective-permute-start.29 = (bf16[1024,2048]{1,0:T(8,128)(2,1)}, bf16[1024,2048]{1,0:T(8,128)(2,1)S(1)}, u32[]{:S(2)}, u32[]{:S(2)}) collective-permute-start(bf16[1024,2048]{1,0:T(8,128)(2,1)} %get-tuple-element.268), channel_id=1, source_target_pairs={{0,2},{1,3},{2,0},{3,1},{4,6},{5,7},{6,4},{7,5},{8,10},{9,11},{10,... | collective-permute-start | bytes 12582920 | tf_op jit(solution)/shard_map/ppermute | solution.py:707
  334.0 30.1 %collective-permute-start.30 = (bf16[512,768]{1,0:T(8,128)(2,1)S(1)}, bf16[512,768]{1,0:T(8,128)(2,1)S(1)}, u32[]{:S(2)}, u32[]{:S(2)}) collective-permute-start(bf16[512,768]{1,0:T(8,128)(2,1)S(1)} %get-tuple-element.269), channel_id=1, source_target_pairs={{0,1},{1,0},{2,3},{3,2},{4,5},{5,4},{6,7},{7,6},{8,9},{9,8},{10,11... | collective-permute-start | bytes 2359304 | tf_op jit(solution)/shard_map/ppermute | solution.py:707
  334.9 29.2 %collective-permute-start.28 = (bf16[8,48,768]{2,1,0:T(8,128)(2,1)}, bf16[8,48,768]{2,1,0:T(8,128)(2,1)S(1)}, u32[]{:S(2)}, u32[]{:S(2)}) collective-permute-start(bf16[8,48,768]{2,1,0:T(8,128)(2,1)} %get-tuple-element.267), channel_id=1, source_target_pairs={{0,16},{1,17},{2,18},{3,19},{4,20},{5,21},{6,22},{7,23},{8,24},{9,... | collective-permute-start | bytes 1769480 | tf_op jit(solution)/shard_map/ppermute | solution.py:707
  367.3 33.1 %collective-permute-start.33 = (bf16[2,256,1280]{2,1,0:T(8,128)(2,1)S(1)}, bf16[2,256,1280]{2,1,0:T(8,128)(2,1)S(1)}, u32[]{:S(2)}, u32[]{:S(2)}) collective-permute-start(bf16[2,256,1280]{2,1,0:T(8,128)(2,1)S(1)} %fusion.17), channel_id=1, source_target_pairs={{0,4},{1,5},{2,6},{3,7},{4,0},{5,1},{6,2},{7,3},{8,12},{9,13},{10,... | collective-permute-start | bytes 3932168 | tf_op jit(solution)/shard_map/ppermute | solution.py:707
  368.1 32.3 %collective-permute-start.32 = (bf16[4,1024,128]{2,1,0:T(8,128)(2,1)}, bf16[4,1024,128]{2,1,0:T(8,128)(2,1)}, u32[]{:S(2)}, u32[]{:S(2)}) collective-permute-start(bf16[4,1024,128]{2,1,0:T(8,128)(2,1)} %get-tuple-element.278), channel_id=1, source_target_pairs={{0,1},{1,0},{2,3},{3,2},{4,5},{5,4},{6,7},{7,6},{8,9},{9,8},{10,11... | collective-permute-start | bytes 3145736 | tf_op jit(solution)/shard_map/ppermute | solution.py:707
  368.9 31.5 %collective-permute-start.34 = (bf16[2,256,768]{2,1,0:T(8,128)(2,1)}, bf16[2,256,768]{2,1,0:T(8,128)(2,1)}, u32[]{:S(2)}, u32[]{:S(2)}) collective-permute-start(bf16[2,256,768]{2,1,0:T(8,128)(2,1)} %fusion.25), channel_id=1, source_target_pairs={{0,8},{1,9},{2,10},{3,11},{4,12},{5,13},{6,14},{7,15},{8,0},{9,1},... | collective-permute-start | bytes 2359304 | tf_op jit(solution)/shard_map/ppermute | solution.py:707
  368.9 29.4 %collective-permute-start.31 = (bf16[8,48,768]{2,1,0:T(8,128)(2,1)}, bf16[8,48,768]{2,1,0:T(8,128)(2,1)}, u32[]{:S(2)}, u32[]{:S(2)}) collective-permute-start(bf16[8,48,768]{2,1,0:T(8,128)(2,1)} %get-tuple-element.277), channel_id=1, source_target_pairs={{0,16},{1,17},{2,18},{3,19},{4,20},{5,21},{6,22},{7,23},{8,24},{9,... | collective-permute-start | bytes 1769480 | tf_op jit(solution)/shard_map/ppermute | solution.py:707
  400.5 37.3 %collective-permute-start.36 = (bf16[1024,2048]{1,0:T(8,128)(2,1)}, bf16[1024,2048]{1,0:T(8,128)(2,1)}, u32[]{:S(2)}, u32[]{:S(2)}) collective-permute-start(bf16[1024,2048]{1,0:T(8,128)(2,1)} %normal_rows_sent.1), channel_id=1, source_target_pairs={{0,2},{1,3},{2,0},{3,1},{4,6},{5,7},{6,4},{7,5},{8,10},{9,11},{10,... | collective-permute-start | bytes 12582920 | tf_op jit(solution)/shard_map/ppermute | solution.py:707
  408.0 29.7 %all-to-all-start.3 = ((bf16[8,128,768]{2,1,0:T(8,128)(2,1)}), bf16[8,128,768]{2,1,0:T(8,128)(2,1)S(1)}, u32[]{:S(2)}, u32[]{:S(2)}) async-start(bf16[8,128,768]{2,1,0:T(8,128)(2,1)} %bitcast.124), calls=%async_computation.3 | async-start | bytes 3145728 | tf_op jit(solution)/shard_map/all_to_all | solution.py:710
  411.9 25.9 %collective-permute-start.37 = (bf16[4,1024,128]{2,1,0:T(8,128)(2,1)}, bf16[4,1024,128]{2,1,0:T(8,128)(2,1)}, u32[]{:S(2)}, u32[]{:S(2)}) collective-permute-start(bf16[4,1024,128]{2,1,0:T(8,128)(2,1)} %get-tuple-element.293), channel_id=1, source_target_pairs={{0,1},{1,0},{2,3},{3,2},{4,5},{5,4},{6,7},{7,6},{8,9},{9,8},{10,11... | collective-permute-start | bytes 3145736 | tf_op jit(solution)/shard_map/ppermute | solution.py:707
  413.3 22.2 %collective-permute-start.35 = (bf16[1,1024,128]{2,1,0:T(8,128)(2,1)}, bf16[1,1024,128]{2,1,0:T(8,128)(2,1)S(1)}, u32[]{:S(2)}, u32[]{:S(2)}) collective-permute-start(bf16[1,1024,128]{2,1,0:T(8,128)(2,1)} %slice.258), channel_id=1, source_target_pairs={{0,16},{1,17},{2,18},{3,19},{4,20},{5,21},{6,22},{7,23},{8,24},{9,... | collective-permute-start | bytes 786440 | tf_op jit(solution)/shard_map/ppermute | solution.py:707
  443.9 39.9 %collective-permute-start.38 = (bf16[2,256,1280]{2,1,0:T(8,128)(2,1)}, bf16[2,256,1280]{2,1,0:T(8,128)(2,1)}, u32[]{:S(2)}, u32[]{:S(2)}) collective-permute-start(bf16[2,256,1280]{2,1,0:T(8,128)(2,1)} %fusion.18), channel_id=1, source_target_pairs={{0,4},{1,5},{2,6},{3,7},{4,0},{5,1},{6,2},{7,3},{8,12},{9,13},{10,... | collective-permute-start | bytes 3932168 | tf_op jit(solution)/shard_map/ppermute | solution.py:707
  445.8 34.9 %collective-permute-start.39 = (bf16[2,256,768]{2,1,0:T(8,128)(2,1)}, bf16[2,256,768]{2,1,0:T(8,128)(2,1)S(1)}, u32[]{:S(2)}, u32[]{:S(2)}) collective-permute-start(bf16[2,256,768]{2,1,0:T(8,128)(2,1)} %fusion.26), channel_id=1, source_target_pairs={{0,8},{1,9},{2,10},{3,11},{4,12},{5,13},{6,14},{7,15},{8,0},{9,1},... | collective-permute-start | bytes 2359304 | tf_op jit(solution)/shard_map/ppermute | solution.py:707
  447.4 36.3 %collective-permute-start.40 = (bf16[3,1024,128]{2,1,0:T(8,128)(2,1)S(1)}, bf16[3,1024,128]{2,1,0:T(8,128)(2,1)S(1)}, u32[]{:S(2)}, u32[]{:S(2)}) collective-permute-start(bf16[3,1024,128]{2,1,0:T(8,128)(2,1)S(1)} %slice.259), channel_id=1, source_target_pairs={{0,16},{1,17},{2,18},{3,19},{4,20},{5,21},{6,22},{7,23},{8,24},{9,... | collective-permute-start | bytes 2359304 | tf_op jit(solution)/shard_map/ppermute | solution.py:707
  448.7 35.1 %collective-permute-start.41 = (bf16[384,1024]{1,0:T(8,128)(2,1)}, bf16[384,1024]{1,0:T(8,128)(2,1)S(1)}, u32[]{:S(2)}, u32[]{:S(2)}) collective-permute-start(bf16[384,1024]{1,0:T(8,128)(2,1)} %get-tuple-element.308), channel_id=1, source_target_pairs={{0,1},{1,0},{2,3},{3,2},{4,5},{5,4},{6,7},{7,6},{8,9},{9,8},{10,11... | collective-permute-start | bytes 2359304 | tf_op jit(solution)/shard_map/ppermute | solution.py:707
  501.8 15.9 %all-to-all-start.4 = ((bf16[8,3,128,128]{3,2,1,0:T(8,128)(2,1)}), bf16[8,3,128,128]{3,2,1,0:T(8,128)(2,1)}, u32[]{:S(2)}, u32[]{:S(2)}) async-start(bf16[8,3,128,128]{3,2,1,0:T(8,128)(2,1)} %bitcast.115), calls=%async_computation.4 | async-start | bytes 1572864 | tf_op jit(solution)/shard_map/all_to_all | solution.py:710
  522.4 20.4 %collective-permute-start.44 = (bf16[256,1280]{1,0:T(8,128)(2,1)}, bf16[256,1280]{1,0:T(8,128)(2,1)}, u32[]{:S(2)}, u32[]{:S(2)}) collective-permute-start(bf16[256,1280]{1,0:T(8,128)(2,1)} %fusion.21), channel_id=1, source_target_pairs={{0,8},{1,9},{2,10},{3,11},{4,12},{5,13},{6,14},{7,15},{8,0},{9,1},... | collective-permute-start | bytes 1966088 | tf_op jit(solution)/shard_map/ppermute | solution.py:707
  524.2 17.1 %collective-permute-start.45 = (bf16[256,768]{1,0:T(8,128)(2,1)}, bf16[256,768]{1,0:T(8,128)(2,1)S(1)}, u32[]{:S(2)}, u32[]{:S(2)}) collective-permute-start(bf16[256,768]{1,0:T(8,128)(2,1)} %fusion.31), channel_id=1, source_target_pairs={{0,4},{1,5},{2,6},{3,7},{4,0},{5,1},{6,2},{7,3},{8,12},{9,13},{10,... | collective-permute-start | bytes 1179656 | tf_op jit(solution)/shard_map/ppermute | solution.py:707
  (62 other events, 867.8 us)

commit v6 on v4

--- a/solution.py
+++ b/solution.py
@@ -235,7 +235,7 @@
 def mlp_kernel(masks, steps, here, vec, x_even, x_odd, dy_even, dy_odd, *rest):
     count = len(masks)
     gu_parts, down_parts = rest[: 2 * count], rest[2 * count : 3 * count]
-    normed, grads_out, hidden, d_joined, gu, down, rows, sems, row_sems = rest[-9:]
+    normed, grads_out, hidden, d_joined, gu, down, rows, lows, sems, row_sems = rest[-10:]
     step = pl.program_id(0)
     slot = normed.shape[0]
 
@@ -244,34 +244,39 @@
         sources = (x_odd, dy_odd) if n % 2 else (x_even, dy_even)
         return [
             pltpu.make_async_copy(
-                source.at[spot], rows.at[n % 2, pl.ds(m * slot, slot)], row_sems.at[n % 2, m]
+                source.at[spot], rows.at[n % 3, pl.ds(m * slot, slot)], row_sems.at[n % 3, m]
             )
             for m, source in enumerate(sources)
         ]
 
+    def prepared(n):
+        return normalize(rows[n, :slot].astype(F32), vec[0:1], vec[1:2])[0].astype(BF16)
+
     @pl.when(step == 0)
     def _():
-        for copy in fetch(0):
+        for copy in fetch(0) + fetch(1):
             copy.start()
         copies = place_gu(here, gu_parts, masks, gu, sems, 0)
         target = by_columns(down, down.shape[4] // 2)
         copies += place(here, down_parts, masks, target, sems, 2 * count)
-        for copy in copies:
+        for copy in copies + fetch(0):
             copy.wait()
+        lows[0] = prepared(0)
 
     for n in range(steps):
 
         @pl.when(step == n)
         def _(n=n):
+            if n + 2 < steps:
+                for copy in fetch(n + 2):
+                    copy.start()
             if n + 1 < steps:
                 for copy in fetch(n + 1):
-                    copy.start()
-            for copy in fetch(n):
-                copy.wait()
-
-    now = step % 2
-    low = normalize(rows[now, :slot].astype(F32), vec[0:1], vec[1:2])[0].astype(BF16)
-    dy = rows[now, slot:]
+                    copy.wait()
+
+    low = lows[step % 2]
+    dy = rows[step % 3, slot:]
+    lows[(step + 1) % 2] = prepared((step + 1) % 3)
     normed[...] = low
     grads_out[...] = dy
     wide = gu.shape[5]
@@ -308,9 +313,10 @@
             scratch_shapes=[
                 pltpu.VMEM((n_y, n_a, n_t, n_b, w_rows, wide), BF16),
                 pltpu.VMEM((n_a, 1, n_b, unit, width), BF16),
-                pltpu.VMEM((2, 2 * slot, width), BF16),
+                pltpu.VMEM((3, 2 * slot, width), BF16),
+                pltpu.VMEM((2, slot, width), BF16),
                 pltpu.SemaphoreType.DMA((3 * len(masks),)),
-                pltpu.SemaphoreType.DMA((2, 2)),
+                pltpu.SemaphoreType.DMA((3, 2)),
             ],
         ),
         out_shape=[

time: 552 us -> 554 us (level)
  no operation moved by 1% of the time
where the time goes in v6:
time: 554 us; the launch traced here: 548 us
  Pallas kernels  196 us (35%)
  waiting for transfers between devices  185 us (33%)
  starting transfers between devices  72.4 us (13%)
  other arithmetic  56 us (10%)
  local copies, waits for them, and re-layouts  35.9 us (6%)
    ppermute x46, waiting for transfers between devices, swap(): return lax.ppermute(value, AXES, [(i, i ^ mask) for i in range(total)])  154 us
    pallas_call x3, Pallas kernels, row_blocks(): pl.pallas_call(kernel, grid_spec=pltpu.PrefetchScalarGridSpec(num_scalar_...  51.8 us
    ppermute x46, starting transfers between devices, swap(): return lax.ppermute(value, AXES, [(i, i ^ mask) for i in range(total)])  50.6 us
    pallas_call x1, Pallas kernels, mlp(): pl.pallas_call(functools.partial(mlp_kernel, masks, n_t), grid_spec=pltpu...  34.9 us
    pallas_call x1, Pallas kernels, attention(): pl.pallas_call(functools.partial(attention_kernel, masks), grid_spec=pltp...  33.6 us
    all_to_all x1, waiting for transfers between devices, per_device(): lax.all_to_all(packed, AXES, split_axis=0, concat_axis=0, tiled=True)  27 us
    pallas_call x1, Pallas kernels, grads_cols(): pl.pallas_call(grads_cols_kernel, grid_spec=pltpu.PrefetchScalarGridSpec(...  21 us
    pallas_call x1, Pallas kernels, grads_attention(): pl.pallas_call(grads_attention_kernel, grid_spec=pltpu.PrefetchScalarGrid...  18.9 us
  transfers between devices with their start and end apart: 52, of which 23 were waited for; matrix products, arithmetic and copies ran while one was open for 12% of the time, Pallas kernels for 34%

profile of v6, /device:TPU:0, one launch (start us, length us, event | category | flops | bytes accessed | tf_op | source)
XLA Modules:
  0.0 547.8 jit_solution(11388788432789331906)
XLA Ops:
  0.7 3.1 collective-permute-start
  6.8 2.7 collective-permute-start.2
  11.9 2.6 all-to-all-start
  15.2 6.7 %prep.1 = (bf16[8,128,384]{2,1,0:T(8,128)(2,1)}, bf16[8,128,768]{2,1,0:T(8,128)(2,1)}) custom-call(f32[128,3072]{1,0:T(8,128)} %w.3, f32[128,5632]{1,0:T(8,128)} %w.2), custom_call_target="tpu_custom_call" | custom-call | bytes 14417920 | tf_op jit(solution)/shard_map/prep/pallas_call | solution.py:157
  21.9 27.0 %all-to-all-done = f32[32,1,384]{2,1,0:T(1,128)S(1)} async-done(((f32[32,1,384]{2,1,0:T(1,128)}), f32[32,1,384]{2,1,0:T(1,128)S(1)}, u32[]{:S(2)}, u32[]{:S(2)}) %all-to-all-start) | async-done | bytes 49184 | tf_op jit(solution)/shard_map/all_to_all | solution.py:737
  49.8 3.6 all-to-all-start.1
  64.0 13.0 %collective-permute-done.4.rest_5_.rest_1_ = bf16[1,128,1024]{2,1,0:T(8,128)(2,1)} collective-permute-done((bf16[1,128,1024]{2,1,0:T(8,128)(2,1)}, bf16[1,128,1024]{2,1,0:T(8,128)(2,1)}, u32[]{:S(2)}, u32[]{:S(2)}) %collective-permute-start.4) | collective-permute-done | bytes 262176 | tf_op jit(solution)/shard_map/ppermute | solution.py:713
  85.4 36.4 %collective-permute-done.8.rest_11_.rest_7_ = bf16[1,384,1024]{2,1,0:T(8,128)(2,1)S(1)} collective-permute-done((bf16[1,384,1024]{2,1,0:T(8,128)(2,1)S(1)}, bf16[1,384,1024]{2,1,0:T(8,128)(2,1)S(1)}, u32[]{:S(2)}, u32[]{:S(2)}) %collective-permute-start.8) | collective-permute-done | bytes 786464 | tf_op jit(solution)/shard_map/ppermute | solution.py:713
  121.9 2.3 collective-permute-done.6.rest_1_.rest_5_
  128.2 2.3 constant_dynamic-update-slice_fusion.2
  137.2 2.3 constant_dynamic-update-slice_fusion.1
  139.5 19.3 %collective-permute-done.11.rest_5_.rest_9_ = bf16[3,128,768]{2,1,0:T(8,128)(2,1)S(1)} collective-permute-done((bf16[3,128,768]{2,1,0:T(8,128)(2,1)S(1)}, bf16[3,128,768]{2,1,0:T(8,128)(2,1)S(1)}, u32[]{:S(2)}, u32[]{:S(2)}) %collective-permute-start.11) | collective-permute-done | bytes 589856 | tf_op jit(solution)/shard_map/ppermute | solution.py:713
  158.8 6.4 %collective-permute-done.12.rest_6_.rest_10_ = bf16[3,128,768]{2,1,0:T(8,128)(2,1)S(1)} collective-permute-done((bf16[3,128,768]{2,1,0:T(8,128)(2,1)S(1)}, bf16[3,128,768]{2,1,0:T(8,128)(2,1)S(1)}, u32[]{:S(2)}, u32[]{:S(2)}) %collective-permute-start.12) | collective-permute-done | bytes 589856 | tf_op jit(solution)/shard_map/ppermute | solution.py:713
  165.2 7.6 %collective-permute-done.15 = bf16[256,2048]{1,0:T(8,128)(2,1)S(1)} collective-permute-done((bf16[256,2048]{1,0:T(8,128)(2,1)S(1)}, bf16[256,2048]{1,0:T(8,128)(2,1)S(1)}, u32[]{:S(2)}, u32[]{:S(2)}) %collective-permute-start.15) | collective-permute-done | bytes 1048608 | tf_op jit(solution)/shard_map/ppermute | solution.py:713
  175.5 3.7 all-to-all-start.2
  179.3 15.6 %collective-permute-done.16.rest_7_.rest_11_ = bf16[3,128,768]{2,1,0:T(8,128)(2,1)S(1)} collective-permute-done((bf16[3,128,768]{2,1,0:T(8,128)(2,1)S(1)}, bf16[3,128,768]{2,1,0:T(8,128)(2,1)S(1)}, u32[]{:S(2)}, u32[]{:S(2)}) %collective-permute-start.16) | collective-permute-done | bytes 589856 | tf_op jit(solution)/shard_map/ppermute | solution.py:713
  198.6 34.9 %mlp.1 = (bf16[2048,2048]{1,0:T(8,128)(2,1)}, bf16[2048,2048]{1,0:T(8,128)(2,1)}, bf16[2048,768]{1,0:T(8,128)(2,1)}, bf16[2,2048,768]{2,1,0:T(8,128)(2,1)}) custom-call(s32[4]{0:T(128)} %pad_add_fusion.1.here, f32[2,2048]{1,0:T(2,128)} %slice.184.vec, bf16[1024,2048]{1,0:T(8,128)(2,1)} %constant_dynamic-update-slice_fusion.x_even, ...), custom_call_target="tpu_custom_call" | custom-call | tf_op jit(solution)/shard_map/mlp/pallas_call | solution.py:300
  235.9 11.5 %grads_down.1 = (bf16[384,1024]{1,0:T(8,128)(2,1)}, f32[384,1024]{1,0:T(8,128)}, bf16[384,1024]{1,0:T(8,128)(2,1)}, f32[384,1024]{1,0:T(8,128)}) custom-call(s32[2]{0:T(128)} %pad_add_fusion.where, bf16[2048,768]{1,0:T(8,128)(2,1)} %get-tuple-element.221.far.near.hidden, bf16[2048,768]{1,0:T(8,128)(2,1)} %get-tuple-element.221.far.near.hidden, ...), custom_call_target="tpu_custom_call" | custom-call | flops 6442450944 | bytes 16252928 | tf_op jit(solution)/shard_map/grads_down/pallas_call | solution.py:517
  247.4 5.3 collective-permute-done.22.rest_3_
  253.5 21.0 %grads_gate_up.1 = (bf16[1024,768]{1,0:T(8,128)(2,1)}, f32[1024,768]{1,0:T(8,128)}, bf16[1024,768]{1,0:T(8,128)(2,1)}, f32[1024,768]{1,0:T(8,128)}) custom-call(s32[2]{0:T(128)} %pad_add_fusion.where, bf16[2048,2048]{1,0:T(8,128)(2,1)} %get-tuple-element.228.left.normed.tall, bf16[2,2048,768]{2,1,0:T(8,128)(2,1)} %get-tuple-element.229.d_sent.d_kept.d_joined, ...), custom_call_target="tpu_custom_call" | custom-call | tf_op jit(solution)/shard_map/grads_gate_up/pallas_call | solution.py:484
  279.2 33.6 %attention.1 = (bf16[2048,256]{1,0:T(8,128)(2,1)}, bf16[2048,768]{1,0:T(8,128)(2,1)}, f32[8,1,768]{2,1,0:T(1,128)}) custom-call(s32[4]{0:T(128)} %pad_add_fusion.1.here, s32[8]{0:T(128)} %convert_element_type.294.lengths, bf16[2048,2048]{1,0:T(8,128)(2,1)} %get-tuple-element.228.left.normed.tall, bf16[2048,2048]{1,0:T(8,128)(2,1)} %get-tuple-element.222.dy_sent.dy_kept.dy, ...), custom_call_target="tpu_custom_call" | custom-call | flops 12884901888 | bytes 41943040 | tf_op jit(solution)/shard_map/attention/pallas_call | solution.py:413
  316.7 16.9 %branch_rows.1 = (bf16[1024,2048]{1,0:T(8,128)(2,1)}, bf16[1024,2048]{1,0:T(8,128)(2,1)}) custom-call(s32[4]{0:T(128)} %pad_add_fusion.1.here, bf16[2048,256]{1,0:T(8,128)(2,1)} %get-tuple-element.261.o.left, bf16[2048,768]{1,0:T(8,128)(2,1)} %get-tuple-element.221.far.near.hidden, bf16[1,128,1024]{2,1,0:T(8,128)(2,1)} %convert_bitcast_fusion.rest_4_.rest_0_, ...), custom_call_target="tpu_custom_call" | custom-call | tf_op jit(solution)/shard_map/branch_rows/pallas_call | solution.py:612
  337.6 18.9 %grads_attention.1 = (bf16[2,4,1024,128]{3,2,1,0:T(8,128)(2,1)}, f32[2,4,1024,128]{3,2,1,0:T(8,128)}) custom-call(s32[2]{0:T(128)} %pad_add_fusion.where, bf16[2048,2048]{1,0:T(8,128)(2,1)} %get-tuple-element.228.left.normed.tall, bf16[2048,768]{1,0:T(8,128)(2,1)} %get-tuple-element.270.d_qkv, bf16[2048,256]{1,0:T(8,128)(2,1)} %get-tuple-element.261.o.left, ...), custom_call_target="tpu_custom_call" | custom-call | tf_op jit(solution)/shard_map/grads_attention/pallas_call | solution.py:571
  356.5 3.2 slice_bitcast_fusion.1
  359.7 5.9 %collective-permute-done.28 = bf16[8,48,768]{2,1,0:T(8,128)(2,1)S(1)} collective-permute-done((bf16[8,48,768]{2,1,0:T(8,128)(2,1)}, bf16[8,48,768]{2,1,0:T(8,128)(2,1)S(1)}, u32[]{:S(2)}, u32[]{:S(2)}) %collective-permute-start.28) | collective-permute-done | bytes 589856 | tf_op jit(solution)/shard_map/ppermute | solution.py:713
  370.3 3.3 collective-permute-start.31
  373.6 17.5 %normal_rows_sent.1 = bf16[1024,2048]{1,0:T(8,128)(2,1)} custom-call(s32[4]{0:T(128)} %pad_add_fusion.1.here, bf16[2048,768]{1,0:T(8,128)(2,1)} %get-tuple-element.270.d_qkv, bf16[2,2048,768]{2,1,0:T(8,128)(2,1)} %get-tuple-element.229.d_sent.d_kept.d_joined, bf16[8,128,384]{2,1,0:T(8,128)(2,1)} %copy-done.6, bf16[8,128,384]{2,1,0:T(8,128)(2,1)} %copy-done.18, ...), custom_call_target="tpu_custom_call" | custom-call | tf_op jit(solution)/shard_map/normal_rows_sent/pallas_call | solution.py:612
  391.1 8.7 %collective-permute-done.31 = bf16[8,48,768]{2,1,0:T(8,128)(2,1)} collective-permute-done((bf16[8,48,768]{2,1,0:T(8,128)(2,1)}, bf16[8,48,768]{2,1,0:T(8,128)(2,1)}, u32[]{:S(2)}, u32[]{:S(2)}) %collective-permute-start.31) | collective-permute-done | bytes 589856 | tf_op jit(solution)/shard_map/ppermute | solution.py:713
  406.5 2.9 fusion
  409.4 3.8 all-to-all-start.3
  416.7 17.5 %normal_rows_kept.1 = bf16[1024,2048]{1,0:T(8,128)(2,1)} custom-call(s32[4]{0:T(128)} %pad_add_fusion.1.here, bf16[2048,768]{1,0:T(8,128)(2,1)} %get-tuple-element.270.d_qkv, bf16[2,2048,768]{2,1,0:T(8,128)(2,1)} %get-tuple-element.229.d_sent.d_kept.d_joined, bf16[8,128,384]{2,1,0:T(8,128)(2,1)} %copy-done.6, bf16[8,128,384]{2,1,0:T(8,128)(2,1)} %copy-done.18, ...), custom_call_target="tpu_custom_call" | custom-call | tf_op jit(solution)/shard_map/normal_rows_kept/pallas_call | solution.py:612
  434.2 2.7 collective-permute-done.35
  439.2 3.0 fusion.26
  442.2 3.1 fusion.18
  452.0 10.3 %finish_gate_up.1 = (f32[128,5632]{1,0:T(8,128)}, f32[128,5632]{1,0:T(8,128)}, f32[128,5632]{1,0:T(8,128)}) custom-call(bf16[8,128,768]{2,1,0:T(8,128)(2,1)} %copy-done.8, f32[128,5632]{1,0:T(8,128)} %w.2, f32[128,5632]{1,0:T(8,128)} %m.2, f32[128,5632]{1,0:T(8,128)} %v.2), custom_call_target="tpu_custom_call" | custom-call | flops 14417920 | bytes 18743296 | tf_op jit(solution)/shard_map/finish_gate_up/pallas_call | solution.py:215
  462.3 2.2 fusion.31
  464.5 2.4 fusion.21
  466.9 15.8 %collective-permute-done.39 = bf16[2,256,768]{2,1,0:T(8,128)(2,1)S(1)} collective-permute-done((bf16[2,256,768]{2,1,0:T(8,128)(2,1)}, bf16[2,256,768]{2,1,0:T(8,128)(2,1)S(1)}, u32[]{:S(2)}, u32[]{:S(2)}) %collective-permute-start.39) | collective-permute-done | bytes 786464 | tf_op jit(solution)/shard_map/ppermute | solution.py:713
  482.7 3.1 collective-permute-done.40
  488.0 2.6 fusion.20
  495.5 5.1 multiply_subtract_fusion
  500.6 3.2 collective-permute-done.42
  509.7 3.8 all-to-all-start.4
  516.8 2.9 multiply_subtract_fusion.1
  521.4 4.2 all-to-all-start.5
  535.0 2.4 fusion.11
  537.4 2.5 all-to-all-done.5.g
  539.8 7.5 %finish_qkv.1 = (f32[128,3072]{1,0:T(8,128)}, f32[128,3072]{1,0:T(8,128)}, f32[128,3072]{1,0:T(8,128)}) custom-call(bf16[8,3,128,128]{3,2,1,0:T(8,128)(2,1)} %all-to-all-done.5.g, f32[128,3072]{1,0:T(8,128)} %w.3, f32[128,3072]{1,0:T(8,128)} %m.3, f32[128,3072]{1,0:T(8,128)} %v.3), custom_call_target="tpu_custom_call" | custom-call | flops 7864320 | bytes 10223616 | tf_op jit(solution)/shard_map/finish_qkv/pallas_call | solution.py:215
  (291 shorter events, 109.7 us)
Async XLA Ops:
  0.7 48.2 %collective-permute-start = (bf16[256,2048]{1,0:T(8,128)(2,1)}, bf16[256,2048]{1,0:T(8,128)(2,1)}, u32[]{:S(2)}, u32[]{:S(2)}) collective-permute-start(bf16[256,2048]{1,0:T(8,128)(2,1)} %param.18), channel_id=1, source_target_pairs={{0,8},{1,9},{2,10},{3,11},{4,12},{5,13},{6,14},{7,15},{8,0},{9,1},... | collective-permute-start | bytes 3145736 | tf_op jit(solution)/shard_map/ppermute | solution.py:713
  3.8 45.1 %collective-permute-start.1 = (bf16[256,2048]{1,0:T(8,128)(2,1)}, bf16[256,2048]{1,0:T(8,128)(2,1)}, u32[]{:S(2)}, u32[]{:S(2)}) collective-permute-start(bf16[256,2048]{1,0:T(8,128)(2,1)} %param.18), channel_id=1, source_target_pairs={{0,4},{1,5},{2,6},{3,7},{4,0},{5,1},{6,2},{7,3},{8,12},{9,13},{10,... | collective-permute-start | bytes 3145736 | tf_op jit(solution)/shard_map/ppermute | solution.py:713
  6.8 42.0 %collective-permute-start.2 = (bf16[1,384,1024]{2,1,0:T(8,128)(2,1)S(1)}, bf16[1,384,1024]{2,1,0:T(8,128)(2,1)S(1)}, u32[]{:S(2)}, u32[]{:S(2)}) collective-permute-start(bf16[1,384,1024]{2,1,0:T(8,128)(2,1)S(1)} %pad_bitcast_fusion.rest_8_.rest_4_), channel_id=1, source_target_pairs={{0,16},{1,17},{2,18},{3,19},{4,20},{5,21},{6,22},{7,23},{8,24},{9,... | collective-permute-start | bytes 2359304 | tf_op jit(solution)/shard_map/ppermute | solution.py:713
  9.5 39.4 %collective-permute-start.3 = (bf16[1,384,1024]{2,1,0:T(8,128)(2,1)S(1)}, bf16[1,384,1024]{2,1,0:T(8,128)(2,1)S(1)}, u32[]{:S(2)}, u32[]{:S(2)}) collective-permute-start(bf16[1,384,1024]{2,1,0:T(8,128)(2,1)S(1)} %pad_bitcast_fusion.rest_8_.rest_4_), channel_id=1, source_target_pairs={{0,1},{1,0},{2,3},{3,2},{4,5},{5,4},{6,7},{7,6},{8,9},{9,8},{10,11... | collective-permute-start | bytes 2359304 | tf_op jit(solution)/shard_map/ppermute | solution.py:713
  11.9 36.9 %all-to-all-start = ((f32[32,1,384]{2,1,0:T(1,128)}), f32[32,1,384]{2,1,0:T(1,128)S(1)}, u32[]{:S(2)}, u32[]{:S(2)}) async-start(f32[32,1,384]{2,1,0:T(1,128)} %broadcast_in_dim.60), calls=%async_computation | async-start | bytes 98304 | tf_op jit(solution)/shard_map/all_to_all | solution.py:737
  49.8 29.2 %all-to-all-start.1 = ((bf16[8,128,768]{2,1,0:T(8,128)(2,1)}), bf16[8,128,768]{2,1,0:T(8,128)(2,1)S(1)}, u32[]{:S(2)}, u32[]{:S(2)}) async-start(bf16[8,128,768]{2,1,0:T(8,128)(2,1)} %get-tuple-element.180), calls=%async_computation.1 | async-start | bytes 3145728 | tf_op jit(solution)/shard_map/all_to_all | solution.py:716
  56.7 20.3 %collective-permute-start.4 = (bf16[1,128,1024]{2,1,0:T(8,128)(2,1)}, bf16[1,128,1024]{2,1,0:T(8,128)(2,1)}, u32[]{:S(2)}, u32[]{:S(2)}) collective-permute-start(bf16[1,128,1024]{2,1,0:T(8,128)(2,1)} %convert_bitcast_fusion.rest_4_.rest_0_), channel_id=1, source_target_pairs={{0,16},{1,17},{2,18},{3,19},{4,20},{5,21},{6,22},{7,23},{8,24},{9,... | collective-permute-start | bytes 786440 | tf_op jit(solution)/shard_map/ppermute | solution.py:713
  57.0 20.1 %collective-permute-start.5 = (bf16[1,128,1024]{2,1,0:T(8,128)(2,1)}, bf16[1,128,1024]{2,1,0:T(8,128)(2,1)}, u32[]{:S(2)}, u32[]{:S(2)}) collective-permute-start(bf16[1,128,1024]{2,1,0:T(8,128)(2,1)} %convert_bitcast_fusion.rest_4_.rest_0_), channel_id=1, source_target_pairs={{0,1},{1,0},{2,3},{3,2},{4,5},{5,4},{6,7},{7,6},{8,9},{9,8},{10,11... | collective-permute-start | bytes 786440 | tf_op jit(solution)/shard_map/ppermute | solution.py:713
  79.0 45.1 %collective-permute-start.10 = (bf16[256,2048]{1,0:T(8,128)(2,1)}, bf16[256,2048]{1,0:T(8,128)(2,1)S(1)}, u32[]{:S(2)}, u32[]{:S(2)}) collective-permute-start(bf16[256,2048]{1,0:T(8,128)(2,1)} %param.19), channel_id=1, source_target_pairs={{0,4},{1,5},{2,6},{3,7},{4,0},{5,1},{6,2},{7,3},{8,12},{9,13},{10,... | collective-permute-start | bytes 3145736 | tf_op jit(solution)/shard_map/ppermute | solution.py:713
  80.5 45.7 %collective-permute-start.9 = (bf16[256,2048]{1,0:T(8,128)(2,1)}, bf16[256,2048]{1,0:T(8,128)(2,1)S(1)}, u32[]{:S(2)}, u32[]{:S(2)}) collective-permute-start(bf16[256,2048]{1,0:T(8,128)(2,1)} %param.19), channel_id=1, source_target_pairs={{0,8},{1,9},{2,10},{3,11},{4,12},{5,13},{6,14},{7,15},{8,0},{9,1},... | collective-permute-start | bytes 3145736 | tf_op jit(solution)/shard_map/ppermute | solution.py:713
  81.0 43.1 %collective-permute-start.6 = (bf16[5,128,768]{2,1,0:T(8,128)(2,1)S(1)}, bf16[5,128,768]{2,1,0:T(8,128)(2,1)S(1)}, u32[]{:S(2)}, u32[]{:S(2)}) collective-permute-start(bf16[5,128,768]{2,1,0:T(8,128)(2,1)S(1)} %slice.189.rest_0_.rest_4_), channel_id=1, source_target_pairs={{0,16},{1,17},{2,18},{3,19},{4,20},{5,21},{6,22},{7,23},{8,24},{9,... | collective-permute-start | bytes 2949128 | tf_op jit(solution)/shard_map/ppermute | solution.py:713
  82.3 41.9 %collective-permute-start.7 = (bf16[5,128,768]{2,1,0:T(8,128)(2,1)S(1)}, bf16[5,128,768]{2,1,0:T(8,128)(2,1)S(1)}, u32[]{:S(2)}, u32[]{:S(2)}) collective-permute-start(bf16[5,128,768]{2,1,0:T(8,128)(2,1)S(1)} %slice.189.rest_0_.rest_4_), channel_id=1, source_target_pairs={{0,1},{1,0},{2,3},{3,2},{4,5},{5,4},{6,7},{7,6},{8,9},{9,8},{10,11... | collective-permute-start | bytes 2949128 | tf_op jit(solution)/shard_map/ppermute | solution.py:713
  82.7 39.2 %collective-permute-start.8 = (bf16[1,384,1024]{2,1,0:T(8,128)(2,1)S(1)}, bf16[1,384,1024]{2,1,0:T(8,128)(2,1)S(1)}, u32[]{:S(2)}, u32[]{:S(2)}) collective-permute-start(bf16[1,384,1024]{2,1,0:T(8,128)(2,1)S(1)} %collective-permute-done.2.rest_9_.rest_5_), channel_id=1, source_target_pairs={{0,1},{1,0},{2,3},{3,2},{4,5},{5,4},{6,7},{7,6},{8,9},{9,8},{10,11... | collective-permute-start | bytes 2359304 | tf_op jit(solution)/shard_map/ppermute | solution.py:713
  126.2 39.1 %collective-permute-start.14 = (bf16[256,2048]{1,0:T(8,128)(2,1)}, bf16[256,2048]{1,0:T(8,128)(2,1)S(1)}, u32[]{:S(2)}, u32[]{:S(2)}) collective-permute-start(bf16[256,2048]{1,0:T(8,128)(2,1)} %collective-permute-done), channel_id=1, source_target_pairs={{0,4},{1,5},{2,6},{3,7},{4,0},{5,1},{6,2},{7,3},{8,12},{9,13},{10,... | collective-permute-start | bytes 3145736 | tf_op jit(solution)/shard_map/ppermute | solution.py:713
  126.7 46.2 %collective-permute-start.15 = (bf16[256,2048]{1,0:T(8,128)(2,1)S(1)}, bf16[256,2048]{1,0:T(8,128)(2,1)S(1)}, u32[]{:S(2)}, u32[]{:S(2)}) collective-permute-start(bf16[256,2048]{1,0:T(8,128)(2,1)S(1)} %collective-permute-done.9), channel_id=1, source_target_pairs={{0,4},{1,5},{2,6},{3,7},{4,0},{5,1},{6,2},{7,3},{8,12},{9,13},{10,... | collective-permute-start | bytes 3145736 | tf_op jit(solution)/shard_map/ppermute | solution.py:713
  130.5 34.7 %collective-permute-start.13 = (bf16[5,128,768]{2,1,0:T(8,128)(2,1)S(1)}, bf16[5,128,768]{2,1,0:T(8,128)(2,1)S(1)}, u32[]{:S(2)}, u32[]{:S(2)}) collective-permute-start(bf16[5,128,768]{2,1,0:T(8,128)(2,1)S(1)} %collective-permute-done.6.rest_1_.rest_5_), channel_id=1, source_target_pairs={{0,1},{1,0},{2,3},{3,2},{4,5},{5,4},{6,7},{7,6},{8,9},{9,8},{10,11... | collective-permute-start | bytes 2949128 | tf_op jit(solution)/shard_map/ppermute | solution.py:713
  132.0 26.8 %collective-permute-start.11 = (bf16[3,128,768]{2,1,0:T(8,128)(2,1)S(1)}, bf16[3,128,768]{2,1,0:T(8,128)(2,1)S(1)}, u32[]{:S(2)}, u32[]{:S(2)}) collective-permute-start(bf16[3,128,768]{2,1,0:T(8,128)(2,1)S(1)} %slice.190.rest_4_.rest_8_), channel_id=1, source_target_pairs={{0,16},{1,17},{2,18},{3,19},{4,20},{5,21},{6,22},{7,23},{8,24},{9,... | collective-permute-start | bytes 1769480 | tf_op jit(solution)/shard_map/ppermute | solution.py:713
  133.8 31.4 %collective-permute-start.12 = (bf16[3,128,768]{2,1,0:T(8,128)(2,1)S(1)}, bf16[3,128,768]{2,1,0:T(8,128)(2,1)S(1)}, u32[]{:S(2)}, u32[]{:S(2)}) collective-permute-start(bf16[3,128,768]{2,1,0:T(8,128)(2,1)S(1)} %slice.190.rest_4_.rest_8_), channel_id=1, source_target_pairs={{0,1},{1,0},{2,3},{3,2},{4,5},{5,4},{6,7},{7,6},{8,9},{9,8},{10,11... | collective-permute-start | bytes 1769480 | tf_op jit(solution)/shard_map/ppermute | solution.py:713
  173.9 21.0 %collective-permute-start.18 = (bf16[1024,2048]{1,0:T(8,128)(2,1)}, bf16[1024,2048]{1,0:T(8,128)(2,1)}, u32[]{:S(2)}, u32[]{:S(2)}) collective-permute-start(bf16[1024,2048]{1,0:T(8,128)(2,1)} %constant_dynamic-update-slice_fusion.4.dy_even), channel_id=1, source_target_pairs={{0,2},{1,3},{2,0},{3,1},{4,6},{5,7},{6,4},{7,5},{8,10},{9,11},{10,... | collective-permute-start | bytes 12582920 | tf_op jit(solution)/shard_map/ppermute | solution.py:713
  175.0 20.0 %collective-permute-start.17 = (bf16[1024,2048]{1,0:T(8,128)(2,1)}, bf16[1024,2048]{1,0:T(8,128)(2,1)}, u32[]{:S(2)}, u32[]{:S(2)}) collective-permute-start(bf16[1024,2048]{1,0:T(8,128)(2,1)} %constant_dynamic-update-slice_fusion.x_even), channel_id=1, source_target_pairs={{0,2},{1,3},{2,0},{3,1},{4,6},{5,7},{6,4},{7,5},{8,10},{9,11},{10,... | collective-permute-start | bytes 12582920 | tf_op jit(solution)/shard_map/ppermute | solution.py:713
  175.5 19.5 %all-to-all-start.2 = ((bf16[8,128,384]{2,1,0:T(8,128)(2,1)}), bf16[8,128,384]{2,1,0:T(8,128)(2,1)S(1)}, u32[]{:S(2)}, u32[]{:S(2)}) async-start(bf16[8,128,384]{2,1,0:T(8,128)(2,1)} %get-tuple-element.196), calls=%async_computation.2 | async-start | bytes 1572864 | tf_op jit(solution)/shard_map/all_to_all | solution.py:716
  179.2 15.7 %collective-permute-start.16 = (bf16[3,128,768]{2,1,0:T(8,128)(2,1)S(1)}, bf16[3,128,768]{2,1,0:T(8,128)(2,1)S(1)}, u32[]{:S(2)}, u32[]{:S(2)}) collective-permute-start(bf16[3,128,768]{2,1,0:T(8,128)(2,1)S(1)} %collective-permute-done.11.rest_5_.rest_9_), channel_id=1, source_target_pairs={{0,1},{1,0},{2,3},{3,2},{4,5},{5,4},{6,7},{7,6},{8,9},{9,8},{10,11... | collective-permute-start | bytes 1769480 | tf_op jit(solution)/shard_map/ppermute | solution.py:713
  195.0 38.6 %collective-permute-start.19 = (bf16[8,128,384]{2,1,0:T(8,128)(2,1)S(1)}, bf16[8,128,384]{2,1,0:T(8,128)(2,1)S(1)}, u32[]{:S(2)}, u32[]{:S(2)}) collective-permute-start(bf16[8,128,384]{2,1,0:T(8,128)(2,1)S(1)} %all-to-all-done.2.rest_0_), channel_id=1, source_target_pairs={{0,16},{1,17},{2,18},{3,19},{4,20},{5,21},{6,22},{7,23},{8,24},{9,... | collective-permute-start | bytes 2359304 | tf_op jit(solution)/shard_map/ppermute | solution.py:713
  195.9 37.7 %collective-permute-start.20 = (bf16[8,128,384]{2,1,0:T(8,128)(2,1)S(1)}, bf16[8,128,384]{2,1,0:T(8,128)(2,1)S(1)}, u32[]{:S(2)}, u32[]{:S(2)}) collective-permute-start(bf16[8,128,384]{2,1,0:T(8,128)(2,1)S(1)} %all-to-all-done.2.rest_0_), channel_id=1, source_target_pairs={{0,1},{1,0},{2,3},{3,2},{4,5},{5,4},{6,7},{7,6},{8,9},{9,8},{10,11... | collective-permute-start | bytes 2359304 | tf_op jit(solution)/shard_map/ppermute | solution.py:713
  196.7 36.8 %collective-permute-start.21 = (bf16[1,128,1024]{2,1,0:T(8,128)(2,1)}, bf16[1,128,1024]{2,1,0:T(8,128)(2,1)S(1)}, u32[]{:S(2)}, u32[]{:S(2)}) collective-permute-start(bf16[1,128,1024]{2,1,0:T(8,128)(2,1)} %collective-permute-done.4.rest_5_.rest_1_), channel_id=1, source_target_pairs={{0,1},{1,0},{2,3},{3,2},{4,5},{5,4},{6,7},{7,6},{8,9},{9,8},{10,11... | collective-permute-start | bytes 786440 | tf_op jit(solution)/shard_map/ppermute | solution.py:713
  234.5 18.3 %collective-permute-start.22 = (bf16[8,128,384]{2,1,0:T(8,128)(2,1)S(1)}, bf16[8,128,384]{2,1,0:T(8,128)(2,1)S(1)}, u32[]{:S(2)}, u32[]{:S(2)}) collective-permute-start(bf16[8,128,384]{2,1,0:T(8,128)(2,1)S(1)} %collective-permute-done.19.rest_1_), channel_id=1, source_target_pairs={{0,1},{1,0},{2,3},{3,2},{4,5},{5,4},{6,7},{7,6},{8,9},{9,8},{10,11... | collective-permute-start | bytes 2359304 | tf_op jit(solution)/shard_map/ppermute | solution.py:713
  252.8 21.8 %collective-permute-start.23 = (bf16[384,1024]{1,0:T(8,128)(2,1)}, bf16[384,1024]{1,0:T(8,128)(2,1)S(1)}, u32[]{:S(2)}, u32[]{:S(2)}) collective-permute-start(bf16[384,1024]{1,0:T(8,128)(2,1)} %get-tuple-element.232), channel_id=1, source_target_pairs={{0,1},{1,0},{2,3},{3,2},{4,5},{5,4},{6,7},{7,6},{8,9},{9,8},{10,11... | collective-permute-start | bytes 2359304 | tf_op jit(solution)/shard_map/ppermute | solution.py:713
  274.6 38.3 %collective-permute-start.25 = (bf16[1024,768]{1,0:T(8,128)(2,1)}, bf16[1024,768]{1,0:T(8,128)(2,1)S(1)}, u32[]{:S(2)}, u32[]{:S(2)}) collective-permute-start(bf16[1024,768]{1,0:T(8,128)(2,1)} %get-tuple-element.238), channel_id=1, source_target_pairs={{0,1},{1,0},{2,3},{3,2},{4,5},{5,4},{6,7},{7,6},{8,9},{9,8},{10,11... | collective-permute-start | bytes 4718600 | tf_op jit(solution)/shard_map/ppermute | solution.py:713
  277.0 35.8 %collective-permute-start.24 = (bf16[384,1024]{1,0:T(8,128)(2,1)}, bf16[384,1024]{1,0:T(8,128)(2,1)S(1)}, u32[]{:S(2)}, u32[]{:S(2)}) collective-permute-start(bf16[384,1024]{1,0:T(8,128)(2,1)} %add_convert_fusion.4), channel_id=1, source_target_pairs={{0,16},{1,17},{2,18},{3,19},{4,20},{5,21},{6,22},{7,23},{8,24},{9,... | collective-permute-start | bytes 2359304 | tf_op jit(solution)/shard_map/ppermute | solution.py:713
  312.8 21.7 %collective-permute-start.27 = (bf16[512,768]{1,0:T(8,128)(2,1)S(1)}, bf16[512,768]{1,0:T(8,128)(2,1)}, u32[]{:S(2)}, u32[]{:S(2)}) collective-permute-start(bf16[512,768]{1,0:T(8,128)(2,1)S(1)} %get-tuple-element.257), channel_id=1, source_target_pairs={{0,1},{1,0},{2,3},{3,2},{4,5},{5,4},{6,7},{7,6},{8,9},{9,8},{10,11... | collective-permute-start | bytes 2359304 | tf_op jit(solution)/shard_map/ppermute | solution.py:713
  315.6 18.9 %collective-permute-start.26 = (bf16[8,32,768]{2,1,0:T(8,128)(2,1)}, bf16[8,32,768]{2,1,0:T(8,128)(2,1)S(1)}, u32[]{:S(2)}, u32[]{:S(2)}) collective-permute-start(bf16[8,32,768]{2,1,0:T(8,128)(2,1)} %fusion.27), channel_id=1, source_target_pairs={{0,16},{1,17},{2,18},{3,19},{4,20},{5,21},{6,22},{7,23},{8,24},{9,... | collective-permute-start | bytes 1179656 | tf_op jit(solution)/shard_map/ppermute | solution.py:713
  335.3 30.3 %collective-permute-start.29 = (bf16[1024,2048]{1,0:T(8,128)(2,1)}, bf16[1024,2048]{1,0:T(8,128)(2,1)S(1)}, u32[]{:S(2)}, u32[]{:S(2)}) collective-permute-start(bf16[1024,2048]{1,0:T(8,128)(2,1)} %get-tuple-element.266), channel_id=1, source_target_pairs={{0,2},{1,3},{2,0},{3,1},{4,6},{5,7},{6,4},{7,5},{8,10},{9,11},{10,... | collective-permute-start | bytes 12582920 | tf_op jit(solution)/shard_map/ppermute | solution.py:713
  335.3 30.2 %collective-permute-start.30 = (bf16[512,768]{1,0:T(8,128)(2,1)S(1)}, bf16[512,768]{1,0:T(8,128)(2,1)S(1)}, u32[]{:S(2)}, u32[]{:S(2)}) collective-permute-start(bf16[512,768]{1,0:T(8,128)(2,1)S(1)} %get-tuple-element.267), channel_id=1, source_target_pairs={{0,1},{1,0},{2,3},{3,2},{4,5},{5,4},{6,7},{7,6},{8,9},{9,8},{10,11... | collective-permute-start | bytes 2359304 | tf_op jit(solution)/shard_map/ppermute | solution.py:713
  336.4 29.2 %collective-permute-start.28 = (bf16[8,48,768]{2,1,0:T(8,128)(2,1)}, bf16[8,48,768]{2,1,0:T(8,128)(2,1)S(1)}, u32[]{:S(2)}, u32[]{:S(2)}) collective-permute-start(bf16[8,48,768]{2,1,0:T(8,128)(2,1)} %get-tuple-element.265), channel_id=1, source_target_pairs={{0,16},{1,17},{2,18},{3,19},{4,20},{5,21},{6,22},{7,23},{8,24},{9,... | collective-permute-start | bytes 1769480 | tf_op jit(solution)/shard_map/ppermute | solution.py:713
  368.7 33.1 %collective-permute-start.33 = (bf16[2,256,1280]{2,1,0:T(8,128)(2,1)S(1)}, bf16[2,256,1280]{2,1,0:T(8,128)(2,1)S(1)}, u32[]{:S(2)}, u32[]{:S(2)}) collective-permute-start(bf16[2,256,1280]{2,1,0:T(8,128)(2,1)S(1)} %fusion.17), channel_id=1, source_target_pairs={{0,4},{1,5},{2,6},{3,7},{4,0},{5,1},{6,2},{7,3},{8,12},{9,13},{10,... | collective-permute-start | bytes 3932168 | tf_op jit(solution)/shard_map/ppermute | solution.py:713
  369.5 32.4 %collective-permute-start.32 = (bf16[4,1024,128]{2,1,0:T(8,128)(2,1)}, bf16[4,1024,128]{2,1,0:T(8,128)(2,1)}, u32[]{:S(2)}, u32[]{:S(2)}) collective-permute-start(bf16[4,1024,128]{2,1,0:T(8,128)(2,1)} %get-tuple-element.276), channel_id=1, source_target_pairs={{0,1},{1,0},{2,3},{3,2},{4,5},{5,4},{6,7},{7,6},{8,9},{9,8},{10,11... | collective-permute-start | bytes 3145736 | tf_op jit(solution)/shard_map/ppermute | solution.py:713
  370.3 31.5 %collective-permute-start.34 = (bf16[2,256,768]{2,1,0:T(8,128)(2,1)}, bf16[2,256,768]{2,1,0:T(8,128)(2,1)}, u32[]{:S(2)}, u32[]{:S(2)}) collective-permute-start(bf16[2,256,768]{2,1,0:T(8,128)(2,1)} %fusion.25), channel_id=1, source_target_pairs={{0,8},{1,9},{2,10},{3,11},{4,12},{5,13},{6,14},{7,15},{8,0},{9,1},... | collective-permute-start | bytes 2359304 | tf_op jit(solution)/shard_map/ppermute | solution.py:713
  370.3 29.4 %collective-permute-start.31 = (bf16[8,48,768]{2,1,0:T(8,128)(2,1)}, bf16[8,48,768]{2,1,0:T(8,128)(2,1)}, u32[]{:S(2)}, u32[]{:S(2)}) collective-permute-start(bf16[8,48,768]{2,1,0:T(8,128)(2,1)} %get-tuple-element.275), channel_id=1, source_target_pairs={{0,16},{1,17},{2,18},{3,19},{4,20},{5,21},{6,22},{7,23},{8,24},{9,... | collective-permute-start | bytes 1769480 | tf_op jit(solution)/shard_map/ppermute | solution.py:713
  401.9 37.3 %collective-permute-start.36 = (bf16[1024,2048]{1,0:T(8,128)(2,1)}, bf16[1024,2048]{1,0:T(8,128)(2,1)}, u32[]{:S(2)}, u32[]{:S(2)}) collective-permute-start(bf16[1024,2048]{1,0:T(8,128)(2,1)} %normal_rows_sent.1), channel_id=1, source_target_pairs={{0,2},{1,3},{2,0},{3,1},{4,6},{5,7},{6,4},{7,5},{8,10},{9,11},{10,... | collective-permute-start | bytes 12582920 | tf_op jit(solution)/shard_map/ppermute | solution.py:713
  409.4 29.7 %all-to-all-start.3 = ((bf16[8,128,768]{2,1,0:T(8,128)(2,1)}), bf16[8,128,768]{2,1,0:T(8,128)(2,1)S(1)}, u32[]{:S(2)}, u32[]{:S(2)}) async-start(bf16[8,128,768]{2,1,0:T(8,128)(2,1)} %bitcast.124), calls=%async_computation.3 | async-start | bytes 3145728 | tf_op jit(solution)/shard_map/all_to_all | solution.py:716
  413.3 25.9 %collective-permute-start.37 = (bf16[4,1024,128]{2,1,0:T(8,128)(2,1)}, bf16[4,1024,128]{2,1,0:T(8,128)(2,1)}, u32[]{:S(2)}, u32[]{:S(2)}) collective-permute-start(bf16[4,1024,128]{2,1,0:T(8,128)(2,1)} %get-tuple-element.291), channel_id=1, source_target_pairs={{0,1},{1,0},{2,3},{3,2},{4,5},{5,4},{6,7},{7,6},{8,9},{9,8},{10,11... | collective-permute-start | bytes 3145736 | tf_op jit(solution)/shard_map/ppermute | solution.py:713
  414.7 22.2 %collective-permute-start.35 = (bf16[1,1024,128]{2,1,0:T(8,128)(2,1)}, bf16[1,1024,128]{2,1,0:T(8,128)(2,1)S(1)}, u32[]{:S(2)}, u32[]{:S(2)}) collective-permute-start(bf16[1,1024,128]{2,1,0:T(8,128)(2,1)} %slice.258), channel_id=1, source_target_pairs={{0,16},{1,17},{2,18},{3,19},{4,20},{5,21},{6,22},{7,23},{8,24},{9,... | collective-permute-start | bytes 786440 | tf_op jit(solution)/shard_map/ppermute | solution.py:713
  445.3 40.5 %collective-permute-start.38 = (bf16[2,256,1280]{2,1,0:T(8,128)(2,1)}, bf16[2,256,1280]{2,1,0:T(8,128)(2,1)}, u32[]{:S(2)}, u32[]{:S(2)}) collective-permute-start(bf16[2,256,1280]{2,1,0:T(8,128)(2,1)} %fusion.18), channel_id=1, source_target_pairs={{0,4},{1,5},{2,6},{3,7},{4,0},{5,1},{6,2},{7,3},{8,12},{9,13},{10,... | collective-permute-start | bytes 3932168 | tf_op jit(solution)/shard_map/ppermute | solution.py:713
  447.8 34.9 %collective-permute-start.39 = (bf16[2,256,768]{2,1,0:T(8,128)(2,1)}, bf16[2,256,768]{2,1,0:T(8,128)(2,1)S(1)}, u32[]{:S(2)}, u32[]{:S(2)}) collective-permute-start(bf16[2,256,768]{2,1,0:T(8,128)(2,1)} %fusion.26), channel_id=1, source_target_pairs={{0,8},{1,9},{2,10},{3,11},{4,12},{5,13},{6,14},{7,15},{8,0},{9,1},... | collective-permute-start | bytes 2359304 | tf_op jit(solution)/shard_map/ppermute | solution.py:713
  449.5 36.3 %collective-permute-start.40 = (bf16[3,1024,128]{2,1,0:T(8,128)(2,1)S(1)}, bf16[3,1024,128]{2,1,0:T(8,128)(2,1)S(1)}, u32[]{:S(2)}, u32[]{:S(2)}) collective-permute-start(bf16[3,1024,128]{2,1,0:T(8,128)(2,1)S(1)} %slice.259), channel_id=1, source_target_pairs={{0,16},{1,17},{2,18},{3,19},{4,20},{5,21},{6,22},{7,23},{8,24},{9,... | collective-permute-start | bytes 2359304 | tf_op jit(solution)/shard_map/ppermute | solution.py:713
  450.7 35.1 %collective-permute-start.41 = (bf16[384,1024]{1,0:T(8,128)(2,1)}, bf16[384,1024]{1,0:T(8,128)(2,1)S(1)}, u32[]{:S(2)}, u32[]{:S(2)}) collective-permute-start(bf16[384,1024]{1,0:T(8,128)(2,1)} %get-tuple-element.306), channel_id=1, source_target_pairs={{0,1},{1,0},{2,3},{3,2},{4,5},{5,4},{6,7},{7,6},{8,9},{9,8},{10,11... | collective-permute-start | bytes 2359304 | tf_op jit(solution)/shard_map/ppermute | solution.py:713
  513.5 18.4 %collective-permute-start.44 = (bf16[256,1280]{1,0:T(8,128)(2,1)}, bf16[256,1280]{1,0:T(8,128)(2,1)}, u32[]{:S(2)}, u32[]{:S(2)}) collective-permute-start(bf16[256,1280]{1,0:T(8,128)(2,1)} %fusion.21), channel_id=1, source_target_pairs={{0,8},{1,9},{2,10},{3,11},{4,12},{5,13},{6,14},{7,15},{8,0},{9,1},... | collective-permute-start | bytes 1966088 | tf_op jit(solution)/shard_map/ppermute | solution.py:713
  521.4 18.4 %all-to-all-start.5 = ((bf16[8,3,128,128]{3,2,1,0:T(8,128)(2,1)}), bf16[8,3,128,128]{3,2,1,0:T(8,128)(2,1)}, u32[]{:S(2)}, u32[]{:S(2)}) async-start(bf16[8,3,128,128]{3,2,1,0:T(8,128)(2,1)} %bitcast.140), calls=%async_computation.5 | async-start | bytes 1572864 | tf_op jit(solution)/shard_map/all_to_all | solution.py:716
  (64 other events, 859.9 us)
